TPU v7x, 128 devices: a whole 4x4x4 slice. The times are simulated.
128 devices in a mesh: dp: 4 (over y), seq: 32 (over x, z, core).
Axes of the slice: x: 4, y: 4, z: 4, core: 2. Of those that a mesh axis runs over, the one named last changes fastest.
Arguments:
- queries: bfloat16 [4, 4096, 1024], P('dp', 'seq'), may hold values from -6 to 6
- keys: bfloat16 [4, 4096, 1024], P('dp', 'seq'), may hold values from -6 to 6
- values: bfloat16 [4, 4096, 1024], P('dp', 'seq'), may hold values from -6 to 6
- strength: bfloat16 [4, 4096, 8], P('dp', 'seq'), may hold values from 0 to 1
- log_decay: float32 [4, 4096, 8], P('dp', 'seq'), may hold values from -2 to 0
- resets: int32 [4, 64], P('dp', 'seq'), may hold values 0 or 1
- out_weight: bfloat16 [1024, 2048], replicated, may hold values from -0.1875 to 0.1875
- cotangent: bfloat16 [4, 4096, 2048], P('dp', 'seq'), may hold values from -6 to 6
Outputs:
- mixed: bfloat16 [4, 4096, 2048], P('dp', 'seq')
- query_grad: bfloat16 [4, 4096, 1024], P('dp', 'seq')
- key_grad: bfloat16 [4, 4096, 1024], P('dp', 'seq')
- value_grad: bfloat16 [4, 4096, 1024], P('dp', 'seq')
- strength_grad: float32 [4, 4096, 8], P('dp', 'seq')
- decay_grad: float32 [4, 4096, 8], P('dp', 'seq')
- weight_grad: float32 [1024, 2048], P(('dp', 'seq'))
All inputs are finite; a program needn't handle non-finite values. No bound on the sum of `resets` on one device may be relied on, other than what follows from the above.
Results may differ from a plain program's by a relative error of at most 0.0049.
Values sent between devices are 32-bit elements; how exact they have to be, the bound alone decides.
No kernel may reach another device: no remote copies, remote signals or barrier semaphores. Data moves between devices by JAX's collectives and lax.ppermute only.
A program may use at most 192 MiB of HBM per device.

v0:
```python
import math

import jax
import jax.numpy as jnp
from jax import lax
from jax.sharding import PartitionSpec as P

SPAN = 64


HIGH = lax.Precision.HIGHEST
EPS = 1e-06


def entering(value, axis, join, neutral, backward):
    count, mine = (lax.axis_size(axis), lax.axis_index(axis))
    pieces = jax.tree.map(lambda part: lax.all_gather(part, axis), value)
    if backward:
        pieces = jax.tree.map(lambda part: part[::-1], pieces)
        mine = count - 1 - mine
    so_far = jax.tree.map(
        lambda part, zero: jnp.full_like(part, 0) + jnp.asarray(zero, part.dtype), value, neutral
    )

    def step(position, so_far):
        longer = join(so_far, jax.tree.map(lambda part: part[position], pieces))
        return jax.tree.map(lambda new, old: jnp.where(position < mine, new, old), longer, so_far)

    return lax.fori_loop(0, count - 1, step, so_far)


def unit_rows(x):
    return x / jnp.sqrt(jnp.sum(x * x, axis=-1, keepdims=True) + EPS)


def rms_rows(x):
    return x / jnp.sqrt(jnp.mean(x * x, axis=-1, keepdims=True) + EPS)


def to_spans(x, heads, size):
    batch, length = (x.shape[0], x.shape[1])
    parts = x.reshape(batch, length // size, size, heads, -1)
    return parts.transpose(1, 0, 3, 2, 4)


def from_spans(x):
    count, batch, heads, size, width = x.shape
    return x.transpose(1, 0, 3, 2, 4).reshape(batch, count * size, heads * width)


def gates_to_spans(x, size):
    batch, length, heads = x.shape
    return x.reshape(batch, length // size, size, heads).transpose(1, 0, 3, 2)


def block_inverse(keys_n, strength_c, decay_c):
    size = decay_c.shape[-1]
    total = jnp.cumsum(decay_c, axis=-1)
    later = total[..., :, None] - total[..., None, :]
    rows = lax.broadcasted_iota(jnp.int32, (size, size), 0)
    cols = lax.broadcasted_iota(jnp.int32, (size, size), 1)
    below = jnp.where(rows > cols, jnp.exp(jnp.where(rows > cols, later, 0.0)), 0.0)
    key_key = jnp.einsum("...tk,...sk->...ts", keys_n, keys_n, precision=HIGH)
    system = strength_c[..., :, None] * below * key_key
    eye = jnp.eye(size, dtype=decay_c.dtype)
    inverse = eye - system
    power = system
    for level in range(size.bit_length() - 2):
        power = jnp.einsum("...ij,...jk->...ik", power, power, precision=HIGH)
        inverse = inverse + jnp.einsum("...ij,...jk->...ik", inverse, power, precision=HIGH)
    return inverse


def span_step(state, pieces):
    queries, keys_n, values_c, strength_c, decay_c, restart, inverse = pieces
    size = decay_c.shape[-1]
    state = state * (1.0 - restart)[:, None, None, None]
    total = jnp.cumsum(decay_c, axis=-1)
    later = total[..., :, None] - total[..., None, :]
    rows = lax.broadcasted_iota(jnp.int32, (size, size), 0)
    cols = lax.broadcasted_iota(jnp.int32, (size, size), 1)
    inside = jnp.where(rows >= cols, jnp.exp(jnp.where(rows >= cols, later, 0.0)), 0.0)
    growth = jnp.exp(total)
    carried = jnp.einsum("bhtk,bhkv->bhtv", keys_n, state, precision=HIGH)
    target = strength_c[..., None] * (values_c - growth[..., None] * carried)
    deltas = jnp.einsum("bhts,bhsv->bhtv", inverse, target, precision=HIGH)
    query_key = jnp.einsum("bhtk,bhsk->bhts", queries, keys_n, precision=HIGH)
    outputs = growth[..., None] * jnp.einsum("bhtk,bhkv->bhtv", queries, state, precision=HIGH)
    outputs = outputs + jnp.einsum("bhts,bhsv->bhtv", inside * query_key, deltas, precision=HIGH)
    fading = jnp.exp(total[..., -1:] - total)
    new_state = growth[..., -1][..., None, None] * state
    new_state = new_state + jnp.einsum(
        "bhsk,bhsv->bhkv", keys_n * fading[..., None], deltas, precision=HIGH
    )
    return (new_state, outputs)


def carry_only(state, pieces):
    return (span_step(state, pieces)[0], None)


def compose(earlier, later):
    joined = jnp.einsum("bhij,bhjk->bhik", later[0], earlier[0], precision=HIGH)
    moved = jnp.einsum("bhij,bhjk->bhik", later[0], earlier[1], precision=HIGH) + later[1]
    return (joined, moved)


def local(queries, keys, values, strength, log_decay, resets, out_weight, cotangent):
    f32 = jnp.float32
    heads = strength.shape[-1]
    batch, length, width = queries.shape
    depth = width // heads
    n_dp = lax.axis_size("dp")
    n_seq = lax.axis_size("seq")
    restart = resets.T.astype(f32)
    q_wide = queries.astype(f32)
    k_wide = keys.astype(f32)
    v_wide = values.astype(f32)
    b_wide = strength.astype(f32)
    qn = unit_rows(to_spans(q_wide, heads, SPAN))
    kn = unit_rows(to_spans(k_wide, heads, SPAN))
    vv = to_spans(v_wide, heads, SPAN)
    bb = gates_to_spans(b_wide, SPAN)
    gg = gates_to_spans(log_decay, SPAN)
    inverses = block_inverse(kn, bb, gg)
    eye = jnp.broadcast_to(jnp.eye(depth, dtype=f32), (batch, heads, depth, depth))
    blank = jnp.zeros_like(eye)
    start = jnp.concatenate([eye, blank], axis=-1)
    widened = jnp.concatenate([jnp.zeros_like(vv), vv], axis=-1)
    carried, _ = lax.scan(carry_only, start, (qn, kn, widened, bb, gg, restart, inverses))
    carry_map = carried[..., :depth]
    carry_add = carried[..., depth:]
    incoming = entering((carry_map, carry_add), "seq", compose, (eye, blank), False)[1]

    def local_heads(q, k, v, b, g):
        qn_local = unit_rows(to_spans(q, heads, SPAN))
        kn_local = unit_rows(to_spans(k, heads, SPAN))
        b_spans = gates_to_spans(b, SPAN)
        g_spans = gates_to_spans(g, SPAN)
        inverse_local = block_inverse(kn_local, b_spans, g_spans)
        pieces = (
            qn_local,
            kn_local,
            to_spans(v, heads, SPAN),
            b_spans,
            g_spans,
            restart,
            inverse_local,
        )
        final, outs_local = lax.scan(span_step, incoming, pieces)
        return (outs_local, final)

    (heads_local, _), pull = jax.vjp(local_heads, q_wide, k_wide, v_wide, b_wide, log_decay)
    normed_spans, norm_pull = jax.vjp(rms_rows, heads_local)
    normed = from_spans(normed_spans).astype(jnp.bfloat16)
    flat = normed[0]
    cot = cotangent[0]
    mixed = jnp.dot(flat, out_weight, preferred_element_type=f32).astype(jnp.bfloat16)[None]
    back = jnp.einsum("td,ed->te", cot, out_weight, preferred_element_type=f32)[None]
    (grad_out,) = norm_pull(to_spans(back, heads, SPAN))

    def from_start(begin):
        return lax.scan(span_step, begin, (qn, kn, vv, bb, gg, restart, inverses))[1]

    _, start_pull = jax.vjp(from_start, incoming)
    (reach,) = start_pull(grad_out)
    carry_back = jnp.swapaxes(carry_map, -1, -2)
    later_grad = entering((carry_back, reach), "seq", compose, (eye, blank), True)[1]
    grad_q, grad_k, grad_v, grad_b, grad_g = pull((grad_out, later_grad))
    scale = 1.0 / math.sqrt(length * n_seq * n_dp)
    summed = lax.psum_scatter(
        lax.dot_general(flat, cot, (((0,), (0,)), ((), ())), preferred_element_type=f32),
        ("dp", "seq"),
        scatter_dimension=0,
        tiled=True,
    )
    weight_grad = summed * scale
    return (
        mixed,
        grad_q.astype(jnp.bfloat16),
        grad_k.astype(jnp.bfloat16),
        grad_v.astype(jnp.bfloat16),
        grad_b,
        grad_g,
        weight_grad,
    )


def solution(mesh):
    return jax.shard_map(
        local,
        mesh=mesh,
        in_specs=(
            P("dp", "seq", None),
            P("dp", "seq", None),
            P("dp", "seq", None),
            P("dp", "seq", None),
            P("dp", "seq", None),
            P("dp", "seq"),
            P(),
            P("dp", "seq", None),
        ),
        out_specs=(
            P("dp", "seq", None),
            P("dp", "seq", None),
            P("dp", "seq", None),
            P("dp", "seq", None),
            P("dp", "seq", None),
            P("dp", "seq", None),
            P(("dp", "seq"), None),
        ),
        check_vma=False,
    )
```

profile of v0, /device:TPU:1, one launch (start us, length us, event | category | flops | bytes accessed | tf_op | source)
XLA Modules:
  0.0 1229.2 jit_solution(11199271259154415514)
XLA Ops:
  25.8 13.5 %while.164 = (s32[]{:T(128)}, f32[1,8,128,256]{3,2,1,0:T(8,128)S(1)}, f32[2,1,8,64]{3,2,1,0:T(8,128)S(1)}, f32[2,1]{0,1:T(1,128)S(1)}, f32[2,1,8,64,128]{4,3,2,1...) while((s32[]{:T(128)}, ...), condition=%wide.region_4.5_spmd, body=%wide.region_2.4_spmd.sunk | while | flops 504856576 | bytes 7637813 | solution.py:130
  30.5 2.1 fusion.435
  37.2 2.2 fusion.435
  45.0 71.9 %all-gather.9.cloned.1.call-done = f32[32,8,128,128]{3,2,1,0:T(8,128)} async-done(((f32[1,8,128,128]{3,2,1,0:T(8,128)}), f32[32,8,128,128]{3,2,1,0:T(8,128)}) %all-gather.9.cloned.1.call-update) | async-done | bytes 16777232 | tf_op jit(solution)/shard_map/all_gather | solution.py:17
  116.9 74.9 %all-gather.11.cloned.1.call-done = f32[32,8,128,128]{3,2,1,0:T(8,128)} async-done(((f32[1,8,128,128]{3,2,1,0:T(8,128)}), f32[32,8,128,128]{3,2,1,0:T(8,128)}) %all-gather.11.cloned.1.call-update) | async-done | bytes 16777232 | tf_op jit(solution)/shard_map/all_gather | solution.py:17
  191.8 61.2 %while.168 = (s32[]{:T(128)}, f32[1,8,128,128]{3,2,1,0:T(8,128)S(1)}, s32[]{:T(128)}, f32[32,1,8,128,128]{4,3,2,1,0:T(8,128)}, f32[32,1,8,128,128]{4,3,2,1,0:T(8,128)}, /*index=5*/s32[]{:T(128)}, s32[]{:T(128)}) while((s32[]{:T(128)}, f32[1,8,128,128]{3,2,1,0:T(8,128)S(1)}, s32[]{:T(128)}, f32[32,1,8,128,128]{4,3,2,1,0:T(8,128)}, ...), condition=%wide.region_6.7_spmd.clone, body=%wide.region_5.6_spmd.clone.sunk | while | flops 201850880 | bytes 3672671 | solution.py:29
  191.8 1.9 fusion.480
  193.8 1.9 fusion.480
  199.6 1.9 fusion.480
  201.6 1.9 fusion.480
  203.6 1.9 fusion.480
  205.6 1.9 fusion.480
  207.5 1.9 fusion.480
  209.5 1.9 fusion.480
  213.4 1.9 fusion.480
  215.4 1.9 fusion.480
  227.1 2.0 fusion.480
  233.1 2.0 fusion.480
  237.1 1.9 fusion.480
  239.0 1.9 fusion.480
  244.9 1.9 fusion.480
  246.9 2.1 fusion.480
  251.1 1.9 fusion.480
  263.9 32.5 %while.165 = (s32[]{:T(128)}, f32[1,8,128,128]{3,2,1,0:T(8,128)S(1)}, f32[2,1,8,64,128]{4,3,2,1,0:T(8,128)}, f32[2,1,1,1,1]{0,4,3,2,1:T(1,128)S(1)}, f32[2,1,8,6...) while((s32[]{:T(128)}, ...), condition=%wide.region_10.11_spmd.clone.clone, body=%wide.region_8.10_spmd.clone.clone.sunk | while | flops 454689792 | bytes 11406345 | solution.py:150
  265.9 2.1 bitcast_dynamic-update-slice_fusion.18
  270.6 1.9 bitcast_dynamic-update-slice_fusion.20
  282.2 2.1 bitcast_dynamic-update-slice_fusion.18
  286.8 2.0 bitcast_dynamic-update-slice_fusion.20
  298.0 3.9 fusion.250
  303.5 4.5 fusion.234
  310.2 9.3 while.166
  319.6 17.8 %while.169 = (s32[]{:T(128)}, f32[1,8,128,128]{2,3,1,0:T(8,128)S(1)}, f32[2,1,8,1,1]{2,4,3,1,0:T(1,128)}, f32[2,1,8,64,1]{3,2,4,1,0:T(8,128)}, f32[2,1,8,64,128]...) while((s32[]{:T(128)}, ...), condition=%wide.region_17.18_spmd.clone, body=%wide.region_16.17_spmd.clone.sunk | while | flops 403767296 | bytes 6049023 | solution.py:163
  326.6 1.9 fusion.493
  335.5 1.9 fusion.493
  339.9 3.7 fusion.208
  343.6 11.6 reverse_bitcast_fusion.1
  355.2 595.4 %reduce-scatter.2.cloned.1.call-done = f32[8,2048]{1,0:T(8,128)} async-done(((f32[1024,2048]{1,0:T(8,128)}), f32[8,2048]{1,0:T(8,128)}) %reduce-scatter.2.cloned.1.call-update) | async-done | bytes 65552 | tf_op jit(solution)/shard_map/reduce_scatter | solution.py:171
  952.1 74.5 %all-gather.15.cloned.1.call-done = f32[32,8,128,128]{3,2,1,0:T(8,128)} async-done(((f32[1,8,128,128]{3,2,1,0:T(8,128)}), f32[32,8,128,128]{3,2,1,0:T(8,128)}) %all-gather.15.cloned.1.call-update) | async-done | bytes 16777232 | tf_op jit(solution)/shard_map/all_gather | solution.py:17
  1026.6 11.6 reverse_bitcast_fusion
  1038.3 60.3 %while.170 = (s32[]{:T(128)}, f32[1,8,128,128]{3,2,1,0:T(8,128)S(1)}, s32[]{:T(128)}, f32[32,1,8,128,128]{4,3,2,1,0:T(8,128)}, f32[32,1,8,128,128]{4,3,2,1,0:T(8,128)}, /*index=5*/s32[]{:T(128)}, s32[]{:T(128)}) while((s32[]{:T(128)}, f32[1,8,128,128]{3,2,1,0:T(8,128)S(1)}, s32[]{:T(128)}, f32[32,1,8,128,128]{4,3,2,1,0:T(8,128)}, ...), condition=%wide.region_19.20_spmd.clone, body=%wide.region_18.19_spmd.clone.sunk | while | flops 201850880 | bytes 3672671 | solution.py:29
  1102.5 71.3 %while.167 = (s32[]{:T(128)}, f32[1,8,128,128]{2,3,1,0:T(8,128)S(1)}, f32[2,1,8,64,128]{4,2,1,3,0:T(8,128)}, f32[2,1,8,64,128]{4,3,2,1,0:T(8,128)}, bf16[2,1,8,6...) while((s32[]{:T(128)}, ...), condition=%wide.region_30.31_spmd.clone.clone, body=%wide.region_20.30_spmd.clone.clone.sunk | while | flops 908626432 | bytes 19639980 | solution.py:150
  1102.7 2.1 convolution_bitcast_fusion.40
  1107.0 2.0 bitcast_dynamic-update-slice_fusion.25
  1110.4 2.3 fusion.470
  1115.2 1.9 constant_dynamic-slice_fusion.30
  1123.8 2.9 fusion.472
  1131.6 2.2 fusion.467
  1136.0 2.2 fusion.477
  1138.2 2.1 convolution_bitcast_fusion.40
  1142.5 2.0 bitcast_dynamic-update-slice_fusion.25
  1145.9 2.3 fusion.470
  1150.8 1.9 constant_dynamic-slice_fusion.30
  1159.4 2.9 fusion.472
  1167.1 2.2 fusion.467
  1171.5 2.2 fusion.477
  1174.0 3.2 fusion.247
  1178.4 2.2 fusion.212
  1180.6 2.0 convolution_bitcast_fusion.31
  1184.3 2.0 convolution_bitcast_fusion.27
  1188.0 2.0 convolution_bitcast_fusion.23
  1191.7 2.2 convolution_bitcast_fusion.19
  1203.2 2.2 convolution_bitcast_fusion.17
  1209.2 2.3 convolution_bitcast_fusion.14
  1211.5 2.5 fusion.258
  (475 shorter events, 257.7 us)
Async XLA Ops:
  7.2 290.8 %copy-start = (bf16[1,128,2048]{2,1,0:T(8,128)(2,1)S(1)}, bf16[1,128,2048]{2,1,0:T(8,128)(2,1)}, u32[]{:S(2)}) copy-start(bf16[1,128,2048]{2,1,0:T(8,128)(2,1)} %param.29) | copy-start | bytes 1572868
  7.2 17.1 %copy-start.24 = (bf16[1,128,1024]{2,1,0:T(8,128)(2,1)S(1)}, bf16[1,128,1024]{2,1,0:T(8,128)(2,1)}, u32[]{:S(2)}) copy-start(bf16[1,128,1024]{2,1,0:T(8,128)(2,1)} %param.24) | copy-start | bytes 786436
  7.2 17.3 %copy-start.41 = (s32[1,2]{1,0:T(1,128)S(1)}, s32[1,2]{1,0:T(1,128)}, u32[]{:S(2)}) copy-start(s32[1,2]{1,0:T(1,128)} %param.27) | copy-start | bytes 28
  7.2 109.7 %all-gather.9.cloned.1.call-start = ((), (), s32[]{:S(2)}) async-start(), calls=%async_computation.2 | async-start | bytes 17301504 | tf_op jit(solution)/shard_map/all_gather | solution.py:17
  7.3 18.5 %copy-start.26 = (pred[64,64]{0,1:T(8,128)(4,1)}, pred[64,64]{0,1:T(8,128)(4,1)S(1)}, u32[]{:S(2)}) copy-start(pred[64,64]{0,1:T(8,128)(4,1)S(1)} %get-tuple-element.2943) | copy-start | bytes 12292
  8.4 4.3 copy-start.14
  8.7 3.6 copy-start.31
  9.3 2.9 copy-start.35
  10.5 15.2 %copy-start.15 = (f32[2,8,64,64]{2,3,1,0:T(8,128)}, f32[2,8,64,64]{2,3,1,0:T(8,128)S(1)}, u32[]{:S(2)}) copy-start(f32[2,8,64,64]{2,3,1,0:T(8,128)S(1)} %fusion.255) | copy-start | bytes 786436
  12.2 13.6 %copy-start.28 = (f32[2,8,64]{2,1,0:T(8,128)}, f32[2,8,64]{2,1,0:T(8,128)S(1)}, u32[]{:S(2)}) copy-start(f32[2,8,64]{2,1,0:T(8,128)S(1)} %copy.308) | copy-start | bytes 12292
  14.1 0.8 copy-start.8
  14.7 11.1 copy-start.2
  16.0 0.8 copy-start.17
  16.8 1.7 copy-start.4
  17.8 5.2 copy-start.18
  18.5 1.7 copy-start.6
  19.5 3.5 copy-start.19
  20.2 2.8 copy-start.21
  21.2 1.8 copy-start.20
  24.5 1.2 copy-start.13
  40.5 151.3 %all-gather.11.cloned.1.call-start = ((), (), s32[]{:S(2)}) async-start(), calls=%async_computation.3 | async-start | bytes 17301504 | tf_op jit(solution)/shard_map/all_gather | solution.py:17
  41.3 302.3 %all-gather.13.cloned.1.call-start = ((), (), s32[]{:S(2)}) async-start(), calls=%async_computation.4 | async-start | bytes 17301504 | tf_op jit(solution)/shard_map/all_gather | solution.py:17
  42.4 908.3 %reduce-scatter.2.cloned.1.call-start = ((), (), s32[]{:S(2)}) async-start(), calls=%async_computation.1 | async-start | bytes 8454144 | tf_op jit(solution)/shard_map/reduce_scatter | solution.py:171
  43.6 1.0 copy-start.11
  43.9 216.8 %copy-start.33 = (f32[2,8,64]{2,1,0:T(8,128)}, f32[2,8,64]{2,1,0:T(8,128)S(1)}, u32[]{:S(2)}) copy-start(f32[2,8,64]{2,1,0:T(8,128)S(1)} %copy.329) | copy-start | bytes 12292
  296.4 1.5 copy-start.42
  296.4 1.5 copy-start.43
  296.5 5.5 copy-start.45
  296.5 11.6 copy-start.30
  296.5 13.7 %copy-start.10 = (f32[2,1,8,64,64]{4,3,2,1,0:T(8,128)}, f32[2,1,8,64,64]{4,3,2,1,0:T(8,128)S(1)}, u32[]{:S(2)}) copy-start(f32[2,1,8,64,64]{4,3,2,1,0:T(8,128)S(1)} %get-tuple-element.3923) | copy-start | bytes 786436
  303.5 4.6 copy-start.22
  303.5 6.7 copy-start.44
  308.1 718.6 %all-gather.15.cloned.1.call-start = ((), (), s32[]{:S(2)}) async-start(), calls=%async_computation.5 | async-start | bytes 17301504 | tf_op jit(solution)/shard_map/all_gather | solution.py:17
  319.6 18.8 %copy-start.37 = (f32[2,8,64]{2,1,0:T(8,128)S(1)}, f32[2,8,64]{2,1,0:T(8,128)}, u32[]{:S(2)}) copy-start(f32[2,8,64]{2,1,0:T(8,128)} %get-tuple-element.2934) | copy-start | bytes 12292
  319.6 20.3 %copy-start.23 = (bf16[1,2,64,8,128]{4,3,2,1,0:T(8,128)(2,1)S(1)}, bf16[1,2,64,8,128]{4,3,2,1,0:T(8,128)(2,1)}, u32[]{:S(2)}) copy-start(bf16[1,2,64,8,128]{4,3,2,1,0:T(8,128)(2,1)} %copy-done.22) | copy-start | bytes 786436
  1173.9 21.8 %copy-start.7 = (f32[2,8,64,64]{3,2,1,0:T(8,128)S(1)}, f32[2,8,64,64]{3,2,1,0:T(8,128)}, u32[]{:S(2)}) copy-start(f32[2,8,64,64]{3,2,1,0:T(8,128)} %copy-done.6) | copy-start | bytes 786436
  1173.9 25.2 %copy-start.5 = (f32[2,8,64,64]{3,2,1,0:T(8,128)S(1)}, f32[2,8,64,64]{3,2,1,0:T(8,128)}, u32[]{:S(2)}) copy-start(f32[2,8,64,64]{3,2,1,0:T(8,128)} %copy-done.4) | copy-start | bytes 786436
  1173.9 26.5 %copy-start.3 = (f32[2,8,64,64]{3,2,1,0:T(8,128)S(1)}, f32[2,8,64,64]{3,2,1,0:T(8,128)}, u32[]{:S(2)}) copy-start(f32[2,8,64,64]{3,2,1,0:T(8,128)} %copy-done.2) | copy-start | bytes 786436
  1173.9 28.0 %copy-start.9 = (f32[2,8,64,64]{3,2,1,0:T(8,128)S(1)}, f32[2,8,64,64]{3,2,1,0:T(8,128)}, u32[]{:S(2)}) copy-start(f32[2,8,64,64]{3,2,1,0:T(8,128)} %copy-done.8) | copy-start | bytes 786436
  1173.9 29.3 %copy-start.27 = (pred[64,64]{0,1:T(8,128)(4,1)S(1)}, pred[64,64]{0,1:T(8,128)(4,1)}, u32[]{:S(2)}) copy-start(pred[64,64]{0,1:T(8,128)(4,1)} %copy-done.26) | copy-start | bytes 12292
  1173.9 29.3 %copy-start.29 = (f32[2,8,64]{2,1,0:T(8,128)S(1)}, f32[2,8,64]{2,1,0:T(8,128)}, u32[]{:S(2)}) copy-start(f32[2,8,64]{2,1,0:T(8,128)} %copy-done.28) | copy-start | bytes 12292
  1178.4 27.1 %copy-start.16 = (f32[2,8,64,64]{2,3,1,0:T(8,128)S(1)}, f32[2,8,64,64]{2,3,1,0:T(8,128)}, u32[]{:S(2)}) copy-start(f32[2,8,64,64]{2,3,1,0:T(8,128)} %copy-done.15) | copy-start | bytes 786436
  1182.6 25.2 %copy-start.39 = (f32[2,1,8,64]{3,2,1,0:T(8,128)S(1)}, f32[2,1,8,64]{3,2,1,0:T(8,128)}, u32[]{:S(2)}) copy-start(f32[2,1,8,64]{3,2,1,0:T(8,128)} %get-tuple-element.1885) | copy-start | bytes 12292
  1182.6 25.9 %copy-start.38 = (f32[2,1,8,64]{3,2,1,0:T(8,128)S(1)}, f32[2,1,8,64]{3,2,1,0:T(8,128)}, u32[]{:S(2)}) copy-start(f32[2,1,8,64]{3,2,1,0:T(8,128)} %get-tuple-element.1884) | copy-start | bytes 12292
  1182.6 26.6 %copy-start.36 = (f32[2,8,64]{2,1,0:T(8,128)S(1)}, f32[2,8,64]{2,1,0:T(8,128)}, u32[]{:S(2)}) copy-start(f32[2,8,64]{2,1,0:T(8,128)} %copy-done.35) | copy-start | bytes 12292
  1186.3 25.2 %copy-start.40 = (f32[2,8,64]{2,1,0:T(8,128)S(1)}, f32[2,8,64]{2,1,0:T(8,128)}, u32[]{:S(2)}) copy-start(f32[2,8,64]{2,1,0:T(8,128)} %get-tuple-element.2932) | copy-start | bytes 12292
  1190.0 24.0 %copy-start.32 = (f32[2,8,64]{2,1,0:T(8,128)S(1)}, f32[2,8,64]{2,1,0:T(8,128)}, u32[]{:S(2)}) copy-start(f32[2,8,64]{2,1,0:T(8,128)} %copy-done.31) | copy-start | bytes 12292
  1193.9 22.5 %copy-start.12 = (f32[16,8,8,128]{3,2,1,0:T(8,128)S(1)}, f32[16,8,8,128]{3,2,1,0:T(8,128)}, u32[]{:S(2)}) copy-start(f32[16,8,8,128]{3,2,1,0:T(8,128)} %copy-done.11) | copy-start | bytes 1572868
  1193.9 22.5 %copy-start.25 = (f32[2,8,64]{1,2,0:T(8,128)S(1)}, f32[2,8,64]{1,2,0:T(8,128)}, u32[]{:S(2)}) copy-start(f32[2,8,64]{1,2,0:T(8,128)} %copy.372) | copy-start | bytes 12292
  1193.9 24.0 %copy-start.34 = (f32[2,8,64]{2,1,0:T(8,128)S(1)}, f32[2,8,64]{2,1,0:T(8,128)}, u32[]{:S(2)}) copy-start(f32[2,8,64]{2,1,0:T(8,128)} %copy-done.33) | copy-start | bytes 12292
  1195.7 26.5 %copy-start.1 = (bf16[1,128,2048]{2,1,0:T(8,128)(2,1)S(1)}, bf16[1,128,2048]{2,1,0:T(8,128)(2,1)}, u32[]{:S(2)}) copy-start(bf16[1,128,2048]{2,1,0:T(8,128)(2,1)} %param.29) | copy-start | bytes 1572868
Sparse Core Ops, SparseCore 0:
  40.6 76.2 all-gather.8
  119.7 71.9 all-gather.10
  194.0 71.9 all-gather.12
  308.2 642.4 reduce-scatter.1
  953.0 73.5 all-gather.14
where the time goes:
time: 1240 us; the launch traced here: 1230 us
  waiting for transfers between devices  817 us (66%)
  matrix products  266 us (21%)
  local copies, waits for them, and re-layouts  89.7 us (7%)
  other arithmetic  36.8 us (3%)
  between operations  15.4 us (1%)
    reduce_scatter x1, waiting for transfers between devices, local(): lax.psum_scatter(lax.dot_general(flat, cot, (((0,), (0,)), ((), ())), pre...  595 us
    all_gather x4, waiting for transfers between devices, entering(): pieces = jax.tree.map(lambda part: lax.all_gather(part, axis), value)  221 us
    dot_general x62, matrix products, compose(): jnp.einsum('bhij,bhjk->bhik', later[0], earlier[1], precision=HIGH)  117 us
    dot_general x15, matrix products, block_inverse(): jnp.einsum('...ij,...jk->...ik', inverse, power, precision=HIGH)  26.3 us
  transfers between devices with their start and end apart: 5, of which 4 were waited for; matrix products, arithmetic and copies ran while one was open for 14% of the time, Pallas kernels for 0%

commit v1 on v0

v1 whole, which is shorter than its diff:
```python
import math

import jax
import jax.numpy as jnp
from jax import lax
from jax.experimental import pallas as pl
from jax.experimental.pallas import tpu as pltpu
from jax.sharding import PartitionSpec as P

f32 = jnp.float32
bf16 = jnp.bfloat16
EPS = 1e-06
C = 128
H = 8
VMEM_LIMIT = 48 * 1024 * 1024

NN = (((1,), (0,)), ((), ()))
NT = (((1,), (1,)), ((), ()))
TN = (((0,), (0,)), ((), ()))


def split(x):
    hi = x.astype(bf16)
    return hi, (x - hi.astype(f32)).astype(bf16)


def dot(a, b, dims=NN):
    return lax.dot_general(a, b, dims, preferred_element_type=f32)


def mm(a, b, dims=NN):
    ah, al = split(a)
    bh, bl = split(b)
    return dot(ah, bh, dims) + (dot(ah, bl, dims) + dot(al, bh, dims))


def tn(a, b):
    return mm(a.T, b)


def split3(x):
    hi = x.astype(bf16)
    rest = x - hi.astype(f32)
    mid = rest.astype(bf16)
    return hi, mid, (rest - mid.astype(f32)).astype(bf16)


def iotas(shape=(C, C)):
    return lax.broadcasted_iota(jnp.int32, shape, 0), lax.broadcasted_iota(jnp.int32, shape, 1)


def head(ref, h):
    return ref[:, h * C : (h + 1) * C].astype(f32)


def unit(x):
    inv = 1.0 / jnp.sqrt(jnp.sum(x * x, axis=-1, keepdims=True) + EPS)
    return x * inv, inv


def gate_tables(g_ref, resets_ref):
    rows, cols = iotas()
    lower = (rows >= cols).astype(bf16)
    upper = (rows <= cols).astype(bf16)
    parts = split3(g_ref[...])
    total_c = sum(dot(lower, part) for part in parts)
    total_r = sum(dot(part, upper, TN) for part in parts)
    r1 = resets_ref[0, 0].astype(f32)
    r2 = resets_ref[0, 1].astype(f32)
    tcol = lax.broadcasted_iota(jnp.int32, (C, 1), 0)
    m_in = (1.0 - r1) * jnp.where(tcol >= 64, 1.0 - r2, 1.0)
    m_out = jnp.where(tcol >= 64, 1.0, 1.0 - r2)
    m_all = (1.0 - r1) * (1.0 - r2)
    doc = jnp.where((rows >= 64) & (cols < 64), 1.0 - r2, 1.0)
    return total_c, total_r, m_in, m_out, m_all, doc


def head_gates(tables, h):
    total_c, total_r, m_in, m_out, m_all, doc = tables
    rows, cols = iotas()
    tc = total_c[:, h : h + 1]
    tr = total_r[h : h + 1, :]
    last = total_c[C - 1 : C, h : h + 1]
    keep = rows >= cols
    inside = jnp.where(keep, jnp.exp(jnp.where(keep, tc - tr, 0.0)), 0.0) * doc
    growth = jnp.exp(tc) * m_in
    fading = jnp.exp(last - tc) * m_out
    g_last = jnp.exp(last) * m_all
    return inside, growth, fading, g_last


def strict(x):
    rows, cols = iotas()
    return jnp.where(rows > cols, x, 0.0)


def spec_v(n):
    return [pl.BlockSpec(memory_space=pltpu.VMEM)] * n


def spec_s(n):
    return [pl.BlockSpec(memory_space=pltpu.SMEM)] * n


def call(kernel, outs, n_smem, *args, flops=0):
    nbytes = sum(a.size * a.dtype.itemsize for a in args) + sum(
        math.prod(s) * jnp.dtype(d).itemsize for s, d in outs
    )
    return pl.pallas_call(
        kernel,
        out_shape=[jax.ShapeDtypeStruct(s, d) for s, d in outs],
        in_specs=spec_s(n_smem) + spec_v(len(args) - n_smem),
        out_specs=spec_v(len(outs)),
        compiler_params=pltpu.CompilerParams(vmem_limit_bytes=VMEM_LIMIT),
        cost_estimate=pl.CostEstimate(flops=flops, bytes_accessed=nbytes, transcendentals=0),
    )(*args)


HEADS = range(H)
SQ = 2 * C * C * C * 3


def maps_kernel(pos, resets, k_ref, v_ref, b_ref, g_ref, keep_ref, send_ref, inv_ref, uw_ref):
    tables = gate_tables(g_ref, resets)
    rows, cols = iotas()
    eye = (rows == cols).astype(f32)
    block = (rows >= 64) == (cols >= 64)
    beta = b_ref[...].astype(f32)
    kn = [unit(head(k_ref, h))[0] for h in HEADS]
    gates = [head_gates(tables, h) for h in HEADS]
    kk = [mm(kn[h], kn[h], NT) for h in HEADS]
    system = [strict(kk[h] * gates[h][0]) * beta[:, h : h + 1] for h in HEADS]
    near = [jnp.where(block, x, 0.0) for x in system]
    far = [jnp.where(block, 0.0, x) for x in system]
    inv = [eye - x for x in near]
    power = [mm(x, x) for x in near]
    for level in range(5):
        if level < 4:
            both = [mm(jnp.concatenate([inv[h], power[h]], axis=0), power[h]) for h in HEADS]
            inv = [inv[h] + both[h][:C] for h in HEADS]
            power = [both[h][C:] for h in HEADS]
        else:
            inv = [inv[h] + mm(inv[h], power[h]) for h in HEADS]
    cross = [mm(far[h], inv[h]) for h in HEADS]
    inv = [inv[h] - mm(inv[h], cross[h]) for h in HEADS]
    uw = []
    for h in HEADS:
        bh = beta[:, h : h + 1]
        right = jnp.concatenate([kn[h] * (bh * gates[h][1]), head(v_ref, h) * bh], axis=1)
        uw.append(mm(inv[h], right))
    maps = []
    for h in HEADS:
        prod = tn(kn[h] * gates[h][2], uw[h])
        maps.append(
            jnp.concatenate([eye * gates[h][3] - prod[:, :C], prod[:, C:]], axis=1)
        )
    for h in HEADS:
        inv_ref[h] = inv[h]
        uw_ref[h] = uw[h]
    first = pos[3] == 0
    for j in range(4):
        keep_ref[j] = jnp.where(first, maps[j], maps[j + 4])
        send_ref[j] = jnp.where(first, maps[j + 4], maps[j])


def compose(later, earlier):
    moved = mm(later[:, :C], earlier)
    return jnp.concatenate([moved[:, :C], moved[:, C:] + later[:, C:]], axis=1)


def pair_kernel(pos, keep_ref, recv_ref, o0, o1, o2, o3, scratch):
    first = pos[3] == 0
    for j in range(4):
        a, b = keep_ref[j], recv_ref[j]
        early = jnp.where(first, a, b)
        late = jnp.where(first, b, a)
        scratch[j] = compose(late, early)
    for r, out in enumerate((o0, o1, o2, o3)):
        out[...] = scratch[(pos[2] + r) % 4]


def group_kernel(pos, x0, x1, x2, x3, maps_ref, prefix_ref, total_ref):
    for r, ref in enumerate((x0, x1, x2, x3)):
        maps_ref[(pos[2] + 4 - r) % 4] = ref[...]
    run = maps_ref[0]
    prefix_ref[0] = run
    for i in range(1, 4):
        run = compose(maps_ref[i], run)
        if i < 3:
            prefix_ref[i] = run
    total_ref[...] = run


def enter_kernel(pos, t0, t1, t2, t3, prefix_ref, totals_ref, o0, o1, o2, o3, scratch):
    for r, ref in enumerate((t0, t1, t2, t3)):
        totals_ref[(pos[1] + 4 - r) % 4] = ref[...]
    x = pos[1]
    s1 = totals_ref[0, :, C:]
    s2 = mm(totals_ref[1, :, :C], s1) + totals_ref[1, :, C:]
    s3 = mm(totals_ref[2, :, :C], s2) + totals_ref[2, :, C:]
    state = jnp.where(x == 0, 0.0, jnp.where(x == 1, s1, jnp.where(x == 2, s2, s3)))
    scratch[0] = state
    for i in range(3):
        scratch[i + 1] = mm(prefix_ref[i, :, :C], state) + prefix_ref[i, :, C:]
    for r, out in enumerate((o0, o1, o2, o3)):
        out[...] = scratch[(pos[2] + r) % 4]


def split_pair_kernel(pos, s0, s1, s2, s3, keep_ref, recv_ref, mine_ref, other_ref, scratch):
    for r, ref in enumerate((s0, s1, s2, s3)):
        scratch[(pos[2] + 4 - r) % 4] = ref[...]
    first = pos[3] == 0
    for j in range(4):
        early = jnp.where(first, keep_ref[j], recv_ref[j])
        start = scratch[j]
        middle = mm(early[:, :C], start) + early[:, C:]
        mine_ref[j] = jnp.where(first, start, middle)
        other_ref[j] = jnp.where(first, middle, start)


def reads_kernel(resets, q_ref, k_ref, g_ref, uw_ref, read_ref):
    tables = gate_tables(g_ref, resets)
    for h in HEADS:
        qn = unit(head(q_ref, h))[0]
        kn = unit(head(k_ref, h))[0]
        inside, growth, _, _ = head_gates(tables, h)
        attn = mm(qn, kn, NT) * inside
        prod = mm(attn, uw_ref[h])
        read_ref[h] = jnp.concatenate([qn * growth - prod[:, :C], prod[:, C:]], axis=1)


def pick(first, mine_ref, other_ref, h):
    a, b = mine_ref[h % 4], other_ref[h % 4]
    return jnp.where(first, a, b) if h < 4 else jnp.where(first, b, a)


def outs_kernel(
    pos, mine_ref, other_ref, read_ref, dn_ref, n_ref, do_ref, keep_ref, send_ref, c0, c1, c2, c3, wide
):
    first = pos[3] == 0
    reach = []
    for h in HEADS:
        state = pick(first, mine_ref, other_ref, h)
        read = read_ref[h]
        out = mm(read[:, :C], state) + read[:, C:]
        inv = 1.0 / jnp.sqrt(jnp.mean(out * out, axis=-1, keepdims=True) + EPS)
        n32 = out * inv
        n16 = n32.astype(bf16)
        n_ref[:, h * C : (h + 1) * C] = n16
        wide[h // 2, :, (h % 2) * C : (h % 2 + 1) * C] = n16.astype(f32)
        dn = dn_ref[:, h * C : (h + 1) * C]
        do = inv * (dn - n32 * jnp.mean(n32 * dn, axis=-1, keepdims=True))
        do_ref[h] = do
        reach.append(tn(read[:, :C], do))
    for j in range(4):
        keep_ref[j] = jnp.where(first, reach[j], reach[j + 4])
        send_ref[j] = jnp.where(first, reach[j + 4], reach[j])
    for r, out_ref in enumerate((c0, c1, c2, c3)):
        out_ref[...] = wide[(pos[0] + r) % 4]


def pair_back_kernel(pos, keep_ref, recv_ref, mkeep_ref, mrecv_ref, o0, o1, o2, o3, scratch):
    first = pos[3] == 0
    for j in range(4):
        a, b = keep_ref[j], recv_ref[j]
        early = jnp.where(first, a, b)
        late = jnp.where(first, b, a)
        early_map = jnp.where(first, mkeep_ref[j, :, :C], mrecv_ref[j, :, :C])
        scratch[j] = early + tn(early_map, late)
    for r, out in enumerate((o0, o1, o2, o3)):
        out[...] = scratch[(pos[2] + r) % 4]


def group_back_kernel(pos, r0, r1, r2, r3, maps_ref, reach_ref, total_ref):
    for r, ref in enumerate((r0, r1, r2, r3)):
        reach_ref[(pos[2] + 4 - r) % 4] = ref[...]
    run = reach_ref[3]
    for i in (2, 1, 0):
        run = reach_ref[i] + tn(maps_ref[i, :, :C], run)
    total_ref[...] = run


def enter_back_kernel(pos, t0, t1, t2, t3, totals_ref, maps_ref, reach_ref, o0, o1, o2, o3, parts, scratch):
    for r, ref in enumerate((t0, t1, t2, t3)):
        parts[(pos[1] + 4 - r) % 4] = ref[...]
    x = pos[1]
    d2 = parts[3]
    d1 = parts[2] + tn(totals_ref[2, :, :C], d2)
    d0 = parts[1] + tn(totals_ref[1, :, :C], d1)
    run = jnp.where(x == 3, 0.0, jnp.where(x == 2, d2, jnp.where(x == 1, d1, d0)))
    scratch[3] = run
    for i in (2, 1, 0):
        run = reach_ref[i + 1] + tn(maps_ref[i + 1, :, :C], run)
        scratch[i] = run
    for r, out in enumerate((o0, o1, o2, o3)):
        out[...] = scratch[(pos[2] + r) % 4]


def split_pair_back_kernel(
    pos, s0, s1, s2, s3, mkeep_ref, mrecv_ref, keep_ref, recv_ref, mine_ref, other_ref, scratch
):
    for r, ref in enumerate((s0, s1, s2, s3)):
        scratch[(pos[2] + 4 - r) % 4] = ref[...]
    first = pos[3] == 0
    for j in range(4):
        late_map = jnp.where(first, mrecv_ref[j, :, :C], mkeep_ref[j, :, :C])
        late = jnp.where(first, recv_ref[j], keep_ref[j])
        end = scratch[j]
        middle = late + tn(late_map, end)
        mine_ref[j] = jnp.where(first, middle, end)
        other_ref[j] = jnp.where(first, end, middle)


def early_grads_kernel(
    pos, resets, q_ref, k_ref, g_ref, mine_ref, other_ref, uw_ref, do_ref,
    dq_ref, delta_ref, dkn_ref, dd_ref, pair_ref, dgrow_ref,
):
    first = pos[3] == 0
    tables = gate_tables(g_ref, resets)
    for h in HEADS:
        state = pick(first, mine_ref, other_ref, h)
        qn, iq = unit(head(q_ref, h))
        kn = unit(head(k_ref, h))[0]
        inside, growth, _, _ = head_gates(tables, h)
        attn = mm(qn, kn, NT) * inside
        uw = uw_ref[h]
        do = do_ref[h]
        delta = uw[:, C:] - mm(uw[:, :C], state)
        delta_ref[h] = delta
        dattn = mm(do, delta, NT)
        back = mm(do, state, NT)
        pair_ref[h] = dattn * attn
        dgrow_ref[h] = jnp.broadcast_to(
            jnp.sum(back * qn, axis=-1, keepdims=True) * growth, (C, C)
        )
        dqk = dattn * inside
        dqn = back * growth + mm(dqk, kn)
        dq = iq * (dqn - qn * jnp.sum(dqn * qn, axis=-1, keepdims=True))
        dq_ref[:, h * C : (h + 1) * C] = dq.astype(bf16)
        dkn_ref[h] = tn(dqk, qn)
        dd_ref[h] = tn(attn, do)


def late_grads_kernel(
    pos, resets, k_ref, v_ref, b_ref, g_ref, mine_ref, other_ref, dmine_ref, dother_ref,
    inv_ref, delta_ref, dkn_ref, dd_ref, pair_ref, dgrow_ref,
    dk_ref, dv_ref, db_ref, dg_ref,
):
    first = pos[3] == 0
    tables = gate_tables(g_ref, resets)
    rows, cols = iotas()
    beta = b_ref[...].astype(f32)
    db_all = jnp.zeros((C, C), f32)
    dt_all = jnp.zeros((C, C), f32)
    is_last = lax.broadcasted_iota(jnp.int32, (C, 1), 0) == C - 1
    for h in HEADS:
        state = pick(first, mine_ref, other_ref, h)
        dstate = pick(first, dmine_ref, dother_ref, h)
        kn, ik = unit(head(k_ref, h))
        inside, growth, fading, g_last = head_gates(tables, h)
        below = strict(inside)
        bh = beta[:, h : h + 1]
        delta = delta_ref[h]
        ddelta = dd_ref[h] + mm(kn, dstate) * fading
        dtarget = tn(inv_ref[h], ddelta)
        dv_ref[:, h * C : (h + 1) * C] = (dtarget * bh).astype(bf16)
        carried = mm(kn, state)
        db = jnp.sum(dtarget * (head(v_ref, h) - carried * growth), axis=-1, keepdims=True)
        dgrow = -jnp.sum(dtarget * carried, axis=-1, keepdims=True) * bh * growth
        dsys = -mm(dtarget, delta, NT)
        raw = mm(kn, kn, NT) * below
        db = db + jnp.sum(dsys * raw, axis=-1, keepdims=True)
        dkk = dsys * below * bh
        pairs = pair_ref[h] + dsys * raw * bh
        dkf = mm(delta, dstate, NT)
        dfade = jnp.sum(dkf * kn, axis=-1, keepdims=True) * fading
        dkn = (
            dkn_ref[h]
            + mm(dkk + dkk.T, kn)
            + dkf * fading
            - mm(dtarget, state, NT) * (bh * growth)
        )
        dk = ik * (dkn - kn * jnp.sum(dkn * kn, axis=-1, keepdims=True))
        dk_ref[:, h * C : (h + 1) * C] = dk.astype(bf16)
        dlast = jnp.sum(dfade, axis=0, keepdims=True) + g_last * jnp.sum(
            jnp.sum(state * dstate, axis=-1, keepdims=True), axis=0, keepdims=True
        )
        dtotal = (
            jnp.sum(pairs - pairs.T, axis=-1, keepdims=True)
            + dgrow_ref[h][:, :1]
            + dgrow
            - dfade
            + jnp.where(is_last, dlast, 0.0)
        )
        db_all = jnp.where(cols == h, db, db_all)
        dt_all = jnp.where(cols == h, dtotal, dt_all)
    upper = (rows <= cols).astype(bf16)
    dg_all = sum(dot(upper, part) for part in split3(dt_all))
    db_ref[...] = db_all[:, :H]
    dg_ref[...] = dg_all[:, :H]


def wgrad_kernel(pos, n0, n1, n2, n3, cot_ref, keep_ref, send_ref):
    order = [(pos[0] + 4 - r) % 4 for r in range(4)]
    ns = [ref[...].astype(bf16).T for ref in (n0, n1, n2, n3)]
    first = pos[3] == 0
    for j in range(8):
        cols = slice(j * 256, (j + 1) * 256)
        total = sum(
            dot(ns[r], cot_ref[order[r], :, cols].astype(bf16)) for r in range(4)
        ).reshape(16, 2, 8, 256)
        a, b = total[:, 0], total[:, 1]
        keep_ref[:, :, cols] = jnp.where(first, a, b)
        send_ref[:, :, cols] = jnp.where(first, b, a)


def wsum_pair_kernel(pos, keep_ref, recv_ref, o0, o1, o2, o3):
    for r, out in enumerate((o0, o1, o2, o3)):
        z = (pos[2] + r) % 4
        for x in range(4):
            out[x] = keep_ref[4 * x + z] + recv_ref[4 * x + z]


def wsum_z_kernel(pos, a0, a1, a2, a3, o0, o1, o2, o3):
    for r, out in enumerate((o0, o1, o2, o3)):
        x = (pos[1] + r) % 4
        out[...] = (a0[x] + a1[x]) + (a2[x] + a3[x])


def wsum_x_kernel(scale, a0, a1, a2, a3, out):
    out[...] = ((a0[...] + a1[...]) + (a2[...] + a3[...])) * scale


def seq_perm(dx, dz, dc=0):
    pairs = []
    for i in range(32):
        x, z, c = i // 8, (i // 2) % 4, i % 2
        pairs.append((i, ((x + dx) % 4) * 8 + ((z + dz) % 4) * 2 + (c ^ dc)))
    return pairs


def swap_core(x):
    return lax.ppermute(x, "seq", seq_perm(0, 0, 1))


def around_z(parts):
    return [parts[0]] + [lax.ppermute(parts[r], "seq", seq_perm(0, r)) for r in (1, 2, 3)]


def around_x(parts):
    return [parts[0]] + [lax.ppermute(parts[r], "seq", seq_perm(r, 0)) for r in (1, 2, 3)]


def around_dp(parts):
    return [parts[0]] + [
        lax.ppermute(parts[r], "dp", [(i, (i + r) % 4) for i in range(4)]) for r in (1, 2, 3)
    ]


def with_scratch(kernel, outs, n_smem, scratch, *args):
    return pl.pallas_call(
        kernel,
        out_shape=[jax.ShapeDtypeStruct(s, f32) for s in outs],
        in_specs=spec_s(n_smem) + spec_v(len(args) - n_smem),
        out_specs=spec_v(len(outs)),
        scratch_shapes=[pltpu.VMEM(s, f32) for s in scratch],
        compiler_params=pltpu.CompilerParams(vmem_limit_bytes=VMEM_LIMIT),
    )(*args)


def local(queries, keys, values, strength, log_decay, resets, out_weight, cotangent):
    q, k, v = queries[0], keys[0], values[0]
    b, g = strength[0], log_decay[0]
    cot = cotangent[0]
    seq = lax.axis_index("seq")
    pos = jnp.stack([lax.axis_index("dp"), seq // 8, (seq // 2) % 4, seq % 2]).astype(jnp.int32)
    n_all = C * lax.axis_size("seq") * lax.axis_size("dp")

    cots = lax.all_gather(cot.astype(f32), "dp")

    mat, mat2 = (C, C), (C, 2 * C)
    mkeep, msend, inverse, uw = call(
        maps_kernel,
        [((4, *mat2), f32), ((4, *mat2), f32), ((H, *mat), f32), ((H, *mat2), f32)],
        2, pos, resets, k, v, b, g, flops=30 * H * SQ,
    )
    mrecv = swap_core(msend)
    parts = with_scratch(pair_kernel, [mat2] * 4, 1, [(4, *mat2)], pos, mkeep, mrecv)
    parts = around_z(parts)
    dn = lax.dot_general(cot, out_weight, NT, preferred_element_type=f32)
    (reads,) = call(
        reads_kernel, [((H, *mat2), f32)], 1, resets, q, k, g, uw, flops=3 * H * SQ
    )
    maps, prefix, total = call(
        group_kernel, [((4, *mat2), f32), ((3, *mat2), f32), (mat2, f32)], 1, pos, *parts
    )
    parts = around_x([total] * 4)
    totals, *parts = with_scratch(
        enter_kernel, [(4, *mat2)] + [mat] * 4, 1, [(4, *mat)], pos, *parts, prefix
    )
    parts = around_z(parts)
    mine, other = with_scratch(
        split_pair_kernel, [(4, *mat)] * 2, 1, [(4, *mat)], pos, *parts, mkeep, mrecv
    )
    other = swap_core(other)

    n16, do, rkeep, rsend, *chunks = pl.pallas_call(
        outs_kernel,
        out_shape=[
            jax.ShapeDtypeStruct(s, d)
            for s, d in [((C, H * C), bf16), ((H, *mat), f32), ((4, *mat), f32), ((4, *mat), f32)]
            + [(mat2, f32)] * 4
        ],
        in_specs=spec_s(1) + spec_v(4),
        out_specs=spec_v(8),
        scratch_shapes=[pltpu.VMEM((4, *mat2), f32)],
        compiler_params=pltpu.CompilerParams(vmem_limit_bytes=VMEM_LIMIT),
    )(pos, mine, other, reads, dn)

    rrecv = swap_core(rsend)
    parts = with_scratch(
        pair_back_kernel, [mat] * 4, 1, [(4, *mat)], pos, rkeep, rrecv, mkeep, mrecv
    )
    parts = around_z(parts)
    chunks = around_dp(chunks)
    mixed = lax.dot_general(n16, out_weight, NN, preferred_element_type=f32).astype(bf16)
    reach, total = call(
        group_back_kernel, [((4, *mat), f32), (mat, f32)], 1, pos, *parts, maps
    )
    parts = around_x([total] * 4)
    wkeep, wsend = call(
        wgrad_kernel, [((16, 8, 2048), f32)] * 2, 1, pos, *chunks, cots, flops=2 * 512 * 256 * 2048
    )
    dq, delta, dkn, dd, pairs, dgrow = call(
        early_grads_kernel,
        [((C, H * C), bf16)] + [((H, *mat), f32)] * 5,
        2, pos, resets, q, k, g, mine, other, uw, do, flops=8 * H * SQ,
    )
    parts = with_scratch(
        enter_back_kernel, [mat] * 4, 1, [(4, *mat), (4, *mat)], pos, *parts, totals, maps, reach
    )
    parts = around_z(parts)
    dmine, dother = with_scratch(
        split_pair_back_kernel, [(4, *mat)] * 2, 1, [(4, *mat)], pos, *parts, mkeep, mrecv, rkeep, rrecv
    )
    dother = swap_core(dother)
    dk, dv, db, dg = call(
        late_grads_kernel,
        [((C, H * C), bf16), ((C, H * C), bf16), ((C, H), f32), ((C, H), f32)],
        2, pos, resets, k, v, b, g, mine, other, dmine, dother, inverse, delta, dkn, dd, pairs, dgrow,
        flops=8 * H * SQ,
    )

    wrecv = swap_core(wsend)
    wparts = call(wsum_pair_kernel, [((4, 8, 2048), f32)] * 4, 1, pos, wkeep, wrecv)
    wparts = around_z(wparts)
    wparts = call(wsum_z_kernel, [((8, 2048), f32)] * 4, 1, pos, *wparts)
    wparts = around_x(wparts)
    scale = 1.0 / math.sqrt(n_all)

    def last(a0, a1, a2, a3, out):
        wsum_x_kernel(scale, a0, a1, a2, a3, out)

    (weight_grad,) = call(last, [((8, 2048), f32)], 0, *wparts)
    return (mixed[None], dq[None], dk[None], dv[None], db[None], dg[None], weight_grad)


def solution(mesh):
    rows = P("dp", "seq", None)
    return jax.shard_map(
        local,
        mesh=mesh,
        in_specs=(rows, rows, rows, rows, rows, P("dp", "seq"), P(), rows),
        out_specs=(rows, rows, rows, rows, rows, rows, P(("dp", "seq"), None)),
        check_vma=False,
    )
```

time: 1240 us -> 155 us (0.12)
  waiting for transfers between devices: 817 us -> 34.9 us
  matrix products: 266 us -> 3.04 us
  local copies, waits for them, and re-layouts: 89.7 us -> 15.6 us
  starting transfers between devices: 0.2 us -> 46.5 us
  Pallas kernels: 0 us -> 37.1 us
  other arithmetic: 36.8 us -> 2.24 us
    reduce_scatter x1 -> x0, waiting for transfers between devices: 595 us -> none  [local(): lax.psum_scatter(lax.dot_general(flat, cot, (((0,), (0,)), ((), ())), pre...]
    dot_general x152 -> x2, matrix products: 266 us -> 3.04 us  [the longest x1 1.52 us: local(): lax.dot_general(n16, out_weight, NN, preferred_element_type=f32)]
    all_gather x4 -> x1, waiting for transfers between devices: 221 us -> 0.01 us  [local(): cots = lax.all_gather(cot.astype(f32), 'dp')]
    ppermute x0 -> x32, starting transfers between devices: none -> 46.5 us  [the longest x15 19.7 us: around_z(): lax.ppermute(parts[r], 'seq', seq_perm(0, r))]
    pallas_call x0 -> x17, Pallas kernels: none -> 37.1 us  [the longest x10 29.2 us: call(): pl.pallas_call(kernel, out_shape=[jax.ShapeDtypeStruct(s, d) for s, d in...]
    ppermute x0 -> x32, waiting for transfers between devices: none -> 34.9 us  [the longest x15 18.6 us: around_z(): lax.ppermute(parts[r], 'seq', seq_perm(0, r))]
    dynamic_slice x14 -> x0, local copies, waits for them, and re-layouts: 14.1 us -> none  [the longest x4 6.26 us: local_heads(): final, outs_local = lax.scan(span_step, incoming, pieces)]
    another operation x24 -> x0, local copies, waits for them, and re-layouts: 12.5 us -> none
  transfers between devices with their start and end apart: 5 -> 33, of which waited for: 4 -> 16; matrix products, arithmetic and copies ran while one was open for 14% -> 4% of each run, Pallas kernels for 0% -> 21%
where the time goes in v1:
time: 155 us; the launch traced here: 154 us
  starting transfers between devices  46.5 us (30%)
  Pallas kernels  37.1 us (24%)
  waiting for transfers between devices  34.9 us (23%)
  local copies, waits for them, and re-layouts  15.6 us (10%)
  between operations  14.4 us (9%)
  matrix products  3.04 us (2%)
  other arithmetic  2.24 us (1%)
    pallas_call x10, Pallas kernels, call(): pl.pallas_call(kernel, out_shape=[jax.ShapeDtypeStruct(s, d) for s, d in...  29.2 us
    ppermute x15, starting transfers between devices, around_z(): lax.ppermute(parts[r], 'seq', seq_perm(0, r))  19.7 us
    ppermute x15, waiting for transfers between devices, around_z(): lax.ppermute(parts[r], 'seq', seq_perm(0, r))  18.6 us
    unnamed x66, local copies, waits for them, and re-layouts  15.6 us
    ppermute x9, starting transfers between devices, around_x(): lax.ppermute(parts[r], 'seq', seq_perm(r, 0))  12.7 us
    ppermute x5, starting transfers between devices, swap_core(): return lax.ppermute(x, 'seq', seq_perm(0, 0, 1))  9.21 us
    ppermute x9, waiting for transfers between devices, around_x(): lax.ppermute(parts[r], 'seq', seq_perm(r, 0))  7.4 us
    pallas_call x6, Pallas kernels, with_scratch(): pl.pallas_call(kernel, out_shape=[jax.ShapeDtypeStruct(s, f32) for s in o...  6.25 us
  transfers between devices with their start and end apart: 33, of which 16 were waited for; matrix products, arithmetic and copies ran while one was open for 4% of the time, Pallas kernels for 21%

profile of v1, /device:TPU:1, one launch (start us, length us, event | category | flops | bytes accessed | tf_op | source)
XLA Modules:
  0.0 153.8 jit_solution(9179874949087443728)
XLA Ops:
  7.2 2.2 %convert_element_type.8 = f32[1,128,2048]{2,1,0:T(8,128)} convert(bf16[1,128,2048]{2,1,0:T(8,128)(2,1)} %param.15) | non-fusion elementwise | flops 262144 | bytes 1572864 | tf_op jit(solution)/shard_map/convert_element_type | solution.py:479
  9.4 0.8 copy.19
  10.2 0.8 copy.20
  11.1 0.9 copy-done
  12.1 0.9 copy-done.12
  13.7 4.7 %shard_map.135 = (f32[4,128,256]{2,1,0:T(8,128)S(1)}, f32[4,128,256]{2,1,0:T(8,128)S(1)}, f32[8,128,128]{2,1,0:T(8,128)S(1)}, f32[8,128,256]{2,1,0:T(8,128)S(1)}) custom-call(s32[4]{0:T(128)S(1)} %pad_add_fusion.pos, s32[1,2]{1,0:T(1,128)S(1)} %copy-done.22, bf16[128,1024]{1,0:T(8,128)(2,1)S(1)} %bitcast.22, bf16[128,1024]{1,0:T(8,128)(2,1)S(1)} %bitcast.32, ...), custom_call_target="tpu_custom_call" | custom-call | flops 3019898880 | bytes 3151896 | tf_op jit(solution)/shard_map/pallas_call | solution.py:109
  18.4 0.8 copy-done.6
  19.2 1.4 collective-permute-start
  20.6 1.5 collective-permute-done.recv_ref.mrecv_ref
  22.1 1.0 shard_map.136
  23.1 1.8 %collective-permute-start.1 = (f32[128,256]{1,0:T(8,128)S(1)}, f32[128,256]{1,0:T(8,128)S(1)}, u32[]{:S(2)}, u32[]{:S(2)}) collective-permute-start(f32[128,256]{1,0:T(8,128)S(1)} %get-tuple-element.68), channel_id=1, source_target_pairs={{0,2},{1,3},{2,4},{3,5},{4,6},{5,7},{6,0},{7,1},{8,10},{9,11},{10,... | collective-permute-start | bytes 393224 | tf_op jit(solution)/shard_map/ppermute | solution.py:447
  24.9 3.3 %collective-permute-start.2 = (f32[128,256]{1,0:T(8,128)S(1)}, f32[128,256]{1,0:T(8,128)S(1)}, u32[]{:S(2)}, u32[]{:S(2)}) collective-permute-start(f32[128,256]{1,0:T(8,128)S(1)} %get-tuple-element.69), channel_id=1, source_target_pairs={{0,4},{1,5},{2,6},{3,7},{4,0},{5,1},{6,2},{7,3},{8,12},{9,13},{10,... | collective-permute-start | bytes 393224 | tf_op jit(solution)/shard_map/ppermute | solution.py:447
  28.2 0.7 collective-permute-start.3
  28.9 1.8 %collective-permute-done.1.x1 = f32[128,256]{1,0:T(8,128)S(1)} collective-permute-done((f32[128,256]{1,0:T(8,128)S(1)}, f32[128,256]{1,0:T(8,128)S(1)}, u32[]{:S(2)}, u32[]{:S(2)}) %collective-permute-start.1) | collective-permute-done | bytes 131104 | tf_op jit(solution)/shard_map/ppermute | solution.py:447
  30.7 3.6 %collective-permute-done.2.x2 = f32[128,256]{1,0:T(8,128)S(1)} collective-permute-done((f32[128,256]{1,0:T(8,128)S(1)}, f32[128,256]{1,0:T(8,128)S(1)}, u32[]{:S(2)}, u32[]{:S(2)}) %collective-permute-start.2) | collective-permute-done | bytes 131104 | tf_op jit(solution)/shard_map/ppermute | solution.py:447
  34.2 1.2 shard_map.137
  35.5 1.3 collective-permute-start.4
  36.8 2.4 %collective-permute-start.5 = (f32[128,256]{1,0:T(8,128)S(1)}, f32[128,256]{1,0:T(8,128)S(1)}, u32[]{:S(2)}, u32[]{:S(2)}) collective-permute-start(f32[128,256]{1,0:T(8,128)S(1)} %get-tuple-element.71.t0), channel_id=1, source_target_pairs={{0,16},{1,17},{2,18},{3,19},{4,20},{5,21},{6,22},{7,23},{8,24},{9,... | collective-permute-start | bytes 393224 | tf_op jit(solution)/shard_map/ppermute | solution.py:451
  39.2 1.2 collective-permute-start.6
  41.0 3.1 %collective-permute-done.5.t2 = f32[128,256]{1,0:T(8,128)S(1)} collective-permute-done((f32[128,256]{1,0:T(8,128)S(1)}, f32[128,256]{1,0:T(8,128)S(1)}, u32[]{:S(2)}, u32[]{:S(2)}) %collective-permute-start.5) | collective-permute-done | bytes 131104 | tf_op jit(solution)/shard_map/ppermute | solution.py:451
  44.8 1.2 shard_map.138
  46.0 0.8 copy-done.4
  46.7 1.5 collective-permute-start.7
  48.2 2.1 %collective-permute-start.8 = (f32[128,128]{1,0:T(8,128)S(1)}, f32[128,128]{1,0:T(8,128)S(1)}, u32[]{:S(2)}, u32[]{:S(2)}) collective-permute-start(f32[128,128]{1,0:T(8,128)S(1)} %get-tuple-element.75), channel_id=1, source_target_pairs={{0,4},{1,5},{2,6},{3,7},{4,0},{5,1},{6,2},{7,3},{8,12},{9,13},{10,... | collective-permute-start | bytes 196616 | tf_op jit(solution)/shard_map/ppermute | solution.py:447
  50.6 3.3 %shard_map.140.read_ref = f32[8,128,256]{2,1,0:T(8,128)S(1)} custom-call(s32[1,2]{1,0:T(1,128)S(1)} %copy-done.22, bf16[128,1024]{1,0:T(8,128)(2,1)S(1)} %bitcast.30, bf16[128,1024]{1,0:T(8,128)(2,1)S(1)} %bitcast.23, f32[128,8]{1,0:T(8,128)S(1)} %bitcast.27, f32[8,128,256]{2,1,0:T(8,128)S(1)} %get-tuple-element.79.uw_ref), custom_call_target="tpu_custom_call" | custom-call | flops 301989888 | bytes 2625544 | tf_op jit(solution)/shard_map/pallas_call | solution.py:109
  53.9 0.8 shard_map.139
  54.8 3.1 %collective-permute-start.10 = (f32[4,128,128]{2,1,0:T(8,128)S(1)}, f32[4,128,128]{2,1,0:T(8,128)S(1)}, u32[]{:S(2)}, u32[]{:S(2)}) collective-permute-start(f32[4,128,128]{2,1,0:T(8,128)S(1)} %get-tuple-element.78), channel_id=1, source_target_pairs={{0,1},{1,0},{2,3},{3,2},{4,5},{5,4},{6,7},{7,6},{8,9},{9,8},{10,11... | collective-permute-start | bytes 786440 | tf_op jit(solution)/shard_map/ppermute | solution.py:443
  57.9 1.5 fusion.1.dn_ref
  59.4 1.7 %shard_map.141 = (bf16[128,1024]{1,0:T(8,128)(2,1)S(1)}, f32[8,128,128]{2,1,0:T(8,128)S(1)}, f32[4,128,128]{2,1,0:T(8,128)S(1)}, f32[4,128,128]{2,1,0:T(8,128)S(...) custom-call(s32[4]{0:T(128)S(1)} %pad_add_fusion.pos, ...), custom_call_target="tpu_custom_call" | custom-call | tf_op jit(solution)/shard_map/pallas_call | solution.py:507
  62.5 0.8 copy-done.24
  64.0 1.2 collective-permute-start.22
  65.2 2.7 %collective-permute-start.23 = (f32[128,256]{1,0:T(8,128)S(1)}, f32[128,256]{1,0:T(8,128)S(1)}, u32[]{:S(2)}, u32[]{:S(2)}) collective-permute-start(f32[128,256]{1,0:T(8,128)S(1)} %get-tuple-element.111), channel_id=1, source_target_pairs={{0,64},{32,96},{64,0},{96,32},{1,65},{33,97},{65,1},{97,33},{2,66}... | collective-permute-start | bytes 393224 | tf_op jit(solution)/shard_map/ppermute | solution.py:456
  67.9 1.0 collective-permute-start.24
  68.9 1.6 %collective-permute-done.22.n1 = f32[128,256]{1,0:T(8,128)S(1)} collective-permute-done((f32[128,256]{1,0:T(8,128)S(1)}, f32[128,256]{1,0:T(8,128)S(1)}, u32[]{:S(2)}, u32[]{:S(2)}) %collective-permute-start.22) | collective-permute-done | bytes 131104 | tf_op jit(solution)/shard_map/ppermute | solution.py:456
  71.1 3.3 %collective-permute-done.23.n2 = f32[128,256]{1,0:T(8,128)S(1)} collective-permute-done((f32[128,256]{1,0:T(8,128)S(1)}, f32[128,256]{1,0:T(8,128)S(1)}, u32[]{:S(2)}, u32[]{:S(2)}) %collective-permute-start.23) | collective-permute-done | bytes 131104 | tf_op jit(solution)/shard_map/ppermute | solution.py:456
  75.7 1.0 copy-done.15
  76.6 0.9 copy-done.17
  77.5 0.9 copy-done.19
  78.4 0.9 copy-done.21
  79.4 3.6 %shard_map.148 = (f32[16,8,2048]{2,1,0:T(8,128)S(1)}, f32[16,8,2048]{2,1,0:T(8,128)S(1)}) custom-call(s32[4]{0:T(128)S(1)} %pad_add_fusion.pos, f32[128,256]{1,0:T(8,128)S(1)} %copy-done.15, f32[128,256]{1,0:T(8,128)S(1)} %copy-done.17, f32[128,256]{1,0:T(8,128)S(1)} %copy-done.19, f32[128,256]{1,0:T(8,128)S(1)} %copy-done.21, ...), custom_call_target="tpu_custom_call" | custom-call | flops 536870912 | bytes 6815760 | tf_op jit(solution)/shard_map/pallas_call | solution.py:109
  82.9 0.9 collective-permute-start.25
  83.9 2.6 %collective-permute-done.11.recv_ref = f32[4,128,128]{2,1,0:T(8,128)S(1)} collective-permute-done((f32[4,128,128]{2,1,0:T(8,128)S(1)}, f32[4,128,128]{2,1,0:T(8,128)S(1)}, u32[]{:S(2)}, u32[]{:S(2)}) %collective-permute-start.11) | collective-permute-done | bytes 262176 | tf_op jit(solution)/shard_map/ppermute | solution.py:443
  86.5 0.9 shard_map.143
  87.4 0.9 collective-permute-start.12
  88.3 2.0 %collective-permute-start.13 = (f32[128,128]{1,0:T(8,128)S(1)}, f32[128,128]{1,0:T(8,128)S(1)}, u32[]{:S(2)}, u32[]{:S(2)}) collective-permute-start(f32[128,128]{1,0:T(8,128)S(1)} %get-tuple-element.87), channel_id=1, source_target_pairs={{0,4},{1,5},{2,6},{3,7},{4,0},{5,1},{6,2},{7,3},{8,12},{9,13},{10,... | collective-permute-start | bytes 196616 | tf_op jit(solution)/shard_map/ppermute | solution.py:447
  90.8 1.0 collective-permute-done.12.r1
  91.8 2.1 %collective-permute-done.13.r2 = f32[128,128]{1,0:T(8,128)S(1)} collective-permute-done((f32[128,128]{1,0:T(8,128)S(1)}, f32[128,128]{1,0:T(8,128)S(1)}, u32[]{:S(2)}, u32[]{:S(2)}) %collective-permute-start.13) | collective-permute-done | bytes 65568 | tf_op jit(solution)/shard_map/ppermute | solution.py:447
  94.3 1.1 shard_map.144
  95.5 1.1 collective-permute-start.15
  96.5 2.5 %collective-permute-start.16 = (f32[128,128]{1,0:T(8,128)S(1)}, f32[128,128]{1,0:T(8,128)S(1)}, u32[]{:S(2)}, u32[]{:S(2)}) collective-permute-start(f32[128,128]{1,0:T(8,128)S(1)} %get-tuple-element.90.t0), channel_id=1, source_target_pairs={{0,16},{1,17},{2,18},{3,19},{4,20},{5,21},{6,22},{7,23},{8,24},{9,... | collective-permute-start | bytes 196616 | tf_op jit(solution)/shard_map/ppermute | solution.py:451
  99.0 0.9 collective-permute-start.17
  99.9 1.5 collective-permute-done.16.t2
  101.4 1.5 collective-permute-done.17.t3
  102.9 1.5 shard_map.145
  104.6 2.3 %collective-permute-start.19 = (f32[128,128]{1,0:T(8,128)S(1)}, f32[128,128]{1,0:T(8,128)S(1)}, u32[]{:S(2)}, u32[]{:S(2)}) collective-permute-start(f32[128,128]{1,0:T(8,128)S(1)} %get-tuple-element.95), channel_id=1, source_target_pairs={{0,4},{1,5},{2,6},{3,7},{4,0},{5,1},{6,2},{7,3},{8,12},{9,13},{10,... | collective-permute-start | bytes 196616 | tf_op jit(solution)/shard_map/ppermute | solution.py:447
  107.2 6.1 %shard_map.142 = (bf16[128,1024]{1,0:T(8,128)(2,1)}, f32[8,128,128]{2,1,0:T(8,128)S(1)}, f32[8,128,128]{2,1,0:T(8,128)S(1)}, f32[8,128,128]{2,1,0:T(8,128)S(1)},...) custom-call(s32[4]{0:T(128)S(1)} %pad_add_fusion.pos, s32[1,2]{1,0:T(1,128)S(1)} %copy-done.23, ...), custom_call_target="tpu_custom_call" | custom-call | flops 805306368 | bytes 5509144 | tf_op jit(solution)/shard_map/pallas_call | solution.py:109
  113.2 0.9 shard_map.146
  114.1 3.7 %collective-permute-start.21 = (f32[4,128,128]{2,1,0:T(8,128)S(1)}, f32[4,128,128]{2,1,0:T(8,128)S(1)}, u32[]{:S(2)}, u32[]{:S(2)}) collective-permute-start(f32[4,128,128]{2,1,0:T(8,128)S(1)} %get-tuple-element.98), channel_id=1, source_target_pairs={{0,1},{1,0},{2,3},{3,2},{4,5},{5,4},{6,7},{7,6},{8,9},{9,8},{10,11... | collective-permute-start | bytes 786440 | tf_op jit(solution)/shard_map/ppermute | solution.py:443
  118.5 1.3 collective-permute-start.26
  120.4 2.0 %collective-permute-start.28 = (f32[4,8,2048]{2,1,0:T(8,128)S(1)}, f32[4,8,2048]{2,1,0:T(8,128)S(1)}, u32[]{:S(2)}, u32[]{:S(2)}) collective-permute-start(f32[4,8,2048]{2,1,0:T(8,128)S(1)} %get-tuple-element.118), channel_id=1, source_target_pairs={{0,6},{1,7},{2,0},{3,1},{4,2},{5,3},{6,4},{7,5},{8,14},{9,15},{10,... | collective-permute-start | bytes 786440 | tf_op jit(solution)/shard_map/ppermute | solution.py:447
  122.4 1.5 fusion
  123.9 9.4 %collective-permute-done.26.a1 = f32[4,8,2048]{2,1,0:T(8,128)S(1)} collective-permute-done((f32[4,8,2048]{2,1,0:T(8,128)S(1)}, f32[4,8,2048]{2,1,0:T(8,128)S(1)}, u32[]{:S(2)}, u32[]{:S(2)}) %collective-permute-start.26) | collective-permute-done | bytes 262176 | tf_op jit(solution)/shard_map/ppermute | solution.py:447
  134.7 2.9 %collective-permute-start.30 = (f32[8,2048]{1,0:T(8,128)S(1)}, f32[8,2048]{1,0:T(8,128)S(1)}, u32[]{:S(2)}, u32[]{:S(2)}) collective-permute-start(f32[8,2048]{1,0:T(8,128)S(1)} %get-tuple-element.121), channel_id=1, source_target_pairs={{0,16},{1,17},{2,18},{3,19},{4,20},{5,21},{6,22},{7,23},{8,24},{9,... | collective-permute-start | bytes 196616 | tf_op jit(solution)/shard_map/ppermute | solution.py:451
  137.6 7.3 %shard_map.147 = (bf16[128,1024]{1,0:T(8,128)(2,1)}, bf16[128,1024]{1,0:T(8,128)(2,1)}, f32[128,8]{1,0:T(8,128)S(1)}, f32[128,8]{1,0:T(8,128)S(1)}) custom-call(s32[4]{0:T(128)S(1)} %pad_add_fusion.pos, s32[1,2]{1,0:T(1,128)S(1)} %copy-done.23, bf16[128,1024]{1,0:T(8,128)(2,1)S(1)} %bitcast.25, bf16[128,1024]{1,0:T(8,128)(2,1)S(1)} %bitcast.33, ...), custom_call_target="tpu_custom_call" | custom-call | flops 805306368 | bytes 5257240 | tf_op jit(solution)/shard_map/pallas_call | solution.py:109
  (90 shorter events, 12.7 us)
Async XLA Ops:
  7.2 68.5 %all-gather.2.cloned.1.call-start = ((), (), s32[]{:S(2)}) async-start(), calls=%async_computation | async-start | bytes 5242880 | tf_op jit(solution)/shard_map/all_gather | solution.py:479
  11.1 1.0 copy-start
  12.1 0.9 copy-start.12
  13.0 0.7 copy-start.22
  13.7 36.9 %copy-start.1 = (bf16[1,128,1024]{2,1,0:T(8,128)(2,1)S(1)}, bf16[1,128,1024]{2,1,0:T(8,128)(2,1)}, u32[]{:S(2)}) copy-start(bf16[1,128,1024]{2,1,0:T(8,128)(2,1)} %param.9) | copy-start | bytes 786436
  13.7 36.9 %copy-start.8 = (bf16[1,128,1024]{2,1,0:T(8,128)(2,1)S(1)}, bf16[1,128,1024]{2,1,0:T(8,128)(2,1)}, u32[]{:S(2)}) copy-start(bf16[1,128,1024]{2,1,0:T(8,128)(2,1)} %param.8) | copy-start | bytes 786436
  18.4 0.8 copy-start.6
  19.2 38.7 %copy-start.28 = (bf16[1024,2048]{1,0:T(8,128)(2,1)S(1)}, bf16[1024,2048]{1,0:T(8,128)(2,1)}, u32[]{:S(2)}) copy-start(bf16[1024,2048]{1,0:T(8,128)(2,1)} %param.14) | copy-start | bytes 12582916
  19.2 38.7 %copy-start.30 = (bf16[1,128,2048]{2,1,0:T(8,128)(2,1)S(1)}, bf16[1,128,2048]{2,1,0:T(8,128)(2,1)}, u32[]{:S(2)}) copy-start(bf16[1,128,2048]{2,1,0:T(8,128)(2,1)} %param.15) | copy-start | bytes 1572868
  19.2 3.0 %collective-permute-start = (f32[4,128,256]{2,1,0:T(8,128)S(1)}, f32[4,128,256]{2,1,0:T(8,128)S(1)}, u32[]{:S(2)}, u32[]{:S(2)}) collective-permute-start(f32[4,128,256]{2,1,0:T(8,128)S(1)} %get-tuple-element.66), channel_id=1, source_target_pairs={{0,1},{1,0},{2,3},{3,2},{4,5},{5,4},{6,7},{7,6},{8,9},{9,8},{10,11... | collective-permute-start | bytes 1572872 | tf_op jit(solution)/shard_map/ppermute | solution.py:443
  23.1 7.6 %collective-permute-start.1 = (f32[128,256]{1,0:T(8,128)S(1)}, f32[128,256]{1,0:T(8,128)S(1)}, u32[]{:S(2)}, u32[]{:S(2)}) collective-permute-start(f32[128,256]{1,0:T(8,128)S(1)} %get-tuple-element.68), channel_id=1, source_target_pairs={{0,2},{1,3},{2,4},{3,5},{4,6},{5,7},{6,0},{7,1},{8,10},{9,11},{10,... | collective-permute-start | bytes 393224 | tf_op jit(solution)/shard_map/ppermute | solution.py:447
  24.9 9.3 %collective-permute-start.2 = (f32[128,256]{1,0:T(8,128)S(1)}, f32[128,256]{1,0:T(8,128)S(1)}, u32[]{:S(2)}, u32[]{:S(2)}) collective-permute-start(f32[128,256]{1,0:T(8,128)S(1)} %get-tuple-element.69), channel_id=1, source_target_pairs={{0,4},{1,5},{2,6},{3,7},{4,0},{5,1},{6,2},{7,3},{8,12},{9,13},{10,... | collective-permute-start | bytes 393224 | tf_op jit(solution)/shard_map/ppermute | solution.py:447
  28.2 6.1 %collective-permute-start.3 = (f32[128,256]{1,0:T(8,128)S(1)}, f32[128,256]{1,0:T(8,128)S(1)}, u32[]{:S(2)}, u32[]{:S(2)}) collective-permute-start(f32[128,256]{1,0:T(8,128)S(1)} %get-tuple-element.70), channel_id=1, source_target_pairs={{0,6},{1,7},{2,0},{3,1},{4,2},{5,3},{6,4},{7,5},{8,14},{9,15},{10,... | collective-permute-start | bytes 393224 | tf_op jit(solution)/shard_map/ppermute | solution.py:447
  35.5 5.5 %collective-permute-start.4 = (f32[128,256]{1,0:T(8,128)S(1)}, f32[128,256]{1,0:T(8,128)S(1)}, u32[]{:S(2)}, u32[]{:S(2)}) collective-permute-start(f32[128,256]{1,0:T(8,128)S(1)} %get-tuple-element.71.t0), channel_id=1, source_target_pairs={{0,8},{1,9},{2,10},{3,11},{4,12},{5,13},{6,14},{7,15},{8,16},{9,17... | collective-permute-start | bytes 393224 | tf_op jit(solution)/shard_map/ppermute | solution.py:451
  36.8 7.3 %collective-permute-start.5 = (f32[128,256]{1,0:T(8,128)S(1)}, f32[128,256]{1,0:T(8,128)S(1)}, u32[]{:S(2)}, u32[]{:S(2)}) collective-permute-start(f32[128,256]{1,0:T(8,128)S(1)} %get-tuple-element.71.t0), channel_id=1, source_target_pairs={{0,16},{1,17},{2,18},{3,19},{4,20},{5,21},{6,22},{7,23},{8,24},{9,... | collective-permute-start | bytes 393224 | tf_op jit(solution)/shard_map/ppermute | solution.py:451
  39.2 5.5 %collective-permute-start.6 = (f32[128,256]{1,0:T(8,128)S(1)}, f32[128,256]{1,0:T(8,128)S(1)}, u32[]{:S(2)}, u32[]{:S(2)}) collective-permute-start(f32[128,256]{1,0:T(8,128)S(1)} %get-tuple-element.71.t0), channel_id=1, source_target_pairs={{0,24},{1,25},{2,26},{3,27},{4,28},{5,29},{6,30},{7,31},{8,0},{9,1... | collective-permute-start | bytes 393224 | tf_op jit(solution)/shard_map/ppermute | solution.py:451
  45.9 0.8 copy-start.4
  46.7 7.1 %collective-permute-start.7 = (f32[128,128]{1,0:T(8,128)S(1)}, f32[128,128]{1,0:T(8,128)S(1)}, u32[]{:S(2)}, u32[]{:S(2)}) collective-permute-start(f32[128,128]{1,0:T(8,128)S(1)} %get-tuple-element.74), channel_id=1, source_target_pairs={{0,2},{1,3},{2,4},{3,5},{4,6},{5,7},{6,0},{7,1},{8,10},{9,11},{10,... | collective-permute-start | bytes 196616 | tf_op jit(solution)/shard_map/ppermute | solution.py:447
  48.2 5.7 %collective-permute-start.8 = (f32[128,128]{1,0:T(8,128)S(1)}, f32[128,128]{1,0:T(8,128)S(1)}, u32[]{:S(2)}, u32[]{:S(2)}) collective-permute-start(f32[128,128]{1,0:T(8,128)S(1)} %get-tuple-element.75), channel_id=1, source_target_pairs={{0,4},{1,5},{2,6},{3,7},{4,0},{5,1},{6,2},{7,3},{8,12},{9,13},{10,... | collective-permute-start | bytes 196616 | tf_op jit(solution)/shard_map/ppermute | solution.py:447
  50.3 3.6 %collective-permute-start.9 = (f32[128,128]{1,0:T(8,128)S(1)}, f32[128,128]{1,0:T(8,128)S(1)}, u32[]{:S(2)}, u32[]{:S(2)}) collective-permute-start(f32[128,128]{1,0:T(8,128)S(1)} %get-tuple-element.76), channel_id=1, source_target_pairs={{0,6},{1,7},{2,0},{3,1},{4,2},{5,3},{6,4},{7,5},{8,14},{9,15},{10,... | collective-permute-start | bytes 196616 | tf_op jit(solution)/shard_map/ppermute | solution.py:447
  54.8 4.6 %collective-permute-start.10 = (f32[4,128,128]{2,1,0:T(8,128)S(1)}, f32[4,128,128]{2,1,0:T(8,128)S(1)}, u32[]{:S(2)}, u32[]{:S(2)}) collective-permute-start(f32[4,128,128]{2,1,0:T(8,128)S(1)} %get-tuple-element.78), channel_id=1, source_target_pairs={{0,1},{1,0},{2,3},{3,2},{4,5},{5,4},{6,7},{7,6},{8,9},{9,8},{10,11... | collective-permute-start | bytes 786440 | tf_op jit(solution)/shard_map/ppermute | solution.py:443
  59.4 1.7 %copy-start.2 = (f32[4,128,128]{2,1,0:T(8,128)}, f32[4,128,128]{2,1,0:T(8,128)S(1)}, u32[]{:S(2)}) copy-start(f32[4,128,128]{2,1,0:T(8,128)S(1)} %collective-permute-done.10.other_ref) | copy-start | bytes 786436
  61.1 0.7 copy-start.10
  61.8 0.7 copy-start.14
  62.5 0.8 copy-start.24
  63.3 0.7 copy-start.26
  64.0 6.5 %collective-permute-start.22 = (f32[128,256]{1,0:T(8,128)S(1)}, f32[128,256]{1,0:T(8,128)S(1)}, u32[]{:S(2)}, u32[]{:S(2)}) collective-permute-start(f32[128,256]{1,0:T(8,128)S(1)} %get-tuple-element.110), channel_id=1, source_target_pairs={{0,32},{32,64},{64,96},{96,0},{1,33},{33,65},{65,97},{97,1},{2,34}... | collective-permute-start | bytes 393224 | tf_op jit(solution)/shard_map/ppermute | solution.py:456
  65.2 9.2 %collective-permute-start.23 = (f32[128,256]{1,0:T(8,128)S(1)}, f32[128,256]{1,0:T(8,128)S(1)}, u32[]{:S(2)}, u32[]{:S(2)}) collective-permute-start(f32[128,256]{1,0:T(8,128)S(1)} %get-tuple-element.111), channel_id=1, source_target_pairs={{0,64},{32,96},{64,0},{96,32},{1,65},{33,97},{65,1},{97,33},{2,66}... | collective-permute-start | bytes 393224 | tf_op jit(solution)/shard_map/ppermute | solution.py:456
  67.9 7.1 %collective-permute-start.24 = (f32[128,256]{1,0:T(8,128)S(1)}, f32[128,256]{1,0:T(8,128)S(1)}, u32[]{:S(2)}, u32[]{:S(2)}) collective-permute-start(f32[128,256]{1,0:T(8,128)S(1)} %get-tuple-element.112), channel_id=1, source_target_pairs={{0,96},{32,0},{64,32},{96,64},{1,97},{33,1},{65,33},{97,65},{2,98}... | collective-permute-start | bytes 393224 | tf_op jit(solution)/shard_map/ppermute | solution.py:456
  70.4 0.6 copy-start.16
  74.3 0.6 copy-start.18
  75.0 0.7 copy-start.20
  75.7 27.2 %copy-start.5 = (f32[4,128,256]{2,1,0:T(8,128)S(1)}, f32[4,128,256]{2,1,0:T(8,128)}, u32[]{:S(2)}) copy-start(f32[4,128,256]{2,1,0:T(8,128)} %copy-done.4) | copy-start | bytes 1572868
  75.7 1.0 copy-start.15
  76.6 0.9 copy-start.17
  77.5 0.9 copy-start.19
  78.4 0.9 copy-start.21
  79.3 4.5 %copy-start.27 = (f32[4,128,128]{2,1,0:T(8,128)S(1)}, f32[4,128,128]{2,1,0:T(8,128)}, u32[]{:S(2)}) copy-start(f32[4,128,128]{2,1,0:T(8,128)} %copy-done.26) | copy-start | bytes 786436
  79.3 27.8 %copy-start.3 = (f32[4,128,128]{2,1,0:T(8,128)S(1)}, f32[4,128,128]{2,1,0:T(8,128)}, u32[]{:S(2)}) copy-start(f32[4,128,128]{2,1,0:T(8,128)} %copy-done.2) | copy-start | bytes 786436
  79.3 27.8 %copy-start.9 = (bf16[1,128,1024]{2,1,0:T(8,128)(2,1)S(1)}, bf16[1,128,1024]{2,1,0:T(8,128)(2,1)}, u32[]{:S(2)}) copy-start(bf16[1,128,1024]{2,1,0:T(8,128)(2,1)} %param.8) | copy-start | bytes 786436
  79.3 27.8 %copy-start.23 = (s32[1,2]{1,0:T(1,128)S(1)}, s32[1,2]{1,0:T(1,128)}, u32[]{:S(2)}) copy-start(s32[1,2]{1,0:T(1,128)} %resets.7) | copy-start | bytes 28
  79.4 27.8 %copy-start.25 = (f32[8,128,128]{2,1,0:T(8,128)S(1)}, f32[8,128,128]{2,1,0:T(8,128)}, u32[]{:S(2)}) copy-start(f32[8,128,128]{2,1,0:T(8,128)} %copy-done.24) | copy-start | bytes 1572868
  82.9 34.9 %collective-permute-start.25 = (f32[16,8,2048]{2,1,0:T(8,128)S(1)}, f32[16,8,2048]{2,1,0:T(8,128)S(1)}, u32[]{:S(2)}, u32[]{:S(2)}) collective-permute-start(f32[16,8,2048]{2,1,0:T(8,128)S(1)} %get-tuple-element.114), channel_id=1, source_target_pairs={{0,1},{1,0},{2,3},{3,2},{4,5},{5,4},{6,7},{7,6},{8,9},{9,8},{10,11... | collective-permute-start | bytes 3145736 | tf_op jit(solution)/shard_map/ppermute | solution.py:443
  83.8 2.7 %collective-permute-start.11 = (f32[4,128,128]{2,1,0:T(8,128)S(1)}, f32[4,128,128]{2,1,0:T(8,128)S(1)}, u32[]{:S(2)}, u32[]{:S(2)}) collective-permute-start(f32[4,128,128]{2,1,0:T(8,128)S(1)} %copy-done.27), channel_id=1, source_target_pairs={{0,1},{1,0},{2,3},{3,2},{4,5},{5,4},{6,7},{7,6},{8,9},{9,8},{10,11... | collective-permute-start | bytes 786440 | tf_op jit(solution)/shard_map/ppermute | solution.py:443
  87.4 4.4 %collective-permute-start.12 = (f32[128,128]{1,0:T(8,128)S(1)}, f32[128,128]{1,0:T(8,128)S(1)}, u32[]{:S(2)}, u32[]{:S(2)}) collective-permute-start(f32[128,128]{1,0:T(8,128)S(1)} %get-tuple-element.86), channel_id=1, source_target_pairs={{0,2},{1,3},{2,4},{3,5},{4,6},{5,7},{6,0},{7,1},{8,10},{9,11},{10,... | collective-permute-start | bytes 196616 | tf_op jit(solution)/shard_map/ppermute | solution.py:447
  88.3 5.6 %collective-permute-start.13 = (f32[128,128]{1,0:T(8,128)S(1)}, f32[128,128]{1,0:T(8,128)S(1)}, u32[]{:S(2)}, u32[]{:S(2)}) collective-permute-start(f32[128,128]{1,0:T(8,128)S(1)} %get-tuple-element.87), channel_id=1, source_target_pairs={{0,4},{1,5},{2,6},{3,7},{4,0},{5,1},{6,2},{7,3},{8,12},{9,13},{10,... | collective-permute-start | bytes 196616 | tf_op jit(solution)/shard_map/ppermute | solution.py:447
  90.3 4.0 %collective-permute-start.14 = (f32[128,128]{1,0:T(8,128)S(1)}, f32[128,128]{1,0:T(8,128)S(1)}, u32[]{:S(2)}, u32[]{:S(2)}) collective-permute-start(f32[128,128]{1,0:T(8,128)S(1)} %get-tuple-element.88), channel_id=1, source_target_pairs={{0,6},{1,7},{2,0},{3,1},{4,2},{5,3},{6,4},{7,5},{8,14},{9,15},{10,... | collective-permute-start | bytes 196616 | tf_op jit(solution)/shard_map/ppermute | solution.py:447
  95.5 4.4 %collective-permute-start.15 = (f32[128,128]{1,0:T(8,128)S(1)}, f32[128,128]{1,0:T(8,128)S(1)}, u32[]{:S(2)}, u32[]{:S(2)}) collective-permute-start(f32[128,128]{1,0:T(8,128)S(1)} %get-tuple-element.90.t0), channel_id=1, source_target_pairs={{0,8},{1,9},{2,10},{3,11},{4,12},{5,13},{6,14},{7,15},{8,16},{9,17... | collective-permute-start | bytes 196616 | tf_op jit(solution)/shard_map/ppermute | solution.py:451
  96.5 4.9 %collective-permute-start.16 = (f32[128,128]{1,0:T(8,128)S(1)}, f32[128,128]{1,0:T(8,128)S(1)}, u32[]{:S(2)}, u32[]{:S(2)}) collective-permute-start(f32[128,128]{1,0:T(8,128)S(1)} %get-tuple-element.90.t0), channel_id=1, source_target_pairs={{0,16},{1,17},{2,18},{3,19},{4,20},{5,21},{6,22},{7,23},{8,24},{9,... | collective-permute-start | bytes 196616 | tf_op jit(solution)/shard_map/ppermute | solution.py:451
  99.0 3.9 %collective-permute-start.17 = (f32[128,128]{1,0:T(8,128)S(1)}, f32[128,128]{1,0:T(8,128)S(1)}, u32[]{:S(2)}, u32[]{:S(2)}) collective-permute-start(f32[128,128]{1,0:T(8,128)S(1)} %get-tuple-element.90.t0), channel_id=1, source_target_pairs={{0,24},{1,25},{2,26},{3,27},{4,28},{5,29},{6,30},{7,31},{8,0},{9,1... | collective-permute-start | bytes 196616 | tf_op jit(solution)/shard_map/ppermute | solution.py:451
  102.9 19.5 %copy-start.11 = (bf16[128,1024]{1,0:T(8,128)(2,1)S(1)}, bf16[128,1024]{1,0:T(8,128)(2,1)}, u32[]{:S(2)}) copy-start(bf16[128,1024]{1,0:T(8,128)(2,1)} %copy-done.10) | copy-start | bytes 786436
  102.9 19.5 %copy-start.29 = (bf16[1024,2048]{1,0:T(8,128)(2,1)S(1)}, bf16[1024,2048]{1,0:T(8,128)(2,1)}, u32[]{:S(2)}) copy-start(bf16[1024,2048]{1,0:T(8,128)(2,1)} %param.14) | copy-start | bytes 12582916
  104.4 8.8 %collective-permute-start.18 = (f32[128,128]{1,0:T(8,128)S(1)}, f32[128,128]{1,0:T(8,128)S(1)}, u32[]{:S(2)}, u32[]{:S(2)}) collective-permute-start(f32[128,128]{1,0:T(8,128)S(1)} %get-tuple-element.94), channel_id=1, source_target_pairs={{0,2},{1,3},{2,4},{3,5},{4,6},{5,7},{6,0},{7,1},{8,10},{9,11},{10,... | collective-permute-start | bytes 196616 | tf_op jit(solution)/shard_map/ppermute | solution.py:447
  104.6 8.7 %collective-permute-start.19 = (f32[128,128]{1,0:T(8,128)S(1)}, f32[128,128]{1,0:T(8,128)S(1)}, u32[]{:S(2)}, u32[]{:S(2)}) collective-permute-start(f32[128,128]{1,0:T(8,128)S(1)} %get-tuple-element.95), channel_id=1, source_target_pairs={{0,4},{1,5},{2,6},{3,7},{4,0},{5,1},{6,2},{7,3},{8,12},{9,13},{10,... | collective-permute-start | bytes 196616 | tf_op jit(solution)/shard_map/ppermute | solution.py:447
  106.9 6.4 %collective-permute-start.20 = (f32[128,128]{1,0:T(8,128)S(1)}, f32[128,128]{1,0:T(8,128)S(1)}, u32[]{:S(2)}, u32[]{:S(2)}) collective-permute-start(f32[128,128]{1,0:T(8,128)S(1)} %get-tuple-element.96), channel_id=1, source_target_pairs={{0,6},{1,7},{2,0},{3,1},{4,2},{5,3},{6,4},{7,5},{8,14},{9,15},{10,... | collective-permute-start | bytes 196616 | tf_op jit(solution)/shard_map/ppermute | solution.py:447
  114.1 23.5 %copy-start.7 = (f32[8,128,128]{2,1,0:T(8,128)S(1)}, f32[8,128,128]{2,1,0:T(8,128)}, u32[]{:S(2)}) copy-start(f32[8,128,128]{2,1,0:T(8,128)} %copy-done.6) | copy-start | bytes 1572868
  114.1 23.5 %copy-start.13 = (bf16[1,128,1024]{2,1,0:T(8,128)(2,1)S(1)}, bf16[1,128,1024]{2,1,0:T(8,128)(2,1)}, u32[]{:S(2)}) copy-start(bf16[1,128,1024]{2,1,0:T(8,128)(2,1)} %param.10) | copy-start | bytes 786436
  114.1 23.5 %collective-permute-start.21 = (f32[4,128,128]{2,1,0:T(8,128)S(1)}, f32[4,128,128]{2,1,0:T(8,128)S(1)}, u32[]{:S(2)}, u32[]{:S(2)}) collective-permute-start(f32[4,128,128]{2,1,0:T(8,128)S(1)} %get-tuple-element.98), channel_id=1, source_target_pairs={{0,1},{1,0},{2,3},{3,2},{4,5},{5,4},{6,7},{7,6},{8,9},{9,8},{10,11... | collective-permute-start | bytes 786440 | tf_op jit(solution)/shard_map/ppermute | solution.py:443
  118.5 14.8 %collective-permute-start.26 = (f32[4,8,2048]{2,1,0:T(8,128)S(1)}, f32[4,8,2048]{2,1,0:T(8,128)S(1)}, u32[]{:S(2)}, u32[]{:S(2)}) collective-permute-start(f32[4,8,2048]{2,1,0:T(8,128)S(1)} %get-tuple-element.116), channel_id=1, source_target_pairs={{0,2},{1,3},{2,4},{3,5},{4,6},{5,7},{6,0},{7,1},{8,10},{9,11},{10,... | collective-permute-start | bytes 786440 | tf_op jit(solution)/shard_map/ppermute | solution.py:447
  119.8 13.6 %collective-permute-start.27 = (f32[4,8,2048]{2,1,0:T(8,128)S(1)}, f32[4,8,2048]{2,1,0:T(8,128)S(1)}, u32[]{:S(2)}, u32[]{:S(2)}) collective-permute-start(f32[4,8,2048]{2,1,0:T(8,128)S(1)} %get-tuple-element.117), channel_id=1, source_target_pairs={{0,4},{1,5},{2,6},{3,7},{4,0},{5,1},{6,2},{7,3},{8,12},{9,13},{10,... | collective-permute-start | bytes 786440 | tf_op jit(solution)/shard_map/ppermute | solution.py:447
  120.4 13.2 %collective-permute-start.28 = (f32[4,8,2048]{2,1,0:T(8,128)S(1)}, f32[4,8,2048]{2,1,0:T(8,128)S(1)}, u32[]{:S(2)}, u32[]{:S(2)}) collective-permute-start(f32[4,8,2048]{2,1,0:T(8,128)S(1)} %get-tuple-element.118), channel_id=1, source_target_pairs={{0,6},{1,7},{2,0},{3,1},{4,2},{5,3},{6,4},{7,5},{8,14},{9,15},{10,... | collective-permute-start | bytes 786440 | tf_op jit(solution)/shard_map/ppermute | solution.py:447
  134.2 12.1 %collective-permute-start.29 = (f32[8,2048]{1,0:T(8,128)S(1)}, f32[8,2048]{1,0:T(8,128)S(1)}, u32[]{:S(2)}, u32[]{:S(2)}) collective-permute-start(f32[8,2048]{1,0:T(8,128)S(1)} %get-tuple-element.120), channel_id=1, source_target_pairs={{0,8},{1,9},{2,10},{3,11},{4,12},{5,13},{6,14},{7,15},{8,16},{9,17... | collective-permute-start | bytes 196616 | tf_op jit(solution)/shard_map/ppermute | solution.py:451
  134.7 11.6 %collective-permute-start.30 = (f32[8,2048]{1,0:T(8,128)S(1)}, f32[8,2048]{1,0:T(8,128)S(1)}, u32[]{:S(2)}, u32[]{:S(2)}) collective-permute-start(f32[8,2048]{1,0:T(8,128)S(1)} %get-tuple-element.121), channel_id=1, source_target_pairs={{0,16},{1,17},{2,18},{3,19},{4,20},{5,21},{6,22},{7,23},{8,24},{9,... | collective-permute-start | bytes 196616 | tf_op jit(solution)/shard_map/ppermute | solution.py:451
  137.6 8.7 %collective-permute-start.31 = (f32[8,2048]{1,0:T(8,128)S(1)}, f32[8,2048]{1,0:T(8,128)S(1)}, u32[]{:S(2)}, u32[]{:S(2)}) collective-permute-start(f32[8,2048]{1,0:T(8,128)S(1)} %get-tuple-element.122), channel_id=1, source_target_pairs={{0,24},{1,25},{2,26},{3,27},{4,28},{5,29},{6,30},{7,31},{8,0},{9,1... | collective-permute-start | bytes 196616 | tf_op jit(solution)/shard_map/ppermute | solution.py:451
Sparse Core Ops, SparseCore 0:
  9.7 51.4 all-gather.1

commit v2 on v1

--- a/solution.py
+++ b/solution.py
@@ -31,7 +31,13 @@
 def mm(a, b, dims=NN):
     ah, al = split(a)
     bh, bl = split(b)
-    return dot(ah, bh, dims) + (dot(ah, bl, dims) + dot(al, bh, dims))
+    left = jnp.concatenate([ah, al], axis=1)
+    if dims == NN and b.shape[1] > C:
+        return dot(left, jnp.concatenate([bh, bh], axis=0)) + dot(ah, bl)
+    n = dims[0][1][0]
+    right = jnp.concatenate([bh, bl], axis=1 - n)
+    both = dot(left, jnp.concatenate([right, right], axis=n), dims)
+    return both[:, :C] + both[:, C:]
 
 
 def tn(a, b):
@@ -63,8 +69,8 @@
     lower = (rows >= cols).astype(bf16)
     upper = (rows <= cols).astype(bf16)
     parts = split3(g_ref[...])
-    total_c = sum(dot(lower, part) for part in parts)
-    total_r = sum(dot(part, upper, TN) for part in parts)
+    total_c = sum(dot(lower, part, NT) for part in parts)
+    total_r = sum(dot(part, upper) for part in parts)
     r1 = resets_ref[0, 0].astype(f32)
     r2 = resets_ref[0, 1].astype(f32)
     tcol = lax.broadcasted_iota(jnp.int32, (C, 1), 0)
@@ -89,6 +95,11 @@
     return inside, growth, fading, g_last
 
 
+def columns(ref):
+    rows, cols = iotas()
+    return dot((rows == cols).astype(bf16), ref[...], NT)
+
+
 def strict(x):
     rows, cols = iotas()
     return jnp.where(rows > cols, x, 0.0)
@@ -102,32 +113,51 @@
     return [pl.BlockSpec(memory_space=pltpu.SMEM)] * n
 
 
-def call(kernel, outs, n_smem, *args, flops=0):
+def call(kernel, outs, n_smem, *args, flops=0, scratch=(), hbm=0, after=(), limit=VMEM_LIMIT):
     nbytes = sum(a.size * a.dtype.itemsize for a in args) + sum(
         math.prod(s) * jnp.dtype(d).itemsize for s, d in outs
     )
+    n_after = len(after)
+
+    def body(*refs):
+        kernel(*refs[n_after:])
+
+    in_specs = (
+        [pl.BlockSpec(memory_space=pl.ANY)] * n_after
+        + spec_s(n_smem)
+        + [pl.BlockSpec(memory_space=pltpu.HBM)] * hbm
+        + spec_v(len(args) - n_smem - hbm)
+    )
     return pl.pallas_call(
-        kernel,
+        body,
         out_shape=[jax.ShapeDtypeStruct(s, d) for s, d in outs],
-        in_specs=spec_s(n_smem) + spec_v(len(args) - n_smem),
+        in_specs=in_specs,
         out_specs=spec_v(len(outs)),
-        compiler_params=pltpu.CompilerParams(vmem_limit_bytes=VMEM_LIMIT),
+        scratch_shapes=list(scratch),
+        compiler_params=pltpu.CompilerParams(vmem_limit_bytes=limit),
         cost_estimate=pl.CostEstimate(flops=flops, bytes_accessed=nbytes, transcendentals=0),
-    )(*args)
+    )(*after, *args)
 
 
 HEADS = range(H)
 SQ = 2 * C * C * C * 3
 
 
-def maps_kernel(pos, resets, k_ref, v_ref, b_ref, g_ref, keep_ref, send_ref, inv_ref, uw_ref):
+def maps_kernel(
+    pos, resets, k_hbm, v_hbm, b_ref, g_ref, keep_ref, send_ref, inv_ref, uw_ref, k_ref, v_ref, sems
+):
+    load_k = pltpu.make_async_copy(k_hbm, k_ref, sems.at[0])
+    load_v = pltpu.make_async_copy(v_hbm, v_ref, sems.at[1])
+    load_k.start()
+    load_v.start()
     tables = gate_tables(g_ref, resets)
     rows, cols = iotas()
     eye = (rows == cols).astype(f32)
     block = (rows >= 64) == (cols >= 64)
-    beta = b_ref[...].astype(f32)
+    beta = columns(b_ref)
+    gates = [head_gates(tables, h) for h in HEADS]
+    load_k.wait()
     kn = [unit(head(k_ref, h))[0] for h in HEADS]
-    gates = [head_gates(tables, h) for h in HEADS]
     kk = [mm(kn[h], kn[h], NT) for h in HEADS]
     system = [strict(kk[h] * gates[h][0]) * beta[:, h : h + 1] for h in HEADS]
     near = [jnp.where(block, x, 0.0) for x in system]
@@ -143,6 +173,7 @@
             inv = [inv[h] + mm(inv[h], power[h]) for h in HEADS]
     cross = [mm(far[h], inv[h]) for h in HEADS]
     inv = [inv[h] - mm(inv[h], cross[h]) for h in HEADS]
+    load_v.wait()
     uw = []
     for h in HEADS:
         bh = beta[:, h : h + 1]
@@ -235,7 +266,7 @@
 
 
 def outs_kernel(
-    pos, mine_ref, other_ref, read_ref, dn_ref, n_ref, do_ref, keep_ref, send_ref, c0, c1, c2, c3, wide
+    pos, mine_ref, other_ref, read_ref, dn_ref, n_ref, do_ref, keep_ref, send_ref
 ):
     first = pos[3] == 0
     reach = []
@@ -245,9 +276,7 @@
         out = mm(read[:, :C], state) + read[:, C:]
         inv = 1.0 / jnp.sqrt(jnp.mean(out * out, axis=-1, keepdims=True) + EPS)
         n32 = out * inv
-        n16 = n32.astype(bf16)
-        n_ref[:, h * C : (h + 1) * C] = n16
-        wide[h // 2, :, (h % 2) * C : (h % 2 + 1) * C] = n16.astype(f32)
+        n_ref[:, h * C : (h + 1) * C] = n32.astype(bf16)
         dn = dn_ref[:, h * C : (h + 1) * C]
         do = inv * (dn - n32 * jnp.mean(n32 * dn, axis=-1, keepdims=True))
         do_ref[h] = do
@@ -255,11 +284,15 @@
     for j in range(4):
         keep_ref[j] = jnp.where(first, reach[j], reach[j + 4])
         send_ref[j] = jnp.where(first, reach[j + 4], reach[j])
+
+
+def pair_back_kernel(
+    pos, keep_ref, recv_ref, mkeep_ref, mrecv_ref, n_ref, o0, o1, o2, o3, c0, c1, c2, c3, scratch, wide
+):
+    for j in range(4):
+        wide[j] = n_ref[:, 2 * j * C : 2 * (j + 1) * C].astype(f32)
     for r, out_ref in enumerate((c0, c1, c2, c3)):
         out_ref[...] = wide[(pos[0] + r) % 4]
-
-
-def pair_back_kernel(pos, keep_ref, recv_ref, mkeep_ref, mrecv_ref, o0, o1, o2, o3, scratch):
     first = pos[3] == 0
     for j in range(4):
         a, b = keep_ref[j], recv_ref[j]
@@ -349,7 +382,7 @@
     first = pos[3] == 0
     tables = gate_tables(g_ref, resets)
     rows, cols = iotas()
-    beta = b_ref[...].astype(f32)
+    beta = columns(b_ref)
     db_all = jnp.zeros((C, C), f32)
     dt_all = jnp.zeros((C, C), f32)
     is_last = lax.broadcasted_iota(jnp.int32, (C, 1), 0) == C - 1
@@ -394,21 +427,28 @@
         )
         db_all = jnp.where(cols == h, db, db_all)
         dt_all = jnp.where(cols == h, dtotal, dt_all)
-    upper = (rows <= cols).astype(bf16)
-    dg_all = sum(dot(upper, part) for part in split3(dt_all))
-    db_ref[...] = db_all[:, :H]
-    dg_ref[...] = dg_all[:, :H]
-
-
-def wgrad_kernel(pos, n0, n1, n2, n3, cot_ref, keep_ref, send_ref):
-    order = [(pos[0] + 4 - r) % 4 for r in range(4)]
+    lower = (rows >= cols).astype(bf16)
+    db_ref[...] = db_all.T[:H]
+    dg_ref[...] = sum(dot(part, lower) for part in split3(dt_all.T[:H]))
+
+
+def widen_kernel(x_ref, o_ref):
+    o_ref[...] = x_ref[...].astype(f32)
+
+
+def relay_kernel(below_ref, above_ref, lower_ref, upper_ref):
+    lower_ref[...] = below_ref[:64, :]
+    upper_ref[...] = above_ref[64:, :]
+
+
+def wgrad_kernel(pos, n0, n1, n2, n3, c0, c1, c3, c2_low, c2_up, keep_ref, send_ref):
     ns = [ref[...].astype(bf16).T for ref in (n0, n1, n2, n3)]
     first = pos[3] == 0
     for j in range(8):
         cols = slice(j * 256, (j + 1) * 256)
-        total = sum(
-            dot(ns[r], cot_ref[order[r], :, cols].astype(bf16)) for r in range(4)
-        ).reshape(16, 2, 8, 256)
+        far = jnp.concatenate([c2_low[:, cols], c2_up[:, cols]], axis=0)
+        cots = (c0[:, cols], c1[:, cols], far, c3[:, cols])
+        total = sum(dot(ns[r], cots[r].astype(bf16)) for r in range(4)).reshape(16, 2, 8, 256)
         a, b = total[:, 0], total[:, 1]
         keep_ref[:, :, cols] = jnp.where(first, a, b)
         send_ref[:, :, cols] = jnp.where(first, b, a)
@@ -451,118 +491,110 @@
     return [parts[0]] + [lax.ppermute(parts[r], "seq", seq_perm(r, 0)) for r in (1, 2, 3)]
 
 
+def step_dp(x, r):
+    return lax.ppermute(x, "dp", [(i, (i + r) % 4) for i in range(4)])
+
+
 def around_dp(parts):
-    return [parts[0]] + [
-        lax.ppermute(parts[r], "dp", [(i, (i + r) % 4) for i in range(4)]) for r in (1, 2, 3)
-    ]
-
-
-def with_scratch(kernel, outs, n_smem, scratch, *args):
-    return pl.pallas_call(
-        kernel,
-        out_shape=[jax.ShapeDtypeStruct(s, f32) for s in outs],
-        in_specs=spec_s(n_smem) + spec_v(len(args) - n_smem),
-        out_specs=spec_v(len(outs)),
-        scratch_shapes=[pltpu.VMEM(s, f32) for s in scratch],
-        compiler_params=pltpu.CompilerParams(vmem_limit_bytes=VMEM_LIMIT),
-    )(*args)
+    return [parts[0]] + [step_dp(parts[r], r) for r in (1, 2, 3)]
 
 
 def local(queries, keys, values, strength, log_decay, resets, out_weight, cotangent):
     q, k, v = queries[0], keys[0], values[0]
-    b, g = strength[0], log_decay[0]
+    b, g = strength[0].T, log_decay[0].T
     cot = cotangent[0]
     seq = lax.axis_index("seq")
     pos = jnp.stack([lax.axis_index("dp"), seq // 8, (seq // 2) % 4, seq % 2]).astype(jnp.int32)
     n_all = C * lax.axis_size("seq") * lax.axis_size("dp")
 
-    cots = lax.all_gather(cot.astype(f32), "dp")
-
     mat, mat2 = (C, C), (C, 2 * C)
+    one, two = (mat, f32), (mat2, f32)
+    four, four2 = ((4, *mat), f32), ((4, *mat2), f32)
+    all1, all2 = ((H, *mat), f32), ((H, *mat2), f32)
+    wide = ((C, H * C), bf16)
+    hold, hold2 = [pltpu.VMEM(*four)], [pltpu.VMEM(*four2)]
+
     mkeep, msend, inverse, uw = call(
         maps_kernel,
-        [((4, *mat2), f32), ((4, *mat2), f32), ((H, *mat), f32), ((H, *mat2), f32)],
-        2, pos, resets, k, v, b, g, flops=30 * H * SQ,
+        [four2, four2, all1, all2],
+        2, pos, resets, k, v, b, g, flops=30 * H * SQ, hbm=2, limit=62 * 1024 * 1024,
+        scratch=[pltpu.VMEM(*wide), pltpu.VMEM(*wide), pltpu.SemaphoreType.DMA((2,))],
     )
     mrecv = swap_core(msend)
-    parts = with_scratch(pair_kernel, [mat2] * 4, 1, [(4, *mat2)], pos, mkeep, mrecv)
+    parts = call(pair_kernel, [two] * 4, 1, pos, mkeep, mrecv, scratch=hold2)
+    own = parts[0]
     parts = around_z(parts)
+    (cot32,) = call(widen_kernel, [((C, 2048), f32)], 0, cot, after=(own,))
+    below, above = step_dp(cot32, 1), step_dp(cot32, 3)
     dn = lax.dot_general(cot, out_weight, NT, preferred_element_type=f32)
-    (reads,) = call(
-        reads_kernel, [((H, *mat2), f32)], 1, resets, q, k, g, uw, flops=3 * H * SQ
-    )
     maps, prefix, total = call(
-        group_kernel, [((4, *mat2), f32), ((3, *mat2), f32), (mat2, f32)], 1, pos, *parts
+        group_kernel, [four2, ((3, *mat2), f32), two], 1, pos, *parts, after=(dn, cot32)
     )
     parts = around_x([total] * 4)
-    totals, *parts = with_scratch(
-        enter_kernel, [(4, *mat2)] + [mat] * 4, 1, [(4, *mat)], pos, *parts, prefix
-    )
+    (reads,) = call(reads_kernel, [all2], 1, resets, q, k, g, uw, flops=3 * H * SQ, after=(total,))
+    totals, *parts = call(
+        enter_kernel, [four2] + [one] * 4, 1, pos, *parts, prefix, scratch=hold, after=(reads,)
+    )
+    own = parts[0]
     parts = around_z(parts)
-    mine, other = with_scratch(
-        split_pair_kernel, [(4, *mat)] * 2, 1, [(4, *mat)], pos, *parts, mkeep, mrecv
-    )
+    lower, upper = call(relay_kernel, [((64, 2048), f32)] * 2, 0, below, above, after=(own,))
+    lower, upper = step_dp(lower, 1), step_dp(upper, 3)
+    mine, other = call(split_pair_kernel, [four] * 2, 1, pos, *parts, mkeep, mrecv, scratch=hold)
     other = swap_core(other)
 
-    n16, do, rkeep, rsend, *chunks = pl.pallas_call(
-        outs_kernel,
-        out_shape=[
-            jax.ShapeDtypeStruct(s, d)
-            for s, d in [((C, H * C), bf16), ((H, *mat), f32), ((4, *mat), f32), ((4, *mat), f32)]
-            + [(mat2, f32)] * 4
-        ],
-        in_specs=spec_s(1) + spec_v(4),
-        out_specs=spec_v(8),
-        scratch_shapes=[pltpu.VMEM((4, *mat2), f32)],
-        compiler_params=pltpu.CompilerParams(vmem_limit_bytes=VMEM_LIMIT),
-    )(pos, mine, other, reads, dn)
+    n16, do, rkeep, rsend = call(
+        outs_kernel, [wide, all1, four, four], 1, pos, mine, other, reads, dn
+    )
 
     rrecv = swap_core(rsend)
-    parts = with_scratch(
-        pair_back_kernel, [mat] * 4, 1, [(4, *mat)], pos, rkeep, rrecv, mkeep, mrecv
-    )
-    parts = around_z(parts)
-    chunks = around_dp(chunks)
+    parts = call(
+        pair_back_kernel, [one] * 4 + [two] * 4, 1, pos, rkeep, rrecv, mkeep, mrecv, n16,
+        scratch=hold + hold2,
+    )
+    chunks = around_dp(parts[4:])
+    parts = around_z(parts[:4])
     mixed = lax.dot_general(n16, out_weight, NN, preferred_element_type=f32).astype(bf16)
-    reach, total = call(
-        group_back_kernel, [((4, *mat), f32), (mat, f32)], 1, pos, *parts, maps
-    )
+    reach, total = call(group_back_kernel, [four, one], 1, pos, *parts, maps, after=(mixed,))
     parts = around_x([total] * 4)
     wkeep, wsend = call(
-        wgrad_kernel, [((16, 8, 2048), f32)] * 2, 1, pos, *chunks, cots, flops=2 * 512 * 256 * 2048
-    )
+        wgrad_kernel,
+        [((16, 8, 2048), f32)] * 2,
+        1, pos, *chunks, cot, below, above, lower, upper, flops=2 * 512 * 256 * 2048, after=(total,),
+    )
+    wrecv = swap_core(wsend)
+    wparts = call(wsum_pair_kernel, [((4, 8, 2048), f32)] * 4, 1, pos, wkeep, wrecv)
+    parts = call(
+        enter_back_kernel, [one] * 4, 1, pos, *parts, totals, maps, reach, scratch=hold + hold,
+        after=(wparts[0],),
+    )
+    own = parts[0]
+    parts = around_z(parts)
+    wparts = around_z(wparts)
     dq, delta, dkn, dd, pairs, dgrow = call(
         early_grads_kernel,
-        [((C, H * C), bf16)] + [((H, *mat), f32)] * 5,
-        2, pos, resets, q, k, g, mine, other, uw, do, flops=8 * H * SQ,
-    )
-    parts = with_scratch(
-        enter_back_kernel, [mat] * 4, 1, [(4, *mat), (4, *mat)], pos, *parts, totals, maps, reach
-    )
-    parts = around_z(parts)
-    dmine, dother = with_scratch(
-        split_pair_back_kernel, [(4, *mat)] * 2, 1, [(4, *mat)], pos, *parts, mkeep, mrecv, rkeep, rrecv
+        [wide] + [all1] * 5,
+        2, pos, resets, q, k, g, mine, other, uw, do, flops=8 * H * SQ, after=(own,),
+    )
+    dmine, dother = call(
+        split_pair_back_kernel, [four] * 2, 1, pos, *parts, mkeep, mrecv, rkeep, rrecv, scratch=hold,
+        after=(delta,),
     )
     dother = swap_core(dother)
+    wparts = call(wsum_z_kernel, [((8, 2048), f32)] * 4, 1, pos, *wparts, after=(dmine,))
     dk, dv, db, dg = call(
         late_grads_kernel,
-        [((C, H * C), bf16), ((C, H * C), bf16), ((C, H), f32), ((C, H), f32)],
+        [wide, wide, ((H, C), f32), ((H, C), f32)],
         2, pos, resets, k, v, b, g, mine, other, dmine, dother, inverse, delta, dkn, dd, pairs, dgrow,
-        flops=8 * H * SQ,
-    )
-
-    wrecv = swap_core(wsend)
-    wparts = call(wsum_pair_kernel, [((4, 8, 2048), f32)] * 4, 1, pos, wkeep, wrecv)
-    wparts = around_z(wparts)
-    wparts = call(wsum_z_kernel, [((8, 2048), f32)] * 4, 1, pos, *wparts)
+        flops=8 * H * SQ, after=(wparts[0],),
+    )
     wparts = around_x(wparts)
     scale = 1.0 / math.sqrt(n_all)
 
     def last(a0, a1, a2, a3, out):
         wsum_x_kernel(scale, a0, a1, a2, a3, out)
 
-    (weight_grad,) = call(last, [((8, 2048), f32)], 0, *wparts)
-    return (mixed[None], dq[None], dk[None], dv[None], db[None], dg[None], weight_grad)
+    (weight_grad,) = call(last, [((8, 2048), f32)], 0, *wparts, after=(db,))
+    return (mixed[None], dq[None], dk[None], dv[None], db.T[None], dg.T[None], weight_grad)
 
 
 def solution(mesh):

time: 155 us -> 118 us (0.76)
  waiting for transfers between devices: 34.9 us -> 20.4 us
  local copies, waits for them, and re-layouts: 15.6 us -> 1.79 us
  between operations: 14.4 us -> 1.03 us
  starting transfers between devices: 46.5 us -> 51 us
  matrix products: 3.04 us -> 6.61 us
  other arithmetic: 2.24 us -> 0.59 us
    unnamed x66 -> x30, local copies, waits for them, and re-layouts: 15.6 us -> 1.79 us
    ppermute x15, waiting for transfers between devices: 18.6 us -> 8.51 us  [around_z(): lax.ppermute(parts[r], 'seq', seq_perm(0, r))]
    ppermute x9, waiting for transfers between devices: 7.4 us -> 3.92 us  [around_x(): lax.ppermute(parts[r], 'seq', seq_perm(r, 0))]
    ppermute x3 -> x7, starting transfers between devices: 4.89 us -> 7.07 us  [step_dp(): return lax.ppermute(x, 'dp', [(i, (i + r) % 4) for i in range(4)])]
    dot_general x1, matrix products: 1.51 us -> 3.7 us  [local(): dn = lax.dot_general(cot, out_weight, NT, preferred_element_type=f32)]
    convert_element_type x1 -> x0, other arithmetic: 2.16 us -> none  [local(): cots = lax.all_gather(cot.astype(f32), 'dp')]
    pallas_call x17 -> x19, Pallas kernels: 37.1 us -> 35.6 us  [call(): pl.pallas_call(body, out_shape=[jax.ShapeDtypeStruct(s, d) for s, d in ou...]
    ppermute x3 -> x7, waiting for transfers between devices: 4.84 us -> 5.02 us  [step_dp(): return lax.ppermute(x, 'dp', [(i, (i + r) % 4) for i in range(4)])]
  transfers between devices with their start and end apart: 33 -> 36, of which waited for: 16 -> 15; matrix products, arithmetic and copies ran while one was open for 4% -> 6% of each run, Pallas kernels for 21% -> 20%
where the time goes in v2:
time: 118 us; the launch traced here: 117 us
  starting transfers between devices  51 us (43%)
  Pallas kernels  35.6 us (30%)
  waiting for transfers between devices  20.4 us (17%)
  matrix products  6.61 us (6%)
  local copies, waits for them, and re-layouts  1.79 us (2%)
    pallas_call x19, Pallas kernels, call(): pl.pallas_call(body, out_shape=[jax.ShapeDtypeStruct(s, d) for s, d in ou...  35.6 us
    ppermute x15, starting transfers between devices, around_z(): lax.ppermute(parts[r], 'seq', seq_perm(0, r))  20.8 us
    ppermute x9, starting transfers between devices, around_x(): lax.ppermute(parts[r], 'seq', seq_perm(r, 0))  13.4 us
    ppermute x5, starting transfers between devices, swap_core(): return lax.ppermute(x, 'seq', seq_perm(0, 0, 1))  9.69 us
    ppermute x15, waiting for transfers between devices, around_z(): lax.ppermute(parts[r], 'seq', seq_perm(0, r))  8.51 us
    ppermute x7, starting transfers between devices, step_dp(): return lax.ppermute(x, 'dp', [(i, (i + r) % 4) for i in range(4)])  7.07 us
    ppermute x7, waiting for transfers between devices, step_dp(): return lax.ppermute(x, 'dp', [(i, (i + r) % 4) for i in range(4)])  5.02 us
    ppermute x9, waiting for transfers between devices, around_x(): lax.ppermute(parts[r], 'seq', seq_perm(r, 0))  3.92 us
  transfers between devices with their start and end apart: 36, of which 15 were waited for; matrix products, arithmetic and copies ran while one was open for 6% of the time, Pallas kernels for 20%

profile of v2, /device:TPU:1, one launch (start us, length us, event | category | flops | bytes accessed | tf_op | source)
XLA Modules:
  0.0 116.9 jit_solution(15183493515243464420)
XLA Ops:
  0.7 0.6 pad_add_fusion.refs_0_.refs_2_.refs_1_
  1.3 6.5 %shard_map.135 = (f32[4,128,256]{2,1,0:T(8,128)}, f32[4,128,256]{2,1,0:T(8,128)}, f32[8,128,128]{2,1,0:T(8,128)}, f32[8,128,256]{2,1,0:T(8,128)}) custom-call(s32[4]{0:T(128)} %pad_add_fusion.refs_0_.refs_2_.refs_1_, s32[1,2]{1,0:T(1,128)} %refs_2_.3, bf16[128,1024]{1,0:T(8,128)(2,1)} %bitcast.32, bf16[128,1024]{1,0:T(8,128)(2,1)} %bitcast.38, ...), custom_call_target="tpu_custom_call" | custom-call | flops 3019898880 | bytes 3151896 | tf_op jit(solution)/shard_map/pallas_call | solution.py:131
  7.8 1.5 %collective-permute-start = (f32[4,128,256]{2,1,0:T(8,128)}, f32[4,128,256]{2,1,0:T(8,128)S(1)}, u32[]{:S(2)}, u32[]{:S(2)}) collective-permute-start(f32[4,128,256]{2,1,0:T(8,128)} %get-tuple-element.68), channel_id=1, source_target_pairs={{0,1},{1,0},{2,3},{3,2},{4,5},{5,4},{6,7},{7,6},{8,9},{9,8},{10,11... | collective-permute-start | bytes 1572872 | tf_op jit(solution)/shard_map/ppermute | solution.py:483
  9.3 1.7 %collective-permute-done.refs_2_.refs_6_.refs_4_.refs_7_ = f32[4,128,256]{2,1,0:T(8,128)S(1)} collective-permute-done((f32[4,128,256]{2,1,0:T(8,128)}, f32[4,128,256]{2,1,0:T(8,128)S(1)}, u32[]{:S(2)}, u32[]{:S(2)}) %collective-permute-start) | collective-permute-done | bytes 524320 | tf_op jit(solution)/shard_map/ppermute | solution.py:483
  11.1 1.0 copy-done
  12.1 0.9 shard_map.136
  13.2 1.4 %collective-permute-start.18 = (f32[128,2048]{1,0:T(8,128)S(1)}, f32[128,2048]{1,0:T(8,128)S(1)}, u32[]{:S(2)}, u32[]{:S(2)}) collective-permute-start(f32[128,2048]{1,0:T(8,128)S(1)} %shard_map.137.refs_1_), channel_id=1, source_target_pairs={{0,32},{32,64},{64,96},{96,0},{1,33},{33,65},{65,97},{97,1},{2,34}... | collective-permute-start | bytes 3145736 | tf_op jit(solution)/shard_map/ppermute | solution.py:495
  14.6 1.5 %collective-permute-start.19 = (f32[128,2048]{1,0:T(8,128)S(1)}, f32[128,2048]{1,0:T(8,128)S(1)}, u32[]{:S(2)}, u32[]{:S(2)}) collective-permute-start(f32[128,2048]{1,0:T(8,128)S(1)} %shard_map.137.refs_1_), channel_id=1, source_target_pairs={{0,96},{32,0},{64,32},{96,64},{1,97},{33,1},{65,33},{97,65},{2,98}... | collective-permute-start | bytes 3145736 | tf_op jit(solution)/shard_map/ppermute | solution.py:495
  16.1 1.6 %collective-permute-start.1 = (f32[128,256]{1,0:T(8,128)S(1)}, f32[128,256]{1,0:T(8,128)S(1)}, u32[]{:S(2)}, u32[]{:S(2)}) collective-permute-start(f32[128,256]{1,0:T(8,128)S(1)} %get-tuple-element.70), channel_id=1, source_target_pairs={{0,2},{1,3},{2,4},{3,5},{4,6},{5,7},{6,0},{7,1},{8,10},{9,11},{10,... | collective-permute-start | bytes 393224 | tf_op jit(solution)/shard_map/ppermute | solution.py:487
  17.8 3.3 %collective-permute-start.2 = (f32[128,256]{1,0:T(8,128)S(1)}, f32[128,256]{1,0:T(8,128)S(1)}, u32[]{:S(2)}, u32[]{:S(2)}) collective-permute-start(f32[128,256]{1,0:T(8,128)S(1)} %get-tuple-element.71), channel_id=1, source_target_pairs={{0,4},{1,5},{2,6},{3,7},{4,0},{5,1},{6,2},{7,3},{8,12},{9,13},{10,... | collective-permute-start | bytes 393224 | tf_op jit(solution)/shard_map/ppermute | solution.py:487
  21.1 0.7 collective-permute-start.3
  21.8 3.7 %fusion.refs_0_.refs_4_ = f32[128,1024]{1,0:T(8,128)S(1)} fusion(bf16[1024,2048]{1,0:T(8,128)(2,1)} %param.14, bf16[1,128,2048]{2,1,0:T(8,128)(2,1)S(1)} %copy-done.2), kind=kOutput, calls=%fused_computation.2 | convolution fusion | flops 536870912 | bytes 5242880 | tf_op jit(solution)/shard_map/dot_general | solution.py:529
  25.5 1.1 collective-permute-done.2.refs_5_
  26.7 1.1 shard_map.138
  27.8 1.3 %collective-permute-start.4 = (f32[128,256]{1,0:T(8,128)S(1)}, f32[128,256]{1,0:T(8,128)S(1)}, u32[]{:S(2)}, u32[]{:S(2)}) collective-permute-start(f32[128,256]{1,0:T(8,128)S(1)} %get-tuple-element.73.refs_0_.refs_2_), channel_id=1, source_target_pairs={{0,8},{1,9},{2,10},{3,11},{4,12},{5,13},{6,14},{7,15},{8,16},{9,17... | collective-permute-start | bytes 393224 | tf_op jit(solution)/shard_map/ppermute | solution.py:491
  29.1 2.4 %collective-permute-start.5 = (f32[128,256]{1,0:T(8,128)S(1)}, f32[128,256]{1,0:T(8,128)S(1)}, u32[]{:S(2)}, u32[]{:S(2)}) collective-permute-start(f32[128,256]{1,0:T(8,128)S(1)} %get-tuple-element.73.refs_0_.refs_2_), channel_id=1, source_target_pairs={{0,16},{1,17},{2,18},{3,19},{4,20},{5,21},{6,22},{7,23},{8,24},{9,... | collective-permute-start | bytes 393224 | tf_op jit(solution)/shard_map/ppermute | solution.py:491
  31.5 1.1 collective-permute-start.6
  32.7 2.0 %shard_map.139.refs_0_.refs_3_ = f32[8,128,256]{2,1,0:T(8,128)S(1)} custom-call(f32[128,256]{1,0:T(8,128)S(1)} %get-tuple-element.73.refs_0_.refs_2_, s32[1,2]{1,0:T(1,128)S(1)} %copy-done.14, bf16[128,1024]{1,0:T(8,128)(2,1)S(1)} %bitcast.36, bf16[128,1024]{1,0:T(8,128)(2,1)S(1)} %bitcast.33, f32[8,128]{1,0:T(8,128)S(1)} %bitcast.41, ...), custom_call_target="tpu_custom_call" | custom-call | flops 301989888 | bytes 2625544 | tf_op jit(solution)/shard_map/pallas_call | solution.py:131
  34.7 1.2 collective-permute-done.5.refs_4_
  35.9 0.7 collective-permute-done.6.refs_5_
  36.6 1.2 shard_map.140
  37.7 2.1 %collective-permute-start.7 = (f32[128,128]{1,0:T(8,128)S(1)}, f32[128,128]{1,0:T(8,128)S(1)}, u32[]{:S(2)}, u32[]{:S(2)}) collective-permute-start(f32[128,128]{1,0:T(8,128)S(1)} %get-tuple-element.77), channel_id=1, source_target_pairs={{0,2},{1,3},{2,4},{3,5},{4,6},{5,7},{6,0},{7,1},{8,10},{9,11},{10,... | collective-permute-start | bytes 196616 | tf_op jit(solution)/shard_map/ppermute | solution.py:487
  39.9 2.0 %collective-permute-start.8 = (f32[128,128]{1,0:T(8,128)S(1)}, f32[128,128]{1,0:T(8,128)S(1)}, u32[]{:S(2)}, u32[]{:S(2)}) collective-permute-start(f32[128,128]{1,0:T(8,128)S(1)} %get-tuple-element.78), channel_id=1, source_target_pairs={{0,4},{1,5},{2,6},{3,7},{4,0},{5,1},{6,2},{7,3},{8,12},{9,13},{10,... | collective-permute-start | bytes 196616 | tf_op jit(solution)/shard_map/ppermute | solution.py:487
  42.3 2.2 %collective-permute-done.8.refs_3_ = f32[128,128]{1,0:T(8,128)S(1)} collective-permute-done((f32[128,128]{1,0:T(8,128)S(1)}, f32[128,128]{1,0:T(8,128)S(1)}, u32[]{:S(2)}, u32[]{:S(2)}) %collective-permute-start.8) | collective-permute-done | bytes 65568 | tf_op jit(solution)/shard_map/ppermute | solution.py:487
  44.5 0.7 collective-permute-done.9.refs_4_
  45.2 0.8 shard_map.141
  46.0 3.5 %collective-permute-start.10 = (f32[4,128,128]{2,1,0:T(8,128)S(1)}, f32[4,128,128]{2,1,0:T(8,128)S(1)}, u32[]{:S(2)}, u32[]{:S(2)}) collective-permute-start(f32[4,128,128]{2,1,0:T(8,128)S(1)} %get-tuple-element.81), channel_id=1, source_target_pairs={{0,1},{1,0},{2,3},{3,2},{4,5},{5,4},{6,7},{7,6},{8,9},{9,8},{10,11... | collective-permute-start | bytes 786440 | tf_op jit(solution)/shard_map/ppermute | solution.py:483
  49.5 1.2 collective-permute-done.10.refs_2_.refs_7_.refs_8_
  50.7 1.5 %shard_map.142 = (bf16[128,1024]{1,0:T(8,128)(2,1)S(1)}, f32[8,128,128]{2,1,0:T(8,128)S(1)}, f32[4,128,128]{2,1,0:T(8,128)S(1)}, f32[4,128,128]{2,1,0:T(8,128)S(1)}) custom-call(s32[4]{0:T(128)S(1)} %copy-done.10, f32[4,128,128]{2,1,0:T(8,128)S(1)} %get-tuple-element.80.refs_1_.refs_6_.refs_7_, ...), custom_call_target="tpu_custom_call" | custom-call | bytes 3407888 | tf_op jit(solution)/shard_map/pallas_call | solution.py:131
  52.9 2.7 %collective-permute-start.21 = (f32[64,2048]{1,0:T(8,128)S(1)}, f32[64,2048]{1,0:T(8,128)S(1)}, u32[]{:S(2)}, u32[]{:S(2)}) collective-permute-start(f32[64,2048]{1,0:T(8,128)S(1)} %get-tuple-element.96), channel_id=1, source_target_pairs={{0,96},{32,0},{64,32},{96,64},{1,97},{33,1},{65,33},{97,65},{2,98}... | collective-permute-start | bytes 1572872 | tf_op jit(solution)/shard_map/ppermute | solution.py:495
  55.5 0.9 shard_map.143
  56.5 2.8 %collective-permute-start.13 = (f32[128,128]{1,0:T(8,128)S(1)}, f32[128,128]{1,0:T(8,128)S(1)}, u32[]{:S(2)}, u32[]{:S(2)}) collective-permute-start(f32[128,128]{1,0:T(8,128)S(1)} %get-tuple-element.87), channel_id=1, source_target_pairs={{0,4},{1,5},{2,6},{3,7},{4,0},{5,1},{6,2},{7,3},{8,12},{9,13},{10,... | collective-permute-start | bytes 196616 | tf_op jit(solution)/shard_map/ppermute | solution.py:487
  59.8 1.3 %collective-permute-done.12.refs_3_ = f32[128,128]{1,0:T(8,128)S(1)} collective-permute-done((f32[128,128]{1,0:T(8,128)S(1)}, f32[128,128]{1,0:T(8,128)S(1)}, u32[]{:S(2)}, u32[]{:S(2)}) %collective-permute-start.12) | collective-permute-done | bytes 65568 | tf_op jit(solution)/shard_map/ppermute | solution.py:487
  61.1 0.7 collective-permute-done.13.refs_4_
  62.4 0.6 collective-permute-done.14.refs_5_
  63.0 0.8 collective-permute-start.17
  63.9 2.9 %convolution_convert_fusion.refs_0_ = bf16[128,2048]{1,0:T(8,128)(2,1)S(1)} fusion(bf16[128,1024]{1,0:T(8,128)(2,1)S(1)} %get-tuple-element.82.refs_5_, bf16[1024,2048]{1,0:T(8,128)(2,1)} %param.14), kind=kOutput, calls=%fused_computation | convolution fusion | flops 537133056 | bytes 4980736 | tf_op jit(solution)/shard_map/dot_general | solution.py:556
  66.8 1.1 shard_map.144
  67.9 2.5 %collective-permute-done.15.refs_3_ = f32[128,256]{1,0:T(8,128)S(1)} collective-permute-done((f32[128,256]{1,0:T(8,128)S(1)}, f32[128,256]{1,0:T(8,128)S(1)}, u32[]{:S(2)}, u32[]{:S(2)}) %collective-permute-start.15) | collective-permute-done | bytes 131104 | tf_op jit(solution)/shard_map/ppermute | solution.py:495
  70.4 2.5 %collective-permute-done.16.refs_4_ = f32[128,256]{1,0:T(8,128)S(1)} collective-permute-done((f32[128,256]{1,0:T(8,128)S(1)}, f32[128,256]{1,0:T(8,128)S(1)}, u32[]{:S(2)}, u32[]{:S(2)}) %collective-permute-start.16) | collective-permute-done | bytes 131104 | tf_op jit(solution)/shard_map/ppermute | solution.py:495
  72.9 2.5 %shard_map.146 = (f32[16,8,2048]{2,1,0:T(8,128)S(1)}, f32[16,8,2048]{2,1,0:T(8,128)S(1)}) custom-call(f32[128,128]{1,0:T(8,128)S(1)} %get-tuple-element.90.refs_0_.refs_2_, s32[4]{0:T(128)S(1)} %copy-done.10, f32[128,256]{1,0:T(8,128)S(1)} %get-tuple-element.91.refs_2_, f32[128,256]{1,0:T(8,128)S(1)} %collective-permute-done.15.refs_3_, ...), custom_call_target="tpu_custom_call" | custom-call | flops 536870912 | bytes 6291472 | tf_op jit(solution)/shard_map/pallas_call | solution.py:131
  75.4 1.2 %collective-permute-start.22 = (f32[16,8,2048]{2,1,0:T(8,128)S(1)}, f32[16,8,2048]{2,1,0:T(8,128)S(1)}, u32[]{:S(2)}, u32[]{:S(2)}) collective-permute-start(f32[16,8,2048]{2,1,0:T(8,128)S(1)} %get-tuple-element.98), channel_id=1, source_target_pairs={{0,1},{1,0},{2,3},{3,2},{4,5},{5,4},{6,7},{7,6},{8,9},{9,8},{10,11... | collective-permute-start | bytes 3145736 | tf_op jit(solution)/shard_map/ppermute | solution.py:483
  76.6 1.0 collective-permute-start.23
  77.6 2.5 %collective-permute-start.24 = (f32[128,128]{1,0:T(8,128)S(1)}, f32[128,128]{1,0:T(8,128)S(1)}, u32[]{:S(2)}, u32[]{:S(2)}) collective-permute-start(f32[128,128]{1,0:T(8,128)S(1)} %get-tuple-element.90.refs_0_.refs_2_), channel_id=1, source_target_pairs={{0,16},{1,17},{2,18},{3,19},{4,20},{5,21},{6,22},{7,23},{8,24},{9,... | collective-permute-start | bytes 196616 | tf_op jit(solution)/shard_map/ppermute | solution.py:491
  80.2 0.8 collective-permute-start.25
  81.0 0.7 shard_map.147
  81.7 2.1 %collective-permute-done.24.refs_4_ = f32[128,128]{1,0:T(8,128)S(1)} collective-permute-done((f32[128,128]{1,0:T(8,128)S(1)}, f32[128,128]{1,0:T(8,128)S(1)}, u32[]{:S(2)}, u32[]{:S(2)}) %collective-permute-start.24) | collective-permute-done | bytes 65568 | tf_op jit(solution)/shard_map/ppermute | solution.py:491
  83.8 1.5 %shard_map.148 = (f32[128,128]{1,0:T(8,128)S(1)}, f32[128,128]{1,0:T(8,128)S(1)}, f32[128,128]{1,0:T(8,128)S(1)}, f32[128,128]{1,0:T(8,128)S(1)}) custom-call(f32[4,8,2048]{2,1,0:T(8,128)S(1)} %get-tuple-element.99.refs_0_.refs_2_, s32[4]{0:T(128)S(1)} %copy-done.10, f32[128,128]{1,0:T(8,128)S(1)} %get-tuple-element.90.refs_0_.refs_2_, ...), custom_call_target="tpu_custom_call" | custom-call | bytes 1835024 | tf_op jit(solution)/shard_map/pallas_call | solution.py:131
  85.3 2.8 %collective-permute-start.27 = (f32[128,128]{1,0:T(8,128)S(1)}, f32[128,128]{1,0:T(8,128)S(1)}, u32[]{:S(2)}, u32[]{:S(2)}) collective-permute-start(f32[128,128]{1,0:T(8,128)S(1)} %get-tuple-element.107), channel_id=1, source_target_pairs={{0,4},{1,5},{2,6},{3,7},{4,0},{5,1},{6,2},{7,3},{8,12},{9,13},{10,... | collective-permute-start | bytes 196616 | tf_op jit(solution)/shard_map/ppermute | solution.py:487
  88.6 1.0 collective-permute-start.29
  89.6 0.8 collective-permute-start.30
  90.4 2.1 %collective-permute-start.31 = (f32[4,8,2048]{2,1,0:T(8,128)S(1)}, f32[4,8,2048]{2,1,0:T(8,128)S(1)}, u32[]{:S(2)}, u32[]{:S(2)}) collective-permute-start(f32[4,8,2048]{2,1,0:T(8,128)S(1)} %get-tuple-element.112), channel_id=1, source_target_pairs={{0,6},{1,7},{2,0},{3,1},{4,2},{5,3},{6,4},{7,5},{8,14},{9,15},{10,... | collective-permute-start | bytes 786440 | tf_op jit(solution)/shard_map/ppermute | solution.py:487
  92.5 5.1 %shard_map.149 = (bf16[128,1024]{1,0:T(8,128)(2,1)}, f32[8,128,128]{2,1,0:T(8,128)S(1)}, f32[8,128,128]{2,1,0:T(8,128)S(1)}, f32[8,128,128]{2,1,0:T(8,128)S(1)},...) custom-call(f32[128,128]{1,0:T(8,128)S(1)} %get-tuple-element.102.refs_0_.refs_2_, s32[4]{0:T(128)S(1)} %copy-done.10, ...), custom_call_target="tpu_custom_call" | custom-call | flops 805306368 | bytes 5509144 | tf_op jit(solution)/shard_map/pallas_call | solution.py:131
  97.6 0.8 shard_map.150
  98.4 3.1 %collective-permute-start.32 = (f32[4,128,128]{2,1,0:T(8,128)S(1)}, f32[4,128,128]{2,1,0:T(8,128)S(1)}, u32[]{:S(2)}, u32[]{:S(2)}) collective-permute-start(f32[4,128,128]{2,1,0:T(8,128)S(1)} %get-tuple-element.114), channel_id=1, source_target_pairs={{0,1},{1,0},{2,3},{3,2},{4,5},{5,4},{6,7},{7,6},{8,9},{9,8},{10,11... | collective-permute-start | bytes 786440 | tf_op jit(solution)/shard_map/ppermute | solution.py:483
  101.5 0.9 collective-permute-done.30.refs_4_
  102.4 0.9 collective-permute-done.31.refs_5_
  103.3 0.6 shard_map.151
  103.9 1.5 %collective-permute-start.33 = (f32[8,2048]{1,0:T(8,128)S(1)}, f32[8,2048]{1,0:T(8,128)S(1)}, u32[]{:S(2)}, u32[]{:S(2)}) collective-permute-start(f32[8,2048]{1,0:T(8,128)S(1)} %get-tuple-element.124), channel_id=1, source_target_pairs={{0,8},{1,9},{2,10},{3,11},{4,12},{5,13},{6,14},{7,15},{8,16},{9,17... | collective-permute-start | bytes 196616 | tf_op jit(solution)/shard_map/ppermute | solution.py:491
  105.4 1.4 %collective-permute-start.34 = (f32[8,2048]{1,0:T(8,128)S(1)}, f32[8,2048]{1,0:T(8,128)S(1)}, u32[]{:S(2)}, u32[]{:S(2)}) collective-permute-start(f32[8,2048]{1,0:T(8,128)S(1)} %get-tuple-element.125), channel_id=1, source_target_pairs={{0,16},{1,17},{2,18},{3,19},{4,20},{5,21},{6,22},{7,23},{8,24},{9,... | collective-permute-start | bytes 196616 | tf_op jit(solution)/shard_map/ppermute | solution.py:491
  106.8 1.2 %collective-permute-start.35 = (f32[8,2048]{1,0:T(8,128)S(1)}, f32[8,2048]{1,0:T(8,128)S(1)}, u32[]{:S(2)}, u32[]{:S(2)}) collective-permute-start(f32[8,2048]{1,0:T(8,128)S(1)} %get-tuple-element.126), channel_id=1, source_target_pairs={{0,24},{1,25},{2,26},{3,27},{4,28},{5,29},{6,30},{7,31},{8,0},{9,1... | collective-permute-start | bytes 196616 | tf_op jit(solution)/shard_map/ppermute | solution.py:491
  108.1 7.5 %shard_map.152 = (bf16[128,1024]{1,0:T(8,128)(2,1)}, bf16[128,1024]{1,0:T(8,128)(2,1)}, f32[8,128]{1,0:T(8,128)}, f32[8,128]{1,0:T(8,128)}) custom-call(f32[8,2048]{1,0:T(8,128)S(1)} %get-tuple-element.113.refs_0_.refs_1_, s32[4]{0:T(128)S(1)} %copy-done.10, s32[1,2]{1,0:T(1,128)S(1)} %copy-done.14, bf16[128,1024]{1,0:T(8,128)(2,1)S(1)} %bitcast.35, ...), custom_call_target="tpu_custom_call" | custom-call | flops 805306368 | bytes 5257240 | tf_op jit(solution)/shard_map/pallas_call | solution.py:131
  115.6 0.7 copy-done.12
  116.3 0.6 shard_map.153
  (60 shorter events, 3.0 us)
Async XLA Ops:
  1.3 9.8 %copy-start.10 = (s32[4]{0:T(128)S(1)}, s32[4]{0:T(128)}, u32[]{:S(2)}) copy-start(s32[4]{0:T(128)} %pad_add_fusion.refs_0_.refs_2_.refs_1_) | copy-start | bytes 52
  1.3 11.8 %copy-start.2 = (bf16[1,128,2048]{2,1,0:T(8,128)(2,1)S(1)}, bf16[1,128,2048]{2,1,0:T(8,128)(2,1)}, u32[]{:S(2)}) copy-start(bf16[1,128,2048]{2,1,0:T(8,128)(2,1)} %param.15) | copy-start | bytes 1572868
  7.8 3.3 %collective-permute-start = (f32[4,128,256]{2,1,0:T(8,128)}, f32[4,128,256]{2,1,0:T(8,128)S(1)}, u32[]{:S(2)}, u32[]{:S(2)}) collective-permute-start(f32[4,128,256]{2,1,0:T(8,128)} %get-tuple-element.68), channel_id=1, source_target_pairs={{0,1},{1,0},{2,3},{3,2},{4,5},{5,4},{6,7},{7,6},{8,9},{9,8},{10,11... | collective-permute-start | bytes 1572872 | tf_op jit(solution)/shard_map/ppermute | solution.py:483
  11.1 1.0 copy-start
  13.0 19.6 %copy-start.5 = (bf16[1,128,1024]{2,1,0:T(8,128)(2,1)S(1)}, bf16[1,128,1024]{2,1,0:T(8,128)(2,1)}, u32[]{:S(2)}) copy-start(bf16[1,128,1024]{2,1,0:T(8,128)(2,1)} %param.9) | copy-start | bytes 786436
  13.1 19.6 %copy-start.6 = (f32[8,128,256]{2,1,0:T(8,128)S(1)}, f32[8,128,256]{2,1,0:T(8,128)}, u32[]{:S(2)}) copy-start(f32[8,128,256]{2,1,0:T(8,128)} %get-tuple-element.74.refs_5_.refs_8_) | copy-start | bytes 3145732
  13.1 19.6 %copy-start.8 = (bf16[1,128,1024]{2,1,0:T(8,128)(2,1)S(1)}, bf16[1,128,1024]{2,1,0:T(8,128)(2,1)}, u32[]{:S(2)}) copy-start(bf16[1,128,1024]{2,1,0:T(8,128)(2,1)} %param.8) | copy-start | bytes 786436
  13.1 19.6 %copy-start.11 = (f32[1,128,8]{1,2,0:T(8,128)S(1)}, f32[1,128,8]{1,2,0:T(8,128)}, u32[]{:S(2)}) copy-start(f32[1,128,8]{1,2,0:T(8,128)} %param.12) | copy-start | bytes 12292
  13.1 19.6 %copy-start.14 = (s32[1,2]{1,0:T(1,128)S(1)}, s32[1,2]{1,0:T(1,128)}, u32[]{:S(2)}) copy-start(s32[1,2]{1,0:T(1,128)} %refs_2_.3) | copy-start | bytes 28
  13.2 39.5 %collective-permute-start.18 = (f32[128,2048]{1,0:T(8,128)S(1)}, f32[128,2048]{1,0:T(8,128)S(1)}, u32[]{:S(2)}, u32[]{:S(2)}) collective-permute-start(f32[128,2048]{1,0:T(8,128)S(1)} %shard_map.137.refs_1_), channel_id=1, source_target_pairs={{0,32},{32,64},{64,96},{96,0},{1,33},{33,65},{65,97},{97,1},{2,34}... | collective-permute-start | bytes 3145736 | tf_op jit(solution)/shard_map/ppermute | solution.py:495
  14.6 38.1 %collective-permute-start.19 = (f32[128,2048]{1,0:T(8,128)S(1)}, f32[128,2048]{1,0:T(8,128)S(1)}, u32[]{:S(2)}, u32[]{:S(2)}) collective-permute-start(f32[128,2048]{1,0:T(8,128)S(1)} %shard_map.137.refs_1_), channel_id=1, source_target_pairs={{0,96},{32,0},{64,32},{96,64},{1,97},{33,1},{65,33},{97,65},{2,98}... | collective-permute-start | bytes 3145736 | tf_op jit(solution)/shard_map/ppermute | solution.py:495
  16.1 9.4 %collective-permute-start.1 = (f32[128,256]{1,0:T(8,128)S(1)}, f32[128,256]{1,0:T(8,128)S(1)}, u32[]{:S(2)}, u32[]{:S(2)}) collective-permute-start(f32[128,256]{1,0:T(8,128)S(1)} %get-tuple-element.70), channel_id=1, source_target_pairs={{0,2},{1,3},{2,4},{3,5},{4,6},{5,7},{6,0},{7,1},{8,10},{9,11},{10,... | collective-permute-start | bytes 393224 | tf_op jit(solution)/shard_map/ppermute | solution.py:487
  17.8 8.9 %collective-permute-start.2 = (f32[128,256]{1,0:T(8,128)S(1)}, f32[128,256]{1,0:T(8,128)S(1)}, u32[]{:S(2)}, u32[]{:S(2)}) collective-permute-start(f32[128,256]{1,0:T(8,128)S(1)} %get-tuple-element.71), channel_id=1, source_target_pairs={{0,4},{1,5},{2,6},{3,7},{4,0},{5,1},{6,2},{7,3},{8,12},{9,13},{10,... | collective-permute-start | bytes 393224 | tf_op jit(solution)/shard_map/ppermute | solution.py:487
  21.1 5.6 %collective-permute-start.3 = (f32[128,256]{1,0:T(8,128)S(1)}, f32[128,256]{1,0:T(8,128)S(1)}, u32[]{:S(2)}, u32[]{:S(2)}) collective-permute-start(f32[128,256]{1,0:T(8,128)S(1)} %get-tuple-element.72), channel_id=1, source_target_pairs={{0,6},{1,7},{2,0},{3,1},{4,2},{5,3},{6,4},{7,5},{8,14},{9,15},{10,... | collective-permute-start | bytes 393224 | tf_op jit(solution)/shard_map/ppermute | solution.py:487
  25.5 19.7 %copy-start.1 = (f32[4,128,256]{2,1,0:T(8,128)S(1)}, f32[4,128,256]{2,1,0:T(8,128)}, u32[]{:S(2)}) copy-start(f32[4,128,256]{2,1,0:T(8,128)} %get-tuple-element.67.refs_1_.refs_5_.refs_3_.refs_6_) | copy-start | bytes 1572868
  27.8 6.9 %collective-permute-start.4 = (f32[128,256]{1,0:T(8,128)S(1)}, f32[128,256]{1,0:T(8,128)S(1)}, u32[]{:S(2)}, u32[]{:S(2)}) collective-permute-start(f32[128,256]{1,0:T(8,128)S(1)} %get-tuple-element.73.refs_0_.refs_2_), channel_id=1, source_target_pairs={{0,8},{1,9},{2,10},{3,11},{4,12},{5,13},{6,14},{7,15},{8,16},{9,17... | collective-permute-start | bytes 393224 | tf_op jit(solution)/shard_map/ppermute | solution.py:491
  29.1 6.8 %collective-permute-start.5 = (f32[128,256]{1,0:T(8,128)S(1)}, f32[128,256]{1,0:T(8,128)S(1)}, u32[]{:S(2)}, u32[]{:S(2)}) collective-permute-start(f32[128,256]{1,0:T(8,128)S(1)} %get-tuple-element.73.refs_0_.refs_2_), channel_id=1, source_target_pairs={{0,16},{1,17},{2,18},{3,19},{4,20},{5,21},{6,22},{7,23},{8,24},{9,... | collective-permute-start | bytes 393224 | tf_op jit(solution)/shard_map/ppermute | solution.py:491
  31.5 5.0 %collective-permute-start.6 = (f32[128,256]{1,0:T(8,128)S(1)}, f32[128,256]{1,0:T(8,128)S(1)}, u32[]{:S(2)}, u32[]{:S(2)}) collective-permute-start(f32[128,256]{1,0:T(8,128)S(1)} %get-tuple-element.73.refs_0_.refs_2_), channel_id=1, source_target_pairs={{0,24},{1,25},{2,26},{3,27},{4,28},{5,29},{6,30},{7,31},{8,0},{9,1... | collective-permute-start | bytes 393224 | tf_op jit(solution)/shard_map/ppermute | solution.py:491
  37.7 4.6 %collective-permute-start.7 = (f32[128,128]{1,0:T(8,128)S(1)}, f32[128,128]{1,0:T(8,128)S(1)}, u32[]{:S(2)}, u32[]{:S(2)}) collective-permute-start(f32[128,128]{1,0:T(8,128)S(1)} %get-tuple-element.77), channel_id=1, source_target_pairs={{0,2},{1,3},{2,4},{3,5},{4,6},{5,7},{6,0},{7,1},{8,10},{9,11},{10,... | collective-permute-start | bytes 196616 | tf_op jit(solution)/shard_map/ppermute | solution.py:487
  39.9 4.6 %collective-permute-start.8 = (f32[128,128]{1,0:T(8,128)S(1)}, f32[128,128]{1,0:T(8,128)S(1)}, u32[]{:S(2)}, u32[]{:S(2)}) collective-permute-start(f32[128,128]{1,0:T(8,128)S(1)} %get-tuple-element.78), channel_id=1, source_target_pairs={{0,4},{1,5},{2,6},{3,7},{4,0},{5,1},{6,2},{7,3},{8,12},{9,13},{10,... | collective-permute-start | bytes 196616 | tf_op jit(solution)/shard_map/ppermute | solution.py:487
  41.8 3.4 %collective-permute-start.9 = (f32[128,128]{1,0:T(8,128)S(1)}, f32[128,128]{1,0:T(8,128)S(1)}, u32[]{:S(2)}, u32[]{:S(2)}) collective-permute-start(f32[128,128]{1,0:T(8,128)S(1)} %get-tuple-element.79), channel_id=1, source_target_pairs={{0,6},{1,7},{2,0},{3,1},{4,2},{5,3},{6,4},{7,5},{8,14},{9,15},{10,... | collective-permute-start | bytes 196616 | tf_op jit(solution)/shard_map/ppermute | solution.py:487
  46.0 4.7 %collective-permute-start.10 = (f32[4,128,128]{2,1,0:T(8,128)S(1)}, f32[4,128,128]{2,1,0:T(8,128)S(1)}, u32[]{:S(2)}, u32[]{:S(2)}) collective-permute-start(f32[4,128,128]{2,1,0:T(8,128)S(1)} %get-tuple-element.81), channel_id=1, source_target_pairs={{0,1},{1,0},{2,3},{3,2},{4,5},{5,4},{6,7},{7,6},{8,9},{9,8},{10,11... | collective-permute-start | bytes 786440 | tf_op jit(solution)/shard_map/ppermute | solution.py:483
  52.2 3.3 %collective-permute-start.11 = (f32[4,128,128]{2,1,0:T(8,128)S(1)}, f32[4,128,128]{2,1,0:T(8,128)S(1)}, u32[]{:S(2)}, u32[]{:S(2)}) collective-permute-start(f32[4,128,128]{2,1,0:T(8,128)S(1)} %get-tuple-element.84), channel_id=1, source_target_pairs={{0,1},{1,0},{2,3},{3,2},{4,5},{5,4},{6,7},{7,6},{8,9},{9,8},{10,11... | collective-permute-start | bytes 786440 | tf_op jit(solution)/shard_map/ppermute | solution.py:483
  52.7 14.1 %copy-start.3 = (f32[128,2048]{1,0:T(8,128)}, f32[128,2048]{1,0:T(8,128)S(1)}, u32[]{:S(2)}) copy-start(f32[128,2048]{1,0:T(8,128)S(1)} %collective-permute-done.19.refs_2_.refs_8_) | copy-start | bytes 3145732
  52.8 20.1 %collective-permute-start.20 = (f32[64,2048]{1,0:T(8,128)S(1)}, f32[64,2048]{1,0:T(8,128)S(1)}, u32[]{:S(2)}, u32[]{:S(2)}) collective-permute-start(f32[64,2048]{1,0:T(8,128)S(1)} %get-tuple-element.95), channel_id=1, source_target_pairs={{0,32},{32,64},{64,96},{96,0},{1,33},{33,65},{65,97},{97,1},{2,34}... | collective-permute-start | bytes 1572872 | tf_op jit(solution)/shard_map/ppermute | solution.py:495
  52.9 20.1 %collective-permute-start.21 = (f32[64,2048]{1,0:T(8,128)S(1)}, f32[64,2048]{1,0:T(8,128)S(1)}, u32[]{:S(2)}, u32[]{:S(2)}) collective-permute-start(f32[64,2048]{1,0:T(8,128)S(1)} %get-tuple-element.96), channel_id=1, source_target_pairs={{0,96},{32,0},{64,32},{96,64},{1,97},{33,1},{65,33},{97,65},{2,98}... | collective-permute-start | bytes 1572872 | tf_op jit(solution)/shard_map/ppermute | solution.py:495
  56.4 4.7 %collective-permute-start.12 = (f32[128,128]{1,0:T(8,128)S(1)}, f32[128,128]{1,0:T(8,128)S(1)}, u32[]{:S(2)}, u32[]{:S(2)}) collective-permute-start(f32[128,128]{1,0:T(8,128)S(1)} %get-tuple-element.86), channel_id=1, source_target_pairs={{0,2},{1,3},{2,4},{3,5},{4,6},{5,7},{6,0},{7,1},{8,10},{9,11},{10,... | collective-permute-start | bytes 196616 | tf_op jit(solution)/shard_map/ppermute | solution.py:487
  56.5 5.3 %collective-permute-start.13 = (f32[128,128]{1,0:T(8,128)S(1)}, f32[128,128]{1,0:T(8,128)S(1)}, u32[]{:S(2)}, u32[]{:S(2)}) collective-permute-start(f32[128,128]{1,0:T(8,128)S(1)} %get-tuple-element.87), channel_id=1, source_target_pairs={{0,4},{1,5},{2,6},{3,7},{4,0},{5,1},{6,2},{7,3},{8,12},{9,13},{10,... | collective-permute-start | bytes 196616 | tf_op jit(solution)/shard_map/ppermute | solution.py:487
  59.3 3.7 %collective-permute-start.14 = (f32[128,128]{1,0:T(8,128)S(1)}, f32[128,128]{1,0:T(8,128)S(1)}, u32[]{:S(2)}, u32[]{:S(2)}) collective-permute-start(f32[128,128]{1,0:T(8,128)S(1)} %get-tuple-element.88), channel_id=1, source_target_pairs={{0,6},{1,7},{2,0},{3,1},{4,2},{5,3},{6,4},{7,5},{8,14},{9,15},{10,... | collective-permute-start | bytes 196616 | tf_op jit(solution)/shard_map/ppermute | solution.py:487
  61.1 9.3 %collective-permute-start.15 = (f32[128,256]{1,0:T(8,128)S(1)}, f32[128,256]{1,0:T(8,128)S(1)}, u32[]{:S(2)}, u32[]{:S(2)}) collective-permute-start(f32[128,256]{1,0:T(8,128)S(1)} %get-tuple-element.92), channel_id=1, source_target_pairs={{0,32},{32,64},{64,96},{96,0},{1,33},{33,65},{65,97},{97,1},{2,34}... | collective-permute-start | bytes 393224 | tf_op jit(solution)/shard_map/ppermute | solution.py:495
  61.8 11.1 %collective-permute-start.16 = (f32[128,256]{1,0:T(8,128)S(1)}, f32[128,256]{1,0:T(8,128)S(1)}, u32[]{:S(2)}, u32[]{:S(2)}) collective-permute-start(f32[128,256]{1,0:T(8,128)S(1)} %get-tuple-element.93), channel_id=1, source_target_pairs={{0,64},{32,96},{64,0},{96,32},{1,65},{33,97},{65,1},{97,33},{2,66}... | collective-permute-start | bytes 393224 | tf_op jit(solution)/shard_map/ppermute | solution.py:495
  63.0 9.9 %collective-permute-start.17 = (f32[128,256]{1,0:T(8,128)S(1)}, f32[128,256]{1,0:T(8,128)S(1)}, u32[]{:S(2)}, u32[]{:S(2)}) collective-permute-start(f32[128,256]{1,0:T(8,128)S(1)} %get-tuple-element.94), channel_id=1, source_target_pairs={{0,96},{32,0},{64,32},{96,64},{1,97},{33,1},{65,33},{97,65},{2,98}... | collective-permute-start | bytes 393224 | tf_op jit(solution)/shard_map/ppermute | solution.py:495
  66.8 18.5 %copy-start.4 = (bf16[128,2048]{1,0:T(8,128)(2,1)}, bf16[128,2048]{1,0:T(8,128)(2,1)S(1)}, u32[]{:S(2)}) copy-start(bf16[128,2048]{1,0:T(8,128)(2,1)S(1)} %convolution_convert_fusion.refs_0_) | copy-start | bytes 1572868
  75.4 5.6 %collective-permute-start.22 = (f32[16,8,2048]{2,1,0:T(8,128)S(1)}, f32[16,8,2048]{2,1,0:T(8,128)S(1)}, u32[]{:S(2)}, u32[]{:S(2)}) collective-permute-start(f32[16,8,2048]{2,1,0:T(8,128)S(1)} %get-tuple-element.98), channel_id=1, source_target_pairs={{0,1},{1,0},{2,3},{3,2},{4,5},{5,4},{6,7},{7,6},{8,9},{9,8},{10,11... | collective-permute-start | bytes 3145736 | tf_op jit(solution)/shard_map/ppermute | solution.py:483
  76.6 5.0 %collective-permute-start.23 = (f32[128,128]{1,0:T(8,128)S(1)}, f32[128,128]{1,0:T(8,128)S(1)}, u32[]{:S(2)}, u32[]{:S(2)}) collective-permute-start(f32[128,128]{1,0:T(8,128)S(1)} %get-tuple-element.90.refs_0_.refs_2_), channel_id=1, source_target_pairs={{0,8},{1,9},{2,10},{3,11},{4,12},{5,13},{6,14},{7,15},{8,16},{9,17... | collective-permute-start | bytes 196616 | tf_op jit(solution)/shard_map/ppermute | solution.py:491
  77.6 6.1 %collective-permute-start.24 = (f32[128,128]{1,0:T(8,128)S(1)}, f32[128,128]{1,0:T(8,128)S(1)}, u32[]{:S(2)}, u32[]{:S(2)}) collective-permute-start(f32[128,128]{1,0:T(8,128)S(1)} %get-tuple-element.90.refs_0_.refs_2_), channel_id=1, source_target_pairs={{0,16},{1,17},{2,18},{3,19},{4,20},{5,21},{6,22},{7,23},{8,24},{9,... | collective-permute-start | bytes 196616 | tf_op jit(solution)/shard_map/ppermute | solution.py:491
  80.2 3.6 %collective-permute-start.25 = (f32[128,128]{1,0:T(8,128)S(1)}, f32[128,128]{1,0:T(8,128)S(1)}, u32[]{:S(2)}, u32[]{:S(2)}) collective-permute-start(f32[128,128]{1,0:T(8,128)S(1)} %get-tuple-element.90.refs_0_.refs_2_), channel_id=1, source_target_pairs={{0,24},{1,25},{2,26},{3,27},{4,28},{5,29},{6,30},{7,31},{8,0},{9,1... | collective-permute-start | bytes 196616 | tf_op jit(solution)/shard_map/ppermute | solution.py:491
  83.8 24.3 %copy-start.7 = (f32[8,128,128]{2,1,0:T(8,128)S(1)}, f32[8,128,128]{2,1,0:T(8,128)}, u32[]{:S(2)}) copy-start(f32[8,128,128]{2,1,0:T(8,128)} %get-tuple-element.115.refs_11_) | copy-start | bytes 1572868
  83.8 24.3 %copy-start.9 = (bf16[1,128,1024]{2,1,0:T(8,128)(2,1)S(1)}, bf16[1,128,1024]{2,1,0:T(8,128)(2,1)}, u32[]{:S(2)}) copy-start(bf16[1,128,1024]{2,1,0:T(8,128)(2,1)} %param.10) | copy-start | bytes 786436
  83.8 24.3 %copy-start.13 = (bf16[1,128,8]{1,2,0:T(8,128)(2,1)S(1)}, bf16[1,128,8]{1,2,0:T(8,128)(2,1)}, u32[]{:S(2)}) copy-start(bf16[1,128,8]{1,2,0:T(8,128)(2,1)} %param.11) | copy-start | bytes 6148
  85.3 5.1 %collective-permute-start.26 = (f32[128,128]{1,0:T(8,128)S(1)}, f32[128,128]{1,0:T(8,128)S(1)}, u32[]{:S(2)}, u32[]{:S(2)}) collective-permute-start(f32[128,128]{1,0:T(8,128)S(1)} %get-tuple-element.106), channel_id=1, source_target_pairs={{0,2},{1,3},{2,4},{3,5},{4,6},{5,7},{6,0},{7,1},{8,10},{9,11},{10,... | collective-permute-start | bytes 196616 | tf_op jit(solution)/shard_map/ppermute | solution.py:487
  85.3 12.2 %collective-permute-start.27 = (f32[128,128]{1,0:T(8,128)S(1)}, f32[128,128]{1,0:T(8,128)S(1)}, u32[]{:S(2)}, u32[]{:S(2)}) collective-permute-start(f32[128,128]{1,0:T(8,128)S(1)} %get-tuple-element.107), channel_id=1, source_target_pairs={{0,4},{1,5},{2,6},{3,7},{4,0},{5,1},{6,2},{7,3},{8,12},{9,13},{10,... | collective-permute-start | bytes 196616 | tf_op jit(solution)/shard_map/ppermute | solution.py:487
  88.2 9.4 %collective-permute-start.28 = (f32[128,128]{1,0:T(8,128)S(1)}, f32[128,128]{1,0:T(8,128)S(1)}, u32[]{:S(2)}, u32[]{:S(2)}) collective-permute-start(f32[128,128]{1,0:T(8,128)S(1)} %get-tuple-element.108), channel_id=1, source_target_pairs={{0,6},{1,7},{2,0},{3,1},{4,2},{5,3},{6,4},{7,5},{8,14},{9,15},{10,... | collective-permute-start | bytes 196616 | tf_op jit(solution)/shard_map/ppermute | solution.py:487
  88.6 12.9 %collective-permute-start.29 = (f32[4,8,2048]{2,1,0:T(8,128)S(1)}, f32[4,8,2048]{2,1,0:T(8,128)S(1)}, u32[]{:S(2)}, u32[]{:S(2)}) collective-permute-start(f32[4,8,2048]{2,1,0:T(8,128)S(1)} %get-tuple-element.110), channel_id=1, source_target_pairs={{0,2},{1,3},{2,4},{3,5},{4,6},{5,7},{6,0},{7,1},{8,10},{9,11},{10,... | collective-permute-start | bytes 786440 | tf_op jit(solution)/shard_map/ppermute | solution.py:487
  89.6 12.8 %collective-permute-start.30 = (f32[4,8,2048]{2,1,0:T(8,128)S(1)}, f32[4,8,2048]{2,1,0:T(8,128)S(1)}, u32[]{:S(2)}, u32[]{:S(2)}) collective-permute-start(f32[4,8,2048]{2,1,0:T(8,128)S(1)} %get-tuple-element.111), channel_id=1, source_target_pairs={{0,4},{1,5},{2,6},{3,7},{4,0},{5,1},{6,2},{7,3},{8,12},{9,13},{10,... | collective-permute-start | bytes 786440 | tf_op jit(solution)/shard_map/ppermute | solution.py:487
  90.4 12.9 %collective-permute-start.31 = (f32[4,8,2048]{2,1,0:T(8,128)S(1)}, f32[4,8,2048]{2,1,0:T(8,128)S(1)}, u32[]{:S(2)}, u32[]{:S(2)}) collective-permute-start(f32[4,8,2048]{2,1,0:T(8,128)S(1)} %get-tuple-element.112), channel_id=1, source_target_pairs={{0,6},{1,7},{2,0},{3,1},{4,2},{5,3},{6,4},{7,5},{8,14},{9,15},{10,... | collective-permute-start | bytes 786440 | tf_op jit(solution)/shard_map/ppermute | solution.py:487
  98.4 9.6 %collective-permute-start.32 = (f32[4,128,128]{2,1,0:T(8,128)S(1)}, f32[4,128,128]{2,1,0:T(8,128)S(1)}, u32[]{:S(2)}, u32[]{:S(2)}) collective-permute-start(f32[4,128,128]{2,1,0:T(8,128)S(1)} %get-tuple-element.114), channel_id=1, source_target_pairs={{0,1},{1,0},{2,3},{3,2},{4,5},{5,4},{6,7},{7,6},{8,9},{9,8},{10,11... | collective-permute-start | bytes 786440 | tf_op jit(solution)/shard_map/ppermute | solution.py:483
  103.9 11.7 %collective-permute-start.33 = (f32[8,2048]{1,0:T(8,128)S(1)}, f32[8,2048]{1,0:T(8,128)S(1)}, u32[]{:S(2)}, u32[]{:S(2)}) collective-permute-start(f32[8,2048]{1,0:T(8,128)S(1)} %get-tuple-element.124), channel_id=1, source_target_pairs={{0,8},{1,9},{2,10},{3,11},{4,12},{5,13},{6,14},{7,15},{8,16},{9,17... | collective-permute-start | bytes 196616 | tf_op jit(solution)/shard_map/ppermute | solution.py:491
  105.4 10.1 %collective-permute-start.34 = (f32[8,2048]{1,0:T(8,128)S(1)}, f32[8,2048]{1,0:T(8,128)S(1)}, u32[]{:S(2)}, u32[]{:S(2)}) collective-permute-start(f32[8,2048]{1,0:T(8,128)S(1)} %get-tuple-element.125), channel_id=1, source_target_pairs={{0,16},{1,17},{2,18},{3,19},{4,20},{5,21},{6,22},{7,23},{8,24},{9,... | collective-permute-start | bytes 196616 | tf_op jit(solution)/shard_map/ppermute | solution.py:491
  106.8 8.8 %collective-permute-start.35 = (f32[8,2048]{1,0:T(8,128)S(1)}, f32[8,2048]{1,0:T(8,128)S(1)}, u32[]{:S(2)}, u32[]{:S(2)}) collective-permute-start(f32[8,2048]{1,0:T(8,128)S(1)} %get-tuple-element.126), channel_id=1, source_target_pairs={{0,24},{1,25},{2,26},{3,27},{4,28},{5,29},{6,30},{7,31},{8,0},{9,1... | collective-permute-start | bytes 196616 | tf_op jit(solution)/shard_map/ppermute | solution.py:491
  115.6 0.7 copy-start.12

commit v3 on v2

v3 whole, which is shorter than its diff:
```python
import functools
import math

import jax
import jax.numpy as jnp
from jax import lax
from jax.experimental import pallas as pl
from jax.experimental.pallas import tpu as pltpu
from jax.sharding import PartitionSpec as P

f32 = jnp.float32
bf16 = jnp.bfloat16
EPS = 1e-06
C = 128
H = 8
VMEM_LIMIT = 48 * 1024 * 1024
FIRST_LIMIT = 62 * 1024 * 1024

NN = (((1,), (0,)), ((), ()))
NT = (((1,), (1,)), ((), ()))
TN = (((0,), (0,)), ((), ()))


def split(x):
    hi = x.astype(bf16)
    return hi, (x - hi.astype(f32)).astype(bf16)


def dot(a, b, dims=NN):
    return lax.dot_general(a, b, dims, preferred_element_type=f32)


def mm(a, b, dims=NN):
    ah, al = split(a)
    bh, bl = split(b)
    left = jnp.concatenate([ah, al], axis=1)
    n = dims[0][1][0]
    if b.shape[1 - n] > C:
        return dot(left, jnp.concatenate([bh, bh], axis=n), dims) + dot(ah, bl, dims)
    right = jnp.concatenate([bh, bl], axis=1 - n)
    both = dot(left, jnp.concatenate([right, right], axis=n), dims)
    return both[:, :C] + both[:, C:]


def tn(a, b):
    return mm(a.T, b)


def split3(x):
    hi = x.astype(bf16)
    rest = x - hi.astype(f32)
    mid = rest.astype(bf16)
    return hi, mid, (rest - mid.astype(f32)).astype(bf16)


def iotas(shape=(C, C)):
    return lax.broadcasted_iota(jnp.int32, shape, 0), lax.broadcasted_iota(jnp.int32, shape, 1)


def head(ref, h):
    return ref[:, h * C : (h + 1) * C].astype(f32)


def unit(x):
    inv = 1.0 / jnp.sqrt(jnp.sum(x * x, axis=-1, keepdims=True) + EPS)
    return x * inv, inv


def gate_tables(resets, b_ref, g_ref):
    rows, cols = iotas()
    lower = (rows >= cols).astype(bf16)
    upper = (rows <= cols).astype(bf16)
    parts = split3(g_ref[...])
    total_c = sum(dot(lower, part, NT) for part in parts)
    total_r = sum(dot(part, upper) for part in parts)
    beta = dot((rows == cols).astype(bf16), b_ref[...], NT)
    keep1 = 1.0 - resets[0, 0].astype(f32)
    keep2 = 1.0 - resets[0, 1].astype(f32)
    late = lax.broadcasted_iota(jnp.int32, (C, H), 0) >= 64
    growth = jnp.exp(total_c) * (keep1 * jnp.where(late, keep2, 1.0))
    last = total_c[C - 1 : C]
    fading = jnp.exp(last - total_c) * jnp.where(late, 1.0, keep2)
    g_last = jnp.exp(last) * (keep1 * keep2)
    doc = jnp.where((rows >= 64) & (cols < 64), keep2, 1.0)
    return total_c, total_r, growth, fading, g_last, beta, doc


def head_gates(tables, h):
    total_c, total_r, growth, fading, g_last, beta, doc = tables
    rows, cols = iotas()
    keep = rows >= cols
    later = total_c[:, h : h + 1] - total_r[h : h + 1, :]
    inside = jnp.where(keep, jnp.exp(jnp.where(keep, later, 0.0)), 0.0) * doc
    return inside, growth[:, h : h + 1], fading[:, h : h + 1], g_last[:, h : h + 1], beta[:, h : h + 1]


def place():
    seq = lax.axis_index("seq")
    return lax.axis_index("dp"), seq // 8, (seq // 2) % 4, seq % 2


def strict(x):
    rows, cols = iotas()
    return jnp.where(rows > cols, x, 0.0)


def spec_v(n):
    return [pl.BlockSpec(memory_space=pltpu.VMEM)] * n


def call(kernel, outs, n_smem, *args, us=1.0, scratch=(), hbm=(), after=(), limit=VMEM_LIMIT):
    n_after = len(after)

    def body(*refs):
        kernel(*refs[n_after:])

    in_specs = [pl.BlockSpec(memory_space=pl.ANY)] * n_after + [
        pl.BlockSpec(
            memory_space=pltpu.SMEM if i < n_smem else pltpu.HBM if i in hbm else pltpu.VMEM
        )
        for i in range(len(args))
    ]
    return pl.pallas_call(
        body,
        out_shape=[jax.ShapeDtypeStruct(s, d) for s, d in outs],
        in_specs=in_specs,
        out_specs=spec_v(len(outs)),
        scratch_shapes=list(scratch),
        compiler_params=pltpu.CompilerParams(vmem_limit_bytes=limit),
        cost_estimate=pl.CostEstimate(flops=0, bytes_accessed=1, transcendentals=0),
    )(*after, *args)


HEADS = range(H)


def maps_kernel(
    resets, b_ref, g_ref, k_hbm, v_hbm, keep_ref, send_ref, inv_ref, uw_ref, k_ref, v_ref, sems
):
    load_k = pltpu.make_async_copy(k_hbm, k_ref, sems.at[0])
    load_v = pltpu.make_async_copy(v_hbm, v_ref, sems.at[1])
    load_k.start()
    load_v.start()
    tables = gate_tables(resets, b_ref, g_ref)
    rows, cols = iotas()
    eye = (rows == cols).astype(f32)
    block = (rows >= 64) == (cols >= 64)
    gates = [head_gates(tables, h) for h in HEADS]
    load_k.wait()
    kn = [unit(head(k_ref, h))[0] for h in HEADS]
    kk = [mm(kn[h], kn[h], NT) for h in HEADS]
    system = [strict(kk[h] * gates[h][0]) * gates[h][4] for h in HEADS]
    near = [jnp.where(block, x, 0.0) for x in system]
    far = [jnp.where(block, 0.0, x) for x in system]
    inv = [eye - x for x in near]
    power = [mm(x, x) for x in near]
    for level in range(5):
        if level < 4:
            both = [mm(jnp.concatenate([inv[h], power[h]], axis=0), power[h]) for h in HEADS]
            inv = [inv[h] + both[h][:C] for h in HEADS]
            power = [both[h][C:] for h in HEADS]
        else:
            inv = [inv[h] + mm(inv[h], power[h]) for h in HEADS]
    cross = [mm(far[h], inv[h]) for h in HEADS]
    inv = [inv[h] - mm(inv[h], cross[h]) for h in HEADS]
    load_v.wait()
    uw = []
    for h in HEADS:
        bh = gates[h][4]
        right = jnp.concatenate([kn[h] * (bh * gates[h][1]), head(v_ref, h) * bh], axis=1)
        uw.append(mm(inv[h], right))
    maps = []
    for h in HEADS:
        prod = tn(kn[h] * gates[h][2], uw[h])
        maps.append(
            jnp.concatenate([eye * gates[h][3] - prod[:, :C], prod[:, C:]], axis=1)
        )
    for h in HEADS:
        inv_ref[h] = inv[h]
        uw_ref[h] = uw[h]
    first = place()[3] == 0
    for j in range(4):
        keep_ref[j] = jnp.where(first, maps[j], maps[j + 4])
        send_ref[j] = jnp.where(first, maps[j + 4], maps[j])


def compose(later, earlier):
    moved = mm(later[:, :C], earlier)
    return jnp.concatenate([moved[:, :C], moved[:, C:] + later[:, C:]], axis=1)


def pair_kernel(keep_ref, recv_ref, o0, o1, o2, o3, scratch):
    first = place()[3] == 0
    for j in range(4):
        a, b = keep_ref[j], recv_ref[j]
        early = jnp.where(first, a, b)
        late = jnp.where(first, b, a)
        scratch[j] = compose(late, early)
    for r, out in enumerate((o0, o1, o2, o3)):
        out[...] = scratch[(place()[2] + r) % 4]


def group_kernel(x0, x1, x2, x3, maps_ref, prefix_ref, total_ref):
    for r, ref in enumerate((x0, x1, x2, x3)):
        maps_ref[(place()[2] + 4 - r) % 4] = ref[...]
    run = maps_ref[0]
    prefix_ref[0] = run
    for i in range(1, 4):
        run = compose(maps_ref[i], run)
        if i < 3:
            prefix_ref[i] = run
    total_ref[...] = run


def enter_kernel(t0, t1, t2, t3, prefix_ref, totals_ref, o0, o1, o2, o3, scratch):
    for r, ref in enumerate((t0, t1, t2, t3)):
        totals_ref[(place()[1] + 4 - r) % 4] = ref[...]
    x = place()[1]
    s1 = totals_ref[0, :, C:]
    s2 = mm(totals_ref[1, :, :C], s1) + totals_ref[1, :, C:]
    s3 = mm(totals_ref[2, :, :C], s2) + totals_ref[2, :, C:]
    state = jnp.where(x == 0, 0.0, jnp.where(x == 1, s1, jnp.where(x == 2, s2, s3)))
    scratch[0] = state
    for i in range(3):
        scratch[i + 1] = mm(prefix_ref[i, :, :C], state) + prefix_ref[i, :, C:]
    for r, out in enumerate((o0, o1, o2, o3)):
        out[...] = scratch[(place()[2] + r) % 4]


def split_pair_kernel(s0, s1, s2, s3, keep_ref, recv_ref, mine_ref, other_ref, scratch):
    for r, ref in enumerate((s0, s1, s2, s3)):
        scratch[(place()[2] + 4 - r) % 4] = ref[...]
    first = place()[3] == 0
    for j in range(4):
        early = jnp.where(first, keep_ref[j], recv_ref[j])
        start = scratch[j]
        middle = mm(early[:, :C], start) + early[:, C:]
        mine_ref[j] = jnp.where(first, start, middle)
        other_ref[j] = jnp.where(first, middle, start)


def reads_kernel(
    resets, b_ref, g_ref, q_ref, k_ref, uw_ref, inv_ref,
    read_ref, inside_ref, attn_ref, kk_ref, kn_ref, qn_ref, invt_ref,
    growth_ref, fading_ref, beta_ref, iq_ref, ik_ref, last_ref,
):
    tables = gate_tables(resets, b_ref, g_ref)
    growth_ref[...] = tables[2]
    fading_ref[...] = tables[3]
    last_ref[...] = tables[4]
    beta_ref[...] = tables[5]
    cols = lax.broadcasted_iota(jnp.int32, (C, H), 1)
    iq_all = jnp.zeros((C, H), f32)
    ik_all = jnp.zeros((C, H), f32)
    for h in HEADS:
        qn, iq = unit(head(q_ref, h))
        kn, ik = unit(head(k_ref, h))
        inside, growth, _, _, _ = head_gates(tables, h)
        inner = mm(jnp.concatenate([qn, kn], axis=0), kn, NT)
        attn = inner[:C] * inside
        prod = mm(attn, uw_ref[h])
        read_ref[h] = jnp.concatenate([qn * growth - prod[:, :C], prod[:, C:]], axis=1)
        inside_ref[h] = inside
        attn_ref[h] = attn
        kk_ref[h] = inner[C:]
        kn_ref[h] = kn
        qn_ref[h] = qn
        invt_ref[h] = inv_ref[h].T
        iq_all = jnp.where(cols == h, iq, iq_all)
        ik_all = jnp.where(cols == h, ik, ik_all)
    iq_ref[...] = iq_all
    ik_ref[...] = ik_all


def pick(first, mine_ref, other_ref, h):
    a, b = mine_ref[h % 4], other_ref[h % 4]
    return jnp.where(first, a, b) if h < 4 else jnp.where(first, b, a)


def outs_kernel(
    mine_ref, other_ref, read_ref, dn_ref, n_ref, do_ref, keep_ref, send_ref
):
    first = place()[3] == 0
    reach = []
    for h in HEADS:
        state = pick(first, mine_ref, other_ref, h)
        read = read_ref[h]
        out = mm(read[:, :C], state) + read[:, C:]
        inv = 1.0 / jnp.sqrt(jnp.mean(out * out, axis=-1, keepdims=True) + EPS)
        n32 = out * inv
        n_ref[:, h * C : (h + 1) * C] = n32.astype(bf16)
        dn = dn_ref[:, h * C : (h + 1) * C]
        do = inv * (dn - n32 * jnp.mean(n32 * dn, axis=-1, keepdims=True))
        do_ref[h] = do
        reach.append(tn(read[:, :C], do))
    for j in range(4):
        keep_ref[j] = jnp.where(first, reach[j], reach[j + 4])
        send_ref[j] = jnp.where(first, reach[j + 4], reach[j])


def pair_back_kernel(
    keep_ref, recv_ref, mkeep_ref, mrecv_ref, n_ref, o0, o1, o2, o3, c0, c1, c2, c3, scratch, wide
):
    for j in range(4):
        wide[j] = n_ref[:, 2 * j * C : 2 * (j + 1) * C].astype(f32)
    for r, out_ref in enumerate((c0, c1, c2, c3)):
        out_ref[...] = wide[(place()[0] + r) % 4]
    first = place()[3] == 0
    for j in range(4):
        a, b = keep_ref[j], recv_ref[j]
        early = jnp.where(first, a, b)
        late = jnp.where(first, b, a)
        early_map = jnp.where(first, mkeep_ref[j, :, :C], mrecv_ref[j, :, :C])
        scratch[j] = early + tn(early_map, late)
    for r, out in enumerate((o0, o1, o2, o3)):
        out[...] = scratch[(place()[2] + r) % 4]


def group_back_kernel(r0, r1, r2, r3, maps_ref, reach_ref, total_ref):
    for r, ref in enumerate((r0, r1, r2, r3)):
        reach_ref[(place()[2] + 4 - r) % 4] = ref[...]
    run = reach_ref[3]
    for i in (2, 1, 0):
        run = reach_ref[i] + tn(maps_ref[i, :, :C], run)
    total_ref[...] = run


def enter_back_kernel(t0, t1, t2, t3, totals_ref, maps_ref, reach_ref, o0, o1, o2, o3, parts, scratch):
    for r, ref in enumerate((t0, t1, t2, t3)):
        parts[(place()[1] + 4 - r) % 4] = ref[...]
    x = place()[1]
    d2 = parts[3]
    d1 = parts[2] + tn(totals_ref[2, :, :C], d2)
    d0 = parts[1] + tn(totals_ref[1, :, :C], d1)
    run = jnp.where(x == 3, 0.0, jnp.where(x == 2, d2, jnp.where(x == 1, d1, d0)))
    scratch[3] = run
    for i in (2, 1, 0):
        run = reach_ref[i + 1] + tn(maps_ref[i + 1, :, :C], run)
        scratch[i] = run
    for r, out in enumerate((o0, o1, o2, o3)):
        out[...] = scratch[(place()[2] + r) % 4]


def split_pair_back_kernel(
    s0, s1, s2, s3, mkeep_ref, mrecv_ref, keep_ref, recv_ref, mine_ref, other_ref, scratch
):
    for r, ref in enumerate((s0, s1, s2, s3)):
        scratch[(place()[2] + 4 - r) % 4] = ref[...]
    first = place()[3] == 0
    for j in range(4):
        late_map = jnp.where(first, mrecv_ref[j, :, :C], mkeep_ref[j, :, :C])
        late = jnp.where(first, recv_ref[j], keep_ref[j])
        end = scratch[j]
        middle = late + tn(late_map, end)
        mine_ref[j] = jnp.where(first, middle, end)
        other_ref[j] = jnp.where(first, end, middle)


def early_grads_kernel(
    half, mine_ref, other_ref, uw_ref, do_ref, inside_ref, attn_ref, kn_ref, qn_ref, growth_ref, iq_ref, *refs
):
    dq_ref, delta_ref, dkn_ref, dd_ref, carried_ref, rowpart_ref, colpart_ref = refs[half:]
    first = place()[3] == 0
    _, cols = iotas()
    row8 = lax.broadcasted_iota(jnp.int32, (H, C), 0)
    row_all = jnp.zeros((C, C), f32)
    col_all = jnp.zeros((H, C), f32)
    if half:
        dq_ref[:, : 4 * C] = refs[0][...]
    for i in range(4):
        h = 4 * half + i
        state = pick(first, mine_ref, other_ref, h)
        qn, kn, attn = qn_ref[h], kn_ref[h], attn_ref[h]
        uw = uw_ref[h]
        do = do_ref[h]
        moved = mm(jnp.concatenate([uw[:, :C], kn], axis=0), state)
        delta = uw[:, C:] - moved[:C]
        both = mm(do, jnp.concatenate([delta, state], axis=0), NT)
        dattn, back = both[:, :C], both[:, C:] * growth_ref[:, h : h + 1]
        dqk = dattn * inside_ref[h]
        dqn = back + mm(dqk, kn)
        dq = iq_ref[:, h : h + 1] * (dqn - qn * jnp.sum(dqn * qn, axis=-1, keepdims=True))
        dq_ref[:, h * C : (h + 1) * C] = dq.astype(bf16)
        pairs = dattn * attn
        row = jnp.sum(pairs + back * qn, axis=-1, keepdims=True)
        row_all = jnp.where(cols == h, row, row_all)
        col_all = jnp.where(row8 == h, jnp.sum(pairs, axis=0, keepdims=True), col_all)
        dkn_ref[i] = tn(dqk, qn)
        dd_ref[i] = tn(attn, do)
        delta_ref[i] = delta
        carried_ref[i] = moved[C:]
    rowpart_ref[...] = row_all
    colpart_ref[...] = col_all


EARLY = 6


def late_grads_kernel(
    v_ref, mine_ref, other_ref, dmine_ref, dother_ref, inside_ref, kk_ref, kn_ref, invt_ref,
    growth_ref, fading_ref, beta_ref, ik_ref, last_ref, *refs
):
    early = refs[: 2 * EARLY]
    dk_ref, dv_ref, db_ref, dg_ref = refs[2 * EARLY :]
    first = place()[3] == 0
    rows, cols = iotas()
    row8 = lax.broadcasted_iota(jnp.int32, (H, C), 0)
    row_all = early[4][...] + early[EARLY + 4][...]
    col_all = early[5][...] + early[EARLY + 5][...]
    db_all = jnp.zeros((C, C), f32)
    is_last = lax.broadcasted_iota(jnp.int32, (C, 1), 0) == C - 1
    for h in HEADS:
        delta, dkn, dd, carried = (
            ref[h % 4] for ref in early[h // 4 * EARLY : h // 4 * EARLY + 4]
        )
        kk, invt, kn = kk_ref[h], invt_ref[h], kn_ref[h]
        state = pick(first, mine_ref, other_ref, h)
        dstate = pick(first, dmine_ref, dother_ref, h)
        growth, fading, g_last, bh = (
            ref[:, h : h + 1] for ref in (growth_ref, fading_ref, last_ref, beta_ref)
        )
        below = strict(inside_ref[h])
        ddelta = dd + mm(kn, dstate) * fading
        dtarget = mm(invt, ddelta)
        dv_ref[:, h * C : (h + 1) * C] = (dtarget * bh).astype(bf16)
        both = mm(dtarget, jnp.concatenate([delta, state], axis=0), NT)
        dsys, dts = -(both[:, :C] * below), both[:, C:]
        raw = dsys * kk
        dkk = dsys * bh
        dkf = mm(delta, dstate, NT) * fading
        dcar = dtarget * carried * growth
        db = jnp.sum(dtarget * head(v_ref, h) - dcar + raw, axis=-1, keepdims=True)
        pairs = raw * bh
        dfade = dkf * kn
        dlast = jnp.sum(dfade + g_last * (state * dstate), axis=0, keepdims=True)
        dtotal = jnp.sum(pairs - dcar * bh - dfade, axis=-1, keepdims=True)
        dtotal = dtotal + jnp.where(is_last, jnp.sum(dlast, axis=-1, keepdims=True), 0.0)
        dkn = dkn + mm(dkk + dkk.T, kn) + dkf - dts * (bh * growth)
        dk = ik_ref[:, h : h + 1] * (dkn - kn * jnp.sum(dkn * kn, axis=-1, keepdims=True))
        dk_ref[:, h * C : (h + 1) * C] = dk.astype(bf16)
        db_all = jnp.where(cols == h, db, db_all)
        row_all = row_all + jnp.where(cols == h, dtotal, 0.0)
        col_all = col_all + jnp.where(row8 == h, jnp.sum(pairs, axis=0, keepdims=True), 0.0)
    lower = (rows >= cols).astype(bf16)
    db_ref[...] = db_all.T[:H]
    dg_ref[...] = sum(dot(part, lower) for part in split3(row_all.T[:H] - col_all))


def widen_kernel(cot_ref, wide_ref):
    wide_ref[...] = cot_ref[...].astype(f32)


def relay_kernel(below_ref, above_ref, lower_ref, upper_ref):
    lower_ref[...] = below_ref[:64, :]
    upper_ref[...] = above_ref[64:, :]


def wgrad_kernel(n0, n1, n2, n3, c0, c1, c3, c2_low, c2_up, keep_ref, send_ref):
    ns = [ref[...].astype(bf16).T for ref in (n0, n1, n2, n3)]
    first = place()[3] == 0
    for j in range(8):
        cols = slice(j * 256, (j + 1) * 256)
        far = jnp.concatenate([c2_low[:, cols], c2_up[:, cols]], axis=0)
        cots = (c0[:, cols], c1[:, cols], far, c3[:, cols])
        total = sum(dot(ns[r], cots[r].astype(bf16)) for r in range(4)).reshape(16, 2, 8, 256)
        a, b = total[:, 0], total[:, 1]
        keep_ref[:, :, cols] = jnp.where(first, a, b)
        send_ref[:, :, cols] = jnp.where(first, b, a)


def wsum_pair_kernel(keep_ref, recv_ref, o0, o1, o2, o3):
    for r, out in enumerate((o0, o1, o2, o3)):
        z = (place()[2] + r) % 4
        for x in range(4):
            out[x] = keep_ref[4 * x + z] + recv_ref[4 * x + z]


def wsum_z_kernel(a0, a1, a2, a3, o0, o1, o2, o3):
    for r, out in enumerate((o0, o1, o2, o3)):
        x = (place()[1] + r) % 4
        out[...] = (a0[x] + a1[x]) + (a2[x] + a3[x])


def wsum_x_kernel(scale, a0, a1, a2, a3, out):
    out[...] = ((a0[...] + a1[...]) + (a2[...] + a3[...])) * scale


def seq_perm(dx, dz, dc=0):
    pairs = []
    for i in range(32):
        x, z, c = i // 8, (i // 2) % 4, i % 2
        pairs.append((i, ((x + dx) % 4) * 8 + ((z + dz) % 4) * 2 + (c ^ dc)))
    return pairs


def swap_core(x):
    return lax.ppermute(x, "seq", seq_perm(0, 0, 1))


def around_z(parts):
    moved = {r: lax.ppermute(parts[r], "seq", seq_perm(0, r)) for r in (1, 2, 3)}
    return [parts[0], moved[1], moved[2], moved[3]]


def around_x(parts):
    moved = {r: lax.ppermute(parts[r], "seq", seq_perm(r, 0)) for r in (1, 2, 3)}
    return [parts[0], moved[1], moved[2], moved[3]]


def step_dp(x, r):
    return lax.ppermute(x, "dp", [(i, (i + r) % 4) for i in range(4)])


def around_dp(parts):
    moved = {r: step_dp(parts[r], r) for r in (1, 2, 3)}
    return [parts[0], moved[1], moved[2], moved[3]]


def local(queries, keys, values, strength, log_decay, resets, out_weight, cotangent):
    q, k, v = queries[0], keys[0], values[0]
    cot = cotangent[0]
    gates = (resets, strength[0].T, log_decay[0].T)
    n_all = C * lax.axis_size("seq") * lax.axis_size("dp")

    mat, mat2 = (C, C), (C, 2 * C)
    one, two = (mat, f32), (mat2, f32)
    four, four2 = ((4, *mat), f32), ((4, *mat2), f32)
    all1, all2 = ((H, *mat), f32), ((H, *mat2), f32)
    wide = ((C, H * C), bf16)
    hold, hold2 = [pltpu.VMEM(*four)], [pltpu.VMEM(*four2)]

    mkeep, msend, inverse, uw = call(
        maps_kernel,
        [four2, four2, all1, all2],
        1, *gates, k, v, us=6, hbm=(3, 4), limit=FIRST_LIMIT,
        scratch=[pltpu.VMEM(*wide), pltpu.VMEM(*wide), pltpu.SemaphoreType.DMA((2,))],
    )
    mrecv = swap_core(msend)
    parts = call(pair_kernel, [two] * 4, 0, mkeep, mrecv, scratch=hold2)
    own = parts[0]
    parts = around_z(parts)
    (cot32,) = call(widen_kernel, [((C, 2048), f32)], 0, cot, after=(own,))
    dn = lax.dot_general(cot, out_weight, NT, preferred_element_type=f32)
    below, above = step_dp(cot32, 1), step_dp(cot32, 3)
    maps, prefix, total = call(
        group_kernel, [four2, ((3, *mat2), f32), two], 0, *parts, after=(dn, cot32)
    )
    parts = around_x([total] * 4)
    reads, inside, attn, kk, kn, qn, invt, growth, fading, beta, iq, ik, last_decay = call(
        reads_kernel,
        [all2] + [all1] * 6 + [((C, H), f32)] * 5 + [((1, H), f32)],
        1, *gates, q, k, uw, inverse, us=3, after=(total,),
    )
    totals, *parts = call(
        enter_kernel, [four2] + [one] * 4, 0, *parts, prefix, us=1.2, scratch=hold, after=(reads,)
    )
    own = parts[0]
    parts = around_z(parts)
    lower, upper = call(relay_kernel, [((64, 2048), f32)] * 2, 0, below, above, after=(own,))
    lower, upper = step_dp(lower, 1), step_dp(upper, 3)
    mine, other = call(split_pair_kernel, [four] * 2, 0, *parts, mkeep, mrecv, scratch=hold)
    other = swap_core(other)

    n16, do, rkeep, rsend = call(
        outs_kernel, [wide, all1, four, four], 0, mine, other, reads, dn, us=1.6
    )

    rrecv = swap_core(rsend)
    parts = call(
        pair_back_kernel, [one] * 4 + [two] * 4, 0, rkeep, rrecv, mkeep, mrecv, n16,
        scratch=hold + hold2,
    )
    chunks = around_dp(parts[4:])
    own = parts[0]
    parts = around_z(parts[:4])

    def early_grads(half, token, *done):
        return call(
            functools.partial(early_grads_kernel, half),
            [((C, 4 * (1 + half) * C), bf16)] + [four] * 4 + [one, ((H, C), f32)],
            0, mine, other, uw, do, inside, attn, kn, qn, growth, iq, *done, us=2.2, after=(token,),
        )

    early0 = early_grads(0, own)
    mixed = lax.dot_general(n16, out_weight, NN, preferred_element_type=f32).astype(bf16)
    reach, total = call(group_back_kernel, [four, one], 0, *parts, maps, after=(early0[0],))
    parts = around_x([total] * 4)
    wkeep, wsend = call(
        wgrad_kernel,
        [((16, 8, 2048), f32)] * 2,
        0, *chunks, cot, below, above, lower, upper, us=2.5, after=(total,),
    )
    wrecv = swap_core(wsend)
    wparts = call(wsum_pair_kernel, [((4, 8, 2048), f32)] * 4, 0, wkeep, wrecv)
    parts = call(
        enter_back_kernel, [one] * 4, 0, *parts, totals, maps, reach, us=1.5, scratch=hold + hold,
        after=(wparts[0],),
    )
    early1 = early_grads(1, parts[0], early0[0])
    parts = around_z(parts)
    wsent = around_z(wparts)
    dmine, dother = call(
        split_pair_back_kernel, [four] * 2, 0, *parts, mkeep, mrecv, rkeep, rrecv, scratch=hold,
        after=(early1[0], mixed),
    )
    dother = swap_core(dother)
    wparts = call(wsum_z_kernel, [((8, 2048), f32)] * 4, 0, *wsent, after=(dmine,))
    dk, dv, db, dg = call(
        late_grads_kernel,
        [wide, wide, ((H, C), f32), ((H, C), f32)],
        0, v, mine, other, dmine, dother, inside, kk, kn, invt, growth, fading, beta, ik, last_decay,
        *early0[1:], *early1[1:], us=6, after=(wparts[0],),
    )
    wparts = around_x(wparts)
    scale = 1.0 / math.sqrt(n_all)

    def last(a0, a1, a2, a3, out):
        wsum_x_kernel(scale, a0, a1, a2, a3, out)

    (weight_grad,) = call(last, [((8, 2048), f32)], 0, *wparts, after=(db,))
    dq = early1[0]
    return (mixed[None], dq[None], dk[None], dv[None], db.T[None], dg.T[None], weight_grad)


def solution(mesh):
    rows = P("dp", "seq", None)
    return jax.shard_map(
        local,
        mesh=mesh,
        in_specs=(rows, rows, rows, rows, rows, P("dp", "seq"), P(), rows),
        out_specs=(rows, rows, rows, rows, rows, rows, P(("dp", "seq"), None)),
        check_vma=False,
    )
```

time: 118 us -> 110 us (0.932)
  Pallas kernels: 35.6 us -> 28.7 us
  local copies, waits for them, and re-layouts: 1.79 us -> 6 us
  waiting for transfers between devices: 20.4 us -> 16.3 us
    pallas_call x19 -> x20, Pallas kernels: 35.6 us -> 28.7 us  [call(): pl.pallas_call(body, out_shape=[jax.ShapeDtypeStruct(s, d) for s, d in ou...]
    unnamed x30 -> x48, local copies, waits for them, and re-layouts: 1.79 us -> 6 us
    ppermute x7, waiting for transfers between devices: 5.02 us -> 2.55 us  [step_dp(): return lax.ppermute(x, 'dp', [(i, (i + r) % 4) for i in range(4)])]
  transfers between devices with their start and end apart: 36 -> 36, of which waited for: 15 -> 13; matrix products, arithmetic and copies ran while one was open for 6% -> 6% of each run, Pallas kernels for 20% -> 16%
where the time goes in v3:
time: 110 us; the launch traced here: 109 us
  starting transfers between devices  50.4 us (46%)
  Pallas kernels  28.7 us (26%)
  waiting for transfers between devices  16.3 us (15%)
  matrix products  6.62 us (6%)
  local copies, waits for them, and re-layouts  6 us (5%)
    pallas_call x20, Pallas kernels, call(): pl.pallas_call(body, out_shape=[jax.ShapeDtypeStruct(s, d) for s, d in ou...  28.7 us
    ppermute x15, starting transfers between devices, around_z(): lax.ppermute(parts[r], 'seq', seq_perm(0, r))  20.8 us
    ppermute x9, starting transfers between devices, around_x(): lax.ppermute(parts[r], 'seq', seq_perm(r, 0))  13.1 us
    ppermute x5, starting transfers between devices, swap_core(): return lax.ppermute(x, 'seq', seq_perm(0, 0, 1))  10 us
    ppermute x15, waiting for transfers between devices, around_z(): lax.ppermute(parts[r], 'seq', seq_perm(0, r))  7.85 us
    ppermute x7, starting transfers between devices, step_dp(): return lax.ppermute(x, 'dp', [(i, (i + r) % 4) for i in range(4)])  6.44 us
    unnamed x48, local copies, waits for them, and re-layouts  6 us
    dot_general x1, matrix products, local(): dn = lax.dot_general(cot, out_weight, NT, preferred_element_type=f32)  3.7 us
  transfers between devices with their start and end apart: 36, of which 13 were waited for; matrix products, arithmetic and copies ran while one was open for 6% of the time, Pallas kernels for 16%

profile of v3, /device:TPU:1, one launch (start us, length us, event | category | flops | bytes accessed | tf_op | source)
XLA Modules:
  0.0 109.0 jit_solution(15494644671675038264)
XLA Ops:
  0.6 6.5 %shard_map.135 = (f32[4,128,256]{2,1,0:T(8,128)}, f32[4,128,256]{2,1,0:T(8,128)}, f32[8,128,128]{2,1,0:T(8,128)}, f32[8,128,256]{2,1,0:T(8,128)}) custom-call(s32[1,2]{1,0:T(1,128)} %refs_1_.1, bf16[8,128]{1,0:T(8,128)(2,1)} %bitcast.36, f32[8,128]{1,0:T(8,128)} %bitcast.34, bf16[128,1024]{1,0:T(8,128)(2,1)} %bitcast.30, bf16[128,1024]{1,0:T(8,128)(2,1)} %bitcast.28), custom_call_target="tpu_custom_call" | custom-call | bytes 1 | tf_op jit(solution)/shard_map/pallas_call | solution.py:123
  7.1 1.5 %collective-permute-start = (f32[4,128,256]{2,1,0:T(8,128)}, f32[4,128,256]{2,1,0:T(8,128)S(1)}, u32[]{:S(2)}, u32[]{:S(2)}) collective-permute-start(f32[4,128,256]{2,1,0:T(8,128)} %get-tuple-element.89), channel_id=1, source_target_pairs={{0,1},{1,0},{2,3},{3,2},{4,5},{5,4},{6,7},{7,6},{8,9},{9,8},{10,11... | collective-permute-start | bytes 1572872 | tf_op jit(solution)/shard_map/ppermute | solution.py:497
  8.6 1.7 %collective-permute-done.refs_1_.refs_5_.refs_3_.refs_7_ = f32[4,128,256]{2,1,0:T(8,128)S(1)} collective-permute-done((f32[4,128,256]{2,1,0:T(8,128)}, f32[4,128,256]{2,1,0:T(8,128)S(1)}, u32[]{:S(2)}, u32[]{:S(2)}) %collective-permute-start) | collective-permute-done | bytes 524320 | tf_op jit(solution)/shard_map/ppermute | solution.py:497
  10.4 1.0 copy-done.1
  11.4 0.4 shard_map.136
  11.8 1.0 copy-done.3
  12.9 1.5 %collective-permute-start.18 = (f32[128,2048]{1,0:T(8,128)S(1)}, f32[128,2048]{1,0:T(8,128)S(1)}, u32[]{:S(2)}, u32[]{:S(2)}) collective-permute-start(f32[128,2048]{1,0:T(8,128)S(1)} %shard_map.137.refs_1_), channel_id=1, source_target_pairs={{0,32},{32,64},{64,96},{96,0},{1,33},{33,65},{65,97},{97,1},{2,34}... | collective-permute-start | bytes 3145736 | tf_op jit(solution)/shard_map/ppermute | solution.py:511
  14.4 1.5 %collective-permute-start.19 = (f32[128,2048]{1,0:T(8,128)S(1)}, f32[128,2048]{1,0:T(8,128)S(1)}, u32[]{:S(2)}, u32[]{:S(2)}) collective-permute-start(f32[128,2048]{1,0:T(8,128)S(1)} %shard_map.137.refs_1_), channel_id=1, source_target_pairs={{0,96},{32,0},{64,32},{96,64},{1,97},{33,1},{65,33},{97,65},{2,98}... | collective-permute-start | bytes 3145736 | tf_op jit(solution)/shard_map/ppermute | solution.py:511
  15.9 1.6 %collective-permute-start.1 = (f32[128,256]{1,0:T(8,128)S(1)}, f32[128,256]{1,0:T(8,128)S(1)}, u32[]{:S(2)}, u32[]{:S(2)}) collective-permute-start(f32[128,256]{1,0:T(8,128)S(1)} %get-tuple-element.91), channel_id=1, source_target_pairs={{0,2},{1,3},{2,4},{3,5},{4,6},{5,7},{6,0},{7,1},{8,10},{9,11},{10,... | collective-permute-start | bytes 393224 | tf_op jit(solution)/shard_map/ppermute | solution.py:501
  17.5 3.3 %collective-permute-start.2 = (f32[128,256]{1,0:T(8,128)S(1)}, f32[128,256]{1,0:T(8,128)S(1)}, u32[]{:S(2)}, u32[]{:S(2)}) collective-permute-start(f32[128,256]{1,0:T(8,128)S(1)} %get-tuple-element.92), channel_id=1, source_target_pairs={{0,4},{1,5},{2,6},{3,7},{4,0},{5,1},{6,2},{7,3},{8,12},{9,13},{10,... | collective-permute-start | bytes 393224 | tf_op jit(solution)/shard_map/ppermute | solution.py:501
  20.9 0.7 collective-permute-start.3
  21.6 3.7 %fusion.refs_0_.refs_3_ = f32[128,1024]{1,0:T(8,128)S(1)} fusion(bf16[1024,2048]{1,0:T(8,128)(2,1)} %param.14, bf16[1,128,2048]{2,1,0:T(8,128)(2,1)S(1)} %copy-done.3), kind=kOutput, calls=%fused_computation.1 | convolution fusion | flops 536870912 | bytes 5242880 | tf_op jit(solution)/shard_map/dot_general | solution.py:543
  25.3 1.1 %collective-permute-done.2.refs_4_ = f32[128,256]{1,0:T(8,128)S(1)} collective-permute-done((f32[128,256]{1,0:T(8,128)S(1)}, f32[128,256]{1,0:T(8,128)S(1)}, u32[]{:S(2)}, u32[]{:S(2)}) %collective-permute-start.2) | collective-permute-done | bytes 131104 | tf_op jit(solution)/shard_map/ppermute | solution.py:501
  26.4 0.6 shard_map.138
  27.1 1.3 %collective-permute-start.4 = (f32[128,256]{1,0:T(8,128)S(1)}, f32[128,256]{1,0:T(8,128)S(1)}, u32[]{:S(2)}, u32[]{:S(2)}) collective-permute-start(f32[128,256]{1,0:T(8,128)S(1)} %get-tuple-element.94.refs_0_.refs_1_), channel_id=1, source_target_pairs={{0,8},{1,9},{2,10},{3,11},{4,12},{5,13},{6,14},{7,15},{8,16},{9,17... | collective-permute-start | bytes 393224 | tf_op jit(solution)/shard_map/ppermute | solution.py:506
  28.4 2.5 %collective-permute-start.5 = (f32[128,256]{1,0:T(8,128)S(1)}, f32[128,256]{1,0:T(8,128)S(1)}, u32[]{:S(2)}, u32[]{:S(2)}) collective-permute-start(f32[128,256]{1,0:T(8,128)S(1)} %get-tuple-element.94.refs_0_.refs_1_), channel_id=1, source_target_pairs={{0,16},{1,17},{2,18},{3,19},{4,20},{5,21},{6,22},{7,23},{8,24},{9,... | collective-permute-start | bytes 393224 | tf_op jit(solution)/shard_map/ppermute | solution.py:506
  30.8 1.1 %collective-permute-start.6 = (f32[128,256]{1,0:T(8,128)S(1)}, f32[128,256]{1,0:T(8,128)S(1)}, u32[]{:S(2)}, u32[]{:S(2)}) collective-permute-start(f32[128,256]{1,0:T(8,128)S(1)} %get-tuple-element.94.refs_0_.refs_1_), channel_id=1, source_target_pairs={{0,24},{1,25},{2,26},{3,27},{4,28},{5,29},{6,30},{7,31},{8,0},{9,1... | collective-permute-start | bytes 393224 | tf_op jit(solution)/shard_map/ppermute | solution.py:506
  32.0 2.8 %shard_map.139 = (f32[8,128,256]{2,1,0:T(8,128)S(1)}, f32[8,128,128]{2,1,0:T(8,128)S(1)}, f32[8,128,128]{2,1,0:T(8,128)S(1)}, f32[8,128,128]{2,1,0:T(8,128)S(1)}...) custom-call(f32[128,256]{1,0:T(8,128)S(1)} %get-tuple-element.94.ref, ...), custom_call_target="tpu_custom_call" | custom-call | bytes 1 | tf_op jit(solution)/shard_map/pallas_call | solution.py:123
  34.8 0.8 copy-done.9
  35.8 0.6 shard_map.140
  36.5 2.1 %collective-permute-start.7 = (f32[128,128]{1,0:T(8,128)S(1)}, f32[128,128]{1,0:T(8,128)S(1)}, u32[]{:S(2)}, u32[]{:S(2)}) collective-permute-start(f32[128,128]{1,0:T(8,128)S(1)} %get-tuple-element.100), channel_id=1, source_target_pairs={{0,2},{1,3},{2,4},{3,5},{4,6},{5,7},{6,0},{7,1},{8,10},{9,11},{10,... | collective-permute-start | bytes 196616 | tf_op jit(solution)/shard_map/ppermute | solution.py:501
  38.6 2.0 %collective-permute-start.8 = (f32[128,128]{1,0:T(8,128)S(1)}, f32[128,128]{1,0:T(8,128)S(1)}, u32[]{:S(2)}, u32[]{:S(2)}) collective-permute-start(f32[128,128]{1,0:T(8,128)S(1)} %get-tuple-element.101), channel_id=1, source_target_pairs={{0,4},{1,5},{2,6},{3,7},{4,0},{5,1},{6,2},{7,3},{8,12},{9,13},{10,... | collective-permute-start | bytes 196616 | tf_op jit(solution)/shard_map/ppermute | solution.py:501
  40.5 0.5 collective-permute-start.9
  41.1 2.1 %collective-permute-done.8.refs_2_ = f32[128,128]{1,0:T(8,128)S(1)} collective-permute-done((f32[128,128]{1,0:T(8,128)S(1)}, f32[128,128]{1,0:T(8,128)S(1)}, u32[]{:S(2)}, u32[]{:S(2)}) %collective-permute-start.8) | collective-permute-done | bytes 65568 | tf_op jit(solution)/shard_map/ppermute | solution.py:501
  43.2 0.7 collective-permute-done.9.refs_3_
  44.2 3.5 %collective-permute-start.10 = (f32[4,128,128]{2,1,0:T(8,128)S(1)}, f32[4,128,128]{2,1,0:T(8,128)S(1)}, u32[]{:S(2)}, u32[]{:S(2)}) collective-permute-start(f32[4,128,128]{2,1,0:T(8,128)S(1)} %get-tuple-element.104), channel_id=1, source_target_pairs={{0,1},{1,0},{2,3},{3,2},{4,5},{5,4},{6,7},{7,6},{8,9},{9,8},{10,11... | collective-permute-start | bytes 786440 | tf_op jit(solution)/shard_map/ppermute | solution.py:497
  47.9 2.7 %collective-permute-start.21 = (f32[64,2048]{1,0:T(8,128)S(1)}, f32[64,2048]{1,0:T(8,128)S(1)}, u32[]{:S(2)}, u32[]{:S(2)}) collective-permute-start(f32[64,2048]{1,0:T(8,128)S(1)} %get-tuple-element.127), channel_id=1, source_target_pairs={{0,96},{32,0},{64,32},{96,64},{1,97},{33,1},{65,33},{97,65},{2,98}... | collective-permute-start | bytes 1572872 | tf_op jit(solution)/shard_map/ppermute | solution.py:511
  50.6 1.0 shard_map.142
  51.6 0.7 collective-permute-start.11
  52.3 1.2 %collective-permute-done.11.refs_1_.refs_9_ = f32[4,128,128]{2,1,0:T(8,128)S(1)} collective-permute-done((f32[4,128,128]{2,1,0:T(8,128)S(1)}, f32[4,128,128]{2,1,0:T(8,128)S(1)}, u32[]{:S(2)}, u32[]{:S(2)}) %collective-permute-start.11) | collective-permute-done | bytes 262176 | tf_op jit(solution)/shard_map/ppermute | solution.py:497
  53.4 0.4 shard_map.143
  54.0 2.9 %collective-permute-start.13 = (f32[128,128]{1,0:T(8,128)S(1)}, f32[128,128]{1,0:T(8,128)S(1)}, u32[]{:S(2)}, u32[]{:S(2)}) collective-permute-start(f32[128,128]{1,0:T(8,128)S(1)} %get-tuple-element.118), channel_id=1, source_target_pairs={{0,4},{1,5},{2,6},{3,7},{4,0},{5,1},{6,2},{7,3},{8,12},{9,13},{10,... | collective-permute-start | bytes 196616 | tf_op jit(solution)/shard_map/ppermute | solution.py:501
  57.2 1.3 %collective-permute-done.12.refs_2_ = f32[128,128]{1,0:T(8,128)S(1)} collective-permute-done((f32[128,128]{1,0:T(8,128)S(1)}, f32[128,128]{1,0:T(8,128)S(1)}, u32[]{:S(2)}, u32[]{:S(2)}) %collective-permute-start.12) | collective-permute-done | bytes 65568 | tf_op jit(solution)/shard_map/ppermute | solution.py:501
  58.5 1.3 %collective-permute-done.13.refs_3_ = f32[128,128]{1,0:T(8,128)S(1)} collective-permute-done((f32[128,128]{1,0:T(8,128)S(1)}, f32[128,128]{1,0:T(8,128)S(1)}, u32[]{:S(2)}, u32[]{:S(2)}) %collective-permute-start.13) | collective-permute-done | bytes 65568 | tf_op jit(solution)/shard_map/ppermute | solution.py:501
  60.1 0.7 collective-permute-done.14.refs_4_
  61.2 2.3 %shard_map.144 = (bf16[128,512]{1,0:T(8,128)(2,1)S(1)}, f32[4,128,128]{2,1,0:T(8,128)S(1)}, f32[4,128,128]{2,1,0:T(8,128)S(1)}, f32[4,128,128]{2,1,0:T(8,128)S(1...) custom-call(f32[128,128]{1,0:T(8,128)S(1)} %get-tuple-element.108.refs_0_.refs_1_, ...), custom_call_target="tpu_custom_call" | custom-call | bytes 1 | tf_op jit(solution)/shard_map/pallas_call | solution.py:123
  63.6 0.7 copy-done.14
  64.3 0.7 copy-done.16
  65.0 0.6 shard_map.145
  65.6 2.5 %collective-permute-done.16.refs_3_ = f32[128,256]{1,0:T(8,128)S(1)} collective-permute-done((f32[128,256]{1,0:T(8,128)S(1)}, f32[128,256]{1,0:T(8,128)S(1)}, u32[]{:S(2)}, u32[]{:S(2)}) %collective-permute-start.16) | collective-permute-done | bytes 131104 | tf_op jit(solution)/shard_map/ppermute | solution.py:511
  68.1 2.5 %shard_map.147 = (f32[16,8,2048]{2,1,0:T(8,128)S(1)}, f32[16,8,2048]{2,1,0:T(8,128)S(1)}) custom-call(f32[128,128]{1,0:T(8,128)S(1)} %get-tuple-element.121.refs_0_.refs_1_, f32[128,256]{1,0:T(8,128)S(1)} %get-tuple-element.122.refs_1_, f32[128,256]{1,0:T(8,128)S(1)} %collective-permute-done.15.refs_2_, f32[128,256]{1,0:T(8,128)S(1)} %collective-permute-done.16.refs_3_, ...), custom_call_target="tpu_custom_call" | custom-call | bytes 1 | tf_op jit(solution)/shard_map/pallas_call | solution.py:123
  70.6 1.3 %collective-permute-start.22 = (f32[16,8,2048]{2,1,0:T(8,128)S(1)}, f32[16,8,2048]{2,1,0:T(8,128)S(1)}, u32[]{:S(2)}, u32[]{:S(2)}) collective-permute-start(f32[16,8,2048]{2,1,0:T(8,128)S(1)} %get-tuple-element.129), channel_id=1, source_target_pairs={{0,1},{1,0},{2,3},{3,2},{4,5},{5,4},{6,7},{7,6},{8,9},{9,8},{10,11... | collective-permute-start | bytes 3145736 | tf_op jit(solution)/shard_map/ppermute | solution.py:497
  72.0 1.1 collective-permute-start.23
  73.0 2.6 %collective-permute-start.24 = (f32[128,128]{1,0:T(8,128)S(1)}, f32[128,128]{1,0:T(8,128)S(1)}, u32[]{:S(2)}, u32[]{:S(2)}) collective-permute-start(f32[128,128]{1,0:T(8,128)S(1)} %get-tuple-element.121.refs_0_.refs_1_), channel_id=1, source_target_pairs={{0,16},{1,17},{2,18},{3,19},{4,20},{5,21},{6,22},{7,23},{8,24},{9,... | collective-permute-start | bytes 196616 | tf_op jit(solution)/shard_map/ppermute | solution.py:506
  75.6 0.7 collective-permute-start.25
  76.4 0.4 collective-permute-done.23.refs_2_
  76.8 2.3 %collective-permute-done.24.refs_3_ = f32[128,128]{1,0:T(8,128)S(1)} collective-permute-done((f32[128,128]{1,0:T(8,128)S(1)}, f32[128,128]{1,0:T(8,128)S(1)}, u32[]{:S(2)}, u32[]{:S(2)}) %collective-permute-start.24) | collective-permute-done | bytes 65568 | tf_op jit(solution)/shard_map/ppermute | solution.py:506
  79.2 0.9 shard_map.149
  80.2 2.4 %collective-permute-start.27 = (f32[128,128]{1,0:T(8,128)S(1)}, f32[128,128]{1,0:T(8,128)S(1)}, u32[]{:S(2)}, u32[]{:S(2)}) collective-permute-start(f32[128,128]{1,0:T(8,128)S(1)} %get-tuple-element.136), channel_id=1, source_target_pairs={{0,4},{1,5},{2,6},{3,7},{4,0},{5,1},{6,2},{7,3},{8,12},{9,13},{10,... | collective-permute-start | bytes 196616 | tf_op jit(solution)/shard_map/ppermute | solution.py:501
  82.6 0.5 collective-permute-start.28
  83.1 1.0 collective-permute-start.29
  84.1 1.1 %collective-permute-start.30 = (f32[4,8,2048]{2,1,0:T(8,128)S(1)}, f32[4,8,2048]{2,1,0:T(8,128)S(1)}, u32[]{:S(2)}, u32[]{:S(2)}) collective-permute-start(f32[4,8,2048]{2,1,0:T(8,128)S(1)} %get-tuple-element.140), channel_id=1, source_target_pairs={{0,4},{1,5},{2,6},{3,7},{4,0},{5,1},{6,2},{7,3},{8,12},{9,13},{10,... | collective-permute-start | bytes 786440 | tf_op jit(solution)/shard_map/ppermute | solution.py:501
  85.2 2.1 %collective-permute-start.31 = (f32[4,8,2048]{2,1,0:T(8,128)S(1)}, f32[4,8,2048]{2,1,0:T(8,128)S(1)}, u32[]{:S(2)}, u32[]{:S(2)}) collective-permute-start(f32[4,8,2048]{2,1,0:T(8,128)S(1)} %get-tuple-element.141), channel_id=1, source_target_pairs={{0,6},{1,7},{2,0},{3,1},{4,2},{5,3},{6,4},{7,5},{8,14},{9,15},{10,... | collective-permute-start | bytes 786440 | tf_op jit(solution)/shard_map/ppermute | solution.py:501
  87.3 2.9 %convolution_convert_fusion.refs_1_ = bf16[128,2048]{1,0:T(8,128)(2,1)S(1)} fusion(bf16[128,1024]{1,0:T(8,128)(2,1)S(1)} %get-tuple-element.105.refs_4_, bf16[1024,2048]{1,0:T(8,128)(2,1)} %param.14), kind=kOutput, calls=%fused_computation | convolution fusion | flops 537133056 | bytes 4980736 | tf_op jit(solution)/shard_map/dot_general | solution.py:585
  90.3 3.0 %shard_map.150 = (bf16[128,1024]{1,0:T(8,128)(2,1)}, f32[4,128,128]{2,1,0:T(8,128)S(1)}, f32[4,128,128]{2,1,0:T(8,128)S(1)}, f32[4,128,128]{2,1,0:T(8,128)S(1)},...) custom-call(f32[128,128]{1,0:T(8,128)S(1)} %get-tuple-element.133.refs_0_.refs_2_, ...), custom_call_target="tpu_custom_call" | custom-call | bytes 1 | tf_op jit(solution)/shard_map/pallas_call | solution.py:123
  93.3 0.9 copy-done.18
  94.6 3.1 %collective-permute-start.32 = (f32[4,128,128]{2,1,0:T(8,128)S(1)}, f32[4,128,128]{2,1,0:T(8,128)S(1)}, u32[]{:S(2)}, u32[]{:S(2)}) collective-permute-start(f32[4,128,128]{2,1,0:T(8,128)S(1)} %get-tuple-element.143), channel_id=1, source_target_pairs={{0,1},{1,0},{2,3},{3,2},{4,5},{5,4},{6,7},{7,6},{8,9},{9,8},{10,11... | collective-permute-start | bytes 786440 | tf_op jit(solution)/shard_map/ppermute | solution.py:497
  97.7 0.5 collective-permute-done.31.refs_4_
  98.2 1.3 %collective-permute-start.33 = (f32[8,2048]{1,0:T(8,128)S(1)}, f32[8,2048]{1,0:T(8,128)S(1)}, u32[]{:S(2)}, u32[]{:S(2)}) collective-permute-start(f32[8,2048]{1,0:T(8,128)S(1)} %get-tuple-element.166), channel_id=1, source_target_pairs={{0,8},{1,9},{2,10},{3,11},{4,12},{5,13},{6,14},{7,15},{8,16},{9,17... | collective-permute-start | bytes 196616 | tf_op jit(solution)/shard_map/ppermute | solution.py:506
  99.5 1.6 %collective-permute-start.34 = (f32[8,2048]{1,0:T(8,128)S(1)}, f32[8,2048]{1,0:T(8,128)S(1)}, u32[]{:S(2)}, u32[]{:S(2)}) collective-permute-start(f32[8,2048]{1,0:T(8,128)S(1)} %get-tuple-element.167), channel_id=1, source_target_pairs={{0,16},{1,17},{2,18},{3,19},{4,20},{5,21},{6,22},{7,23},{8,24},{9,... | collective-permute-start | bytes 196616 | tf_op jit(solution)/shard_map/ppermute | solution.py:506
  101.1 0.9 collective-permute-start.35
  102.1 5.5 %shard_map.153 = (bf16[128,1024]{1,0:T(8,128)(2,1)}, bf16[128,1024]{1,0:T(8,128)(2,1)}, f32[8,128]{1,0:T(8,128)}, f32[8,128]{1,0:T(8,128)}) custom-call(f32[8,2048]{1,0:T(8,128)S(1)} %get-tuple-element.142.refs_0_.refs_1_, bf16[128,1024]{1,0:T(8,128)(2,1)S(1)} %bitcast.29, f32[4,128,128]{2,1,0:T(8,128)S(1)} %get-tuple-element.103.refs_0_.refs_1_.refs_2_, ...), custom_call_target="tpu_custom_call" | custom-call | bytes 1 | tf_op jit(solution)/shard_map/pallas_call | solution.py:123
  107.7 0.7 copy-done.22
  108.4 0.6 shard_map.154
  (78 shorter events, 2.6 us)
Async XLA Ops:
  7.1 3.2 %collective-permute-start = (f32[4,128,256]{2,1,0:T(8,128)}, f32[4,128,256]{2,1,0:T(8,128)S(1)}, u32[]{:S(2)}, u32[]{:S(2)}) collective-permute-start(f32[4,128,256]{2,1,0:T(8,128)} %get-tuple-element.89), channel_id=1, source_target_pairs={{0,1},{1,0},{2,3},{3,2},{4,5},{5,4},{6,7},{7,6},{8,9},{9,8},{10,11... | collective-permute-start | bytes 1572872 | tf_op jit(solution)/shard_map/ppermute | solution.py:497
  10.3 1.0 copy-start.1
  11.8 1.0 copy-start.3
  12.8 19.1 %copy-start.8 = (bf16[1,128,1024]{2,1,0:T(8,128)(2,1)S(1)}, bf16[1,128,1024]{2,1,0:T(8,128)(2,1)}, u32[]{:S(2)}) copy-start(bf16[1,128,1024]{2,1,0:T(8,128)(2,1)} %param.9) | copy-start | bytes 786436
  12.8 19.1 %copy-start.13 = (f32[8,128,128]{2,1,0:T(8,128)S(1)}, f32[8,128,128]{2,1,0:T(8,128)}, u32[]{:S(2)}) copy-start(f32[8,128,128]{2,1,0:T(8,128)} %get-tuple-element.96.refs_7_) | copy-start | bytes 1572868
  12.8 19.1 %copy-start.19 = (bf16[1,128,1024]{2,1,0:T(8,128)(2,1)S(1)}, bf16[1,128,1024]{2,1,0:T(8,128)(2,1)}, u32[]{:S(2)}) copy-start(bf16[1,128,1024]{2,1,0:T(8,128)(2,1)} %param.8) | copy-start | bytes 786436
  12.8 19.1 %copy-start.20 = (f32[1,128,8]{1,2,0:T(8,128)S(1)}, f32[1,128,8]{1,2,0:T(8,128)}, u32[]{:S(2)}) copy-start(f32[1,128,8]{1,2,0:T(8,128)} %param.12) | copy-start | bytes 12292
  12.8 19.1 %copy-start.21 = (bf16[1,128,8]{1,2,0:T(8,128)(2,1)S(1)}, bf16[1,128,8]{1,2,0:T(8,128)(2,1)}, u32[]{:S(2)}) copy-start(bf16[1,128,8]{1,2,0:T(8,128)(2,1)} %param.11) | copy-start | bytes 6148
  12.8 19.1 %copy-start.23 = (s32[1,2]{1,0:T(1,128)S(1)}, s32[1,2]{1,0:T(1,128)}, u32[]{:S(2)}) copy-start(s32[1,2]{1,0:T(1,128)} %refs_1_.1) | copy-start | bytes 28
  12.9 34.8 %collective-permute-start.18 = (f32[128,2048]{1,0:T(8,128)S(1)}, f32[128,2048]{1,0:T(8,128)S(1)}, u32[]{:S(2)}, u32[]{:S(2)}) collective-permute-start(f32[128,2048]{1,0:T(8,128)S(1)} %shard_map.137.refs_1_), channel_id=1, source_target_pairs={{0,32},{32,64},{64,96},{96,0},{1,33},{33,65},{65,97},{97,1},{2,34}... | collective-permute-start | bytes 3145736 | tf_op jit(solution)/shard_map/ppermute | solution.py:511
  14.4 33.3 %collective-permute-start.19 = (f32[128,2048]{1,0:T(8,128)S(1)}, f32[128,2048]{1,0:T(8,128)S(1)}, u32[]{:S(2)}, u32[]{:S(2)}) collective-permute-start(f32[128,2048]{1,0:T(8,128)S(1)} %shard_map.137.refs_1_), channel_id=1, source_target_pairs={{0,96},{32,0},{64,32},{96,64},{1,97},{33,1},{65,33},{97,65},{2,98}... | collective-permute-start | bytes 3145736 | tf_op jit(solution)/shard_map/ppermute | solution.py:511
  15.9 9.4 %collective-permute-start.1 = (f32[128,256]{1,0:T(8,128)S(1)}, f32[128,256]{1,0:T(8,128)S(1)}, u32[]{:S(2)}, u32[]{:S(2)}) collective-permute-start(f32[128,256]{1,0:T(8,128)S(1)} %get-tuple-element.91), channel_id=1, source_target_pairs={{0,2},{1,3},{2,4},{3,5},{4,6},{5,7},{6,0},{7,1},{8,10},{9,11},{10,... | collective-permute-start | bytes 393224 | tf_op jit(solution)/shard_map/ppermute | solution.py:501
  17.5 8.9 %collective-permute-start.2 = (f32[128,256]{1,0:T(8,128)S(1)}, f32[128,256]{1,0:T(8,128)S(1)}, u32[]{:S(2)}, u32[]{:S(2)}) collective-permute-start(f32[128,256]{1,0:T(8,128)S(1)} %get-tuple-element.92), channel_id=1, source_target_pairs={{0,4},{1,5},{2,6},{3,7},{4,0},{5,1},{6,2},{7,3},{8,12},{9,13},{10,... | collective-permute-start | bytes 393224 | tf_op jit(solution)/shard_map/ppermute | solution.py:501
  20.9 5.6 %collective-permute-start.3 = (f32[128,256]{1,0:T(8,128)S(1)}, f32[128,256]{1,0:T(8,128)S(1)}, u32[]{:S(2)}, u32[]{:S(2)}) collective-permute-start(f32[128,256]{1,0:T(8,128)S(1)} %get-tuple-element.93), channel_id=1, source_target_pairs={{0,6},{1,7},{2,0},{3,1},{4,2},{5,3},{6,4},{7,5},{8,14},{9,15},{10,... | collective-permute-start | bytes 393224 | tf_op jit(solution)/shard_map/ppermute | solution.py:501
  25.3 18.6 %copy-start.2 = (f32[4,128,256]{2,1,0:T(8,128)S(1)}, f32[4,128,256]{2,1,0:T(8,128)}, u32[]{:S(2)}) copy-start(f32[4,128,256]{2,1,0:T(8,128)} %get-tuple-element.88.refs_0_.refs_4_.refs_2_.refs_6_) | copy-start | bytes 1572868
  27.1 8.6 %collective-permute-start.4 = (f32[128,256]{1,0:T(8,128)S(1)}, f32[128,256]{1,0:T(8,128)S(1)}, u32[]{:S(2)}, u32[]{:S(2)}) collective-permute-start(f32[128,256]{1,0:T(8,128)S(1)} %get-tuple-element.94.refs_0_.refs_1_), channel_id=1, source_target_pairs={{0,8},{1,9},{2,10},{3,11},{4,12},{5,13},{6,14},{7,15},{8,16},{9,17... | collective-permute-start | bytes 393224 | tf_op jit(solution)/shard_map/ppermute | solution.py:506
  28.4 7.3 %collective-permute-start.5 = (f32[128,256]{1,0:T(8,128)S(1)}, f32[128,256]{1,0:T(8,128)S(1)}, u32[]{:S(2)}, u32[]{:S(2)}) collective-permute-start(f32[128,256]{1,0:T(8,128)S(1)} %get-tuple-element.94.refs_0_.refs_1_), channel_id=1, source_target_pairs={{0,16},{1,17},{2,18},{3,19},{4,20},{5,21},{6,22},{7,23},{8,24},{9,... | collective-permute-start | bytes 393224 | tf_op jit(solution)/shard_map/ppermute | solution.py:506
  30.8 5.0 %collective-permute-start.6 = (f32[128,256]{1,0:T(8,128)S(1)}, f32[128,256]{1,0:T(8,128)S(1)}, u32[]{:S(2)}, u32[]{:S(2)}) collective-permute-start(f32[128,256]{1,0:T(8,128)S(1)} %get-tuple-element.94.refs_0_.refs_1_), channel_id=1, source_target_pairs={{0,24},{1,25},{2,26},{3,27},{4,28},{5,29},{6,30},{7,31},{8,0},{9,1... | collective-permute-start | bytes 393224 | tf_op jit(solution)/shard_map/ppermute | solution.py:506
  34.8 0.8 copy-start.9
  36.5 11.2 %copy-start.11 = (f32[4,128,256]{2,1,0:T(8,128)}, f32[4,128,256]{2,1,0:T(8,128)S(1)}, u32[]{:S(2)}) copy-start(f32[4,128,256]{2,1,0:T(8,128)S(1)} %get-tuple-element.131.refs_5_) | copy-start | bytes 1572868
  36.5 24.8 %copy-start = (f32[8,128,256]{2,1,0:T(8,128)S(1)}, f32[8,128,256]{2,1,0:T(8,128)}, u32[]{:S(2)}) copy-start(f32[8,128,256]{2,1,0:T(8,128)} %get-tuple-element.95.refs_6_.refs_3_) | copy-start | bytes 3145732
  36.5 4.5 %collective-permute-start.7 = (f32[128,128]{1,0:T(8,128)S(1)}, f32[128,128]{1,0:T(8,128)S(1)}, u32[]{:S(2)}, u32[]{:S(2)}) collective-permute-start(f32[128,128]{1,0:T(8,128)S(1)} %get-tuple-element.100), channel_id=1, source_target_pairs={{0,2},{1,3},{2,4},{3,5},{4,6},{5,7},{6,0},{7,1},{8,10},{9,11},{10,... | collective-permute-start | bytes 196616 | tf_op jit(solution)/shard_map/ppermute | solution.py:501
  38.6 4.6 %collective-permute-start.8 = (f32[128,128]{1,0:T(8,128)S(1)}, f32[128,128]{1,0:T(8,128)S(1)}, u32[]{:S(2)}, u32[]{:S(2)}) collective-permute-start(f32[128,128]{1,0:T(8,128)S(1)} %get-tuple-element.101), channel_id=1, source_target_pairs={{0,4},{1,5},{2,6},{3,7},{4,0},{5,1},{6,2},{7,3},{8,12},{9,13},{10,... | collective-permute-start | bytes 196616 | tf_op jit(solution)/shard_map/ppermute | solution.py:501
  40.5 3.4 %collective-permute-start.9 = (f32[128,128]{1,0:T(8,128)S(1)}, f32[128,128]{1,0:T(8,128)S(1)}, u32[]{:S(2)}, u32[]{:S(2)}) collective-permute-start(f32[128,128]{1,0:T(8,128)S(1)} %get-tuple-element.102), channel_id=1, source_target_pairs={{0,6},{1,7},{2,0},{3,1},{4,2},{5,3},{6,4},{7,5},{8,14},{9,15},{10,... | collective-permute-start | bytes 196616 | tf_op jit(solution)/shard_map/ppermute | solution.py:501
  44.2 6.3 %collective-permute-start.10 = (f32[4,128,128]{2,1,0:T(8,128)S(1)}, f32[4,128,128]{2,1,0:T(8,128)S(1)}, u32[]{:S(2)}, u32[]{:S(2)}) collective-permute-start(f32[4,128,128]{2,1,0:T(8,128)S(1)} %get-tuple-element.104), channel_id=1, source_target_pairs={{0,1},{1,0},{2,3},{3,2},{4,5},{5,4},{6,7},{7,6},{8,9},{9,8},{10,11... | collective-permute-start | bytes 786440 | tf_op jit(solution)/shard_map/ppermute | solution.py:497
  47.7 15.8 %copy-start.5 = (f32[128,2048]{1,0:T(8,128)}, f32[128,2048]{1,0:T(8,128)S(1)}, u32[]{:S(2)}) copy-start(f32[128,2048]{1,0:T(8,128)S(1)} %collective-permute-done.19.refs_2_.refs_7_) | copy-start | bytes 3145732
  47.8 20.3 %collective-permute-start.20 = (f32[64,2048]{1,0:T(8,128)S(1)}, f32[64,2048]{1,0:T(8,128)S(1)}, u32[]{:S(2)}, u32[]{:S(2)}) collective-permute-start(f32[64,2048]{1,0:T(8,128)S(1)} %get-tuple-element.126), channel_id=1, source_target_pairs={{0,32},{32,64},{64,96},{96,0},{1,33},{33,65},{65,97},{97,1},{2,34}... | collective-permute-start | bytes 1572872 | tf_op jit(solution)/shard_map/ppermute | solution.py:511
  47.9 20.2 %collective-permute-start.21 = (f32[64,2048]{1,0:T(8,128)S(1)}, f32[64,2048]{1,0:T(8,128)S(1)}, u32[]{:S(2)}, u32[]{:S(2)}) collective-permute-start(f32[64,2048]{1,0:T(8,128)S(1)} %get-tuple-element.127), channel_id=1, source_target_pairs={{0,96},{32,0},{64,32},{96,64},{1,97},{33,1},{65,33},{97,65},{2,98}... | collective-permute-start | bytes 1572872 | tf_op jit(solution)/shard_map/ppermute | solution.py:511
  50.6 17.5 %copy-start.4 = (bf16[1,128,2048]{2,1,0:T(8,128)(2,1)S(1)}, bf16[1,128,2048]{2,1,0:T(8,128)(2,1)}, u32[]{:S(2)}) copy-start(bf16[1,128,2048]{2,1,0:T(8,128)(2,1)} %param.15) | copy-start | bytes 1572868
  51.6 1.8 %collective-permute-start.11 = (f32[4,128,128]{2,1,0:T(8,128)S(1)}, f32[4,128,128]{2,1,0:T(8,128)S(1)}, u32[]{:S(2)}, u32[]{:S(2)}) collective-permute-start(f32[4,128,128]{2,1,0:T(8,128)S(1)} %get-tuple-element.107), channel_id=1, source_target_pairs={{0,1},{1,0},{2,3},{3,2},{4,5},{5,4},{6,7},{7,6},{8,9},{9,8},{10,11... | collective-permute-start | bytes 786440 | tf_op jit(solution)/shard_map/ppermute | solution.py:497
  53.8 4.7 %collective-permute-start.12 = (f32[128,128]{1,0:T(8,128)S(1)}, f32[128,128]{1,0:T(8,128)S(1)}, u32[]{:S(2)}, u32[]{:S(2)}) collective-permute-start(f32[128,128]{1,0:T(8,128)S(1)} %get-tuple-element.117), channel_id=1, source_target_pairs={{0,2},{1,3},{2,4},{3,5},{4,6},{5,7},{6,0},{7,1},{8,10},{9,11},{10,... | collective-permute-start | bytes 196616 | tf_op jit(solution)/shard_map/ppermute | solution.py:501
  54.0 5.8 %collective-permute-start.13 = (f32[128,128]{1,0:T(8,128)S(1)}, f32[128,128]{1,0:T(8,128)S(1)}, u32[]{:S(2)}, u32[]{:S(2)}) collective-permute-start(f32[128,128]{1,0:T(8,128)S(1)} %get-tuple-element.118), channel_id=1, source_target_pairs={{0,4},{1,5},{2,6},{3,7},{4,0},{5,1},{6,2},{7,3},{8,12},{9,13},{10,... | collective-permute-start | bytes 196616 | tf_op jit(solution)/shard_map/ppermute | solution.py:501
  56.8 4.0 %collective-permute-start.14 = (f32[128,128]{1,0:T(8,128)S(1)}, f32[128,128]{1,0:T(8,128)S(1)}, u32[]{:S(2)}, u32[]{:S(2)}) collective-permute-start(f32[128,128]{1,0:T(8,128)S(1)} %get-tuple-element.119), channel_id=1, source_target_pairs={{0,6},{1,7},{2,0},{3,1},{4,2},{5,3},{6,4},{7,5},{8,14},{9,15},{10,... | collective-permute-start | bytes 196616 | tf_op jit(solution)/shard_map/ppermute | solution.py:501
  58.5 7.1 %collective-permute-start.15 = (f32[128,256]{1,0:T(8,128)S(1)}, f32[128,256]{1,0:T(8,128)S(1)}, u32[]{:S(2)}, u32[]{:S(2)}) collective-permute-start(f32[128,256]{1,0:T(8,128)S(1)} %get-tuple-element.123), channel_id=1, source_target_pairs={{0,32},{32,64},{64,96},{96,0},{1,33},{33,65},{65,97},{97,1},{2,34}... | collective-permute-start | bytes 393224 | tf_op jit(solution)/shard_map/ppermute | solution.py:511
  59.8 8.3 %collective-permute-start.16 = (f32[128,256]{1,0:T(8,128)S(1)}, f32[128,256]{1,0:T(8,128)S(1)}, u32[]{:S(2)}, u32[]{:S(2)}) collective-permute-start(f32[128,256]{1,0:T(8,128)S(1)} %get-tuple-element.124), channel_id=1, source_target_pairs={{0,64},{32,96},{64,0},{96,32},{1,65},{33,97},{65,1},{97,33},{2,66}... | collective-permute-start | bytes 393224 | tf_op jit(solution)/shard_map/ppermute | solution.py:511
  60.9 7.2 %collective-permute-start.17 = (f32[128,256]{1,0:T(8,128)S(1)}, f32[128,256]{1,0:T(8,128)S(1)}, u32[]{:S(2)}, u32[]{:S(2)}) collective-permute-start(f32[128,256]{1,0:T(8,128)S(1)} %get-tuple-element.125), channel_id=1, source_target_pairs={{0,96},{32,0},{64,32},{96,64},{1,97},{33,1},{65,33},{97,65},{2,98}... | collective-permute-start | bytes 393224 | tf_op jit(solution)/shard_map/ppermute | solution.py:511
  63.6 0.7 copy-start.14
  64.3 0.7 copy-start.16
  65.0 14.2 %copy-start.12 = (f32[4,128,256]{2,1,0:T(8,128)S(1)}, f32[4,128,256]{2,1,0:T(8,128)}, u32[]{:S(2)}) copy-start(f32[4,128,256]{2,1,0:T(8,128)} %copy-done.11) | copy-start | bytes 1572868
  70.6 5.7 %collective-permute-start.22 = (f32[16,8,2048]{2,1,0:T(8,128)S(1)}, f32[16,8,2048]{2,1,0:T(8,128)S(1)}, u32[]{:S(2)}, u32[]{:S(2)}) collective-permute-start(f32[16,8,2048]{2,1,0:T(8,128)S(1)} %get-tuple-element.129), channel_id=1, source_target_pairs={{0,1},{1,0},{2,3},{3,2},{4,5},{5,4},{6,7},{7,6},{8,9},{9,8},{10,11... | collective-permute-start | bytes 3145736 | tf_op jit(solution)/shard_map/ppermute | solution.py:497
  72.0 4.9 %collective-permute-start.23 = (f32[128,128]{1,0:T(8,128)S(1)}, f32[128,128]{1,0:T(8,128)S(1)}, u32[]{:S(2)}, u32[]{:S(2)}) collective-permute-start(f32[128,128]{1,0:T(8,128)S(1)} %get-tuple-element.121.refs_0_.refs_1_), channel_id=1, source_target_pairs={{0,8},{1,9},{2,10},{3,11},{4,12},{5,13},{6,14},{7,15},{8,16},{9,17... | collective-permute-start | bytes 196616 | tf_op jit(solution)/shard_map/ppermute | solution.py:506
  73.0 6.1 %collective-permute-start.24 = (f32[128,128]{1,0:T(8,128)S(1)}, f32[128,128]{1,0:T(8,128)S(1)}, u32[]{:S(2)}, u32[]{:S(2)}) collective-permute-start(f32[128,128]{1,0:T(8,128)S(1)} %get-tuple-element.121.refs_0_.refs_1_), channel_id=1, source_target_pairs={{0,16},{1,17},{2,18},{3,19},{4,20},{5,21},{6,22},{7,23},{8,24},{9,... | collective-permute-start | bytes 196616 | tf_op jit(solution)/shard_map/ppermute | solution.py:506
  75.6 3.6 %collective-permute-start.25 = (f32[128,128]{1,0:T(8,128)S(1)}, f32[128,128]{1,0:T(8,128)S(1)}, u32[]{:S(2)}, u32[]{:S(2)}) collective-permute-start(f32[128,128]{1,0:T(8,128)S(1)} %get-tuple-element.121.refs_0_.refs_1_), channel_id=1, source_target_pairs={{0,24},{1,25},{2,26},{3,27},{4,28},{5,29},{6,30},{7,31},{8,0},{9,1... | collective-permute-start | bytes 196616 | tf_op jit(solution)/shard_map/ppermute | solution.py:506
  80.1 5.1 %collective-permute-start.26 = (f32[128,128]{1,0:T(8,128)S(1)}, f32[128,128]{1,0:T(8,128)S(1)}, u32[]{:S(2)}, u32[]{:S(2)}) collective-permute-start(f32[128,128]{1,0:T(8,128)S(1)} %get-tuple-element.135), channel_id=1, source_target_pairs={{0,2},{1,3},{2,4},{3,5},{4,6},{5,7},{6,0},{7,1},{8,10},{9,11},{10,... | collective-permute-start | bytes 196616 | tf_op jit(solution)/shard_map/ppermute | solution.py:501
  80.2 13.1 %collective-permute-start.27 = (f32[128,128]{1,0:T(8,128)S(1)}, f32[128,128]{1,0:T(8,128)S(1)}, u32[]{:S(2)}, u32[]{:S(2)}) collective-permute-start(f32[128,128]{1,0:T(8,128)S(1)} %get-tuple-element.136), channel_id=1, source_target_pairs={{0,4},{1,5},{2,6},{3,7},{4,0},{5,1},{6,2},{7,3},{8,12},{9,13},{10,... | collective-permute-start | bytes 196616 | tf_op jit(solution)/shard_map/ppermute | solution.py:501
  82.6 10.7 %collective-permute-start.28 = (f32[128,128]{1,0:T(8,128)S(1)}, f32[128,128]{1,0:T(8,128)S(1)}, u32[]{:S(2)}, u32[]{:S(2)}) collective-permute-start(f32[128,128]{1,0:T(8,128)S(1)} %get-tuple-element.137), channel_id=1, source_target_pairs={{0,6},{1,7},{2,0},{3,1},{4,2},{5,3},{6,4},{7,5},{8,14},{9,15},{10,... | collective-permute-start | bytes 196616 | tf_op jit(solution)/shard_map/ppermute | solution.py:501
  83.1 14.5 %collective-permute-start.29 = (f32[4,8,2048]{2,1,0:T(8,128)S(1)}, f32[4,8,2048]{2,1,0:T(8,128)S(1)}, u32[]{:S(2)}, u32[]{:S(2)}) collective-permute-start(f32[4,8,2048]{2,1,0:T(8,128)S(1)} %get-tuple-element.139), channel_id=1, source_target_pairs={{0,2},{1,3},{2,4},{3,5},{4,6},{5,7},{6,0},{7,1},{8,10},{9,11},{10,... | collective-permute-start | bytes 786440 | tf_op jit(solution)/shard_map/ppermute | solution.py:501
  84.1 13.6 %collective-permute-start.30 = (f32[4,8,2048]{2,1,0:T(8,128)S(1)}, f32[4,8,2048]{2,1,0:T(8,128)S(1)}, u32[]{:S(2)}, u32[]{:S(2)}) collective-permute-start(f32[4,8,2048]{2,1,0:T(8,128)S(1)} %get-tuple-element.140), channel_id=1, source_target_pairs={{0,4},{1,5},{2,6},{3,7},{4,0},{5,1},{6,2},{7,3},{8,12},{9,13},{10,... | collective-permute-start | bytes 786440 | tf_op jit(solution)/shard_map/ppermute | solution.py:501
  85.2 12.9 %collective-permute-start.31 = (f32[4,8,2048]{2,1,0:T(8,128)S(1)}, f32[4,8,2048]{2,1,0:T(8,128)S(1)}, u32[]{:S(2)}, u32[]{:S(2)}) collective-permute-start(f32[4,8,2048]{2,1,0:T(8,128)S(1)} %get-tuple-element.141), channel_id=1, source_target_pairs={{0,6},{1,7},{2,0},{3,1},{4,2},{5,3},{6,4},{7,5},{8,14},{9,15},{10,... | collective-permute-start | bytes 786440 | tf_op jit(solution)/shard_map/ppermute | solution.py:501
  90.2 8.0 %copy-start.6 = (bf16[128,2048]{1,0:T(8,128)(2,1)}, bf16[128,2048]{1,0:T(8,128)(2,1)S(1)}, u32[]{:S(2)}) copy-start(bf16[128,2048]{1,0:T(8,128)(2,1)S(1)} %convolution_convert_fusion.refs_1_) | copy-start | bytes 1572868
  90.2 11.8 %copy-start.7 = (bf16[1,128,1024]{2,1,0:T(8,128)(2,1)S(1)}, bf16[1,128,1024]{2,1,0:T(8,128)(2,1)}, u32[]{:S(2)}) copy-start(bf16[1,128,1024]{2,1,0:T(8,128)(2,1)} %param.10) | copy-start | bytes 786436
  90.3 11.8 %copy-start.10 = (f32[8,128,128]{2,1,0:T(8,128)S(1)}, f32[8,128,128]{2,1,0:T(8,128)}, u32[]{:S(2)}) copy-start(f32[8,128,128]{2,1,0:T(8,128)} %copy-done.9) | copy-start | bytes 1572868
  90.3 11.8 %copy-start.15 = (f32[4,128,128]{2,1,0:T(8,128)S(1)}, f32[4,128,128]{2,1,0:T(8,128)}, u32[]{:S(2)}) copy-start(f32[4,128,128]{2,1,0:T(8,128)} %copy-done.14) | copy-start | bytes 786436
  90.3 11.8 %copy-start.17 = (f32[4,128,128]{2,1,0:T(8,128)S(1)}, f32[4,128,128]{2,1,0:T(8,128)}, u32[]{:S(2)}) copy-start(f32[4,128,128]{2,1,0:T(8,128)} %copy-done.16) | copy-start | bytes 786436
  93.3 1.0 copy-start.18
  94.6 7.5 %collective-permute-start.32 = (f32[4,128,128]{2,1,0:T(8,128)S(1)}, f32[4,128,128]{2,1,0:T(8,128)S(1)}, u32[]{:S(2)}, u32[]{:S(2)}) collective-permute-start(f32[4,128,128]{2,1,0:T(8,128)S(1)} %get-tuple-element.143), channel_id=1, source_target_pairs={{0,1},{1,0},{2,3},{3,2},{4,5},{5,4},{6,7},{7,6},{8,9},{9,8},{10,11... | collective-permute-start | bytes 786440 | tf_op jit(solution)/shard_map/ppermute | solution.py:497
  98.2 9.4 %collective-permute-start.33 = (f32[8,2048]{1,0:T(8,128)S(1)}, f32[8,2048]{1,0:T(8,128)S(1)}, u32[]{:S(2)}, u32[]{:S(2)}) collective-permute-start(f32[8,2048]{1,0:T(8,128)S(1)} %get-tuple-element.166), channel_id=1, source_target_pairs={{0,8},{1,9},{2,10},{3,11},{4,12},{5,13},{6,14},{7,15},{8,16},{9,17... | collective-permute-start | bytes 196616 | tf_op jit(solution)/shard_map/ppermute | solution.py:506
  99.5 8.1 %collective-permute-start.34 = (f32[8,2048]{1,0:T(8,128)S(1)}, f32[8,2048]{1,0:T(8,128)S(1)}, u32[]{:S(2)}, u32[]{:S(2)}) collective-permute-start(f32[8,2048]{1,0:T(8,128)S(1)} %get-tuple-element.167), channel_id=1, source_target_pairs={{0,16},{1,17},{2,18},{3,19},{4,20},{5,21},{6,22},{7,23},{8,24},{9,... | collective-permute-start | bytes 196616 | tf_op jit(solution)/shard_map/ppermute | solution.py:506
  101.1 6.5 %collective-permute-start.35 = (f32[8,2048]{1,0:T(8,128)S(1)}, f32[8,2048]{1,0:T(8,128)S(1)}, u32[]{:S(2)}, u32[]{:S(2)}) collective-permute-start(f32[8,2048]{1,0:T(8,128)S(1)} %get-tuple-element.168), channel_id=1, source_target_pairs={{0,24},{1,25},{2,26},{3,27},{4,28},{5,29},{6,30},{7,31},{8,0},{9,1... | collective-permute-start | bytes 196616 | tf_op jit(solution)/shard_map/ppermute | solution.py:506
  107.7 0.7 copy-start.22

commit v4 on v3

--- a/solution.py
+++ b/solution.py
@@ -13,7 +13,7 @@
 EPS = 1e-06
 C = 128
 H = 8
-VMEM_LIMIT = 48 * 1024 * 1024
+VMEM_LIMIT = 24 * 1024 * 1024
 FIRST_LIMIT = 62 * 1024 * 1024
 
 NN = (((1,), (0,)), ((), ()))
@@ -240,9 +240,9 @@
 
 
 def reads_kernel(
-    resets, b_ref, g_ref, q_ref, k_ref, uw_ref, inv_ref,
+    resets, b_ref, g_ref, q_ref, k_ref, uw_ref, inv_ref, mkeep_ref, mrecv_ref,
     read_ref, inside_ref, attn_ref, kk_ref, kn_ref, qn_ref, invt_ref,
-    growth_ref, fading_ref, beta_ref, iq_ref, ik_ref, last_ref,
+    growth_ref, fading_ref, beta_ref, iq_ref, ik_ref, last_ref, early_ref, late_ref,
 ):
     tables = gate_tables(resets, b_ref, g_ref)
     growth_ref[...] = tables[2]
@@ -268,6 +268,11 @@
         invt_ref[h] = inv_ref[h].T
         iq_all = jnp.where(cols == h, iq, iq_all)
         ik_all = jnp.where(cols == h, ik, ik_all)
+    first = place()[3] == 0
+    for j in range(4):
+        a, b = mkeep_ref[j, :, :C], mrecv_ref[j, :, :C]
+        early_ref[j] = jnp.where(first, a, b).T
+        late_ref[j] = jnp.where(first, b, a).T
     iq_ref[...] = iq_all
     ik_ref[...] = ik_all
 
@@ -299,7 +304,7 @@
 
 
 def pair_back_kernel(
-    keep_ref, recv_ref, mkeep_ref, mrecv_ref, n_ref, o0, o1, o2, o3, c0, c1, c2, c3, scratch, wide
+    keep_ref, recv_ref, early_ref, n_ref, o0, o1, o2, o3, c0, c1, c2, c3, scratch, wide
 ):
     for j in range(4):
         wide[j] = n_ref[:, 2 * j * C : 2 * (j + 1) * C].astype(f32)
@@ -310,8 +315,7 @@
         a, b = keep_ref[j], recv_ref[j]
         early = jnp.where(first, a, b)
         late = jnp.where(first, b, a)
-        early_map = jnp.where(first, mkeep_ref[j, :, :C], mrecv_ref[j, :, :C])
-        scratch[j] = early + tn(early_map, late)
+        scratch[j] = early + mm(early_ref[j], late)
     for r, out in enumerate((o0, o1, o2, o3)):
         out[...] = scratch[(place()[2] + r) % 4]
 
@@ -342,16 +346,15 @@
 
 
 def split_pair_back_kernel(
-    s0, s1, s2, s3, mkeep_ref, mrecv_ref, keep_ref, recv_ref, mine_ref, other_ref, scratch
+    s0, s1, s2, s3, late_ref, keep_ref, recv_ref, mine_ref, other_ref, scratch
 ):
     for r, ref in enumerate((s0, s1, s2, s3)):
         scratch[(place()[2] + 4 - r) % 4] = ref[...]
     first = place()[3] == 0
     for j in range(4):
-        late_map = jnp.where(first, mrecv_ref[j, :, :C], mkeep_ref[j, :, :C])
         late = jnp.where(first, recv_ref[j], keep_ref[j])
         end = scratch[j]
-        middle = late + tn(late_map, end)
+        middle = late + mm(late_ref[j], end)
         mine_ref[j] = jnp.where(first, middle, end)
         other_ref[j] = jnp.where(first, end, middle)
 
@@ -401,7 +404,7 @@
     growth_ref, fading_ref, beta_ref, ik_ref, last_ref, *refs
 ):
     early = refs[: 2 * EARLY]
-    dk_ref, dv_ref, db_ref, dg_ref = refs[2 * EARLY :]
+    dk_ref, dv_ref, db_ref, dg_ref, mark_ref = refs[2 * EARLY :]
     first = place()[3] == 0
     rows, cols = iotas()
     row8 = lax.broadcasted_iota(jnp.int32, (H, C), 0)
@@ -442,6 +445,7 @@
         row_all = row_all + jnp.where(cols == h, dtotal, 0.0)
         col_all = col_all + jnp.where(row8 == h, jnp.sum(pairs, axis=0, keepdims=True), 0.0)
     lower = (rows >= cols).astype(bf16)
+    mark_ref[...] = col_all
     db_ref[...] = db_all.T[:H]
     dg_ref[...] = sum(dot(part, lower) for part in split3(row_all.T[:H] - col_all))
 
@@ -470,18 +474,18 @@
 
 def wsum_pair_kernel(keep_ref, recv_ref, o0, o1, o2, o3):
     for r, out in enumerate((o0, o1, o2, o3)):
+        x = (place()[1] + r) % 4
+        for z in range(4):
+            out[z] = keep_ref[4 * x + z] + recv_ref[4 * x + z]
+
+
+def wsum_first_kernel(a0, a1, a2, a3, o0, o1, o2, o3):
+    for r, out in enumerate((o0, o1, o2, o3)):
         z = (place()[2] + r) % 4
-        for x in range(4):
-            out[x] = keep_ref[4 * x + z] + recv_ref[4 * x + z]
-
-
-def wsum_z_kernel(a0, a1, a2, a3, o0, o1, o2, o3):
-    for r, out in enumerate((o0, o1, o2, o3)):
-        x = (place()[1] + r) % 4
-        out[...] = (a0[x] + a1[x]) + (a2[x] + a3[x])
-
-
-def wsum_x_kernel(scale, a0, a1, a2, a3, out):
+        out[...] = (a0[z] + a1[z]) + (a2[z] + a3[z])
+
+
+def wsum_last_kernel(scale, a0, a1, a2, a3, out):
     out[...] = ((a0[...] + a1[...]) + (a2[...] + a3[...])) * scale
 
 
@@ -539,17 +543,17 @@
     parts = call(pair_kernel, [two] * 4, 0, mkeep, mrecv, scratch=hold2)
     own = parts[0]
     parts = around_z(parts)
-    (cot32,) = call(widen_kernel, [((C, 2048), f32)], 0, cot, after=(own,))
+    (cot32,) = call(widen_kernel, [((C, 2048), f32)], 0, cot, after=(mkeep,))
     dn = lax.dot_general(cot, out_weight, NT, preferred_element_type=f32)
     below, above = step_dp(cot32, 1), step_dp(cot32, 3)
     maps, prefix, total = call(
         group_kernel, [four2, ((3, *mat2), f32), two], 0, *parts, after=(dn, cot32)
     )
     parts = around_x([total] * 4)
-    reads, inside, attn, kk, kn, qn, invt, growth, fading, beta, iq, ik, last_decay = call(
+    reads, inside, attn, kk, kn, qn, invt, growth, fading, beta, iq, ik, last_decay, early_t, late_t = call(
         reads_kernel,
-        [all2] + [all1] * 6 + [((C, H), f32)] * 5 + [((1, H), f32)],
-        1, *gates, q, k, uw, inverse, us=3, after=(total,),
+        [all2] + [all1] * 6 + [((C, H), f32)] * 5 + [((1, H), f32), four, four],
+        1, *gates, q, k, uw, inverse, mkeep, mrecv, us=3, after=(total,),
     )
     totals, *parts = call(
         enter_kernel, [four2] + [one] * 4, 0, *parts, prefix, us=1.2, scratch=hold, after=(reads,)
@@ -567,7 +571,7 @@
 
     rrecv = swap_core(rsend)
     parts = call(
-        pair_back_kernel, [one] * 4 + [two] * 4, 0, rkeep, rrecv, mkeep, mrecv, n16,
+        pair_back_kernel, [one] * 4 + [two] * 4, 0, rkeep, rrecv, early_t, n16,
         scratch=hold + hold2,
     )
     chunks = around_dp(parts[4:])
@@ -583,41 +587,41 @@
 
     early0 = early_grads(0, own)
     mixed = lax.dot_general(n16, out_weight, NN, preferred_element_type=f32).astype(bf16)
-    reach, total = call(group_back_kernel, [four, one], 0, *parts, maps, after=(early0[0],))
+    reach, total = call(group_back_kernel, [four, one], 0, *parts, maps)
     parts = around_x([total] * 4)
+    early1 = early_grads(1, total, early0[0])
     wkeep, wsend = call(
         wgrad_kernel,
         [((16, 8, 2048), f32)] * 2,
-        0, *chunks, cot, below, above, lower, upper, us=2.5, after=(total,),
+        0, *chunks, cot, below, above, lower, upper, us=2.5, after=(total, early0[0]),
     )
     wrecv = swap_core(wsend)
     wparts = call(wsum_pair_kernel, [((4, 8, 2048), f32)] * 4, 0, wkeep, wrecv)
     parts = call(
         enter_back_kernel, [one] * 4, 0, *parts, totals, maps, reach, us=1.5, scratch=hold + hold,
+        after=(wparts[0], early1[1], mixed),
+    )
+    parts = around_z(parts)
+    wsent = around_x(wparts)
+    wparts = call(wsum_first_kernel, [((8, 2048), f32)] * 4, 0, *wsent)
+    dmine, dother = call(
+        split_pair_back_kernel, [four] * 2, 0, *parts, late_t, rkeep, rrecv, scratch=hold,
         after=(wparts[0],),
     )
-    early1 = early_grads(1, parts[0], early0[0])
-    parts = around_z(parts)
-    wsent = around_z(wparts)
-    dmine, dother = call(
-        split_pair_back_kernel, [four] * 2, 0, *parts, mkeep, mrecv, rkeep, rrecv, scratch=hold,
-        after=(early1[0], mixed),
-    )
     dother = swap_core(dother)
-    wparts = call(wsum_z_kernel, [((8, 2048), f32)] * 4, 0, *wsent, after=(dmine,))
-    dk, dv, db, dg = call(
+    dk, dv, db, dg, mark = call(
         late_grads_kernel,
-        [wide, wide, ((H, C), f32), ((H, C), f32)],
+        [wide, wide, ((H, C), f32), ((H, C), f32), ((H, C), f32)],
         0, v, mine, other, dmine, dother, inside, kk, kn, invt, growth, fading, beta, ik, last_decay,
         *early0[1:], *early1[1:], us=6, after=(wparts[0],),
     )
-    wparts = around_x(wparts)
+    wparts = around_z(wparts)
     scale = 1.0 / math.sqrt(n_all)
 
     def last(a0, a1, a2, a3, out):
-        wsum_x_kernel(scale, a0, a1, a2, a3, out)
-
-    (weight_grad,) = call(last, [((8, 2048), f32)], 0, *wparts, after=(db,))
+        wsum_last_kernel(scale, a0, a1, a2, a3, out)
+
+    (weight_grad,) = call(last, [((8, 2048), f32)], 0, *wparts, after=(mark,))
     dq = early1[0]
     return (mixed[None], dq[None], dk[None], dv[None], db.T[None], dg.T[None], weight_grad)
 

time: 110 us -> 104 us (0.945)
  local copies, waits for them, and re-layouts: 6 us -> 2.15 us
  waiting for transfers between devices: 16.3 us -> 18.5 us
  Pallas kernels: 28.7 us -> 26.6 us
  matrix products: 6.62 us -> 4.61 us
    unnamed x48 -> x28, local copies, waits for them, and re-layouts: 6 us -> 2.15 us
    ppermute x9, waiting for transfers between devices: 2.97 us -> 5.55 us  [around_x(): lax.ppermute(parts[r], 'seq', seq_perm(r, 0))]
    dot_general x1, matrix products: 2.92 us -> 0.74 us  [local(): lax.dot_general(n16, out_weight, NN, preferred_element_type=f32)]
    pallas_call x20, Pallas kernels: 28.7 us -> 26.6 us  [call(): pl.pallas_call(body, out_shape=[jax.ShapeDtypeStruct(s, d) for s, d in ou...]
    ppermute x5, starting transfers between devices: 10 us -> 12.1 us  [swap_core(): return lax.ppermute(x, 'seq', seq_perm(0, 0, 1))]
    ppermute x5, waiting for transfers between devices: 2.92 us -> 1.17 us  [swap_core(): return lax.ppermute(x, 'seq', seq_perm(0, 0, 1))]
    ppermute x7, waiting for transfers between devices: 2.55 us -> 4.07 us  [step_dp(): return lax.ppermute(x, 'dp', [(i, (i + r) % 4) for i in range(4)])]
  transfers between devices with their start and end apart: 36 -> 36, of which waited for: 13 -> 14; matrix products, arithmetic and copies ran while one was open for 6% -> 4% of each run, Pallas kernels for 16% -> 17%
where the time goes in v4:
time: 104 us
  starting transfers between devices  51.1 us (49%)
  Pallas kernels  26.6 us (26%)
  waiting for transfers between devices  18.5 us (18%)
  matrix products  4.61 us (4%)
  local copies, waits for them, and re-layouts  2.15 us (2%)
    pallas_call x20, Pallas kernels, call(): pl.pallas_call(body, out_shape=[jax.ShapeDtypeStruct(s, d) for s, d in ou...  26.6 us
    ppermute x15, starting transfers between devices, around_z(): lax.ppermute(parts[r], 'seq', seq_perm(0, r))  20.3 us
    ppermute x9, starting transfers between devices, around_x(): lax.ppermute(parts[r], 'seq', seq_perm(r, 0))  12.3 us
    ppermute x5, starting transfers between devices, swap_core(): return lax.ppermute(x, 'seq', seq_perm(0, 0, 1))  12.1 us
    ppermute x15, waiting for transfers between devices, around_z(): lax.ppermute(parts[r], 'seq', seq_perm(0, r))  7.69 us
    ppermute x7, starting transfers between devices, step_dp(): return lax.ppermute(x, 'dp', [(i, (i + r) % 4) for i in range(4)])  6.42 us
    ppermute x9, waiting for transfers between devices, around_x(): lax.ppermute(parts[r], 'seq', seq_perm(r, 0))  5.55 us
    ppermute x7, waiting for transfers between devices, step_dp(): return lax.ppermute(x, 'dp', [(i, (i + r) % 4) for i in range(4)])  4.07 us
  transfers between devices with their start and end apart: 36, of which 14 were waited for; matrix products, arithmetic and copies ran while one was open for 4% of the time, Pallas kernels for 17%

profile of v4, /device:TPU:1, one launch (start us, length us, event | category | flops | bytes accessed | tf_op | source)
XLA Modules:
  0.0 103.9 jit_solution(8108365386531976698)
XLA Ops:
  0.6 6.5 %shard_map.135 = (f32[4,128,256]{2,1,0:T(8,128)}, f32[4,128,256]{2,1,0:T(8,128)}, f32[8,128,128]{2,1,0:T(8,128)}, f32[8,128,256]{2,1,0:T(8,128)}) custom-call(s32[1,2]{1,0:T(1,128)} %refs_1_.1, bf16[8,128]{1,0:T(8,128)(2,1)} %bitcast.35, f32[8,128]{1,0:T(8,128)} %bitcast.33, bf16[128,1024]{1,0:T(8,128)(2,1)} %bitcast.28, bf16[128,1024]{1,0:T(8,128)(2,1)} %bitcast.30), custom_call_target="tpu_custom_call" | custom-call | bytes 1 | tf_op jit(solution)/shard_map/pallas_call | solution.py:123
  7.1 1.5 %collective-permute-start = (f32[4,128,256]{2,1,0:T(8,128)}, f32[4,128,256]{2,1,0:T(8,128)S(1)}, u32[]{:S(2)}, u32[]{:S(2)}) collective-permute-start(f32[4,128,256]{2,1,0:T(8,128)} %get-tuple-element.92), channel_id=1, source_target_pairs={{0,1},{1,0},{2,3},{3,2},{4,5},{5,4},{6,7},{7,6},{8,9},{9,8},{10,11... | collective-permute-start | bytes 1572872 | tf_op jit(solution)/shard_map/ppermute | solution.py:501
  8.6 1.0 copy-done.1
  9.7 1.0 copy-done.3
  10.9 1.5 %collective-permute-start.18 = (f32[128,2048]{1,0:T(8,128)S(1)}, f32[128,2048]{1,0:T(8,128)S(1)}, u32[]{:S(2)}, u32[]{:S(2)}) collective-permute-start(f32[128,2048]{1,0:T(8,128)S(1)} %shard_map.136.refs_1_), channel_id=1, source_target_pairs={{0,32},{32,64},{64,96},{96,0},{1,33},{33,65},{65,97},{97,1},{2,34}... | collective-permute-start | bytes 3145736 | tf_op jit(solution)/shard_map/ppermute | solution.py:515
  12.3 1.5 %collective-permute-start.19 = (f32[128,2048]{1,0:T(8,128)S(1)}, f32[128,2048]{1,0:T(8,128)S(1)}, u32[]{:S(2)}, u32[]{:S(2)}) collective-permute-start(f32[128,2048]{1,0:T(8,128)S(1)} %shard_map.136.refs_1_), channel_id=1, source_target_pairs={{0,96},{32,0},{64,32},{96,64},{1,97},{33,1},{65,33},{97,65},{2,98}... | collective-permute-start | bytes 3145736 | tf_op jit(solution)/shard_map/ppermute | solution.py:515
  13.8 0.4 shard_map.137
  14.2 1.7 %collective-permute-start.1 = (f32[128,256]{1,0:T(8,128)S(1)}, f32[128,256]{1,0:T(8,128)S(1)}, u32[]{:S(2)}, u32[]{:S(2)}) collective-permute-start(f32[128,256]{1,0:T(8,128)S(1)} %get-tuple-element.94), channel_id=1, source_target_pairs={{0,2},{1,3},{2,4},{3,5},{4,6},{5,7},{6,0},{7,1},{8,10},{9,11},{10,... | collective-permute-start | bytes 393224 | tf_op jit(solution)/shard_map/ppermute | solution.py:505
  15.9 3.3 %collective-permute-start.2 = (f32[128,256]{1,0:T(8,128)S(1)}, f32[128,256]{1,0:T(8,128)S(1)}, u32[]{:S(2)}, u32[]{:S(2)}) collective-permute-start(f32[128,256]{1,0:T(8,128)S(1)} %get-tuple-element.95), channel_id=1, source_target_pairs={{0,4},{1,5},{2,6},{3,7},{4,0},{5,1},{6,2},{7,3},{8,12},{9,13},{10,... | collective-permute-start | bytes 393224 | tf_op jit(solution)/shard_map/ppermute | solution.py:505
  19.2 0.7 collective-permute-start.3
  19.9 3.9 %fusion.refs_0_.refs_3_ = f32[128,1024]{1,0:T(8,128)S(1)} fusion(bf16[1024,2048]{1,0:T(8,128)(2,1)} %param.14, bf16[1,128,2048]{2,1,0:T(8,128)(2,1)} %param.15), kind=kOutput, calls=%fused_computation.1 | convolution fusion | flops 536870912 | bytes 5242880 | tf_op jit(solution)/shard_map/dot_general | solution.py:547
  23.8 1.3 %collective-permute-done.2.refs_4_ = f32[128,256]{1,0:T(8,128)S(1)} collective-permute-done((f32[128,256]{1,0:T(8,128)S(1)}, f32[128,256]{1,0:T(8,128)S(1)}, u32[]{:S(2)}, u32[]{:S(2)}) %collective-permute-start.2) | collective-permute-done | bytes 131104 | tf_op jit(solution)/shard_map/ppermute | solution.py:505
  25.2 0.6 shard_map.138
  25.8 1.3 %collective-permute-start.4 = (f32[128,256]{1,0:T(8,128)S(1)}, f32[128,256]{1,0:T(8,128)S(1)}, u32[]{:S(2)}, u32[]{:S(2)}) collective-permute-start(f32[128,256]{1,0:T(8,128)S(1)} %get-tuple-element.97.refs_0_.refs_1_), channel_id=1, source_target_pairs={{0,8},{1,9},{2,10},{3,11},{4,12},{5,13},{6,14},{7,15},{8,16},{9,17... | collective-permute-start | bytes 393224 | tf_op jit(solution)/shard_map/ppermute | solution.py:510
  27.1 2.4 %collective-permute-start.5 = (f32[128,256]{1,0:T(8,128)S(1)}, f32[128,256]{1,0:T(8,128)S(1)}, u32[]{:S(2)}, u32[]{:S(2)}) collective-permute-start(f32[128,256]{1,0:T(8,128)S(1)} %get-tuple-element.97.refs_0_.refs_1_), channel_id=1, source_target_pairs={{0,16},{1,17},{2,18},{3,19},{4,20},{5,21},{6,22},{7,23},{8,24},{9,... | collective-permute-start | bytes 393224 | tf_op jit(solution)/shard_map/ppermute | solution.py:510
  29.5 1.2 %collective-permute-start.6 = (f32[128,256]{1,0:T(8,128)S(1)}, f32[128,256]{1,0:T(8,128)S(1)}, u32[]{:S(2)}, u32[]{:S(2)}) collective-permute-start(f32[128,256]{1,0:T(8,128)S(1)} %get-tuple-element.97.refs_0_.refs_1_), channel_id=1, source_target_pairs={{0,24},{1,25},{2,26},{3,27},{4,28},{5,29},{6,30},{7,31},{8,0},{9,1... | collective-permute-start | bytes 393224 | tf_op jit(solution)/shard_map/ppermute | solution.py:510
  30.8 2.1 %shard_map.139 = (f32[8,128,256]{2,1,0:T(8,128)S(1)}, f32[8,128,128]{2,1,0:T(8,128)S(1)}, f32[8,128,128]{2,1,0:T(8,128)S(1)}, f32[8,128,128]{2,1,0:T(8,128)S(1)}...) custom-call(f32[128,256]{1,0:T(8,128)S(1)} %get-tuple-element.97.ref, ...), custom_call_target="tpu_custom_call" | custom-call | bytes 1 | tf_op jit(solution)/shard_map/pallas_call | solution.py:123
  32.9 1.4 %collective-permute-done.5.refs_3_ = f32[128,256]{1,0:T(8,128)S(1)} collective-permute-done((f32[128,256]{1,0:T(8,128)S(1)}, f32[128,256]{1,0:T(8,128)S(1)}, u32[]{:S(2)}, u32[]{:S(2)}) %collective-permute-start.5) | collective-permute-done | bytes 131104 | tf_op jit(solution)/shard_map/ppermute | solution.py:510
  34.3 0.6 collective-permute-done.6.refs_4_
  34.9 0.6 shard_map.140
  35.5 1.6 %collective-permute-start.7 = (f32[128,128]{1,0:T(8,128)S(1)}, f32[128,128]{1,0:T(8,128)S(1)}, u32[]{:S(2)}, u32[]{:S(2)}) collective-permute-start(f32[128,128]{1,0:T(8,128)S(1)} %get-tuple-element.103), channel_id=1, source_target_pairs={{0,2},{1,3},{2,4},{3,5},{4,6},{5,7},{6,0},{7,1},{8,10},{9,11},{10,... | collective-permute-start | bytes 196616 | tf_op jit(solution)/shard_map/ppermute | solution.py:505
  37.1 2.0 %collective-permute-start.8 = (f32[128,128]{1,0:T(8,128)S(1)}, f32[128,128]{1,0:T(8,128)S(1)}, u32[]{:S(2)}, u32[]{:S(2)}) collective-permute-start(f32[128,128]{1,0:T(8,128)S(1)} %get-tuple-element.104), channel_id=1, source_target_pairs={{0,4},{1,5},{2,6},{3,7},{4,0},{5,1},{6,2},{7,3},{8,12},{9,13},{10,... | collective-permute-start | bytes 196616 | tf_op jit(solution)/shard_map/ppermute | solution.py:505
  39.2 0.4 collective-permute-start.9
  39.6 0.3 collective-permute-done.7.refs_1_
  39.9 1.8 %collective-permute-done.8.refs_2_ = f32[128,128]{1,0:T(8,128)S(1)} collective-permute-done((f32[128,128]{1,0:T(8,128)S(1)}, f32[128,128]{1,0:T(8,128)S(1)}, u32[]{:S(2)}, u32[]{:S(2)}) %collective-permute-start.8) | collective-permute-done | bytes 65568 | tf_op jit(solution)/shard_map/ppermute | solution.py:505
  41.7 0.8 collective-permute-done.9.refs_3_
  42.6 0.3 shard_map.141
  42.8 3.4 %collective-permute-start.10 = (f32[4,128,128]{2,1,0:T(8,128)S(1)}, f32[4,128,128]{2,1,0:T(8,128)S(1)}, u32[]{:S(2)}, u32[]{:S(2)}) collective-permute-start(f32[4,128,128]{2,1,0:T(8,128)S(1)} %get-tuple-element.107), channel_id=1, source_target_pairs={{0,1},{1,0},{2,3},{3,2},{4,5},{5,4},{6,7},{7,6},{8,9},{9,8},{10,11... | collective-permute-start | bytes 786440 | tf_op jit(solution)/shard_map/ppermute | solution.py:501
  46.4 2.7 %collective-permute-start.21 = (f32[64,2048]{1,0:T(8,128)S(1)}, f32[64,2048]{1,0:T(8,128)S(1)}, u32[]{:S(2)}, u32[]{:S(2)}) collective-permute-start(f32[64,2048]{1,0:T(8,128)S(1)} %get-tuple-element.132), channel_id=1, source_target_pairs={{0,96},{32,0},{64,32},{96,64},{1,97},{33,1},{65,33},{97,65},{2,98}... | collective-permute-start | bytes 1572872 | tf_op jit(solution)/shard_map/ppermute | solution.py:515
  49.1 1.0 shard_map.142
  50.1 0.7 collective-permute-start.11
  50.8 1.2 %collective-permute-done.11.refs_1_.refs_7_ = f32[4,128,128]{2,1,0:T(8,128)S(1)} collective-permute-done((f32[4,128,128]{2,1,0:T(8,128)S(1)}, f32[4,128,128]{2,1,0:T(8,128)S(1)}, u32[]{:S(2)}, u32[]{:S(2)}) %collective-permute-start.11) | collective-permute-done | bytes 262176 | tf_op jit(solution)/shard_map/ppermute | solution.py:501
  51.9 0.3 shard_map.143
  52.3 2.8 %collective-permute-start.13 = (f32[128,128]{1,0:T(8,128)S(1)}, f32[128,128]{1,0:T(8,128)S(1)}, u32[]{:S(2)}, u32[]{:S(2)}) collective-permute-start(f32[128,128]{1,0:T(8,128)S(1)} %get-tuple-element.114), channel_id=1, source_target_pairs={{0,4},{1,5},{2,6},{3,7},{4,0},{5,1},{6,2},{7,3},{8,12},{9,13},{10,... | collective-permute-start | bytes 196616 | tf_op jit(solution)/shard_map/ppermute | solution.py:505
  55.1 0.5 collective-permute-start.14
  55.6 1.3 %collective-permute-done.12.refs_1_ = f32[128,128]{1,0:T(8,128)S(1)} collective-permute-done((f32[128,128]{1,0:T(8,128)S(1)}, f32[128,128]{1,0:T(8,128)S(1)}, u32[]{:S(2)}, u32[]{:S(2)}) %collective-permute-start.12) | collective-permute-done | bytes 65568 | tf_op jit(solution)/shard_map/ppermute | solution.py:505
  56.9 1.2 %collective-permute-done.13.refs_2_ = f32[128,128]{1,0:T(8,128)S(1)} collective-permute-done((f32[128,128]{1,0:T(8,128)S(1)}, f32[128,128]{1,0:T(8,128)S(1)}, u32[]{:S(2)}, u32[]{:S(2)}) %collective-permute-start.13) | collective-permute-done | bytes 65568 | tf_op jit(solution)/shard_map/ppermute | solution.py:505
  58.1 0.2 collective-permute-start.16
  58.3 0.9 collective-permute-done.14.refs_3_
  59.2 0.5 collective-permute-start.17
  59.7 2.3 %shard_map.145 = (bf16[128,512]{1,0:T(8,128)(2,1)S(1)}, f32[4,128,128]{2,1,0:T(8,128)S(1)}, f32[4,128,128]{2,1,0:T(8,128)S(1)}, f32[4,128,128]{2,1,0:T(8,128)S(1...) custom-call(f32[128,128]{1,0:T(8,128)S(1)} %get-tuple-element.112.refs_0_, ...), custom_call_target="tpu_custom_call" | custom-call | bytes 1 | tf_op jit(solution)/shard_map/pallas_call | solution.py:123
  62.0 0.6 shard_map.144
  62.7 3.9 %collective-permute-done.16.refs_4_ = f32[128,256]{1,0:T(8,128)S(1)} collective-permute-done((f32[128,256]{1,0:T(8,128)S(1)}, f32[128,256]{1,0:T(8,128)S(1)}, u32[]{:S(2)}, u32[]{:S(2)}) %collective-permute-start.16) | collective-permute-done | bytes 131104 | tf_op jit(solution)/shard_map/ppermute | solution.py:515
  66.6 1.3 %shard_map.148 = (f32[16,8,2048]{2,1,0:T(8,128)S(1)}, f32[16,8,2048]{2,1,0:T(8,128)S(1)}) custom-call(f32[128,128]{1,0:T(8,128)S(1)} %get-tuple-element.117.refs_0_.refs_3_, bf16[128,512]{1,0:T(8,128)(2,1)S(1)} %get-tuple-element.125.refs_11_.refs_1_, f32[128,256]{1,0:T(8,128)S(1)} %get-tuple-element.127.refs_2_, ...), custom_call_target="tpu_custom_call" | custom-call | bytes 1 | tf_op jit(solution)/shard_map/pallas_call | solution.py:123
  67.9 1.3 %collective-permute-start.22 = (f32[16,8,2048]{2,1,0:T(8,128)S(1)}, f32[16,8,2048]{2,1,0:T(8,128)S(1)}, u32[]{:S(2)}, u32[]{:S(2)}) collective-permute-start(f32[16,8,2048]{2,1,0:T(8,128)S(1)} %get-tuple-element.134), channel_id=1, source_target_pairs={{0,1},{1,0},{2,3},{3,2},{4,5},{5,4},{6,7},{7,6},{8,9},{9,8},{10,11... | collective-permute-start | bytes 3145736 | tf_op jit(solution)/shard_map/ppermute | solution.py:501
  69.2 1.0 collective-permute-start.26
  70.3 2.4 %collective-permute-start.27 = (f32[128,128]{1,0:T(8,128)S(1)}, f32[128,128]{1,0:T(8,128)S(1)}, u32[]{:S(2)}, u32[]{:S(2)}) collective-permute-start(f32[128,128]{1,0:T(8,128)S(1)} %get-tuple-element.117.refs_0_.refs_3_), channel_id=1, source_target_pairs={{0,16},{1,17},{2,18},{3,19},{4,20},{5,21},{6,22},{7,23},{8,24},{9,... | collective-permute-start | bytes 196616 | tf_op jit(solution)/shard_map/ppermute | solution.py:510
  72.7 1.0 collective-permute-start.28
  73.8 0.5 collective-permute-start.23
  74.3 0.8 collective-permute-start.24
  75.1 1.7 %collective-permute-start.25 = (f32[4,8,2048]{2,1,0:T(8,128)S(1)}, f32[4,8,2048]{2,1,0:T(8,128)S(1)}, u32[]{:S(2)}, u32[]{:S(2)}) collective-permute-start(f32[4,8,2048]{2,1,0:T(8,128)S(1)} %get-tuple-element.138), channel_id=1, source_target_pairs={{0,24},{1,25},{2,26},{3,27},{4,28},{5,29},{6,30},{7,31},{8,0},{9,1... | collective-permute-start | bytes 786440 | tf_op jit(solution)/shard_map/ppermute | solution.py:510
  76.8 0.7 convolution_convert_fusion.refs_2_
  77.6 3.0 %shard_map.146 = (bf16[128,1024]{1,0:T(8,128)(2,1)}, f32[4,128,128]{2,1,0:T(8,128)S(1)}, f32[4,128,128]{2,1,0:T(8,128)S(1)}, f32[4,128,128]{2,1,0:T(8,128)S(1)},...) custom-call(f32[128,128]{1,0:T(8,128)S(1)} %get-tuple-element.117.refs_0_.refs_3_, ...), custom_call_target="tpu_custom_call" | custom-call | bytes 1 | tf_op jit(solution)/shard_map/pallas_call | solution.py:123
  80.6 0.9 shard_map.151
  81.5 0.3 collective-permute-start.29
  81.8 2.7 %collective-permute-start.30 = (f32[128,128]{1,0:T(8,128)S(1)}, f32[128,128]{1,0:T(8,128)S(1)}, u32[]{:S(2)}, u32[]{:S(2)}) collective-permute-start(f32[128,128]{1,0:T(8,128)S(1)} %get-tuple-element.145), channel_id=1, source_target_pairs={{0,4},{1,5},{2,6},{3,7},{4,0},{5,1},{6,2},{7,3},{8,12},{9,13},{10,... | collective-permute-start | bytes 196616 | tf_op jit(solution)/shard_map/ppermute | solution.py:505
  84.6 0.3 collective-permute-start.31
  84.9 2.3 %collective-permute-done.24.refs_2_ = f32[4,8,2048]{2,1,0:T(8,128)S(1)} collective-permute-done((f32[4,8,2048]{2,1,0:T(8,128)S(1)}, f32[4,8,2048]{2,1,0:T(8,128)S(1)}, u32[]{:S(2)}, u32[]{:S(2)}) %collective-permute-start.24) | collective-permute-done | bytes 262176 | tf_op jit(solution)/shard_map/ppermute | solution.py:510
  87.2 1.2 %collective-permute-done.25.refs_3_ = f32[4,8,2048]{2,1,0:T(8,128)S(1)} collective-permute-done((f32[4,8,2048]{2,1,0:T(8,128)S(1)}, f32[4,8,2048]{2,1,0:T(8,128)S(1)}, u32[]{:S(2)}, u32[]{:S(2)}) %collective-permute-start.25) | collective-permute-done | bytes 262176 | tf_op jit(solution)/shard_map/ppermute | solution.py:510
  88.5 0.3 shard_map.152
  88.8 5.2 %collective-permute-start.32 = (f32[4,128,128]{2,1,0:T(8,128)S(1)}, f32[4,128,128]{2,1,0:T(8,128)S(1)}, u32[]{:S(2)}, u32[]{:S(2)}) collective-permute-start(f32[4,128,128]{2,1,0:T(8,128)S(1)} %get-tuple-element.149), channel_id=1, source_target_pairs={{0,1},{1,0},{2,3},{3,2},{4,5},{5,4},{6,7},{7,6},{8,9},{9,8},{10,11... | collective-permute-start | bytes 786440 | tf_op jit(solution)/shard_map/ppermute | solution.py:501
  94.0 3.8 %collective-permute-start.34 = (f32[8,2048]{1,0:T(8,128)S(1)}, f32[8,2048]{1,0:T(8,128)S(1)}, u32[]{:S(2)}, u32[]{:S(2)}) collective-permute-start(f32[8,2048]{1,0:T(8,128)S(1)} %get-tuple-element.173), channel_id=1, source_target_pairs={{0,4},{1,5},{2,6},{3,7},{4,0},{5,1},{6,2},{7,3},{8,12},{9,13},{10,... | collective-permute-start | bytes 196616 | tf_op jit(solution)/shard_map/ppermute | solution.py:505
  97.8 5.5 %shard_map.153 = (bf16[128,1024]{1,0:T(8,128)(2,1)}, bf16[128,1024]{1,0:T(8,128)(2,1)}, f32[8,128]{1,0:T(8,128)}, f32[8,128]{1,0:T(8,128)}, f32[8,128]{1,0:T(8,128)S(1)}) custom-call(f32[8,2048]{1,0:T(8,128)S(1)} %get-tuple-element.139.refs_0_.refs_1_, bf16[128,1024]{1,0:T(8,128)(2,1)S(1)} %bitcast.31, ...), custom_call_target="tpu_custom_call" | custom-call | bytes 1 | tf_op jit(solution)/shard_map/pallas_call | solution.py:123
  103.3 0.6 shard_map.154
  (58 shorter events, 0.7 us)
Async XLA Ops:
  7.1 6.7 %collective-permute-start = (f32[4,128,256]{2,1,0:T(8,128)}, f32[4,128,256]{2,1,0:T(8,128)S(1)}, u32[]{:S(2)}, u32[]{:S(2)}) collective-permute-start(f32[4,128,256]{2,1,0:T(8,128)} %get-tuple-element.92), channel_id=1, source_target_pairs={{0,1},{1,0},{2,3},{3,2},{4,5},{5,4},{6,7},{7,6},{8,9},{9,8},{10,11... | collective-permute-start | bytes 1572872 | tf_op jit(solution)/shard_map/ppermute | solution.py:501
  8.6 1.0 %copy-start.1 = (f32[4,128,256]{2,1,0:T(8,128)S(1)}, f32[4,128,256]{2,1,0:T(8,128)}, u32[]{:S(2)}) copy-start(f32[4,128,256]{2,1,0:T(8,128)} %get-tuple-element.91.refs_0_.refs_8_.refs_4_) | copy-start | bytes 1572868
  9.7 1.0 %copy-start.3 = (bf16[1,128,2048]{2,1,0:T(8,128)(2,1)S(1)}, bf16[1,128,2048]{2,1,0:T(8,128)(2,1)}, u32[]{:S(2)}) copy-start(bf16[1,128,2048]{2,1,0:T(8,128)(2,1)} %param.15) | copy-start | bytes 1572868
  10.8 19.9 %copy-start = (f32[8,128,256]{2,1,0:T(8,128)S(1)}, f32[8,128,256]{2,1,0:T(8,128)}, u32[]{:S(2)}) copy-start(f32[8,128,256]{2,1,0:T(8,128)} %get-tuple-element.98.refs_6_.refs_3_) | copy-start | bytes 3145732
  10.8 19.9 %copy-start.2 = (f32[4,128,256]{2,1,0:T(8,128)S(1)}, f32[4,128,256]{2,1,0:T(8,128)}, u32[]{:S(2)}) copy-start(f32[4,128,256]{2,1,0:T(8,128)} %get-tuple-element.91.refs_0_.refs_8_.refs_4_) | copy-start | bytes 1572868
  10.8 19.9 %copy-start.6 = (bf16[1,128,1024]{2,1,0:T(8,128)(2,1)S(1)}, bf16[1,128,1024]{2,1,0:T(8,128)(2,1)}, u32[]{:S(2)}) copy-start(bf16[1,128,1024]{2,1,0:T(8,128)(2,1)} %param.9) | copy-start | bytes 786436
  10.8 19.9 %copy-start.8 = (f32[8,128,128]{2,1,0:T(8,128)S(1)}, f32[8,128,128]{2,1,0:T(8,128)}, u32[]{:S(2)}) copy-start(f32[8,128,128]{2,1,0:T(8,128)} %get-tuple-element.99.refs_7_) | copy-start | bytes 1572868
  10.8 19.9 %copy-start.9 = (bf16[1,128,1024]{2,1,0:T(8,128)(2,1)S(1)}, bf16[1,128,1024]{2,1,0:T(8,128)(2,1)}, u32[]{:S(2)}) copy-start(bf16[1,128,1024]{2,1,0:T(8,128)(2,1)} %param.8) | copy-start | bytes 786436
  10.8 19.9 %copy-start.10 = (f32[1,128,8]{1,2,0:T(8,128)S(1)}, f32[1,128,8]{1,2,0:T(8,128)}, u32[]{:S(2)}) copy-start(f32[1,128,8]{1,2,0:T(8,128)} %param.12) | copy-start | bytes 12292
  10.8 19.9 %copy-start.11 = (bf16[1,128,8]{1,2,0:T(8,128)(2,1)S(1)}, bf16[1,128,8]{1,2,0:T(8,128)(2,1)}, u32[]{:S(2)}) copy-start(bf16[1,128,8]{1,2,0:T(8,128)(2,1)} %param.11) | copy-start | bytes 6148
  10.8 19.9 %copy-start.12 = (s32[1,2]{1,0:T(1,128)S(1)}, s32[1,2]{1,0:T(1,128)}, u32[]{:S(2)}) copy-start(s32[1,2]{1,0:T(1,128)} %refs_1_.1) | copy-start | bytes 28
  10.9 35.4 %collective-permute-start.18 = (f32[128,2048]{1,0:T(8,128)S(1)}, f32[128,2048]{1,0:T(8,128)S(1)}, u32[]{:S(2)}, u32[]{:S(2)}) collective-permute-start(f32[128,2048]{1,0:T(8,128)S(1)} %shard_map.136.refs_1_), channel_id=1, source_target_pairs={{0,32},{32,64},{64,96},{96,0},{1,33},{33,65},{65,97},{97,1},{2,34}... | collective-permute-start | bytes 3145736 | tf_op jit(solution)/shard_map/ppermute | solution.py:515
  12.3 34.0 %collective-permute-start.19 = (f32[128,2048]{1,0:T(8,128)S(1)}, f32[128,2048]{1,0:T(8,128)S(1)}, u32[]{:S(2)}, u32[]{:S(2)}) collective-permute-start(f32[128,2048]{1,0:T(8,128)S(1)} %shard_map.136.refs_1_), channel_id=1, source_target_pairs={{0,96},{32,0},{64,32},{96,64},{1,97},{33,1},{65,33},{97,65},{2,98}... | collective-permute-start | bytes 3145736 | tf_op jit(solution)/shard_map/ppermute | solution.py:515
  14.2 9.6 %collective-permute-start.1 = (f32[128,256]{1,0:T(8,128)S(1)}, f32[128,256]{1,0:T(8,128)S(1)}, u32[]{:S(2)}, u32[]{:S(2)}) collective-permute-start(f32[128,256]{1,0:T(8,128)S(1)} %get-tuple-element.94), channel_id=1, source_target_pairs={{0,2},{1,3},{2,4},{3,5},{4,6},{5,7},{6,0},{7,1},{8,10},{9,11},{10,... | collective-permute-start | bytes 393224 | tf_op jit(solution)/shard_map/ppermute | solution.py:505
  15.9 9.3 %collective-permute-start.2 = (f32[128,256]{1,0:T(8,128)S(1)}, f32[128,256]{1,0:T(8,128)S(1)}, u32[]{:S(2)}, u32[]{:S(2)}) collective-permute-start(f32[128,256]{1,0:T(8,128)S(1)} %get-tuple-element.95), channel_id=1, source_target_pairs={{0,4},{1,5},{2,6},{3,7},{4,0},{5,1},{6,2},{7,3},{8,12},{9,13},{10,... | collective-permute-start | bytes 393224 | tf_op jit(solution)/shard_map/ppermute | solution.py:505
  19.2 6.0 %collective-permute-start.3 = (f32[128,256]{1,0:T(8,128)S(1)}, f32[128,256]{1,0:T(8,128)S(1)}, u32[]{:S(2)}, u32[]{:S(2)}) collective-permute-start(f32[128,256]{1,0:T(8,128)S(1)} %get-tuple-element.96), channel_id=1, source_target_pairs={{0,6},{1,7},{2,0},{3,1},{4,2},{5,3},{6,4},{7,5},{8,14},{9,15},{10,... | collective-permute-start | bytes 393224 | tf_op jit(solution)/shard_map/ppermute | solution.py:505
  25.8 7.1 %collective-permute-start.4 = (f32[128,256]{1,0:T(8,128)S(1)}, f32[128,256]{1,0:T(8,128)S(1)}, u32[]{:S(2)}, u32[]{:S(2)}) collective-permute-start(f32[128,256]{1,0:T(8,128)S(1)} %get-tuple-element.97.refs_0_.refs_1_), channel_id=1, source_target_pairs={{0,8},{1,9},{2,10},{3,11},{4,12},{5,13},{6,14},{7,15},{8,16},{9,17... | collective-permute-start | bytes 393224 | tf_op jit(solution)/shard_map/ppermute | solution.py:510
  27.1 7.2 %collective-permute-start.5 = (f32[128,256]{1,0:T(8,128)S(1)}, f32[128,256]{1,0:T(8,128)S(1)}, u32[]{:S(2)}, u32[]{:S(2)}) collective-permute-start(f32[128,256]{1,0:T(8,128)S(1)} %get-tuple-element.97.refs_0_.refs_1_), channel_id=1, source_target_pairs={{0,16},{1,17},{2,18},{3,19},{4,20},{5,21},{6,22},{7,23},{8,24},{9,... | collective-permute-start | bytes 393224 | tf_op jit(solution)/shard_map/ppermute | solution.py:510
  29.5 5.4 %collective-permute-start.6 = (f32[128,256]{1,0:T(8,128)S(1)}, f32[128,256]{1,0:T(8,128)S(1)}, u32[]{:S(2)}, u32[]{:S(2)}) collective-permute-start(f32[128,256]{1,0:T(8,128)S(1)} %get-tuple-element.97.refs_0_.refs_1_), channel_id=1, source_target_pairs={{0,24},{1,25},{2,26},{3,27},{4,28},{5,29},{6,30},{7,31},{8,0},{9,1... | collective-permute-start | bytes 393224 | tf_op jit(solution)/shard_map/ppermute | solution.py:510
  35.5 4.4 %collective-permute-start.7 = (f32[128,128]{1,0:T(8,128)S(1)}, f32[128,128]{1,0:T(8,128)S(1)}, u32[]{:S(2)}, u32[]{:S(2)}) collective-permute-start(f32[128,128]{1,0:T(8,128)S(1)} %get-tuple-element.103), channel_id=1, source_target_pairs={{0,2},{1,3},{2,4},{3,5},{4,6},{5,7},{6,0},{7,1},{8,10},{9,11},{10,... | collective-permute-start | bytes 196616 | tf_op jit(solution)/shard_map/ppermute | solution.py:505
  37.1 4.6 %collective-permute-start.8 = (f32[128,128]{1,0:T(8,128)S(1)}, f32[128,128]{1,0:T(8,128)S(1)}, u32[]{:S(2)}, u32[]{:S(2)}) collective-permute-start(f32[128,128]{1,0:T(8,128)S(1)} %get-tuple-element.104), channel_id=1, source_target_pairs={{0,4},{1,5},{2,6},{3,7},{4,0},{5,1},{6,2},{7,3},{8,12},{9,13},{10,... | collective-permute-start | bytes 196616 | tf_op jit(solution)/shard_map/ppermute | solution.py:505
  39.2 3.4 %collective-permute-start.9 = (f32[128,128]{1,0:T(8,128)S(1)}, f32[128,128]{1,0:T(8,128)S(1)}, u32[]{:S(2)}, u32[]{:S(2)}) collective-permute-start(f32[128,128]{1,0:T(8,128)S(1)} %get-tuple-element.105), channel_id=1, source_target_pairs={{0,6},{1,7},{2,0},{3,1},{4,2},{5,3},{6,4},{7,5},{8,14},{9,15},{10,... | collective-permute-start | bytes 196616 | tf_op jit(solution)/shard_map/ppermute | solution.py:505
  42.8 6.3 %collective-permute-start.10 = (f32[4,128,128]{2,1,0:T(8,128)S(1)}, f32[4,128,128]{2,1,0:T(8,128)S(1)}, u32[]{:S(2)}, u32[]{:S(2)}) collective-permute-start(f32[4,128,128]{2,1,0:T(8,128)S(1)} %get-tuple-element.107), channel_id=1, source_target_pairs={{0,1},{1,0},{2,3},{3,2},{4,5},{5,4},{6,7},{7,6},{8,9},{9,8},{10,11... | collective-permute-start | bytes 786440 | tf_op jit(solution)/shard_map/ppermute | solution.py:501
  46.3 20.3 %copy-start.4 = (bf16[1,128,2048]{2,1,0:T(8,128)(2,1)S(1)}, bf16[1,128,2048]{2,1,0:T(8,128)(2,1)}, u32[]{:S(2)}) copy-start(bf16[1,128,2048]{2,1,0:T(8,128)(2,1)} %param.15) | copy-start | bytes 1572868
  46.4 20.3 %collective-permute-start.20 = (f32[64,2048]{1,0:T(8,128)S(1)}, f32[64,2048]{1,0:T(8,128)S(1)}, u32[]{:S(2)}, u32[]{:S(2)}) collective-permute-start(f32[64,2048]{1,0:T(8,128)S(1)} %get-tuple-element.131), channel_id=1, source_target_pairs={{0,32},{32,64},{64,96},{96,0},{1,33},{33,65},{65,97},{97,1},{2,34}... | collective-permute-start | bytes 1572872 | tf_op jit(solution)/shard_map/ppermute | solution.py:515
  46.4 20.2 %collective-permute-start.21 = (f32[64,2048]{1,0:T(8,128)S(1)}, f32[64,2048]{1,0:T(8,128)S(1)}, u32[]{:S(2)}, u32[]{:S(2)}) collective-permute-start(f32[64,2048]{1,0:T(8,128)S(1)} %get-tuple-element.132), channel_id=1, source_target_pairs={{0,96},{32,0},{64,32},{96,64},{1,97},{33,1},{65,33},{97,65},{2,98}... | collective-permute-start | bytes 1572872 | tf_op jit(solution)/shard_map/ppermute | solution.py:515
  50.1 1.8 %collective-permute-start.11 = (f32[4,128,128]{2,1,0:T(8,128)S(1)}, f32[4,128,128]{2,1,0:T(8,128)S(1)}, u32[]{:S(2)}, u32[]{:S(2)}) collective-permute-start(f32[4,128,128]{2,1,0:T(8,128)S(1)} %get-tuple-element.110), channel_id=1, source_target_pairs={{0,1},{1,0},{2,3},{3,2},{4,5},{5,4},{6,7},{7,6},{8,9},{9,8},{10,11... | collective-permute-start | bytes 786440 | tf_op jit(solution)/shard_map/ppermute | solution.py:501
  52.2 4.7 %collective-permute-start.12 = (f32[128,128]{1,0:T(8,128)S(1)}, f32[128,128]{1,0:T(8,128)S(1)}, u32[]{:S(2)}, u32[]{:S(2)}) collective-permute-start(f32[128,128]{1,0:T(8,128)S(1)} %get-tuple-element.113), channel_id=1, source_target_pairs={{0,2},{1,3},{2,4},{3,5},{4,6},{5,7},{6,0},{7,1},{8,10},{9,11},{10,... | collective-permute-start | bytes 196616 | tf_op jit(solution)/shard_map/ppermute | solution.py:505
  52.3 5.8 %collective-permute-start.13 = (f32[128,128]{1,0:T(8,128)S(1)}, f32[128,128]{1,0:T(8,128)S(1)}, u32[]{:S(2)}, u32[]{:S(2)}) collective-permute-start(f32[128,128]{1,0:T(8,128)S(1)} %get-tuple-element.114), channel_id=1, source_target_pairs={{0,4},{1,5},{2,6},{3,7},{4,0},{5,1},{6,2},{7,3},{8,12},{9,13},{10,... | collective-permute-start | bytes 196616 | tf_op jit(solution)/shard_map/ppermute | solution.py:505
  55.1 4.0 %collective-permute-start.14 = (f32[128,128]{1,0:T(8,128)S(1)}, f32[128,128]{1,0:T(8,128)S(1)}, u32[]{:S(2)}, u32[]{:S(2)}) collective-permute-start(f32[128,128]{1,0:T(8,128)S(1)} %get-tuple-element.115), channel_id=1, source_target_pairs={{0,6},{1,7},{2,0},{3,1},{4,2},{5,3},{6,4},{7,5},{8,14},{9,15},{10,... | collective-permute-start | bytes 196616 | tf_op jit(solution)/shard_map/ppermute | solution.py:505
  56.9 5.8 %collective-permute-start.15 = (f32[128,256]{1,0:T(8,128)S(1)}, f32[128,256]{1,0:T(8,128)S(1)}, u32[]{:S(2)}, u32[]{:S(2)}) collective-permute-start(f32[128,256]{1,0:T(8,128)S(1)} %get-tuple-element.128), channel_id=1, source_target_pairs={{0,32},{32,64},{64,96},{96,0},{1,33},{33,65},{65,97},{97,1},{2,34}... | collective-permute-start | bytes 393224 | tf_op jit(solution)/shard_map/ppermute | solution.py:515
  58.1 8.5 %collective-permute-start.16 = (f32[128,256]{1,0:T(8,128)S(1)}, f32[128,256]{1,0:T(8,128)S(1)}, u32[]{:S(2)}, u32[]{:S(2)}) collective-permute-start(f32[128,256]{1,0:T(8,128)S(1)} %get-tuple-element.129), channel_id=1, source_target_pairs={{0,64},{32,96},{64,0},{96,32},{1,65},{33,97},{65,1},{97,33},{2,66}... | collective-permute-start | bytes 393224 | tf_op jit(solution)/shard_map/ppermute | solution.py:515
  59.2 7.4 %collective-permute-start.17 = (f32[128,256]{1,0:T(8,128)S(1)}, f32[128,256]{1,0:T(8,128)S(1)}, u32[]{:S(2)}, u32[]{:S(2)}) collective-permute-start(f32[128,256]{1,0:T(8,128)S(1)} %get-tuple-element.130), channel_id=1, source_target_pairs={{0,96},{32,0},{64,32},{96,64},{1,97},{33,1},{65,33},{97,65},{2,98}... | collective-permute-start | bytes 393224 | tf_op jit(solution)/shard_map/ppermute | solution.py:515
  62.0 14.8 %copy-start.13 = (bf16[1024,2048]{1,0:T(8,128)(2,1)S(1)}, bf16[1024,2048]{1,0:T(8,128)(2,1)}, u32[]{:S(2)}) copy-start(bf16[1024,2048]{1,0:T(8,128)(2,1)} %param.14) | copy-start | bytes 12582916
  67.9 5.7 %collective-permute-start.22 = (f32[16,8,2048]{2,1,0:T(8,128)S(1)}, f32[16,8,2048]{2,1,0:T(8,128)S(1)}, u32[]{:S(2)}, u32[]{:S(2)}) collective-permute-start(f32[16,8,2048]{2,1,0:T(8,128)S(1)} %get-tuple-element.134), channel_id=1, source_target_pairs={{0,1},{1,0},{2,3},{3,2},{4,5},{5,4},{6,7},{7,6},{8,9},{9,8},{10,11... | collective-permute-start | bytes 3145736 | tf_op jit(solution)/shard_map/ppermute | solution.py:501
  69.2 5.9 %collective-permute-start.26 = (f32[128,128]{1,0:T(8,128)S(1)}, f32[128,128]{1,0:T(8,128)S(1)}, u32[]{:S(2)}, u32[]{:S(2)}) collective-permute-start(f32[128,128]{1,0:T(8,128)S(1)} %get-tuple-element.117.refs_0_.refs_3_), channel_id=1, source_target_pairs={{0,8},{1,9},{2,10},{3,11},{4,12},{5,13},{6,14},{7,15},{8,16},{9,17... | collective-permute-start | bytes 196616 | tf_op jit(solution)/shard_map/ppermute | solution.py:510
  70.3 10.3 %collective-permute-start.27 = (f32[128,128]{1,0:T(8,128)S(1)}, f32[128,128]{1,0:T(8,128)S(1)}, u32[]{:S(2)}, u32[]{:S(2)}) collective-permute-start(f32[128,128]{1,0:T(8,128)S(1)} %get-tuple-element.117.refs_0_.refs_3_), channel_id=1, source_target_pairs={{0,16},{1,17},{2,18},{3,19},{4,20},{5,21},{6,22},{7,23},{8,24},{9,... | collective-permute-start | bytes 196616 | tf_op jit(solution)/shard_map/ppermute | solution.py:510
  72.7 7.9 %collective-permute-start.28 = (f32[128,128]{1,0:T(8,128)S(1)}, f32[128,128]{1,0:T(8,128)S(1)}, u32[]{:S(2)}, u32[]{:S(2)}) collective-permute-start(f32[128,128]{1,0:T(8,128)S(1)} %get-tuple-element.117.refs_0_.refs_3_), channel_id=1, source_target_pairs={{0,24},{1,25},{2,26},{3,27},{4,28},{5,29},{6,30},{7,31},{8,0},{9,1... | collective-permute-start | bytes 196616 | tf_op jit(solution)/shard_map/ppermute | solution.py:510
  73.8 10.8 %collective-permute-start.23 = (f32[4,8,2048]{2,1,0:T(8,128)S(1)}, f32[4,8,2048]{2,1,0:T(8,128)S(1)}, u32[]{:S(2)}, u32[]{:S(2)}) collective-permute-start(f32[4,8,2048]{2,1,0:T(8,128)S(1)} %get-tuple-element.136), channel_id=1, source_target_pairs={{0,8},{1,9},{2,10},{3,11},{4,12},{5,13},{6,14},{7,15},{8,16},{9,17... | collective-permute-start | bytes 786440 | tf_op jit(solution)/shard_map/ppermute | solution.py:510
  74.3 12.9 %collective-permute-start.24 = (f32[4,8,2048]{2,1,0:T(8,128)S(1)}, f32[4,8,2048]{2,1,0:T(8,128)S(1)}, u32[]{:S(2)}, u32[]{:S(2)}) collective-permute-start(f32[4,8,2048]{2,1,0:T(8,128)S(1)} %get-tuple-element.137), channel_id=1, source_target_pairs={{0,16},{1,17},{2,18},{3,19},{4,20},{5,21},{6,22},{7,23},{8,24},{9,... | collective-permute-start | bytes 786440 | tf_op jit(solution)/shard_map/ppermute | solution.py:510
  75.1 13.3 %collective-permute-start.25 = (f32[4,8,2048]{2,1,0:T(8,128)S(1)}, f32[4,8,2048]{2,1,0:T(8,128)S(1)}, u32[]{:S(2)}, u32[]{:S(2)}) collective-permute-start(f32[4,8,2048]{2,1,0:T(8,128)S(1)} %get-tuple-element.138), channel_id=1, source_target_pairs={{0,24},{1,25},{2,26},{3,27},{4,28},{5,29},{6,30},{7,31},{8,0},{9,1... | collective-permute-start | bytes 786440 | tf_op jit(solution)/shard_map/ppermute | solution.py:510
  77.6 11.3 %copy-start.5 = (bf16[128,2048]{1,0:T(8,128)(2,1)}, bf16[128,2048]{1,0:T(8,128)(2,1)S(1)}, u32[]{:S(2)}) copy-start(bf16[128,2048]{1,0:T(8,128)(2,1)S(1)} %convolution_convert_fusion.refs_2_) | copy-start | bytes 1572868
  77.6 20.2 %copy-start.7 = (bf16[1,128,1024]{2,1,0:T(8,128)(2,1)S(1)}, bf16[1,128,1024]{2,1,0:T(8,128)(2,1)}, u32[]{:S(2)}) copy-start(bf16[1,128,1024]{2,1,0:T(8,128)(2,1)} %param.10) | copy-start | bytes 786436
  81.5 7.0 %collective-permute-start.29 = (f32[128,128]{1,0:T(8,128)S(1)}, f32[128,128]{1,0:T(8,128)S(1)}, u32[]{:S(2)}, u32[]{:S(2)}) collective-permute-start(f32[128,128]{1,0:T(8,128)S(1)} %get-tuple-element.144), channel_id=1, source_target_pairs={{0,2},{1,3},{2,4},{3,5},{4,6},{5,7},{6,0},{7,1},{8,10},{9,11},{10,... | collective-permute-start | bytes 196616 | tf_op jit(solution)/shard_map/ppermute | solution.py:505
  81.8 6.7 %collective-permute-start.30 = (f32[128,128]{1,0:T(8,128)S(1)}, f32[128,128]{1,0:T(8,128)S(1)}, u32[]{:S(2)}, u32[]{:S(2)}) collective-permute-start(f32[128,128]{1,0:T(8,128)S(1)} %get-tuple-element.145), channel_id=1, source_target_pairs={{0,4},{1,5},{2,6},{3,7},{4,0},{5,1},{6,2},{7,3},{8,12},{9,13},{10,... | collective-permute-start | bytes 196616 | tf_op jit(solution)/shard_map/ppermute | solution.py:505
  84.6 4.0 %collective-permute-start.31 = (f32[128,128]{1,0:T(8,128)S(1)}, f32[128,128]{1,0:T(8,128)S(1)}, u32[]{:S(2)}, u32[]{:S(2)}) collective-permute-start(f32[128,128]{1,0:T(8,128)S(1)} %get-tuple-element.146), channel_id=1, source_target_pairs={{0,6},{1,7},{2,0},{3,1},{4,2},{5,3},{6,4},{7,5},{8,14},{9,15},{10,... | collective-permute-start | bytes 196616 | tf_op jit(solution)/shard_map/ppermute | solution.py:505
  88.8 9.0 %collective-permute-start.32 = (f32[4,128,128]{2,1,0:T(8,128)S(1)}, f32[4,128,128]{2,1,0:T(8,128)S(1)}, u32[]{:S(2)}, u32[]{:S(2)}) collective-permute-start(f32[4,128,128]{2,1,0:T(8,128)S(1)} %get-tuple-element.149), channel_id=1, source_target_pairs={{0,1},{1,0},{2,3},{3,2},{4,5},{5,4},{6,7},{7,6},{8,9},{9,8},{10,11... | collective-permute-start | bytes 786440 | tf_op jit(solution)/shard_map/ppermute | solution.py:501
  94.0 9.3 %collective-permute-start.33 = (f32[8,2048]{1,0:T(8,128)S(1)}, f32[8,2048]{1,0:T(8,128)S(1)}, u32[]{:S(2)}, u32[]{:S(2)}) collective-permute-start(f32[8,2048]{1,0:T(8,128)S(1)} %get-tuple-element.172), channel_id=1, source_target_pairs={{0,2},{1,3},{2,4},{3,5},{4,6},{5,7},{6,0},{7,1},{8,10},{9,11},{10,... | collective-permute-start | bytes 196616 | tf_op jit(solution)/shard_map/ppermute | solution.py:505
  94.0 9.3 %collective-permute-start.34 = (f32[8,2048]{1,0:T(8,128)S(1)}, f32[8,2048]{1,0:T(8,128)S(1)}, u32[]{:S(2)}, u32[]{:S(2)}) collective-permute-start(f32[8,2048]{1,0:T(8,128)S(1)} %get-tuple-element.173), channel_id=1, source_target_pairs={{0,4},{1,5},{2,6},{3,7},{4,0},{5,1},{6,2},{7,3},{8,12},{9,13},{10,... | collective-permute-start | bytes 196616 | tf_op jit(solution)/shard_map/ppermute | solution.py:505
  97.8 5.5 %collective-permute-start.35 = (f32[8,2048]{1,0:T(8,128)S(1)}, f32[8,2048]{1,0:T(8,128)S(1)}, u32[]{:S(2)}, u32[]{:S(2)}) collective-permute-start(f32[8,2048]{1,0:T(8,128)S(1)} %get-tuple-element.174), channel_id=1, source_target_pairs={{0,6},{1,7},{2,0},{3,1},{4,2},{5,3},{6,4},{7,5},{8,14},{9,15},{10,... | collective-permute-start | bytes 196616 | tf_op jit(solution)/shard_map/ppermute | solution.py:505

commit v5 on v4

--- a/solution.py
+++ b/solution.py
@@ -135,12 +135,14 @@
 
 
 def maps_kernel(
-    resets, b_ref, g_ref, k_hbm, v_hbm, keep_ref, send_ref, inv_ref, uw_ref, k_ref, v_ref, sems
+    resets, b_ref, g_ref, k_hbm, v_hbm, cot_hbm, keep_ref, send_ref, inv_ref, uw_ref, wide_ref, k_ref, v_ref, cot_ref, sems
 ):
     load_k = pltpu.make_async_copy(k_hbm, k_ref, sems.at[0])
     load_v = pltpu.make_async_copy(v_hbm, v_ref, sems.at[1])
+    load_cot = pltpu.make_async_copy(cot_hbm, cot_ref, sems.at[2])
     load_k.start()
     load_v.start()
+    load_cot.start()
     tables = gate_tables(resets, b_ref, g_ref)
     rows, cols = iotas()
     eye = (rows == cols).astype(f32)
@@ -163,6 +165,8 @@
             inv = [inv[h] + mm(inv[h], power[h]) for h in HEADS]
     cross = [mm(far[h], inv[h]) for h in HEADS]
     inv = [inv[h] - mm(inv[h], cross[h]) for h in HEADS]
+    load_cot.wait()
+    wide_ref[...] = cot_ref[...].astype(f32)
     load_v.wait()
     uw = []
     for h in HEADS:
@@ -252,22 +256,29 @@
     cols = lax.broadcasted_iota(jnp.int32, (C, H), 1)
     iq_all = jnp.zeros((C, H), f32)
     ik_all = jnp.zeros((C, H), f32)
-    for h in HEADS:
-        qn, iq = unit(head(q_ref, h))
-        kn, ik = unit(head(k_ref, h))
-        inside, growth, _, _, _ = head_gates(tables, h)
-        inner = mm(jnp.concatenate([qn, kn], axis=0), kn, NT)
-        attn = inner[:C] * inside
-        prod = mm(attn, uw_ref[h])
-        read_ref[h] = jnp.concatenate([qn * growth - prod[:, :C], prod[:, C:]], axis=1)
-        inside_ref[h] = inside
-        attn_ref[h] = attn
-        kk_ref[h] = inner[C:]
-        kn_ref[h] = kn
-        qn_ref[h] = qn
-        invt_ref[h] = inv_ref[h].T
-        iq_all = jnp.where(cols == h, iq, iq_all)
-        ik_all = jnp.where(cols == h, ik, ik_all)
+    for group in (range(0, 4), range(4, 8)):
+        qn, kn, inside, attn = {}, {}, {}, {}
+        for h in group:
+            qn[h], iq = unit(head(q_ref, h))
+            kn[h], ik = unit(head(k_ref, h))
+            inside[h], growth, _, _, _ = head_gates(tables, h)
+            iq_all = jnp.where(cols == h, iq, iq_all)
+            ik_all = jnp.where(cols == h, ik, ik_all)
+            inside_ref[h] = inside[h]
+            kn_ref[h] = kn[h]
+            qn_ref[h] = qn[h]
+            invt_ref[h] = inv_ref[h].T
+        inner = {h: mm(jnp.concatenate([qn[h], kn[h]], axis=0), kn[h], NT) for h in group}
+        for h in group:
+            attn[h] = inner[h][:C] * inside[h]
+            attn_ref[h] = attn[h]
+            kk_ref[h] = inner[h][C:]
+        prod = {h: mm(attn[h], uw_ref[h]) for h in group}
+        for h in group:
+            growth = tables[2][:, h : h + 1]
+            read_ref[h] = jnp.concatenate(
+                [qn[h] * growth - prod[h][:, :C], prod[h][:, C:]], axis=1
+            )
     first = place()[3] == 0
     for j in range(4):
         a, b = mkeep_ref[j, :, :C], mrecv_ref[j, :, :C]
@@ -286,18 +297,17 @@
     mine_ref, other_ref, read_ref, dn_ref, n_ref, do_ref, keep_ref, send_ref
 ):
     first = place()[3] == 0
-    reach = []
+    outs = [
+        mm(read_ref[h, :, :C], pick(first, mine_ref, other_ref, h)) + read_ref[h, :, C:] for h in HEADS
+    ]
     for h in HEADS:
-        state = pick(first, mine_ref, other_ref, h)
-        read = read_ref[h]
-        out = mm(read[:, :C], state) + read[:, C:]
+        out = outs[h]
         inv = 1.0 / jnp.sqrt(jnp.mean(out * out, axis=-1, keepdims=True) + EPS)
         n32 = out * inv
         n_ref[:, h * C : (h + 1) * C] = n32.astype(bf16)
         dn = dn_ref[:, h * C : (h + 1) * C]
-        do = inv * (dn - n32 * jnp.mean(n32 * dn, axis=-1, keepdims=True))
-        do_ref[h] = do
-        reach.append(tn(read[:, :C], do))
+        do_ref[h] = inv * (dn - n32 * jnp.mean(n32 * dn, axis=-1, keepdims=True))
+    reach = [tn(read_ref[h, :, :C], do_ref[h]) for h in HEADS]
     for j in range(4):
         keep_ref[j] = jnp.where(first, reach[j], reach[j + 4])
         send_ref[j] = jnp.where(first, reach[j + 4], reach[j])
@@ -370,28 +380,34 @@
     col_all = jnp.zeros((H, C), f32)
     if half:
         dq_ref[:, : 4 * C] = refs[0][...]
-    for i in range(4):
-        h = 4 * half + i
-        state = pick(first, mine_ref, other_ref, h)
-        qn, kn, attn = qn_ref[h], kn_ref[h], attn_ref[h]
-        uw = uw_ref[h]
-        do = do_ref[h]
-        moved = mm(jnp.concatenate([uw[:, :C], kn], axis=0), state)
-        delta = uw[:, C:] - moved[:C]
-        both = mm(do, jnp.concatenate([delta, state], axis=0), NT)
-        dattn, back = both[:, :C], both[:, C:] * growth_ref[:, h : h + 1]
-        dqk = dattn * inside_ref[h]
-        dqn = back + mm(dqk, kn)
-        dq = iq_ref[:, h : h + 1] * (dqn - qn * jnp.sum(dqn * qn, axis=-1, keepdims=True))
+    group = range(4 * half, 4 * half + 4)
+    state = {h: pick(first, mine_ref, other_ref, h) for h in group}
+    moved = {
+        h: mm(jnp.concatenate([uw_ref[h, :, :C], kn_ref[h]], axis=0), state[h]) for h in group
+    }
+    delta = {h: uw_ref[h, :, C:] - moved[h][:C] for h in group}
+    for h in group:
+        dd_ref[h % 4] = tn(attn_ref[h], do_ref[h])
+        delta_ref[h % 4] = delta[h]
+        carried_ref[h % 4] = moved[h][C:]
+    both = {
+        h: mm(do_ref[h], jnp.concatenate([delta[h], state[h]], axis=0), NT) for h in group
+    }
+    dqk = {h: both[h][:, :C] * inside_ref[h] for h in group}
+    back = {h: both[h][:, C:] * growth_ref[:, h : h + 1] for h in group}
+    dqn = {h: back[h] + mm(dqk[h], kn_ref[h]) for h in group}
+    for h in group:
+        dkn_ref[h % 4] = tn(dqk[h], qn_ref[h])
+    for h in group:
+        qn = qn_ref[h]
+        dq = iq_ref[:, h : h + 1] * (
+            dqn[h] - qn * jnp.sum(dqn[h] * qn, axis=-1, keepdims=True)
+        )
         dq_ref[:, h * C : (h + 1) * C] = dq.astype(bf16)
-        pairs = dattn * attn
-        row = jnp.sum(pairs + back * qn, axis=-1, keepdims=True)
+        pairs = both[h][:, :C] * attn_ref[h]
+        row = jnp.sum(pairs + back[h] * qn, axis=-1, keepdims=True)
         row_all = jnp.where(cols == h, row, row_all)
         col_all = jnp.where(row8 == h, jnp.sum(pairs, axis=0, keepdims=True), col_all)
-        dkn_ref[i] = tn(dqk, qn)
-        dd_ref[i] = tn(attn, do)
-        delta_ref[i] = delta
-        carried_ref[i] = moved[C:]
     rowpart_ref[...] = row_all
     colpart_ref[...] = col_all
 
@@ -412,46 +428,46 @@
     col_all = early[5][...] + early[EARLY + 5][...]
     db_all = jnp.zeros((C, C), f32)
     is_last = lax.broadcasted_iota(jnp.int32, (C, 1), 0) == C - 1
-    for h in HEADS:
+    for group in (range(0, 4), range(4, 8)):
         delta, dkn, dd, carried = (
-            ref[h % 4] for ref in early[h // 4 * EARLY : h // 4 * EARLY + 4]
+            {h: early[h // 4 * EARLY + part][h % 4] for h in group} for part in range(4)
         )
-        kk, invt, kn = kk_ref[h], invt_ref[h], kn_ref[h]
-        state = pick(first, mine_ref, other_ref, h)
-        dstate = pick(first, dmine_ref, dother_ref, h)
+        state = {h: pick(first, mine_ref, other_ref, h) for h in group}
+        dstate = {h: pick(first, dmine_ref, dother_ref, h) for h in group}
         growth, fading, g_last, bh = (
-            ref[:, h : h + 1] for ref in (growth_ref, fading_ref, last_ref, beta_ref)
+            {h: ref[:, h : h + 1] for h in group} for ref in (growth_ref, fading_ref, last_ref, beta_ref)
         )
-        below = strict(inside_ref[h])
-        ddelta = dd + mm(kn, dstate) * fading
-        dtarget = mm(invt, ddelta)
-        dv_ref[:, h * C : (h + 1) * C] = (dtarget * bh).astype(bf16)
-        both = mm(dtarget, jnp.concatenate([delta, state], axis=0), NT)
-        dsys, dts = -(both[:, :C] * below), both[:, C:]
-        raw = dsys * kk
-        dkk = dsys * bh
-        dkf = mm(delta, dstate, NT) * fading
-        dcar = dtarget * carried * growth
-        db = jnp.sum(dtarget * head(v_ref, h) - dcar + raw, axis=-1, keepdims=True)
-        pairs = raw * bh
-        dfade = dkf * kn
-        dlast = jnp.sum(dfade + g_last * (state * dstate), axis=0, keepdims=True)
-        dtotal = jnp.sum(pairs - dcar * bh - dfade, axis=-1, keepdims=True)
-        dtotal = dtotal + jnp.where(is_last, jnp.sum(dlast, axis=-1, keepdims=True), 0.0)
-        dkn = dkn + mm(dkk + dkk.T, kn) + dkf - dts * (bh * growth)
-        dk = ik_ref[:, h : h + 1] * (dkn - kn * jnp.sum(dkn * kn, axis=-1, keepdims=True))
-        dk_ref[:, h * C : (h + 1) * C] = dk.astype(bf16)
-        db_all = jnp.where(cols == h, db, db_all)
-        row_all = row_all + jnp.where(cols == h, dtotal, 0.0)
-        col_all = col_all + jnp.where(row8 == h, jnp.sum(pairs, axis=0, keepdims=True), 0.0)
+        ddelta = {h: dd[h] + mm(kn_ref[h], dstate[h]) * fading[h] for h in group}
+        dkf = {h: mm(delta[h], dstate[h], NT) * fading[h] for h in group}
+        dtarget = {h: mm(invt_ref[h], ddelta[h]) for h in group}
+        both = {
+            h: mm(dtarget[h], jnp.concatenate([delta[h], state[h]], axis=0), NT) for h in group
+        }
+        dsys = {h: -(both[h][:, :C] * strict(inside_ref[h])) for h in group}
+        dkk = {h: dsys[h] * bh[h] for h in group}
+        inner = {h: mm(dkk[h] + dkk[h].T, kn_ref[h]) for h in group}
+        for h in group:
+            dv_ref[:, h * C : (h + 1) * C] = (dtarget[h] * bh[h]).astype(bf16)
+            raw = dsys[h] * kk_ref[h]
+            dcar = dtarget[h] * carried[h] * growth[h]
+            db = jnp.sum(dtarget[h] * head(v_ref, h) - dcar + raw, axis=-1, keepdims=True)
+            pairs = raw * bh[h]
+            dfade = dkf[h] * kn_ref[h]
+            dlast = jnp.sum(dfade + g_last[h] * (state[h] * dstate[h]), axis=0, keepdims=True)
+            dtotal = jnp.sum(pairs - dcar * bh[h] - dfade, axis=-1, keepdims=True)
+            dtotal = dtotal + jnp.where(is_last, jnp.sum(dlast, axis=-1, keepdims=True), 0.0)
+            grad = dkn[h] + inner[h] + dkf[h] - both[h][:, C:] * (bh[h] * growth[h])
+            dk = ik_ref[:, h : h + 1] * (
+                grad - kn_ref[h] * jnp.sum(grad * kn_ref[h], axis=-1, keepdims=True)
+            )
+            dk_ref[:, h * C : (h + 1) * C] = dk.astype(bf16)
+            db_all = jnp.where(cols == h, db, db_all)
+            row_all = row_all + jnp.where(cols == h, dtotal, 0.0)
+            col_all = col_all + jnp.where(row8 == h, jnp.sum(pairs, axis=0, keepdims=True), 0.0)
     lower = (rows >= cols).astype(bf16)
     mark_ref[...] = col_all
     db_ref[...] = db_all.T[:H]
     dg_ref[...] = sum(dot(part, lower) for part in split3(row_all.T[:H] - col_all))
-
-
-def widen_kernel(cot_ref, wide_ref):
-    wide_ref[...] = cot_ref[...].astype(f32)
 
 
 def relay_kernel(below_ref, above_ref, lower_ref, upper_ref):
@@ -516,7 +532,7 @@
 
 
 def around_dp(parts):
-    moved = {r: step_dp(parts[r], r) for r in (1, 2, 3)}
+    moved = {r: step_dp(parts[r], r) for r in (2, 1, 3)}
     return [parts[0], moved[1], moved[2], moved[3]]
 
 
@@ -533,17 +549,18 @@
     wide = ((C, H * C), bf16)
     hold, hold2 = [pltpu.VMEM(*four)], [pltpu.VMEM(*four2)]
 
-    mkeep, msend, inverse, uw = call(
+    mkeep, msend, inverse, uw, cot32 = call(
         maps_kernel,
-        [four2, four2, all1, all2],
-        1, *gates, k, v, us=6, hbm=(3, 4), limit=FIRST_LIMIT,
-        scratch=[pltpu.VMEM(*wide), pltpu.VMEM(*wide), pltpu.SemaphoreType.DMA((2,))],
+        [four2, four2, all1, all2, ((C, 2048), f32)],
+        1, *gates, k, v, cot, us=6, hbm=(3, 4, 5), limit=FIRST_LIMIT,
+        scratch=[
+            pltpu.VMEM(*wide), pltpu.VMEM(*wide), pltpu.VMEM((C, 2048), bf16), pltpu.SemaphoreType.DMA((3,)),
+        ],
     )
     mrecv = swap_core(msend)
     parts = call(pair_kernel, [two] * 4, 0, mkeep, mrecv, scratch=hold2)
     own = parts[0]
     parts = around_z(parts)
-    (cot32,) = call(widen_kernel, [((C, 2048), f32)], 0, cot, after=(mkeep,))
     dn = lax.dot_general(cot, out_weight, NT, preferred_element_type=f32)
     below, above = step_dp(cot32, 1), step_dp(cot32, 3)
     maps, prefix, total = call(
@@ -586,20 +603,20 @@
         )
 
     early0 = early_grads(0, own)
+    early1 = early_grads(1, own, early0[0])
     mixed = lax.dot_general(n16, out_weight, NN, preferred_element_type=f32).astype(bf16)
     reach, total = call(group_back_kernel, [four, one], 0, *parts, maps)
     parts = around_x([total] * 4)
-    early1 = early_grads(1, total, early0[0])
     wkeep, wsend = call(
         wgrad_kernel,
         [((16, 8, 2048), f32)] * 2,
-        0, *chunks, cot, below, above, lower, upper, us=2.5, after=(total, early0[0]),
+        0, *chunks, cot, below, above, lower, upper, us=2.5, after=(total, early1[1]),
     )
     wrecv = swap_core(wsend)
     wparts = call(wsum_pair_kernel, [((4, 8, 2048), f32)] * 4, 0, wkeep, wrecv)
     parts = call(
         enter_back_kernel, [one] * 4, 0, *parts, totals, maps, reach, us=1.5, scratch=hold + hold,
-        after=(wparts[0], early1[1], mixed),
+        after=(wparts[0], mixed),
     )
     parts = around_z(parts)
     wsent = around_x(wparts)

time: 104 us -> 102 us (0.981)
  Pallas kernels: 26.6 us -> 22.7 us
  starting transfers between devices: 51.1 us -> 53.3 us
  local copies, waits for them, and re-layouts: 2.15 us -> 1.1 us
    pallas_call x20 -> x19, Pallas kernels: 26.6 us -> 22.7 us  [call(): pl.pallas_call(body, out_shape=[jax.ShapeDtypeStruct(s, d) for s, d in ou...]
    ppermute x9, waiting for transfers between devices: 5.55 us -> 7.49 us  [around_x(): lax.ppermute(parts[r], 'seq', seq_perm(r, 0))]
    ppermute x15, starting transfers between devices: 20.3 us -> 21.8 us  [around_z(): lax.ppermute(parts[r], 'seq', seq_perm(0, r))]
    ppermute x15, waiting for transfers between devices: 7.69 us -> 6.5 us  [around_z(): lax.ppermute(parts[r], 'seq', seq_perm(0, r))]
    unnamed x28, local copies, waits for them, and re-layouts: 2.15 us -> 1.1 us
  transfers between devices with their start and end apart: 36 -> 36, of which waited for: 14 -> 12; matrix products, arithmetic and copies ran while one was open for 4% -> 5% of each run, Pallas kernels for 17% -> 13%
where the time goes in v5:
time: 102 us
  starting transfers between devices  53.3 us (52%)
  Pallas kernels  22.7 us (22%)
  waiting for transfers between devices  19.1 us (19%)
  matrix products  4.59 us (4%)
  local copies, waits for them, and re-layouts  1.1 us (1%)
    pallas_call x19, Pallas kernels, call(): pl.pallas_call(body, out_shape=[jax.ShapeDtypeStruct(s, d) for s, d in ou...  22.7 us
    ppermute x15, starting transfers between devices, around_z(): lax.ppermute(parts[r], 'seq', seq_perm(0, r))  21.8 us
    ppermute x9, starting transfers between devices, around_x(): lax.ppermute(parts[r], 'seq', seq_perm(r, 0))  12.3 us
    ppermute x5, starting transfers between devices, swap_core(): return lax.ppermute(x, 'seq', seq_perm(0, 0, 1))  11.8 us
    ppermute x9, waiting for transfers between devices, around_x(): lax.ppermute(parts[r], 'seq', seq_perm(r, 0))  7.49 us
    ppermute x7, starting transfers between devices, step_dp(): return lax.ppermute(x, 'dp', [(i, (i + r) % 4) for i in range(4)])  7.41 us
    ppermute x15, waiting for transfers between devices, around_z(): lax.ppermute(parts[r], 'seq', seq_perm(0, r))  6.5 us
    ppermute x7, waiting for transfers between devices, step_dp(): return lax.ppermute(x, 'dp', [(i, (i + r) % 4) for i in range(4)])  3.91 us
  transfers between devices with their start and end apart: 36, of which 12 were waited for; matrix products, arithmetic and copies ran while one was open for 5% of the time, Pallas kernels for 13%

profile of v5, /device:TPU:1, one launch (start us, length us, event | category | flops | bytes accessed | tf_op | source)
XLA Modules:
  0.0 101.8 jit_solution(9359103522612004290)
XLA Ops:
  0.6 6.8 %shard_map.135 = (f32[4,128,256]{2,1,0:T(8,128)}, f32[4,128,256]{2,1,0:T(8,128)}, f32[8,128,128]{2,1,0:T(8,128)}, f32[8,128,256]{2,1,0:T(8,128)}, f32[128,2048]{1,0:T(8,128)}) custom-call(s32[1,2]{1,0:T(1,128)} %refs_1_.1, bf16[8,128]{1,0:T(8,128)(2,1)} %bitcast.35, f32[8,128]{1,0:T(8,128)} %bitcast.33, bf16[128,1024]{1,0:T(8,128)(2,1)} %bitcast.28, ...), custom_call_target="tpu_custom_call" | custom-call | bytes 1 | tf_op jit(solution)/shard_map/pallas_call | solution.py:123
  7.4 1.5 %collective-permute-start = (f32[4,128,256]{2,1,0:T(8,128)}, f32[4,128,256]{2,1,0:T(8,128)S(1)}, u32[]{:S(2)}, u32[]{:S(2)}) collective-permute-start(f32[4,128,256]{2,1,0:T(8,128)} %get-tuple-element.94), channel_id=1, source_target_pairs={{0,1},{1,0},{2,3},{3,2},{4,5},{5,4},{6,7},{7,6},{8,9},{9,8},{10,11... | collective-permute-start | bytes 1572872 | tf_op jit(solution)/shard_map/ppermute | solution.py:517
  8.9 1.4 %collective-permute-start.18 = (f32[128,2048]{1,0:T(8,128)}, f32[128,2048]{1,0:T(8,128)S(1)}, u32[]{:S(2)}, u32[]{:S(2)}) collective-permute-start(f32[128,2048]{1,0:T(8,128)} %get-tuple-element.92.refs_1_), channel_id=1, source_target_pairs={{0,32},{32,64},{64,96},{96,0},{1,33},{33,65},{65,97},{97,1},{2,34}... | collective-permute-start | bytes 3145736 | tf_op jit(solution)/shard_map/ppermute | solution.py:531
  10.3 1.4 %collective-permute-start.19 = (f32[128,2048]{1,0:T(8,128)}, f32[128,2048]{1,0:T(8,128)S(1)}, u32[]{:S(2)}, u32[]{:S(2)}) collective-permute-start(f32[128,2048]{1,0:T(8,128)} %get-tuple-element.92.refs_1_), channel_id=1, source_target_pairs={{0,96},{32,0},{64,32},{96,64},{1,97},{33,1},{65,33},{97,65},{2,98}... | collective-permute-start | bytes 3145736 | tf_op jit(solution)/shard_map/ppermute | solution.py:531
  11.8 1.0 %copy-done.2 = f32[4,128,256]{2,1,0:T(8,128)S(1)} copy-done((f32[4,128,256]{2,1,0:T(8,128)S(1)}, f32[4,128,256]{2,1,0:T(8,128)}, u32[]{:S(2)}) %copy-start.2) | copy-done | bytes 524312
  12.9 0.4 shard_map.136
  13.3 1.7 %collective-permute-start.1 = (f32[128,256]{1,0:T(8,128)S(1)}, f32[128,256]{1,0:T(8,128)S(1)}, u32[]{:S(2)}, u32[]{:S(2)}) collective-permute-start(f32[128,256]{1,0:T(8,128)S(1)} %get-tuple-element.96), channel_id=1, source_target_pairs={{0,2},{1,3},{2,4},{3,5},{4,6},{5,7},{6,0},{7,1},{8,10},{9,11},{10,... | collective-permute-start | bytes 393224 | tf_op jit(solution)/shard_map/ppermute | solution.py:521
  15.0 3.3 %collective-permute-start.2 = (f32[128,256]{1,0:T(8,128)S(1)}, f32[128,256]{1,0:T(8,128)S(1)}, u32[]{:S(2)}, u32[]{:S(2)}) collective-permute-start(f32[128,256]{1,0:T(8,128)S(1)} %get-tuple-element.97), channel_id=1, source_target_pairs={{0,4},{1,5},{2,6},{3,7},{4,0},{5,1},{6,2},{7,3},{8,12},{9,13},{10,... | collective-permute-start | bytes 393224 | tf_op jit(solution)/shard_map/ppermute | solution.py:521
  18.3 0.7 collective-permute-start.3
  19.0 3.9 %fusion.refs_0_.refs_3_ = f32[128,1024]{1,0:T(8,128)S(1)} fusion(bf16[1024,2048]{1,0:T(8,128)(2,1)} %param.14, bf16[1,128,2048]{2,1,0:T(8,128)(2,1)} %param.15), kind=kOutput, calls=%fused_computation.1 | convolution fusion | flops 536870912 | bytes 5242880 | tf_op jit(solution)/shard_map/dot_general | solution.py:564
  22.9 1.2 %collective-permute-done.2.refs_4_ = f32[128,256]{1,0:T(8,128)S(1)} collective-permute-done((f32[128,256]{1,0:T(8,128)S(1)}, f32[128,256]{1,0:T(8,128)S(1)}, u32[]{:S(2)}, u32[]{:S(2)}) %collective-permute-start.2) | collective-permute-done | bytes 131104 | tf_op jit(solution)/shard_map/ppermute | solution.py:521
  24.1 0.6 shard_map.137
  24.7 1.3 %collective-permute-start.4 = (f32[128,256]{1,0:T(8,128)S(1)}, f32[128,256]{1,0:T(8,128)S(1)}, u32[]{:S(2)}, u32[]{:S(2)}) collective-permute-start(f32[128,256]{1,0:T(8,128)S(1)} %get-tuple-element.99.refs_0_.refs_1_), channel_id=1, source_target_pairs={{0,8},{1,9},{2,10},{3,11},{4,12},{5,13},{6,14},{7,15},{8,16},{9,17... | collective-permute-start | bytes 393224 | tf_op jit(solution)/shard_map/ppermute | solution.py:526
  26.0 2.5 %collective-permute-start.5 = (f32[128,256]{1,0:T(8,128)S(1)}, f32[128,256]{1,0:T(8,128)S(1)}, u32[]{:S(2)}, u32[]{:S(2)}) collective-permute-start(f32[128,256]{1,0:T(8,128)S(1)} %get-tuple-element.99.refs_0_.refs_1_), channel_id=1, source_target_pairs={{0,16},{1,17},{2,18},{3,19},{4,20},{5,21},{6,22},{7,23},{8,24},{9,... | collective-permute-start | bytes 393224 | tf_op jit(solution)/shard_map/ppermute | solution.py:526
  28.4 1.1 %collective-permute-start.6 = (f32[128,256]{1,0:T(8,128)S(1)}, f32[128,256]{1,0:T(8,128)S(1)}, u32[]{:S(2)}, u32[]{:S(2)}) collective-permute-start(f32[128,256]{1,0:T(8,128)S(1)} %get-tuple-element.99.refs_0_.refs_1_), channel_id=1, source_target_pairs={{0,24},{1,25},{2,26},{3,27},{4,28},{5,29},{6,30},{7,31},{8,0},{9,1... | collective-permute-start | bytes 393224 | tf_op jit(solution)/shard_map/ppermute | solution.py:526
  29.6 2.2 %shard_map.138 = (f32[8,128,256]{2,1,0:T(8,128)S(1)}, f32[8,128,128]{2,1,0:T(8,128)S(1)}, f32[8,128,128]{2,1,0:T(8,128)S(1)}, f32[8,128,128]{2,1,0:T(8,128)S(1)}...) custom-call(f32[128,256]{1,0:T(8,128)S(1)} %get-tuple-element.99.ref, ...), custom_call_target="tpu_custom_call" | custom-call | bytes 1 | tf_op jit(solution)/shard_map/pallas_call | solution.py:123
  31.8 1.2 %collective-permute-done.5.refs_3_ = f32[128,256]{1,0:T(8,128)S(1)} collective-permute-done((f32[128,256]{1,0:T(8,128)S(1)}, f32[128,256]{1,0:T(8,128)S(1)}, u32[]{:S(2)}, u32[]{:S(2)}) %collective-permute-start.5) | collective-permute-done | bytes 131104 | tf_op jit(solution)/shard_map/ppermute | solution.py:526
  33.0 0.6 collective-permute-done.6.refs_4_
  33.6 0.6 shard_map.139
  34.3 1.9 %collective-permute-start.7 = (f32[128,128]{1,0:T(8,128)S(1)}, f32[128,128]{1,0:T(8,128)S(1)}, u32[]{:S(2)}, u32[]{:S(2)}) collective-permute-start(f32[128,128]{1,0:T(8,128)S(1)} %get-tuple-element.105), channel_id=1, source_target_pairs={{0,2},{1,3},{2,4},{3,5},{4,6},{5,7},{6,0},{7,1},{8,10},{9,11},{10,... | collective-permute-start | bytes 196616 | tf_op jit(solution)/shard_map/ppermute | solution.py:521
  36.2 2.0 %collective-permute-start.8 = (f32[128,128]{1,0:T(8,128)S(1)}, f32[128,128]{1,0:T(8,128)S(1)}, u32[]{:S(2)}, u32[]{:S(2)}) collective-permute-start(f32[128,128]{1,0:T(8,128)S(1)} %get-tuple-element.106), channel_id=1, source_target_pairs={{0,4},{1,5},{2,6},{3,7},{4,0},{5,1},{6,2},{7,3},{8,12},{9,13},{10,... | collective-permute-start | bytes 196616 | tf_op jit(solution)/shard_map/ppermute | solution.py:521
  38.1 0.5 collective-permute-start.9
  38.7 2.1 %collective-permute-done.8.refs_2_ = f32[128,128]{1,0:T(8,128)S(1)} collective-permute-done((f32[128,128]{1,0:T(8,128)S(1)}, f32[128,128]{1,0:T(8,128)S(1)}, u32[]{:S(2)}, u32[]{:S(2)}) %collective-permute-start.8) | collective-permute-done | bytes 65568 | tf_op jit(solution)/shard_map/ppermute | solution.py:521
  40.8 0.7 collective-permute-done.9.refs_3_
  41.5 0.3 shard_map.140
  41.8 3.4 %collective-permute-start.10 = (f32[4,128,128]{2,1,0:T(8,128)S(1)}, f32[4,128,128]{2,1,0:T(8,128)S(1)}, u32[]{:S(2)}, u32[]{:S(2)}) collective-permute-start(f32[4,128,128]{2,1,0:T(8,128)S(1)} %get-tuple-element.109), channel_id=1, source_target_pairs={{0,1},{1,0},{2,3},{3,2},{4,5},{5,4},{6,7},{7,6},{8,9},{9,8},{10,11... | collective-permute-start | bytes 786440 | tf_op jit(solution)/shard_map/ppermute | solution.py:517
  45.3 0.5 collective-permute-start.20
  45.8 2.2 %collective-permute-start.21 = (f32[64,2048]{1,0:T(8,128)S(1)}, f32[64,2048]{1,0:T(8,128)S(1)}, u32[]{:S(2)}, u32[]{:S(2)}) collective-permute-start(f32[64,2048]{1,0:T(8,128)S(1)} %get-tuple-element.135), channel_id=1, source_target_pairs={{0,96},{32,0},{64,32},{96,64},{1,97},{33,1},{65,33},{97,65},{2,98}... | collective-permute-start | bytes 1572872 | tf_op jit(solution)/shard_map/ppermute | solution.py:531
  48.1 1.0 shard_map.141
  49.0 0.7 collective-permute-start.11
  49.7 1.2 %collective-permute-done.11.refs_1_.refs_7_ = f32[4,128,128]{2,1,0:T(8,128)S(1)} collective-permute-done((f32[4,128,128]{2,1,0:T(8,128)S(1)}, f32[4,128,128]{2,1,0:T(8,128)S(1)}, u32[]{:S(2)}, u32[]{:S(2)}) %collective-permute-start.11) | collective-permute-done | bytes 262176 | tf_op jit(solution)/shard_map/ppermute | solution.py:517
  50.9 0.3 shard_map.142
  51.3 2.7 %collective-permute-start.13 = (f32[128,128]{1,0:T(8,128)S(1)}, f32[128,128]{1,0:T(8,128)S(1)}, u32[]{:S(2)}, u32[]{:S(2)}) collective-permute-start(f32[128,128]{1,0:T(8,128)S(1)} %get-tuple-element.125), channel_id=1, source_target_pairs={{0,4},{1,5},{2,6},{3,7},{4,0},{5,1},{6,2},{7,3},{8,12},{9,13},{10,... | collective-permute-start | bytes 196616 | tf_op jit(solution)/shard_map/ppermute | solution.py:521
  54.0 0.6 collective-permute-start.14
  54.6 1.3 %collective-permute-done.12.refs_1_ = f32[128,128]{1,0:T(8,128)S(1)} collective-permute-done((f32[128,128]{1,0:T(8,128)S(1)}, f32[128,128]{1,0:T(8,128)S(1)}, u32[]{:S(2)}, u32[]{:S(2)}) %collective-permute-start.12) | collective-permute-done | bytes 65568 | tf_op jit(solution)/shard_map/ppermute | solution.py:521
  55.9 1.0 %collective-permute-done.13.refs_2_ = f32[128,128]{1,0:T(8,128)S(1)} collective-permute-done((f32[128,128]{1,0:T(8,128)S(1)}, f32[128,128]{1,0:T(8,128)S(1)}, u32[]{:S(2)}, u32[]{:S(2)}) %collective-permute-start.13) | collective-permute-done | bytes 65568 | tf_op jit(solution)/shard_map/ppermute | solution.py:521
  56.9 1.0 collective-permute-start.16
  57.9 0.9 collective-permute-start.17
  58.8 1.0 shard_map.143
  59.8 1.7 %shard_map.144 = (bf16[128,1024]{1,0:T(8,128)(2,1)}, f32[4,128,128]{2,1,0:T(8,128)S(1)}, f32[4,128,128]{2,1,0:T(8,128)S(1)}, f32[4,128,128]{2,1,0:T(8,128)S(1)},...) custom-call(f32[128,128]{1,0:T(8,128)S(1)} %get-tuple-element.114.refs_0_, ...), custom_call_target="tpu_custom_call" | custom-call | bytes 1 | tf_op jit(solution)/shard_map/pallas_call | solution.py:123
  61.6 0.6 shard_map.145
  62.1 3.9 %collective-permute-done.16.refs_4_ = f32[128,256]{1,0:T(8,128)S(1)} collective-permute-done((f32[128,256]{1,0:T(8,128)S(1)}, f32[128,256]{1,0:T(8,128)S(1)}, u32[]{:S(2)}, u32[]{:S(2)}) %collective-permute-start.16) | collective-permute-done | bytes 131104 | tf_op jit(solution)/shard_map/ppermute | solution.py:531
  66.0 1.3 %shard_map.147 = (f32[16,8,2048]{2,1,0:T(8,128)S(1)}, f32[16,8,2048]{2,1,0:T(8,128)S(1)}) custom-call(f32[128,128]{1,0:T(8,128)S(1)} %get-tuple-element.128.refs_0_.refs_2_, f32[4,128,128]{2,1,0:T(8,128)S(1)} %get-tuple-element.129.refs_1_.refs_21_, f32[128,256]{1,0:T(8,128)S(1)} %get-tuple-element.130.refs_2_, ...), custom_call_target="tpu_custom_call" | custom-call | bytes 1 | tf_op jit(solution)/shard_map/pallas_call | solution.py:123
  67.3 1.0 collective-permute-start.22
  68.3 1.1 %collective-permute-start.26 = (f32[128,128]{1,0:T(8,128)S(1)}, f32[128,128]{1,0:T(8,128)S(1)}, u32[]{:S(2)}, u32[]{:S(2)}) collective-permute-start(f32[128,128]{1,0:T(8,128)S(1)} %get-tuple-element.128.refs_0_.refs_2_), channel_id=1, source_target_pairs={{0,8},{1,9},{2,10},{3,11},{4,12},{5,13},{6,14},{7,15},{8,16},{9,17... | collective-permute-start | bytes 196616 | tf_op jit(solution)/shard_map/ppermute | solution.py:526
  69.4 2.4 %collective-permute-start.27 = (f32[128,128]{1,0:T(8,128)S(1)}, f32[128,128]{1,0:T(8,128)S(1)}, u32[]{:S(2)}, u32[]{:S(2)}) collective-permute-start(f32[128,128]{1,0:T(8,128)S(1)} %get-tuple-element.128.refs_0_.refs_2_), channel_id=1, source_target_pairs={{0,16},{1,17},{2,18},{3,19},{4,20},{5,21},{6,22},{7,23},{8,24},{9,... | collective-permute-start | bytes 196616 | tf_op jit(solution)/shard_map/ppermute | solution.py:526
  71.7 1.0 %collective-permute-start.28 = (f32[128,128]{1,0:T(8,128)S(1)}, f32[128,128]{1,0:T(8,128)S(1)}, u32[]{:S(2)}, u32[]{:S(2)}) collective-permute-start(f32[128,128]{1,0:T(8,128)S(1)} %get-tuple-element.128.refs_0_.refs_2_), channel_id=1, source_target_pairs={{0,24},{1,25},{2,26},{3,27},{4,28},{5,29},{6,30},{7,31},{8,0},{9,1... | collective-permute-start | bytes 196616 | tf_op jit(solution)/shard_map/ppermute | solution.py:526
  72.8 0.1 shard_map.148
  72.9 0.5 collective-permute-start.23
  73.4 0.8 collective-permute-start.24
  74.2 1.7 %collective-permute-start.25 = (f32[4,8,2048]{2,1,0:T(8,128)S(1)}, f32[4,8,2048]{2,1,0:T(8,128)S(1)}, u32[]{:S(2)}, u32[]{:S(2)}) collective-permute-start(f32[4,8,2048]{2,1,0:T(8,128)S(1)} %get-tuple-element.141), channel_id=1, source_target_pairs={{0,24},{1,25},{2,26},{3,27},{4,28},{5,29},{6,30},{7,31},{8,0},{9,1... | collective-permute-start | bytes 786440 | tf_op jit(solution)/shard_map/ppermute | solution.py:526
  75.9 0.7 convolution_convert_fusion.refs_1_
  76.6 0.9 shard_map.150
  77.6 0.2 collective-permute-start.29
  77.8 2.9 %collective-permute-start.30 = (f32[128,128]{1,0:T(8,128)S(1)}, f32[128,128]{1,0:T(8,128)S(1)}, u32[]{:S(2)}, u32[]{:S(2)}) collective-permute-start(f32[128,128]{1,0:T(8,128)S(1)} %get-tuple-element.147), channel_id=1, source_target_pairs={{0,4},{1,5},{2,6},{3,7},{4,0},{5,1},{6,2},{7,3},{8,12},{9,13},{10,... | collective-permute-start | bytes 196616 | tf_op jit(solution)/shard_map/ppermute | solution.py:521
  80.6 0.9 collective-permute-done.23.refs_1_
  81.6 1.2 %collective-permute-start.31 = (f32[128,128]{1,0:T(8,128)S(1)}, f32[128,128]{1,0:T(8,128)S(1)}, u32[]{:S(2)}, u32[]{:S(2)}) collective-permute-start(f32[128,128]{1,0:T(8,128)S(1)} %get-tuple-element.148), channel_id=1, source_target_pairs={{0,6},{1,7},{2,0},{3,1},{4,2},{5,3},{6,4},{7,5},{8,14},{9,15},{10,... | collective-permute-start | bytes 196616 | tf_op jit(solution)/shard_map/ppermute | solution.py:521
  82.8 3.5 %collective-permute-done.24.refs_2_ = f32[4,8,2048]{2,1,0:T(8,128)S(1)} collective-permute-done((f32[4,8,2048]{2,1,0:T(8,128)S(1)}, f32[4,8,2048]{2,1,0:T(8,128)S(1)}, u32[]{:S(2)}, u32[]{:S(2)}) %collective-permute-start.24) | collective-permute-done | bytes 262176 | tf_op jit(solution)/shard_map/ppermute | solution.py:526
  86.2 1.3 %collective-permute-done.25.refs_3_ = f32[4,8,2048]{2,1,0:T(8,128)S(1)} collective-permute-done((f32[4,8,2048]{2,1,0:T(8,128)S(1)}, f32[4,8,2048]{2,1,0:T(8,128)S(1)}, u32[]{:S(2)}, u32[]{:S(2)}) %collective-permute-start.25) | collective-permute-done | bytes 262176 | tf_op jit(solution)/shard_map/ppermute | solution.py:526
  87.6 0.3 shard_map.151
  87.9 5.3 %collective-permute-start.32 = (f32[4,128,128]{2,1,0:T(8,128)S(1)}, f32[4,128,128]{2,1,0:T(8,128)S(1)}, u32[]{:S(2)}, u32[]{:S(2)}) collective-permute-start(f32[4,128,128]{2,1,0:T(8,128)S(1)} %get-tuple-element.151), channel_id=1, source_target_pairs={{0,1},{1,0},{2,3},{3,2},{4,5},{5,4},{6,7},{7,6},{8,9},{9,8},{10,11... | collective-permute-start | bytes 786440 | tf_op jit(solution)/shard_map/ppermute | solution.py:517
  93.1 4.0 %collective-permute-start.34 = (f32[8,2048]{1,0:T(8,128)S(1)}, f32[8,2048]{1,0:T(8,128)S(1)}, u32[]{:S(2)}, u32[]{:S(2)}) collective-permute-start(f32[8,2048]{1,0:T(8,128)S(1)} %get-tuple-element.175), channel_id=1, source_target_pairs={{0,4},{1,5},{2,6},{3,7},{4,0},{5,1},{6,2},{7,3},{8,12},{9,13},{10,... | collective-permute-start | bytes 196616 | tf_op jit(solution)/shard_map/ppermute | solution.py:521
  97.2 3.9 %shard_map.152 = (bf16[128,1024]{1,0:T(8,128)(2,1)}, bf16[128,1024]{1,0:T(8,128)(2,1)}, f32[8,128]{1,0:T(8,128)}, f32[8,128]{1,0:T(8,128)}, f32[8,128]{1,0:T(8,128)S(1)}) custom-call(f32[8,2048]{1,0:T(8,128)S(1)} %get-tuple-element.142.refs_0_.refs_1_, bf16[128,1024]{1,0:T(8,128)(2,1)S(1)} %bitcast.31, ...), custom_call_target="tpu_custom_call" | custom-call | bytes 1 | tf_op jit(solution)/shard_map/pallas_call | solution.py:123
  101.1 0.7 shard_map.153
  (57 shorter events, 0.4 us)
Async XLA Ops:
  7.4 4.3 %collective-permute-start = (f32[4,128,256]{2,1,0:T(8,128)}, f32[4,128,256]{2,1,0:T(8,128)S(1)}, u32[]{:S(2)}, u32[]{:S(2)}) collective-permute-start(f32[4,128,256]{2,1,0:T(8,128)} %get-tuple-element.94), channel_id=1, source_target_pairs={{0,1},{1,0},{2,3},{3,2},{4,5},{5,4},{6,7},{7,6},{8,9},{9,8},{10,11... | collective-permute-start | bytes 1572872 | tf_op jit(solution)/shard_map/ppermute | solution.py:517
  8.9 36.3 %collective-permute-start.18 = (f32[128,2048]{1,0:T(8,128)}, f32[128,2048]{1,0:T(8,128)S(1)}, u32[]{:S(2)}, u32[]{:S(2)}) collective-permute-start(f32[128,2048]{1,0:T(8,128)} %get-tuple-element.92.refs_1_), channel_id=1, source_target_pairs={{0,32},{32,64},{64,96},{96,0},{1,33},{33,65},{65,97},{97,1},{2,34}... | collective-permute-start | bytes 3145736 | tf_op jit(solution)/shard_map/ppermute | solution.py:531
  10.3 34.9 %collective-permute-start.19 = (f32[128,2048]{1,0:T(8,128)}, f32[128,2048]{1,0:T(8,128)S(1)}, u32[]{:S(2)}, u32[]{:S(2)}) collective-permute-start(f32[128,2048]{1,0:T(8,128)} %get-tuple-element.92.refs_1_), channel_id=1, source_target_pairs={{0,96},{32,0},{64,32},{96,64},{1,97},{33,1},{65,33},{97,65},{2,98}... | collective-permute-start | bytes 3145736 | tf_op jit(solution)/shard_map/ppermute | solution.py:531
  11.8 1.0 %copy-start.2 = (f32[4,128,256]{2,1,0:T(8,128)S(1)}, f32[4,128,256]{2,1,0:T(8,128)}, u32[]{:S(2)}) copy-start(f32[4,128,256]{2,1,0:T(8,128)} %get-tuple-element.93.refs_0_.refs_8_.refs_4_) | copy-start | bytes 1572868
  12.8 11.3 %copy-start.5 = (f32[128,2048]{1,0:T(8,128)S(1)}, f32[128,2048]{1,0:T(8,128)}, u32[]{:S(2)}) copy-start(f32[128,2048]{1,0:T(8,128)} %get-tuple-element.92.refs_1_) | copy-start | bytes 3145732
  12.8 16.8 %copy-start = (f32[8,128,256]{2,1,0:T(8,128)S(1)}, f32[8,128,256]{2,1,0:T(8,128)}, u32[]{:S(2)}) copy-start(f32[8,128,256]{2,1,0:T(8,128)} %get-tuple-element.100.refs_6_.refs_3_) | copy-start | bytes 3145732
  12.8 16.8 %copy-start.3 = (f32[4,128,256]{2,1,0:T(8,128)S(1)}, f32[4,128,256]{2,1,0:T(8,128)}, u32[]{:S(2)}) copy-start(f32[4,128,256]{2,1,0:T(8,128)} %get-tuple-element.93.refs_0_.refs_8_.refs_4_) | copy-start | bytes 1572868
  12.8 16.8 %copy-start.6 = (bf16[1,128,1024]{2,1,0:T(8,128)(2,1)S(1)}, bf16[1,128,1024]{2,1,0:T(8,128)(2,1)}, u32[]{:S(2)}) copy-start(bf16[1,128,1024]{2,1,0:T(8,128)(2,1)} %param.9) | copy-start | bytes 786436
  12.8 16.8 %copy-start.8 = (f32[8,128,128]{2,1,0:T(8,128)S(1)}, f32[8,128,128]{2,1,0:T(8,128)}, u32[]{:S(2)}) copy-start(f32[8,128,128]{2,1,0:T(8,128)} %get-tuple-element.101.refs_7_) | copy-start | bytes 1572868
  12.8 16.8 %copy-start.9 = (bf16[1,128,1024]{2,1,0:T(8,128)(2,1)S(1)}, bf16[1,128,1024]{2,1,0:T(8,128)(2,1)}, u32[]{:S(2)}) copy-start(bf16[1,128,1024]{2,1,0:T(8,128)(2,1)} %param.8) | copy-start | bytes 786436
  12.8 16.8 %copy-start.10 = (f32[1,128,8]{1,2,0:T(8,128)S(1)}, f32[1,128,8]{1,2,0:T(8,128)}, u32[]{:S(2)}) copy-start(f32[1,128,8]{1,2,0:T(8,128)} %param.12) | copy-start | bytes 12292
  12.8 16.8 %copy-start.11 = (bf16[1,128,8]{1,2,0:T(8,128)(2,1)S(1)}, bf16[1,128,8]{1,2,0:T(8,128)(2,1)}, u32[]{:S(2)}) copy-start(bf16[1,128,8]{1,2,0:T(8,128)(2,1)} %param.11) | copy-start | bytes 6148
  12.9 16.8 %copy-start.12 = (s32[1,2]{1,0:T(1,128)S(1)}, s32[1,2]{1,0:T(1,128)}, u32[]{:S(2)}) copy-start(s32[1,2]{1,0:T(1,128)} %refs_1_.1) | copy-start | bytes 28
  13.3 9.6 %collective-permute-start.1 = (f32[128,256]{1,0:T(8,128)S(1)}, f32[128,256]{1,0:T(8,128)S(1)}, u32[]{:S(2)}, u32[]{:S(2)}) collective-permute-start(f32[128,256]{1,0:T(8,128)S(1)} %get-tuple-element.96), channel_id=1, source_target_pairs={{0,2},{1,3},{2,4},{3,5},{4,6},{5,7},{6,0},{7,1},{8,10},{9,11},{10,... | collective-permute-start | bytes 393224 | tf_op jit(solution)/shard_map/ppermute | solution.py:521
  15.0 9.1 %collective-permute-start.2 = (f32[128,256]{1,0:T(8,128)S(1)}, f32[128,256]{1,0:T(8,128)S(1)}, u32[]{:S(2)}, u32[]{:S(2)}) collective-permute-start(f32[128,256]{1,0:T(8,128)S(1)} %get-tuple-element.97), channel_id=1, source_target_pairs={{0,4},{1,5},{2,6},{3,7},{4,0},{5,1},{6,2},{7,3},{8,12},{9,13},{10,... | collective-permute-start | bytes 393224 | tf_op jit(solution)/shard_map/ppermute | solution.py:521
  18.3 5.8 %collective-permute-start.3 = (f32[128,256]{1,0:T(8,128)S(1)}, f32[128,256]{1,0:T(8,128)S(1)}, u32[]{:S(2)}, u32[]{:S(2)}) collective-permute-start(f32[128,256]{1,0:T(8,128)S(1)} %get-tuple-element.98), channel_id=1, source_target_pairs={{0,6},{1,7},{2,0},{3,1},{4,2},{5,3},{6,4},{7,5},{8,14},{9,15},{10,... | collective-permute-start | bytes 393224 | tf_op jit(solution)/shard_map/ppermute | solution.py:521
  24.7 7.1 %collective-permute-start.4 = (f32[128,256]{1,0:T(8,128)S(1)}, f32[128,256]{1,0:T(8,128)S(1)}, u32[]{:S(2)}, u32[]{:S(2)}) collective-permute-start(f32[128,256]{1,0:T(8,128)S(1)} %get-tuple-element.99.refs_0_.refs_1_), channel_id=1, source_target_pairs={{0,8},{1,9},{2,10},{3,11},{4,12},{5,13},{6,14},{7,15},{8,16},{9,17... | collective-permute-start | bytes 393224 | tf_op jit(solution)/shard_map/ppermute | solution.py:526
  26.0 7.1 %collective-permute-start.5 = (f32[128,256]{1,0:T(8,128)S(1)}, f32[128,256]{1,0:T(8,128)S(1)}, u32[]{:S(2)}, u32[]{:S(2)}) collective-permute-start(f32[128,256]{1,0:T(8,128)S(1)} %get-tuple-element.99.refs_0_.refs_1_), channel_id=1, source_target_pairs={{0,16},{1,17},{2,18},{3,19},{4,20},{5,21},{6,22},{7,23},{8,24},{9,... | collective-permute-start | bytes 393224 | tf_op jit(solution)/shard_map/ppermute | solution.py:526
  28.4 5.2 %collective-permute-start.6 = (f32[128,256]{1,0:T(8,128)S(1)}, f32[128,256]{1,0:T(8,128)S(1)}, u32[]{:S(2)}, u32[]{:S(2)}) collective-permute-start(f32[128,256]{1,0:T(8,128)S(1)} %get-tuple-element.99.refs_0_.refs_1_), channel_id=1, source_target_pairs={{0,24},{1,25},{2,26},{3,27},{4,28},{5,29},{6,30},{7,31},{8,0},{9,1... | collective-permute-start | bytes 393224 | tf_op jit(solution)/shard_map/ppermute | solution.py:526
  34.3 4.4 %collective-permute-start.7 = (f32[128,128]{1,0:T(8,128)S(1)}, f32[128,128]{1,0:T(8,128)S(1)}, u32[]{:S(2)}, u32[]{:S(2)}) collective-permute-start(f32[128,128]{1,0:T(8,128)S(1)} %get-tuple-element.105), channel_id=1, source_target_pairs={{0,2},{1,3},{2,4},{3,5},{4,6},{5,7},{6,0},{7,1},{8,10},{9,11},{10,... | collective-permute-start | bytes 196616 | tf_op jit(solution)/shard_map/ppermute | solution.py:521
  36.2 4.6 %collective-permute-start.8 = (f32[128,128]{1,0:T(8,128)S(1)}, f32[128,128]{1,0:T(8,128)S(1)}, u32[]{:S(2)}, u32[]{:S(2)}) collective-permute-start(f32[128,128]{1,0:T(8,128)S(1)} %get-tuple-element.106), channel_id=1, source_target_pairs={{0,4},{1,5},{2,6},{3,7},{4,0},{5,1},{6,2},{7,3},{8,12},{9,13},{10,... | collective-permute-start | bytes 196616 | tf_op jit(solution)/shard_map/ppermute | solution.py:521
  38.1 3.4 %collective-permute-start.9 = (f32[128,128]{1,0:T(8,128)S(1)}, f32[128,128]{1,0:T(8,128)S(1)}, u32[]{:S(2)}, u32[]{:S(2)}) collective-permute-start(f32[128,128]{1,0:T(8,128)S(1)} %get-tuple-element.107), channel_id=1, source_target_pairs={{0,6},{1,7},{2,0},{3,1},{4,2},{5,3},{6,4},{7,5},{8,14},{9,15},{10,... | collective-permute-start | bytes 196616 | tf_op jit(solution)/shard_map/ppermute | solution.py:521
  41.8 6.2 %collective-permute-start.10 = (f32[4,128,128]{2,1,0:T(8,128)S(1)}, f32[4,128,128]{2,1,0:T(8,128)S(1)}, u32[]{:S(2)}, u32[]{:S(2)}) collective-permute-start(f32[4,128,128]{2,1,0:T(8,128)S(1)} %get-tuple-element.109), channel_id=1, source_target_pairs={{0,1},{1,0},{2,3},{3,2},{4,5},{5,4},{6,7},{7,6},{8,9},{9,8},{10,11... | collective-permute-start | bytes 786440 | tf_op jit(solution)/shard_map/ppermute | solution.py:517
  45.3 20.7 %collective-permute-start.20 = (f32[64,2048]{1,0:T(8,128)S(1)}, f32[64,2048]{1,0:T(8,128)S(1)}, u32[]{:S(2)}, u32[]{:S(2)}) collective-permute-start(f32[64,2048]{1,0:T(8,128)S(1)} %get-tuple-element.134), channel_id=1, source_target_pairs={{0,32},{32,64},{64,96},{96,0},{1,33},{33,65},{65,97},{97,1},{2,34}... | collective-permute-start | bytes 1572872 | tf_op jit(solution)/shard_map/ppermute | solution.py:531
  45.8 20.2 %collective-permute-start.21 = (f32[64,2048]{1,0:T(8,128)S(1)}, f32[64,2048]{1,0:T(8,128)S(1)}, u32[]{:S(2)}, u32[]{:S(2)}) collective-permute-start(f32[64,2048]{1,0:T(8,128)S(1)} %get-tuple-element.135), channel_id=1, source_target_pairs={{0,96},{32,0},{64,32},{96,64},{1,97},{33,1},{65,33},{97,65},{2,98}... | collective-permute-start | bytes 1572872 | tf_op jit(solution)/shard_map/ppermute | solution.py:531
  49.0 1.8 %collective-permute-start.11 = (f32[4,128,128]{2,1,0:T(8,128)S(1)}, f32[4,128,128]{2,1,0:T(8,128)S(1)}, u32[]{:S(2)}, u32[]{:S(2)}) collective-permute-start(f32[4,128,128]{2,1,0:T(8,128)S(1)} %get-tuple-element.112), channel_id=1, source_target_pairs={{0,1},{1,0},{2,3},{3,2},{4,5},{5,4},{6,7},{7,6},{8,9},{9,8},{10,11... | collective-permute-start | bytes 786440 | tf_op jit(solution)/shard_map/ppermute | solution.py:517
  51.2 4.7 %collective-permute-start.12 = (f32[128,128]{1,0:T(8,128)S(1)}, f32[128,128]{1,0:T(8,128)S(1)}, u32[]{:S(2)}, u32[]{:S(2)}) collective-permute-start(f32[128,128]{1,0:T(8,128)S(1)} %get-tuple-element.124), channel_id=1, source_target_pairs={{0,2},{1,3},{2,4},{3,5},{4,6},{5,7},{6,0},{7,1},{8,10},{9,11},{10,... | collective-permute-start | bytes 196616 | tf_op jit(solution)/shard_map/ppermute | solution.py:521
  51.3 5.7 %collective-permute-start.13 = (f32[128,128]{1,0:T(8,128)S(1)}, f32[128,128]{1,0:T(8,128)S(1)}, u32[]{:S(2)}, u32[]{:S(2)}) collective-permute-start(f32[128,128]{1,0:T(8,128)S(1)} %get-tuple-element.125), channel_id=1, source_target_pairs={{0,4},{1,5},{2,6},{3,7},{4,0},{5,1},{6,2},{7,3},{8,12},{9,13},{10,... | collective-permute-start | bytes 196616 | tf_op jit(solution)/shard_map/ppermute | solution.py:521
  54.0 3.9 %collective-permute-start.14 = (f32[128,128]{1,0:T(8,128)S(1)}, f32[128,128]{1,0:T(8,128)S(1)}, u32[]{:S(2)}, u32[]{:S(2)}) collective-permute-start(f32[128,128]{1,0:T(8,128)S(1)} %get-tuple-element.126), channel_id=1, source_target_pairs={{0,6},{1,7},{2,0},{3,1},{4,2},{5,3},{6,4},{7,5},{8,14},{9,15},{10,... | collective-permute-start | bytes 196616 | tf_op jit(solution)/shard_map/ppermute | solution.py:521
  55.9 6.2 %collective-permute-start.15 = (f32[128,256]{1,0:T(8,128)S(1)}, f32[128,256]{1,0:T(8,128)S(1)}, u32[]{:S(2)}, u32[]{:S(2)}) collective-permute-start(f32[128,256]{1,0:T(8,128)S(1)} %get-tuple-element.131), channel_id=1, source_target_pairs={{0,32},{32,64},{64,96},{96,0},{1,33},{33,65},{65,97},{97,1},{2,34}... | collective-permute-start | bytes 393224 | tf_op jit(solution)/shard_map/ppermute | solution.py:531
  56.9 9.1 %collective-permute-start.16 = (f32[128,256]{1,0:T(8,128)S(1)}, f32[128,256]{1,0:T(8,128)S(1)}, u32[]{:S(2)}, u32[]{:S(2)}) collective-permute-start(f32[128,256]{1,0:T(8,128)S(1)} %get-tuple-element.132), channel_id=1, source_target_pairs={{0,64},{32,96},{64,0},{96,32},{1,65},{33,97},{65,1},{97,33},{2,66}... | collective-permute-start | bytes 393224 | tf_op jit(solution)/shard_map/ppermute | solution.py:531
  57.9 8.1 %collective-permute-start.17 = (f32[128,256]{1,0:T(8,128)S(1)}, f32[128,256]{1,0:T(8,128)S(1)}, u32[]{:S(2)}, u32[]{:S(2)}) collective-permute-start(f32[128,256]{1,0:T(8,128)S(1)} %get-tuple-element.133), channel_id=1, source_target_pairs={{0,96},{32,0},{64,32},{96,64},{1,97},{33,1},{65,33},{97,65},{2,98}... | collective-permute-start | bytes 393224 | tf_op jit(solution)/shard_map/ppermute | solution.py:531
  58.8 7.2 %copy-start.1 = (bf16[1,128,2048]{2,1,0:T(8,128)(2,1)S(1)}, bf16[1,128,2048]{2,1,0:T(8,128)(2,1)}, u32[]{:S(2)}) copy-start(bf16[1,128,2048]{2,1,0:T(8,128)(2,1)} %param.15) | copy-start | bytes 1572868
  61.6 14.3 %copy-start.13 = (bf16[1024,2048]{1,0:T(8,128)(2,1)S(1)}, bf16[1024,2048]{1,0:T(8,128)(2,1)}, u32[]{:S(2)}) copy-start(bf16[1024,2048]{1,0:T(8,128)(2,1)} %param.14) | copy-start | bytes 12582916
  67.3 5.4 %collective-permute-start.22 = (f32[16,8,2048]{2,1,0:T(8,128)S(1)}, f32[16,8,2048]{2,1,0:T(8,128)S(1)}, u32[]{:S(2)}, u32[]{:S(2)}) collective-permute-start(f32[16,8,2048]{2,1,0:T(8,128)S(1)} %get-tuple-element.137), channel_id=1, source_target_pairs={{0,1},{1,0},{2,3},{3,2},{4,5},{5,4},{6,7},{7,6},{8,9},{9,8},{10,11... | collective-permute-start | bytes 3145736 | tf_op jit(solution)/shard_map/ppermute | solution.py:517
  68.3 5.9 %collective-permute-start.26 = (f32[128,128]{1,0:T(8,128)S(1)}, f32[128,128]{1,0:T(8,128)S(1)}, u32[]{:S(2)}, u32[]{:S(2)}) collective-permute-start(f32[128,128]{1,0:T(8,128)S(1)} %get-tuple-element.128.refs_0_.refs_2_), channel_id=1, source_target_pairs={{0,8},{1,9},{2,10},{3,11},{4,12},{5,13},{6,14},{7,15},{8,16},{9,17... | collective-permute-start | bytes 196616 | tf_op jit(solution)/shard_map/ppermute | solution.py:526
  69.4 7.2 %collective-permute-start.27 = (f32[128,128]{1,0:T(8,128)S(1)}, f32[128,128]{1,0:T(8,128)S(1)}, u32[]{:S(2)}, u32[]{:S(2)}) collective-permute-start(f32[128,128]{1,0:T(8,128)S(1)} %get-tuple-element.128.refs_0_.refs_2_), channel_id=1, source_target_pairs={{0,16},{1,17},{2,18},{3,19},{4,20},{5,21},{6,22},{7,23},{8,24},{9,... | collective-permute-start | bytes 196616 | tf_op jit(solution)/shard_map/ppermute | solution.py:526
  71.7 4.9 %collective-permute-start.28 = (f32[128,128]{1,0:T(8,128)S(1)}, f32[128,128]{1,0:T(8,128)S(1)}, u32[]{:S(2)}, u32[]{:S(2)}) collective-permute-start(f32[128,128]{1,0:T(8,128)S(1)} %get-tuple-element.128.refs_0_.refs_2_), channel_id=1, source_target_pairs={{0,24},{1,25},{2,26},{3,27},{4,28},{5,29},{6,30},{7,31},{8,0},{9,1... | collective-permute-start | bytes 196616 | tf_op jit(solution)/shard_map/ppermute | solution.py:526
  72.9 8.7 %collective-permute-start.23 = (f32[4,8,2048]{2,1,0:T(8,128)S(1)}, f32[4,8,2048]{2,1,0:T(8,128)S(1)}, u32[]{:S(2)}, u32[]{:S(2)}) collective-permute-start(f32[4,8,2048]{2,1,0:T(8,128)S(1)} %get-tuple-element.139), channel_id=1, source_target_pairs={{0,8},{1,9},{2,10},{3,11},{4,12},{5,13},{6,14},{7,15},{8,16},{9,17... | collective-permute-start | bytes 786440 | tf_op jit(solution)/shard_map/ppermute | solution.py:526
  73.4 12.8 %collective-permute-start.24 = (f32[4,8,2048]{2,1,0:T(8,128)S(1)}, f32[4,8,2048]{2,1,0:T(8,128)S(1)}, u32[]{:S(2)}, u32[]{:S(2)}) collective-permute-start(f32[4,8,2048]{2,1,0:T(8,128)S(1)} %get-tuple-element.140), channel_id=1, source_target_pairs={{0,16},{1,17},{2,18},{3,19},{4,20},{5,21},{6,22},{7,23},{8,24},{9,... | collective-permute-start | bytes 786440 | tf_op jit(solution)/shard_map/ppermute | solution.py:526
  74.2 23.0 %copy-start.7 = (bf16[1,128,1024]{2,1,0:T(8,128)(2,1)S(1)}, bf16[1,128,1024]{2,1,0:T(8,128)(2,1)}, u32[]{:S(2)}) copy-start(bf16[1,128,1024]{2,1,0:T(8,128)(2,1)} %param.10) | copy-start | bytes 786436
  74.2 13.3 %collective-permute-start.25 = (f32[4,8,2048]{2,1,0:T(8,128)S(1)}, f32[4,8,2048]{2,1,0:T(8,128)S(1)}, u32[]{:S(2)}, u32[]{:S(2)}) collective-permute-start(f32[4,8,2048]{2,1,0:T(8,128)S(1)} %get-tuple-element.141), channel_id=1, source_target_pairs={{0,24},{1,25},{2,26},{3,27},{4,28},{5,29},{6,30},{7,31},{8,0},{9,1... | collective-permute-start | bytes 786440 | tf_op jit(solution)/shard_map/ppermute | solution.py:526
  76.6 24.5 %copy-start.4 = (bf16[128,2048]{1,0:T(8,128)(2,1)}, bf16[128,2048]{1,0:T(8,128)(2,1)S(1)}, u32[]{:S(2)}) copy-start(bf16[128,2048]{1,0:T(8,128)(2,1)S(1)} %convolution_convert_fusion.refs_1_) | copy-start | bytes 1572868
  77.6 10.0 %collective-permute-start.29 = (f32[128,128]{1,0:T(8,128)S(1)}, f32[128,128]{1,0:T(8,128)S(1)}, u32[]{:S(2)}, u32[]{:S(2)}) collective-permute-start(f32[128,128]{1,0:T(8,128)S(1)} %get-tuple-element.146), channel_id=1, source_target_pairs={{0,2},{1,3},{2,4},{3,5},{4,6},{5,7},{6,0},{7,1},{8,10},{9,11},{10,... | collective-permute-start | bytes 196616 | tf_op jit(solution)/shard_map/ppermute | solution.py:521
  77.8 9.8 %collective-permute-start.30 = (f32[128,128]{1,0:T(8,128)S(1)}, f32[128,128]{1,0:T(8,128)S(1)}, u32[]{:S(2)}, u32[]{:S(2)}) collective-permute-start(f32[128,128]{1,0:T(8,128)S(1)} %get-tuple-element.147), channel_id=1, source_target_pairs={{0,4},{1,5},{2,6},{3,7},{4,0},{5,1},{6,2},{7,3},{8,12},{9,13},{10,... | collective-permute-start | bytes 196616 | tf_op jit(solution)/shard_map/ppermute | solution.py:521
  81.6 6.0 %collective-permute-start.31 = (f32[128,128]{1,0:T(8,128)S(1)}, f32[128,128]{1,0:T(8,128)S(1)}, u32[]{:S(2)}, u32[]{:S(2)}) collective-permute-start(f32[128,128]{1,0:T(8,128)S(1)} %get-tuple-element.148), channel_id=1, source_target_pairs={{0,6},{1,7},{2,0},{3,1},{4,2},{5,3},{6,4},{7,5},{8,14},{9,15},{10,... | collective-permute-start | bytes 196616 | tf_op jit(solution)/shard_map/ppermute | solution.py:521
  87.9 9.3 %collective-permute-start.32 = (f32[4,128,128]{2,1,0:T(8,128)S(1)}, f32[4,128,128]{2,1,0:T(8,128)S(1)}, u32[]{:S(2)}, u32[]{:S(2)}) collective-permute-start(f32[4,128,128]{2,1,0:T(8,128)S(1)} %get-tuple-element.151), channel_id=1, source_target_pairs={{0,1},{1,0},{2,3},{3,2},{4,5},{5,4},{6,7},{7,6},{8,9},{9,8},{10,11... | collective-permute-start | bytes 786440 | tf_op jit(solution)/shard_map/ppermute | solution.py:517
  93.1 8.0 %collective-permute-start.33 = (f32[8,2048]{1,0:T(8,128)S(1)}, f32[8,2048]{1,0:T(8,128)S(1)}, u32[]{:S(2)}, u32[]{:S(2)}) collective-permute-start(f32[8,2048]{1,0:T(8,128)S(1)} %get-tuple-element.174), channel_id=1, source_target_pairs={{0,2},{1,3},{2,4},{3,5},{4,6},{5,7},{6,0},{7,1},{8,10},{9,11},{10,... | collective-permute-start | bytes 196616 | tf_op jit(solution)/shard_map/ppermute | solution.py:521
  93.1 8.0 %collective-permute-start.34 = (f32[8,2048]{1,0:T(8,128)S(1)}, f32[8,2048]{1,0:T(8,128)S(1)}, u32[]{:S(2)}, u32[]{:S(2)}) collective-permute-start(f32[8,2048]{1,0:T(8,128)S(1)} %get-tuple-element.175), channel_id=1, source_target_pairs={{0,4},{1,5},{2,6},{3,7},{4,0},{5,1},{6,2},{7,3},{8,12},{9,13},{10,... | collective-permute-start | bytes 196616 | tf_op jit(solution)/shard_map/ppermute | solution.py:521
  97.2 3.9 %collective-permute-start.35 = (f32[8,2048]{1,0:T(8,128)S(1)}, f32[8,2048]{1,0:T(8,128)S(1)}, u32[]{:S(2)}, u32[]{:S(2)}) collective-permute-start(f32[8,2048]{1,0:T(8,128)S(1)} %get-tuple-element.176), channel_id=1, source_target_pairs={{0,6},{1,7},{2,0},{3,1},{4,2},{5,3},{6,4},{7,5},{8,14},{9,15},{10,... | collective-permute-start | bytes 196616 | tf_op jit(solution)/shard_map/ppermute | solution.py:521

commit v6 on v5

--- a/solution.py
+++ b/solution.py
@@ -370,26 +370,24 @@
 
 
 def early_grads_kernel(
-    half, mine_ref, other_ref, uw_ref, do_ref, inside_ref, attn_ref, kn_ref, qn_ref, growth_ref, iq_ref, *refs
+    mine_ref, other_ref, uw_ref, do_ref, inside_ref, attn_ref, kn_ref, qn_ref, growth_ref, iq_ref,
+    dq_ref, delta_ref, dkn_ref, dd_ref, carried_ref, rowpart_ref, colpart_ref,
 ):
-    dq_ref, delta_ref, dkn_ref, dd_ref, carried_ref, rowpart_ref, colpart_ref = refs[half:]
     first = place()[3] == 0
     _, cols = iotas()
     row8 = lax.broadcasted_iota(jnp.int32, (H, C), 0)
     row_all = jnp.zeros((C, C), f32)
     col_all = jnp.zeros((H, C), f32)
-    if half:
-        dq_ref[:, : 4 * C] = refs[0][...]
-    group = range(4 * half, 4 * half + 4)
+    group = HEADS
     state = {h: pick(first, mine_ref, other_ref, h) for h in group}
     moved = {
         h: mm(jnp.concatenate([uw_ref[h, :, :C], kn_ref[h]], axis=0), state[h]) for h in group
     }
     delta = {h: uw_ref[h, :, C:] - moved[h][:C] for h in group}
     for h in group:
-        dd_ref[h % 4] = tn(attn_ref[h], do_ref[h])
-        delta_ref[h % 4] = delta[h]
-        carried_ref[h % 4] = moved[h][C:]
+        dd_ref[h] = tn(attn_ref[h], do_ref[h])
+        delta_ref[h] = delta[h]
+        carried_ref[h] = moved[h][C:]
     both = {
         h: mm(do_ref[h], jnp.concatenate([delta[h], state[h]], axis=0), NT) for h in group
     }
@@ -397,7 +395,7 @@
     back = {h: both[h][:, C:] * growth_ref[:, h : h + 1] for h in group}
     dqn = {h: back[h] + mm(dqk[h], kn_ref[h]) for h in group}
     for h in group:
-        dkn_ref[h % 4] = tn(dqk[h], qn_ref[h])
+        dkn_ref[h] = tn(dqk[h], qn_ref[h])
     for h in group:
         qn = qn_ref[h]
         dq = iq_ref[:, h : h + 1] * (
@@ -419,18 +417,18 @@
     v_ref, mine_ref, other_ref, dmine_ref, dother_ref, inside_ref, kk_ref, kn_ref, invt_ref,
     growth_ref, fading_ref, beta_ref, ik_ref, last_ref, *refs
 ):
-    early = refs[: 2 * EARLY]
-    dk_ref, dv_ref, db_ref, dg_ref, mark_ref = refs[2 * EARLY :]
+    early = refs[:EARLY]
+    dk_ref, dv_ref, db_ref, dg_ref, mark_ref = refs[EARLY:]
     first = place()[3] == 0
     rows, cols = iotas()
     row8 = lax.broadcasted_iota(jnp.int32, (H, C), 0)
-    row_all = early[4][...] + early[EARLY + 4][...]
-    col_all = early[5][...] + early[EARLY + 5][...]
+    row_all = early[4][...]
+    col_all = early[5][...]
     db_all = jnp.zeros((C, C), f32)
     is_last = lax.broadcasted_iota(jnp.int32, (C, 1), 0) == C - 1
-    for group in (range(0, 4), range(4, 8)):
+    for group in (HEADS,):
         delta, dkn, dd, carried = (
-            {h: early[h // 4 * EARLY + part][h % 4] for h in group} for part in range(4)
+            {h: early[part][h] for h in group} for part in range(4)
         )
         state = {h: pick(first, mine_ref, other_ref, h) for h in group}
         dstate = {h: pick(first, dmine_ref, dother_ref, h) for h in group}
@@ -595,22 +593,18 @@
     own = parts[0]
     parts = around_z(parts[:4])
 
-    def early_grads(half, token, *done):
-        return call(
-            functools.partial(early_grads_kernel, half),
-            [((C, 4 * (1 + half) * C), bf16)] + [four] * 4 + [one, ((H, C), f32)],
-            0, mine, other, uw, do, inside, attn, kn, qn, growth, iq, *done, us=2.2, after=(token,),
-        )
-
-    early0 = early_grads(0, own)
-    early1 = early_grads(1, own, early0[0])
+    early = call(
+        early_grads_kernel,
+        [wide] + [all1] * 4 + [one, ((H, C), f32)],
+        0, mine, other, uw, do, inside, attn, kn, qn, growth, iq, us=2.2, after=(own,),
+    )
     mixed = lax.dot_general(n16, out_weight, NN, preferred_element_type=f32).astype(bf16)
     reach, total = call(group_back_kernel, [four, one], 0, *parts, maps)
     parts = around_x([total] * 4)
     wkeep, wsend = call(
         wgrad_kernel,
         [((16, 8, 2048), f32)] * 2,
-        0, *chunks, cot, below, above, lower, upper, us=2.5, after=(total, early1[1]),
+        0, *chunks, cot, below, above, lower, upper, us=2.5, after=(total, early[1]),
     )
     wrecv = swap_core(wsend)
     wparts = call(wsum_pair_kernel, [((4, 8, 2048), f32)] * 4, 0, wkeep, wrecv)
@@ -630,7 +624,7 @@
         late_grads_kernel,
         [wide, wide, ((H, C), f32), ((H, C), f32), ((H, C), f32)],
         0, v, mine, other, dmine, dother, inside, kk, kn, invt, growth, fading, beta, ik, last_decay,
-        *early0[1:], *early1[1:], us=6, after=(wparts[0],),
+        *early[1:], us=6, after=(wparts[0],),
     )
     wparts = around_z(wparts)
     scale = 1.0 / math.sqrt(n_all)
@@ -639,7 +633,7 @@
         wsum_last_kernel(scale, a0, a1, a2, a3, out)
 
     (weight_grad,) = call(last, [((8, 2048), f32)], 0, *wparts, after=(mark,))
-    dq = early1[0]
+    dq = early[0]
     return (mixed[None], dq[None], dk[None], dv[None], db.T[None], dg.T[None], weight_grad)
 
 

time: 102 us -> 102 us (level)
    pallas_call x19 -> x18, Pallas kernels: 22.7 us -> 22.2 us  [call(): pl.pallas_call(body, out_shape=[jax.ShapeDtypeStruct(s, d) for s, d in ou...]
where the time goes in v6:
time: 102 us
  starting transfers between devices  53.2 us (52%)
  Pallas kernels  22.2 us (22%)
  waiting for transfers between devices  19.6 us (19%)
  matrix products  4.61 us (5%)
  local copies, waits for them, and re-layouts  1.11 us (1%)
    pallas_call x18, Pallas kernels, call(): pl.pallas_call(body, out_shape=[jax.ShapeDtypeStruct(s, d) for s, d in ou...  22.2 us
    ppermute x15, starting transfers between devices, around_z(): lax.ppermute(parts[r], 'seq', seq_perm(0, r))  21.7 us
    ppermute x9, starting transfers between devices, around_x(): lax.ppermute(parts[r], 'seq', seq_perm(r, 0))  12.3 us
    ppermute x5, starting transfers between devices, swap_core(): return lax.ppermute(x, 'seq', seq_perm(0, 0, 1))  11.8 us
    ppermute x9, waiting for transfers between devices, around_x(): lax.ppermute(parts[r], 'seq', seq_perm(r, 0))  7.52 us
    ppermute x7, starting transfers between devices, step_dp(): return lax.ppermute(x, 'dp', [(i, (i + r) % 4) for i in range(4)])  7.38 us
    ppermute x15, waiting for transfers between devices, around_z(): lax.ppermute(parts[r], 'seq', seq_perm(0, r))  6.52 us
    ppermute x7, waiting for transfers between devices, step_dp(): return lax.ppermute(x, 'dp', [(i, (i + r) % 4) for i in range(4)])  4.43 us
  transfers between devices with their start and end apart: 36, of which 12 were waited for; matrix products, arithmetic and copies ran while one was open for 5% of the time, Pallas kernels for 13%

profile of v6, /device:TPU:1, one launch (start us, length us, event | category | flops | bytes accessed | tf_op | source)
XLA Modules:
  0.0 101.7 jit_solution(12722310588867693152)
XLA Ops:
  0.6 6.8 %shard_map.135 = (f32[4,128,256]{2,1,0:T(8,128)}, f32[4,128,256]{2,1,0:T(8,128)}, f32[8,128,128]{2,1,0:T(8,128)}, f32[8,128,256]{2,1,0:T(8,128)}, f32[128,2048]{1,0:T(8,128)}) custom-call(s32[1,2]{1,0:T(1,128)} %refs_1_.1, bf16[8,128]{1,0:T(8,128)(2,1)} %bitcast.35, f32[8,128]{1,0:T(8,128)} %bitcast.33, bf16[128,1024]{1,0:T(8,128)(2,1)} %bitcast.28, ...), custom_call_target="tpu_custom_call" | custom-call | bytes 1 | tf_op jit(solution)/shard_map/pallas_call | solution.py:123
  7.4 1.5 %collective-permute-start = (f32[4,128,256]{2,1,0:T(8,128)}, f32[4,128,256]{2,1,0:T(8,128)S(1)}, u32[]{:S(2)}, u32[]{:S(2)}) collective-permute-start(f32[4,128,256]{2,1,0:T(8,128)} %get-tuple-element.87), channel_id=1, source_target_pairs={{0,1},{1,0},{2,3},{3,2},{4,5},{5,4},{6,7},{7,6},{8,9},{9,8},{10,11... | collective-permute-start | bytes 1572872 | tf_op jit(solution)/shard_map/ppermute | solution.py:515
  8.9 1.4 %collective-permute-start.18 = (f32[128,2048]{1,0:T(8,128)}, f32[128,2048]{1,0:T(8,128)S(1)}, u32[]{:S(2)}, u32[]{:S(2)}) collective-permute-start(f32[128,2048]{1,0:T(8,128)} %get-tuple-element.85.refs_1_), channel_id=1, source_target_pairs={{0,32},{32,64},{64,96},{96,0},{1,33},{33,65},{65,97},{97,1},{2,34}... | collective-permute-start | bytes 3145736 | tf_op jit(solution)/shard_map/ppermute | solution.py:529
  10.3 1.4 %collective-permute-start.19 = (f32[128,2048]{1,0:T(8,128)}, f32[128,2048]{1,0:T(8,128)S(1)}, u32[]{:S(2)}, u32[]{:S(2)}) collective-permute-start(f32[128,2048]{1,0:T(8,128)} %get-tuple-element.85.refs_1_), channel_id=1, source_target_pairs={{0,96},{32,0},{64,32},{96,64},{1,97},{33,1},{65,33},{97,65},{2,98}... | collective-permute-start | bytes 3145736 | tf_op jit(solution)/shard_map/ppermute | solution.py:529
  11.8 1.0 %copy-done.1 = f32[4,128,256]{2,1,0:T(8,128)S(1)} copy-done((f32[4,128,256]{2,1,0:T(8,128)S(1)}, f32[4,128,256]{2,1,0:T(8,128)}, u32[]{:S(2)}) %copy-start.1) | copy-done | bytes 524312
  12.9 0.4 shard_map.136
  13.2 1.7 %collective-permute-start.1 = (f32[128,256]{1,0:T(8,128)S(1)}, f32[128,256]{1,0:T(8,128)S(1)}, u32[]{:S(2)}, u32[]{:S(2)}) collective-permute-start(f32[128,256]{1,0:T(8,128)S(1)} %get-tuple-element.89), channel_id=1, source_target_pairs={{0,2},{1,3},{2,4},{3,5},{4,6},{5,7},{6,0},{7,1},{8,10},{9,11},{10,... | collective-permute-start | bytes 393224 | tf_op jit(solution)/shard_map/ppermute | solution.py:519
  15.0 3.3 %collective-permute-start.2 = (f32[128,256]{1,0:T(8,128)S(1)}, f32[128,256]{1,0:T(8,128)S(1)}, u32[]{:S(2)}, u32[]{:S(2)}) collective-permute-start(f32[128,256]{1,0:T(8,128)S(1)} %get-tuple-element.90), channel_id=1, source_target_pairs={{0,4},{1,5},{2,6},{3,7},{4,0},{5,1},{6,2},{7,3},{8,12},{9,13},{10,... | collective-permute-start | bytes 393224 | tf_op jit(solution)/shard_map/ppermute | solution.py:519
  18.3 0.7 collective-permute-start.3
  19.0 3.9 %fusion.refs_0_.refs_3_ = f32[128,1024]{1,0:T(8,128)S(1)} fusion(bf16[1024,2048]{1,0:T(8,128)(2,1)} %param.14, bf16[1,128,2048]{2,1,0:T(8,128)(2,1)} %param.15), kind=kOutput, calls=%fused_computation.1 | convolution fusion | flops 536870912 | bytes 5242880 | tf_op jit(solution)/shard_map/dot_general | solution.py:562
  22.9 1.2 %collective-permute-done.2.refs_4_ = f32[128,256]{1,0:T(8,128)S(1)} collective-permute-done((f32[128,256]{1,0:T(8,128)S(1)}, f32[128,256]{1,0:T(8,128)S(1)}, u32[]{:S(2)}, u32[]{:S(2)}) %collective-permute-start.2) | collective-permute-done | bytes 131104 | tf_op jit(solution)/shard_map/ppermute | solution.py:519
  24.1 0.6 shard_map.137
  24.7 1.3 %collective-permute-start.4 = (f32[128,256]{1,0:T(8,128)S(1)}, f32[128,256]{1,0:T(8,128)S(1)}, u32[]{:S(2)}, u32[]{:S(2)}) collective-permute-start(f32[128,256]{1,0:T(8,128)S(1)} %get-tuple-element.92.refs_0_.refs_1_), channel_id=1, source_target_pairs={{0,8},{1,9},{2,10},{3,11},{4,12},{5,13},{6,14},{7,15},{8,16},{9,17... | collective-permute-start | bytes 393224 | tf_op jit(solution)/shard_map/ppermute | solution.py:524
  26.0 2.5 %collective-permute-start.5 = (f32[128,256]{1,0:T(8,128)S(1)}, f32[128,256]{1,0:T(8,128)S(1)}, u32[]{:S(2)}, u32[]{:S(2)}) collective-permute-start(f32[128,256]{1,0:T(8,128)S(1)} %get-tuple-element.92.refs_0_.refs_1_), channel_id=1, source_target_pairs={{0,16},{1,17},{2,18},{3,19},{4,20},{5,21},{6,22},{7,23},{8,24},{9,... | collective-permute-start | bytes 393224 | tf_op jit(solution)/shard_map/ppermute | solution.py:524
  28.4 1.1 %collective-permute-start.6 = (f32[128,256]{1,0:T(8,128)S(1)}, f32[128,256]{1,0:T(8,128)S(1)}, u32[]{:S(2)}, u32[]{:S(2)}) collective-permute-start(f32[128,256]{1,0:T(8,128)S(1)} %get-tuple-element.92.refs_0_.refs_1_), channel_id=1, source_target_pairs={{0,24},{1,25},{2,26},{3,27},{4,28},{5,29},{6,30},{7,31},{8,0},{9,1... | collective-permute-start | bytes 393224 | tf_op jit(solution)/shard_map/ppermute | solution.py:524
  29.6 2.2 %shard_map.138 = (f32[8,128,256]{2,1,0:T(8,128)S(1)}, f32[8,128,128]{2,1,0:T(8,128)S(1)}, f32[8,128,128]{2,1,0:T(8,128)S(1)}, f32[8,128,128]{2,1,0:T(8,128)S(1)}...) custom-call(f32[128,256]{1,0:T(8,128)S(1)} %get-tuple-element.92.ref, ...), custom_call_target="tpu_custom_call" | custom-call | bytes 1 | tf_op jit(solution)/shard_map/pallas_call | solution.py:123
  31.8 1.2 %collective-permute-done.5.refs_3_ = f32[128,256]{1,0:T(8,128)S(1)} collective-permute-done((f32[128,256]{1,0:T(8,128)S(1)}, f32[128,256]{1,0:T(8,128)S(1)}, u32[]{:S(2)}, u32[]{:S(2)}) %collective-permute-start.5) | collective-permute-done | bytes 131104 | tf_op jit(solution)/shard_map/ppermute | solution.py:524
  33.0 0.6 collective-permute-done.6.refs_4_
  33.6 0.6 shard_map.139
  34.3 1.9 %collective-permute-start.7 = (f32[128,128]{1,0:T(8,128)S(1)}, f32[128,128]{1,0:T(8,128)S(1)}, u32[]{:S(2)}, u32[]{:S(2)}) collective-permute-start(f32[128,128]{1,0:T(8,128)S(1)} %get-tuple-element.98), channel_id=1, source_target_pairs={{0,2},{1,3},{2,4},{3,5},{4,6},{5,7},{6,0},{7,1},{8,10},{9,11},{10,... | collective-permute-start | bytes 196616 | tf_op jit(solution)/shard_map/ppermute | solution.py:519
  36.2 2.0 %collective-permute-start.8 = (f32[128,128]{1,0:T(8,128)S(1)}, f32[128,128]{1,0:T(8,128)S(1)}, u32[]{:S(2)}, u32[]{:S(2)}) collective-permute-start(f32[128,128]{1,0:T(8,128)S(1)} %get-tuple-element.99), channel_id=1, source_target_pairs={{0,4},{1,5},{2,6},{3,7},{4,0},{5,1},{6,2},{7,3},{8,12},{9,13},{10,... | collective-permute-start | bytes 196616 | tf_op jit(solution)/shard_map/ppermute | solution.py:519
  38.1 0.5 collective-permute-start.9
  38.7 2.1 %collective-permute-done.8.refs_2_ = f32[128,128]{1,0:T(8,128)S(1)} collective-permute-done((f32[128,128]{1,0:T(8,128)S(1)}, f32[128,128]{1,0:T(8,128)S(1)}, u32[]{:S(2)}, u32[]{:S(2)}) %collective-permute-start.8) | collective-permute-done | bytes 65568 | tf_op jit(solution)/shard_map/ppermute | solution.py:519
  40.8 0.7 collective-permute-done.9.refs_3_
  41.5 0.3 shard_map.140
  41.8 3.4 %collective-permute-start.10 = (f32[4,128,128]{2,1,0:T(8,128)S(1)}, f32[4,128,128]{2,1,0:T(8,128)S(1)}, u32[]{:S(2)}, u32[]{:S(2)}) collective-permute-start(f32[4,128,128]{2,1,0:T(8,128)S(1)} %get-tuple-element.102), channel_id=1, source_target_pairs={{0,1},{1,0},{2,3},{3,2},{4,5},{5,4},{6,7},{7,6},{8,9},{9,8},{10,11... | collective-permute-start | bytes 786440 | tf_op jit(solution)/shard_map/ppermute | solution.py:515
  45.3 0.5 collective-permute-start.20
  45.8 2.2 %collective-permute-start.21 = (f32[64,2048]{1,0:T(8,128)S(1)}, f32[64,2048]{1,0:T(8,128)S(1)}, u32[]{:S(2)}, u32[]{:S(2)}) collective-permute-start(f32[64,2048]{1,0:T(8,128)S(1)} %get-tuple-element.127), channel_id=1, source_target_pairs={{0,96},{32,0},{64,32},{96,64},{1,97},{33,1},{65,33},{97,65},{2,98}... | collective-permute-start | bytes 1572872 | tf_op jit(solution)/shard_map/ppermute | solution.py:529
  48.1 1.0 shard_map.141
  49.0 0.7 collective-permute-start.11
  49.7 1.2 %collective-permute-done.11.refs_1_.refs_7_ = f32[4,128,128]{2,1,0:T(8,128)S(1)} collective-permute-done((f32[4,128,128]{2,1,0:T(8,128)S(1)}, f32[4,128,128]{2,1,0:T(8,128)S(1)}, u32[]{:S(2)}, u32[]{:S(2)}) %collective-permute-start.11) | collective-permute-done | bytes 262176 | tf_op jit(solution)/shard_map/ppermute | solution.py:515
  50.9 0.3 shard_map.142
  51.2 0.1 collective-permute-start.12
  51.3 2.7 %collective-permute-start.13 = (f32[128,128]{1,0:T(8,128)S(1)}, f32[128,128]{1,0:T(8,128)S(1)}, u32[]{:S(2)}, u32[]{:S(2)}) collective-permute-start(f32[128,128]{1,0:T(8,128)S(1)} %get-tuple-element.117), channel_id=1, source_target_pairs={{0,4},{1,5},{2,6},{3,7},{4,0},{5,1},{6,2},{7,3},{8,12},{9,13},{10,... | collective-permute-start | bytes 196616 | tf_op jit(solution)/shard_map/ppermute | solution.py:519
  54.0 0.6 collective-permute-start.14
  54.6 1.3 %collective-permute-done.12.refs_1_ = f32[128,128]{1,0:T(8,128)S(1)} collective-permute-done((f32[128,128]{1,0:T(8,128)S(1)}, f32[128,128]{1,0:T(8,128)S(1)}, u32[]{:S(2)}, u32[]{:S(2)}) %collective-permute-start.12) | collective-permute-done | bytes 65568 | tf_op jit(solution)/shard_map/ppermute | solution.py:519
  55.9 1.0 %collective-permute-done.13.refs_2_ = f32[128,128]{1,0:T(8,128)S(1)} collective-permute-done((f32[128,128]{1,0:T(8,128)S(1)}, f32[128,128]{1,0:T(8,128)S(1)}, u32[]{:S(2)}, u32[]{:S(2)}) %collective-permute-start.13) | collective-permute-done | bytes 65568 | tf_op jit(solution)/shard_map/ppermute | solution.py:519
  56.9 0.9 collective-permute-start.16
  57.9 0.9 collective-permute-start.17
  58.8 2.3 %shard_map.143 = (bf16[128,1024]{1,0:T(8,128)(2,1)}, f32[8,128,128]{2,1,0:T(8,128)S(1)}, f32[8,128,128]{2,1,0:T(8,128)S(1)}, f32[8,128,128]{2,1,0:T(8,128)S(1)},...) custom-call(f32[128,128]{1,0:T(8,128)S(1)} %get-tuple-element.107.refs_0_, ...), custom_call_target="tpu_custom_call" | custom-call | bytes 1 | tf_op jit(solution)/shard_map/pallas_call | solution.py:123
  61.1 0.5 shard_map.144
  61.7 4.4 %collective-permute-done.16.refs_4_ = f32[128,256]{1,0:T(8,128)S(1)} collective-permute-done((f32[128,256]{1,0:T(8,128)S(1)}, f32[128,256]{1,0:T(8,128)S(1)}, u32[]{:S(2)}, u32[]{:S(2)}) %collective-permute-start.16) | collective-permute-done | bytes 131104 | tf_op jit(solution)/shard_map/ppermute | solution.py:529
  66.1 1.3 %shard_map.146 = (f32[16,8,2048]{2,1,0:T(8,128)S(1)}, f32[16,8,2048]{2,1,0:T(8,128)S(1)}) custom-call(f32[128,128]{1,0:T(8,128)S(1)} %get-tuple-element.120.refs_0_.refs_2_, f32[8,128,128]{2,1,0:T(8,128)S(1)} %get-tuple-element.121.refs_1_.refs_15_, f32[128,256]{1,0:T(8,128)S(1)} %get-tuple-element.122.refs_2_, ...), custom_call_target="tpu_custom_call" | custom-call | bytes 1 | tf_op jit(solution)/shard_map/pallas_call | solution.py:123
  67.3 1.0 collective-permute-start.22
  68.3 1.1 %collective-permute-start.26 = (f32[128,128]{1,0:T(8,128)S(1)}, f32[128,128]{1,0:T(8,128)S(1)}, u32[]{:S(2)}, u32[]{:S(2)}) collective-permute-start(f32[128,128]{1,0:T(8,128)S(1)} %get-tuple-element.120.refs_0_.refs_2_), channel_id=1, source_target_pairs={{0,8},{1,9},{2,10},{3,11},{4,12},{5,13},{6,14},{7,15},{8,16},{9,17... | collective-permute-start | bytes 196616 | tf_op jit(solution)/shard_map/ppermute | solution.py:524
  69.4 2.4 %collective-permute-start.27 = (f32[128,128]{1,0:T(8,128)S(1)}, f32[128,128]{1,0:T(8,128)S(1)}, u32[]{:S(2)}, u32[]{:S(2)}) collective-permute-start(f32[128,128]{1,0:T(8,128)S(1)} %get-tuple-element.120.refs_0_.refs_2_), channel_id=1, source_target_pairs={{0,16},{1,17},{2,18},{3,19},{4,20},{5,21},{6,22},{7,23},{8,24},{9,... | collective-permute-start | bytes 196616 | tf_op jit(solution)/shard_map/ppermute | solution.py:524
  71.7 1.0 %collective-permute-start.28 = (f32[128,128]{1,0:T(8,128)S(1)}, f32[128,128]{1,0:T(8,128)S(1)}, u32[]{:S(2)}, u32[]{:S(2)}) collective-permute-start(f32[128,128]{1,0:T(8,128)S(1)} %get-tuple-element.120.refs_0_.refs_2_), channel_id=1, source_target_pairs={{0,24},{1,25},{2,26},{3,27},{4,28},{5,29},{6,30},{7,31},{8,0},{9,1... | collective-permute-start | bytes 196616 | tf_op jit(solution)/shard_map/ppermute | solution.py:524
  72.8 0.1 shard_map.147
  72.9 0.5 collective-permute-start.23
  73.4 0.8 collective-permute-start.24
  74.2 1.7 %collective-permute-start.25 = (f32[4,8,2048]{2,1,0:T(8,128)S(1)}, f32[4,8,2048]{2,1,0:T(8,128)S(1)}, u32[]{:S(2)}, u32[]{:S(2)}) collective-permute-start(f32[4,8,2048]{2,1,0:T(8,128)S(1)} %get-tuple-element.133), channel_id=1, source_target_pairs={{0,24},{1,25},{2,26},{3,27},{4,28},{5,29},{6,30},{7,31},{8,0},{9,1... | collective-permute-start | bytes 786440 | tf_op jit(solution)/shard_map/ppermute | solution.py:524
  75.9 0.7 convolution_convert_fusion.refs_1_
  76.7 0.9 shard_map.149
  77.6 0.2 collective-permute-start.29
  77.8 2.9 %collective-permute-start.30 = (f32[128,128]{1,0:T(8,128)S(1)}, f32[128,128]{1,0:T(8,128)S(1)}, u32[]{:S(2)}, u32[]{:S(2)}) collective-permute-start(f32[128,128]{1,0:T(8,128)S(1)} %get-tuple-element.139), channel_id=1, source_target_pairs={{0,4},{1,5},{2,6},{3,7},{4,0},{5,1},{6,2},{7,3},{8,12},{9,13},{10,... | collective-permute-start | bytes 196616 | tf_op jit(solution)/shard_map/ppermute | solution.py:519
  80.6 0.9 collective-permute-done.23.refs_1_
  81.6 1.2 %collective-permute-start.31 = (f32[128,128]{1,0:T(8,128)S(1)}, f32[128,128]{1,0:T(8,128)S(1)}, u32[]{:S(2)}, u32[]{:S(2)}) collective-permute-start(f32[128,128]{1,0:T(8,128)S(1)} %get-tuple-element.140), channel_id=1, source_target_pairs={{0,6},{1,7},{2,0},{3,1},{4,2},{5,3},{6,4},{7,5},{8,14},{9,15},{10,... | collective-permute-start | bytes 196616 | tf_op jit(solution)/shard_map/ppermute | solution.py:519
  82.8 3.5 %collective-permute-done.24.refs_2_ = f32[4,8,2048]{2,1,0:T(8,128)S(1)} collective-permute-done((f32[4,8,2048]{2,1,0:T(8,128)S(1)}, f32[4,8,2048]{2,1,0:T(8,128)S(1)}, u32[]{:S(2)}, u32[]{:S(2)}) %collective-permute-start.24) | collective-permute-done | bytes 262176 | tf_op jit(solution)/shard_map/ppermute | solution.py:524
  86.2 1.3 %collective-permute-done.25.refs_3_ = f32[4,8,2048]{2,1,0:T(8,128)S(1)} collective-permute-done((f32[4,8,2048]{2,1,0:T(8,128)S(1)}, f32[4,8,2048]{2,1,0:T(8,128)S(1)}, u32[]{:S(2)}, u32[]{:S(2)}) %collective-permute-start.25) | collective-permute-done | bytes 262176 | tf_op jit(solution)/shard_map/ppermute | solution.py:524
  87.6 0.3 shard_map.150
  87.9 5.3 %collective-permute-start.32 = (f32[4,128,128]{2,1,0:T(8,128)S(1)}, f32[4,128,128]{2,1,0:T(8,128)S(1)}, u32[]{:S(2)}, u32[]{:S(2)}) collective-permute-start(f32[4,128,128]{2,1,0:T(8,128)S(1)} %get-tuple-element.143), channel_id=1, source_target_pairs={{0,1},{1,0},{2,3},{3,2},{4,5},{5,4},{6,7},{7,6},{8,9},{9,8},{10,11... | collective-permute-start | bytes 786440 | tf_op jit(solution)/shard_map/ppermute | solution.py:515
  93.1 4.0 %collective-permute-start.34 = (f32[8,2048]{1,0:T(8,128)S(1)}, f32[8,2048]{1,0:T(8,128)S(1)}, u32[]{:S(2)}, u32[]{:S(2)}) collective-permute-start(f32[8,2048]{1,0:T(8,128)S(1)} %get-tuple-element.161), channel_id=1, source_target_pairs={{0,4},{1,5},{2,6},{3,7},{4,0},{5,1},{6,2},{7,3},{8,12},{9,13},{10,... | collective-permute-start | bytes 196616 | tf_op jit(solution)/shard_map/ppermute | solution.py:519
  97.2 3.9 %shard_map.151 = (bf16[128,1024]{1,0:T(8,128)(2,1)}, bf16[128,1024]{1,0:T(8,128)(2,1)}, f32[8,128]{1,0:T(8,128)}, f32[8,128]{1,0:T(8,128)}, f32[8,128]{1,0:T(8,128)S(1)}) custom-call(f32[8,2048]{1,0:T(8,128)S(1)} %get-tuple-element.134.refs_0_.refs_1_, bf16[128,1024]{1,0:T(8,128)(2,1)S(1)} %bitcast.31, ...), custom_call_target="tpu_custom_call" | custom-call | bytes 1 | tf_op jit(solution)/shard_map/pallas_call | solution.py:123
  101.1 0.7 shard_map.152
  (56 shorter events, 0.4 us)
Async XLA Ops:
  7.4 4.3 %collective-permute-start = (f32[4,128,256]{2,1,0:T(8,128)}, f32[4,128,256]{2,1,0:T(8,128)S(1)}, u32[]{:S(2)}, u32[]{:S(2)}) collective-permute-start(f32[4,128,256]{2,1,0:T(8,128)} %get-tuple-element.87), channel_id=1, source_target_pairs={{0,1},{1,0},{2,3},{3,2},{4,5},{5,4},{6,7},{7,6},{8,9},{9,8},{10,11... | collective-permute-start | bytes 1572872 | tf_op jit(solution)/shard_map/ppermute | solution.py:515
  8.9 36.3 %collective-permute-start.18 = (f32[128,2048]{1,0:T(8,128)}, f32[128,2048]{1,0:T(8,128)S(1)}, u32[]{:S(2)}, u32[]{:S(2)}) collective-permute-start(f32[128,2048]{1,0:T(8,128)} %get-tuple-element.85.refs_1_), channel_id=1, source_target_pairs={{0,32},{32,64},{64,96},{96,0},{1,33},{33,65},{65,97},{97,1},{2,34}... | collective-permute-start | bytes 3145736 | tf_op jit(solution)/shard_map/ppermute | solution.py:529
  10.3 34.9 %collective-permute-start.19 = (f32[128,2048]{1,0:T(8,128)}, f32[128,2048]{1,0:T(8,128)S(1)}, u32[]{:S(2)}, u32[]{:S(2)}) collective-permute-start(f32[128,2048]{1,0:T(8,128)} %get-tuple-element.85.refs_1_), channel_id=1, source_target_pairs={{0,96},{32,0},{64,32},{96,64},{1,97},{33,1},{65,33},{97,65},{2,98}... | collective-permute-start | bytes 3145736 | tf_op jit(solution)/shard_map/ppermute | solution.py:529
  11.8 1.0 %copy-start.1 = (f32[4,128,256]{2,1,0:T(8,128)S(1)}, f32[4,128,256]{2,1,0:T(8,128)}, u32[]{:S(2)}) copy-start(f32[4,128,256]{2,1,0:T(8,128)} %get-tuple-element.86.refs_0_.refs_8_.refs_4_) | copy-start | bytes 1572868
  12.8 11.3 %copy-start.5 = (f32[128,2048]{1,0:T(8,128)S(1)}, f32[128,2048]{1,0:T(8,128)}, u32[]{:S(2)}) copy-start(f32[128,2048]{1,0:T(8,128)} %get-tuple-element.85.refs_1_) | copy-start | bytes 3145732
  12.8 16.7 %copy-start.2 = (f32[4,128,256]{2,1,0:T(8,128)S(1)}, f32[4,128,256]{2,1,0:T(8,128)}, u32[]{:S(2)}) copy-start(f32[4,128,256]{2,1,0:T(8,128)} %get-tuple-element.86.refs_0_.refs_8_.refs_4_) | copy-start | bytes 1572868
  12.8 16.7 %copy-start.3 = (f32[8,128,256]{2,1,0:T(8,128)S(1)}, f32[8,128,256]{2,1,0:T(8,128)}, u32[]{:S(2)}) copy-start(f32[8,128,256]{2,1,0:T(8,128)} %get-tuple-element.93.refs_6_.refs_3_) | copy-start | bytes 3145732
  12.8 16.7 %copy-start.6 = (bf16[1,128,1024]{2,1,0:T(8,128)(2,1)S(1)}, bf16[1,128,1024]{2,1,0:T(8,128)(2,1)}, u32[]{:S(2)}) copy-start(bf16[1,128,1024]{2,1,0:T(8,128)(2,1)} %param.9) | copy-start | bytes 786436
  12.8 16.7 %copy-start.8 = (f32[8,128,128]{2,1,0:T(8,128)S(1)}, f32[8,128,128]{2,1,0:T(8,128)}, u32[]{:S(2)}) copy-start(f32[8,128,128]{2,1,0:T(8,128)} %get-tuple-element.94.refs_7_) | copy-start | bytes 1572868
  12.8 16.7 %copy-start.9 = (bf16[1,128,1024]{2,1,0:T(8,128)(2,1)S(1)}, bf16[1,128,1024]{2,1,0:T(8,128)(2,1)}, u32[]{:S(2)}) copy-start(bf16[1,128,1024]{2,1,0:T(8,128)(2,1)} %param.8) | copy-start | bytes 786436
  12.8 16.7 %copy-start.10 = (f32[1,128,8]{1,2,0:T(8,128)S(1)}, f32[1,128,8]{1,2,0:T(8,128)}, u32[]{:S(2)}) copy-start(f32[1,128,8]{1,2,0:T(8,128)} %param.12) | copy-start | bytes 12292
  12.9 16.7 %copy-start.11 = (bf16[1,128,8]{1,2,0:T(8,128)(2,1)S(1)}, bf16[1,128,8]{1,2,0:T(8,128)(2,1)}, u32[]{:S(2)}) copy-start(bf16[1,128,8]{1,2,0:T(8,128)(2,1)} %param.11) | copy-start | bytes 6148
  12.9 16.7 %copy-start.12 = (s32[1,2]{1,0:T(1,128)S(1)}, s32[1,2]{1,0:T(1,128)}, u32[]{:S(2)}) copy-start(s32[1,2]{1,0:T(1,128)} %refs_1_.1) | copy-start | bytes 28
  13.2 9.6 %collective-permute-start.1 = (f32[128,256]{1,0:T(8,128)S(1)}, f32[128,256]{1,0:T(8,128)S(1)}, u32[]{:S(2)}, u32[]{:S(2)}) collective-permute-start(f32[128,256]{1,0:T(8,128)S(1)} %get-tuple-element.89), channel_id=1, source_target_pairs={{0,2},{1,3},{2,4},{3,5},{4,6},{5,7},{6,0},{7,1},{8,10},{9,11},{10,... | collective-permute-start | bytes 393224 | tf_op jit(solution)/shard_map/ppermute | solution.py:519
  15.0 9.1 %collective-permute-start.2 = (f32[128,256]{1,0:T(8,128)S(1)}, f32[128,256]{1,0:T(8,128)S(1)}, u32[]{:S(2)}, u32[]{:S(2)}) collective-permute-start(f32[128,256]{1,0:T(8,128)S(1)} %get-tuple-element.90), channel_id=1, source_target_pairs={{0,4},{1,5},{2,6},{3,7},{4,0},{5,1},{6,2},{7,3},{8,12},{9,13},{10,... | collective-permute-start | bytes 393224 | tf_op jit(solution)/shard_map/ppermute | solution.py:519
  18.3 5.8 %collective-permute-start.3 = (f32[128,256]{1,0:T(8,128)S(1)}, f32[128,256]{1,0:T(8,128)S(1)}, u32[]{:S(2)}, u32[]{:S(2)}) collective-permute-start(f32[128,256]{1,0:T(8,128)S(1)} %get-tuple-element.91), channel_id=1, source_target_pairs={{0,6},{1,7},{2,0},{3,1},{4,2},{5,3},{6,4},{7,5},{8,14},{9,15},{10,... | collective-permute-start | bytes 393224 | tf_op jit(solution)/shard_map/ppermute | solution.py:519
  24.7 7.1 %collective-permute-start.4 = (f32[128,256]{1,0:T(8,128)S(1)}, f32[128,256]{1,0:T(8,128)S(1)}, u32[]{:S(2)}, u32[]{:S(2)}) collective-permute-start(f32[128,256]{1,0:T(8,128)S(1)} %get-tuple-element.92.refs_0_.refs_1_), channel_id=1, source_target_pairs={{0,8},{1,9},{2,10},{3,11},{4,12},{5,13},{6,14},{7,15},{8,16},{9,17... | collective-permute-start | bytes 393224 | tf_op jit(solution)/shard_map/ppermute | solution.py:524
  26.0 7.1 %collective-permute-start.5 = (f32[128,256]{1,0:T(8,128)S(1)}, f32[128,256]{1,0:T(8,128)S(1)}, u32[]{:S(2)}, u32[]{:S(2)}) collective-permute-start(f32[128,256]{1,0:T(8,128)S(1)} %get-tuple-element.92.refs_0_.refs_1_), channel_id=1, source_target_pairs={{0,16},{1,17},{2,18},{3,19},{4,20},{5,21},{6,22},{7,23},{8,24},{9,... | collective-permute-start | bytes 393224 | tf_op jit(solution)/shard_map/ppermute | solution.py:524
  28.4 5.2 %collective-permute-start.6 = (f32[128,256]{1,0:T(8,128)S(1)}, f32[128,256]{1,0:T(8,128)S(1)}, u32[]{:S(2)}, u32[]{:S(2)}) collective-permute-start(f32[128,256]{1,0:T(8,128)S(1)} %get-tuple-element.92.refs_0_.refs_1_), channel_id=1, source_target_pairs={{0,24},{1,25},{2,26},{3,27},{4,28},{5,29},{6,30},{7,31},{8,0},{9,1... | collective-permute-start | bytes 393224 | tf_op jit(solution)/shard_map/ppermute | solution.py:524
  34.3 4.4 %collective-permute-start.7 = (f32[128,128]{1,0:T(8,128)S(1)}, f32[128,128]{1,0:T(8,128)S(1)}, u32[]{:S(2)}, u32[]{:S(2)}) collective-permute-start(f32[128,128]{1,0:T(8,128)S(1)} %get-tuple-element.98), channel_id=1, source_target_pairs={{0,2},{1,3},{2,4},{3,5},{4,6},{5,7},{6,0},{7,1},{8,10},{9,11},{10,... | collective-permute-start | bytes 196616 | tf_op jit(solution)/shard_map/ppermute | solution.py:519
  36.2 4.6 %collective-permute-start.8 = (f32[128,128]{1,0:T(8,128)S(1)}, f32[128,128]{1,0:T(8,128)S(1)}, u32[]{:S(2)}, u32[]{:S(2)}) collective-permute-start(f32[128,128]{1,0:T(8,128)S(1)} %get-tuple-element.99), channel_id=1, source_target_pairs={{0,4},{1,5},{2,6},{3,7},{4,0},{5,1},{6,2},{7,3},{8,12},{9,13},{10,... | collective-permute-start | bytes 196616 | tf_op jit(solution)/shard_map/ppermute | solution.py:519
  38.1 3.4 %collective-permute-start.9 = (f32[128,128]{1,0:T(8,128)S(1)}, f32[128,128]{1,0:T(8,128)S(1)}, u32[]{:S(2)}, u32[]{:S(2)}) collective-permute-start(f32[128,128]{1,0:T(8,128)S(1)} %get-tuple-element.100), channel_id=1, source_target_pairs={{0,6},{1,7},{2,0},{3,1},{4,2},{5,3},{6,4},{7,5},{8,14},{9,15},{10,... | collective-permute-start | bytes 196616 | tf_op jit(solution)/shard_map/ppermute | solution.py:519
  41.8 6.3 %collective-permute-start.10 = (f32[4,128,128]{2,1,0:T(8,128)S(1)}, f32[4,128,128]{2,1,0:T(8,128)S(1)}, u32[]{:S(2)}, u32[]{:S(2)}) collective-permute-start(f32[4,128,128]{2,1,0:T(8,128)S(1)} %get-tuple-element.102), channel_id=1, source_target_pairs={{0,1},{1,0},{2,3},{3,2},{4,5},{5,4},{6,7},{7,6},{8,9},{9,8},{10,11... | collective-permute-start | bytes 786440 | tf_op jit(solution)/shard_map/ppermute | solution.py:515
  45.3 20.7 %copy-start = (bf16[1,128,2048]{2,1,0:T(8,128)(2,1)S(1)}, bf16[1,128,2048]{2,1,0:T(8,128)(2,1)}, u32[]{:S(2)}) copy-start(bf16[1,128,2048]{2,1,0:T(8,128)(2,1)} %param.15) | copy-start | bytes 1572868
  45.3 20.7 %collective-permute-start.20 = (f32[64,2048]{1,0:T(8,128)S(1)}, f32[64,2048]{1,0:T(8,128)S(1)}, u32[]{:S(2)}, u32[]{:S(2)}) collective-permute-start(f32[64,2048]{1,0:T(8,128)S(1)} %get-tuple-element.126), channel_id=1, source_target_pairs={{0,32},{32,64},{64,96},{96,0},{1,33},{33,65},{65,97},{97,1},{2,34}... | collective-permute-start | bytes 1572872 | tf_op jit(solution)/shard_map/ppermute | solution.py:529
  45.8 20.2 %collective-permute-start.21 = (f32[64,2048]{1,0:T(8,128)S(1)}, f32[64,2048]{1,0:T(8,128)S(1)}, u32[]{:S(2)}, u32[]{:S(2)}) collective-permute-start(f32[64,2048]{1,0:T(8,128)S(1)} %get-tuple-element.127), channel_id=1, source_target_pairs={{0,96},{32,0},{64,32},{96,64},{1,97},{33,1},{65,33},{97,65},{2,98}... | collective-permute-start | bytes 1572872 | tf_op jit(solution)/shard_map/ppermute | solution.py:529
  49.0 1.8 %collective-permute-start.11 = (f32[4,128,128]{2,1,0:T(8,128)S(1)}, f32[4,128,128]{2,1,0:T(8,128)S(1)}, u32[]{:S(2)}, u32[]{:S(2)}) collective-permute-start(f32[4,128,128]{2,1,0:T(8,128)S(1)} %get-tuple-element.105), channel_id=1, source_target_pairs={{0,1},{1,0},{2,3},{3,2},{4,5},{5,4},{6,7},{7,6},{8,9},{9,8},{10,11... | collective-permute-start | bytes 786440 | tf_op jit(solution)/shard_map/ppermute | solution.py:515
  51.2 4.7 %collective-permute-start.12 = (f32[128,128]{1,0:T(8,128)S(1)}, f32[128,128]{1,0:T(8,128)S(1)}, u32[]{:S(2)}, u32[]{:S(2)}) collective-permute-start(f32[128,128]{1,0:T(8,128)S(1)} %get-tuple-element.116), channel_id=1, source_target_pairs={{0,2},{1,3},{2,4},{3,5},{4,6},{5,7},{6,0},{7,1},{8,10},{9,11},{10,... | collective-permute-start | bytes 196616 | tf_op jit(solution)/shard_map/ppermute | solution.py:519
  51.3 5.7 %collective-permute-start.13 = (f32[128,128]{1,0:T(8,128)S(1)}, f32[128,128]{1,0:T(8,128)S(1)}, u32[]{:S(2)}, u32[]{:S(2)}) collective-permute-start(f32[128,128]{1,0:T(8,128)S(1)} %get-tuple-element.117), channel_id=1, source_target_pairs={{0,4},{1,5},{2,6},{3,7},{4,0},{5,1},{6,2},{7,3},{8,12},{9,13},{10,... | collective-permute-start | bytes 196616 | tf_op jit(solution)/shard_map/ppermute | solution.py:519
  54.0 3.9 %collective-permute-start.14 = (f32[128,128]{1,0:T(8,128)S(1)}, f32[128,128]{1,0:T(8,128)S(1)}, u32[]{:S(2)}, u32[]{:S(2)}) collective-permute-start(f32[128,128]{1,0:T(8,128)S(1)} %get-tuple-element.118), channel_id=1, source_target_pairs={{0,6},{1,7},{2,0},{3,1},{4,2},{5,3},{6,4},{7,5},{8,14},{9,15},{10,... | collective-permute-start | bytes 196616 | tf_op jit(solution)/shard_map/ppermute | solution.py:519
  55.9 5.8 %collective-permute-start.15 = (f32[128,256]{1,0:T(8,128)S(1)}, f32[128,256]{1,0:T(8,128)S(1)}, u32[]{:S(2)}, u32[]{:S(2)}) collective-permute-start(f32[128,256]{1,0:T(8,128)S(1)} %get-tuple-element.123), channel_id=1, source_target_pairs={{0,32},{32,64},{64,96},{96,0},{1,33},{33,65},{65,97},{97,1},{2,34}... | collective-permute-start | bytes 393224 | tf_op jit(solution)/shard_map/ppermute | solution.py:529
  56.9 9.1 %collective-permute-start.16 = (f32[128,256]{1,0:T(8,128)S(1)}, f32[128,256]{1,0:T(8,128)S(1)}, u32[]{:S(2)}, u32[]{:S(2)}) collective-permute-start(f32[128,256]{1,0:T(8,128)S(1)} %get-tuple-element.124), channel_id=1, source_target_pairs={{0,64},{32,96},{64,0},{96,32},{1,65},{33,97},{65,1},{97,33},{2,66}... | collective-permute-start | bytes 393224 | tf_op jit(solution)/shard_map/ppermute | solution.py:529
  57.9 8.1 %collective-permute-start.17 = (f32[128,256]{1,0:T(8,128)S(1)}, f32[128,256]{1,0:T(8,128)S(1)}, u32[]{:S(2)}, u32[]{:S(2)}) collective-permute-start(f32[128,256]{1,0:T(8,128)S(1)} %get-tuple-element.125), channel_id=1, source_target_pairs={{0,96},{32,0},{64,32},{96,64},{1,97},{33,1},{65,33},{97,65},{2,98}... | collective-permute-start | bytes 393224 | tf_op jit(solution)/shard_map/ppermute | solution.py:529
  61.1 14.8 %copy-start.13 = (bf16[1024,2048]{1,0:T(8,128)(2,1)S(1)}, bf16[1024,2048]{1,0:T(8,128)(2,1)}, u32[]{:S(2)}) copy-start(bf16[1024,2048]{1,0:T(8,128)(2,1)} %param.14) | copy-start | bytes 12582916
  67.3 5.4 %collective-permute-start.22 = (f32[16,8,2048]{2,1,0:T(8,128)S(1)}, f32[16,8,2048]{2,1,0:T(8,128)S(1)}, u32[]{:S(2)}, u32[]{:S(2)}) collective-permute-start(f32[16,8,2048]{2,1,0:T(8,128)S(1)} %get-tuple-element.129), channel_id=1, source_target_pairs={{0,1},{1,0},{2,3},{3,2},{4,5},{5,4},{6,7},{7,6},{8,9},{9,8},{10,11... | collective-permute-start | bytes 3145736 | tf_op jit(solution)/shard_map/ppermute | solution.py:515
  68.3 5.9 %collective-permute-start.26 = (f32[128,128]{1,0:T(8,128)S(1)}, f32[128,128]{1,0:T(8,128)S(1)}, u32[]{:S(2)}, u32[]{:S(2)}) collective-permute-start(f32[128,128]{1,0:T(8,128)S(1)} %get-tuple-element.120.refs_0_.refs_2_), channel_id=1, source_target_pairs={{0,8},{1,9},{2,10},{3,11},{4,12},{5,13},{6,14},{7,15},{8,16},{9,17... | collective-permute-start | bytes 196616 | tf_op jit(solution)/shard_map/ppermute | solution.py:524
  69.4 7.3 %collective-permute-start.27 = (f32[128,128]{1,0:T(8,128)S(1)}, f32[128,128]{1,0:T(8,128)S(1)}, u32[]{:S(2)}, u32[]{:S(2)}) collective-permute-start(f32[128,128]{1,0:T(8,128)S(1)} %get-tuple-element.120.refs_0_.refs_2_), channel_id=1, source_target_pairs={{0,16},{1,17},{2,18},{3,19},{4,20},{5,21},{6,22},{7,23},{8,24},{9,... | collective-permute-start | bytes 196616 | tf_op jit(solution)/shard_map/ppermute | solution.py:524
  71.7 4.9 %collective-permute-start.28 = (f32[128,128]{1,0:T(8,128)S(1)}, f32[128,128]{1,0:T(8,128)S(1)}, u32[]{:S(2)}, u32[]{:S(2)}) collective-permute-start(f32[128,128]{1,0:T(8,128)S(1)} %get-tuple-element.120.refs_0_.refs_2_), channel_id=1, source_target_pairs={{0,24},{1,25},{2,26},{3,27},{4,28},{5,29},{6,30},{7,31},{8,0},{9,1... | collective-permute-start | bytes 196616 | tf_op jit(solution)/shard_map/ppermute | solution.py:524
  72.9 8.7 %collective-permute-start.23 = (f32[4,8,2048]{2,1,0:T(8,128)S(1)}, f32[4,8,2048]{2,1,0:T(8,128)S(1)}, u32[]{:S(2)}, u32[]{:S(2)}) collective-permute-start(f32[4,8,2048]{2,1,0:T(8,128)S(1)} %get-tuple-element.131), channel_id=1, source_target_pairs={{0,8},{1,9},{2,10},{3,11},{4,12},{5,13},{6,14},{7,15},{8,16},{9,17... | collective-permute-start | bytes 786440 | tf_op jit(solution)/shard_map/ppermute | solution.py:524
  73.4 12.8 %collective-permute-start.24 = (f32[4,8,2048]{2,1,0:T(8,128)S(1)}, f32[4,8,2048]{2,1,0:T(8,128)S(1)}, u32[]{:S(2)}, u32[]{:S(2)}) collective-permute-start(f32[4,8,2048]{2,1,0:T(8,128)S(1)} %get-tuple-element.132), channel_id=1, source_target_pairs={{0,16},{1,17},{2,18},{3,19},{4,20},{5,21},{6,22},{7,23},{8,24},{9,... | collective-permute-start | bytes 786440 | tf_op jit(solution)/shard_map/ppermute | solution.py:524
  74.2 23.0 %copy-start.7 = (bf16[1,128,1024]{2,1,0:T(8,128)(2,1)S(1)}, bf16[1,128,1024]{2,1,0:T(8,128)(2,1)}, u32[]{:S(2)}) copy-start(bf16[1,128,1024]{2,1,0:T(8,128)(2,1)} %param.10) | copy-start | bytes 786436
  74.2 13.3 %collective-permute-start.25 = (f32[4,8,2048]{2,1,0:T(8,128)S(1)}, f32[4,8,2048]{2,1,0:T(8,128)S(1)}, u32[]{:S(2)}, u32[]{:S(2)}) collective-permute-start(f32[4,8,2048]{2,1,0:T(8,128)S(1)} %get-tuple-element.133), channel_id=1, source_target_pairs={{0,24},{1,25},{2,26},{3,27},{4,28},{5,29},{6,30},{7,31},{8,0},{9,1... | collective-permute-start | bytes 786440 | tf_op jit(solution)/shard_map/ppermute | solution.py:524
  76.6 24.4 %copy-start.4 = (bf16[128,2048]{1,0:T(8,128)(2,1)}, bf16[128,2048]{1,0:T(8,128)(2,1)S(1)}, u32[]{:S(2)}) copy-start(bf16[128,2048]{1,0:T(8,128)(2,1)S(1)} %convolution_convert_fusion.refs_1_) | copy-start | bytes 1572868
  77.6 10.0 %collective-permute-start.29 = (f32[128,128]{1,0:T(8,128)S(1)}, f32[128,128]{1,0:T(8,128)S(1)}, u32[]{:S(2)}, u32[]{:S(2)}) collective-permute-start(f32[128,128]{1,0:T(8,128)S(1)} %get-tuple-element.138), channel_id=1, source_target_pairs={{0,2},{1,3},{2,4},{3,5},{4,6},{5,7},{6,0},{7,1},{8,10},{9,11},{10,... | collective-permute-start | bytes 196616 | tf_op jit(solution)/shard_map/ppermute | solution.py:519
  77.8 9.8 %collective-permute-start.30 = (f32[128,128]{1,0:T(8,128)S(1)}, f32[128,128]{1,0:T(8,128)S(1)}, u32[]{:S(2)}, u32[]{:S(2)}) collective-permute-start(f32[128,128]{1,0:T(8,128)S(1)} %get-tuple-element.139), channel_id=1, source_target_pairs={{0,4},{1,5},{2,6},{3,7},{4,0},{5,1},{6,2},{7,3},{8,12},{9,13},{10,... | collective-permute-start | bytes 196616 | tf_op jit(solution)/shard_map/ppermute | solution.py:519
  81.6 6.0 %collective-permute-start.31 = (f32[128,128]{1,0:T(8,128)S(1)}, f32[128,128]{1,0:T(8,128)S(1)}, u32[]{:S(2)}, u32[]{:S(2)}) collective-permute-start(f32[128,128]{1,0:T(8,128)S(1)} %get-tuple-element.140), channel_id=1, source_target_pairs={{0,6},{1,7},{2,0},{3,1},{4,2},{5,3},{6,4},{7,5},{8,14},{9,15},{10,... | collective-permute-start | bytes 196616 | tf_op jit(solution)/shard_map/ppermute | solution.py:519
  87.9 9.3 %collective-permute-start.32 = (f32[4,128,128]{2,1,0:T(8,128)S(1)}, f32[4,128,128]{2,1,0:T(8,128)S(1)}, u32[]{:S(2)}, u32[]{:S(2)}) collective-permute-start(f32[4,128,128]{2,1,0:T(8,128)S(1)} %get-tuple-element.143), channel_id=1, source_target_pairs={{0,1},{1,0},{2,3},{3,2},{4,5},{5,4},{6,7},{7,6},{8,9},{9,8},{10,11... | collective-permute-start | bytes 786440 | tf_op jit(solution)/shard_map/ppermute | solution.py:515
  93.1 7.9 %collective-permute-start.33 = (f32[8,2048]{1,0:T(8,128)S(1)}, f32[8,2048]{1,0:T(8,128)S(1)}, u32[]{:S(2)}, u32[]{:S(2)}) collective-permute-start(f32[8,2048]{1,0:T(8,128)S(1)} %get-tuple-element.160), channel_id=1, source_target_pairs={{0,2},{1,3},{2,4},{3,5},{4,6},{5,7},{6,0},{7,1},{8,10},{9,11},{10,... | collective-permute-start | bytes 196616 | tf_op jit(solution)/shard_map/ppermute | solution.py:519
  93.1 7.9 %collective-permute-start.34 = (f32[8,2048]{1,0:T(8,128)S(1)}, f32[8,2048]{1,0:T(8,128)S(1)}, u32[]{:S(2)}, u32[]{:S(2)}) collective-permute-start(f32[8,2048]{1,0:T(8,128)S(1)} %get-tuple-element.161), channel_id=1, source_target_pairs={{0,4},{1,5},{2,6},{3,7},{4,0},{5,1},{6,2},{7,3},{8,12},{9,13},{10,... | collective-permute-start | bytes 196616 | tf_op jit(solution)/shard_map/ppermute | solution.py:519
  97.1 3.9 %collective-permute-start.35 = (f32[8,2048]{1,0:T(8,128)S(1)}, f32[8,2048]{1,0:T(8,128)S(1)}, u32[]{:S(2)}, u32[]{:S(2)}) collective-permute-start(f32[8,2048]{1,0:T(8,128)S(1)} %get-tuple-element.162), channel_id=1, source_target_pairs={{0,6},{1,7},{2,0},{3,1},{4,2},{5,3},{6,4},{7,5},{8,14},{9,15},{10,... | collective-permute-start | bytes 196616 | tf_op jit(solution)/shard_map/ppermute | solution.py:519
